TPU v7x, 32 devices: a whole 2x2x4 slice. The times are simulated.
32 devices in a mesh: seq: 8 (over y, x, core), head: 4 (over z).
Axes of the slice: x: 2, y: 2, z: 4, core: 2. Of those that a mesh axis runs over, the one named last changes fastest.
Arguments:
- tokens: bfloat16 [4096, 2, 2048], P(('seq', 'head')), may hold values from -6 to 6
- cotangent: bfloat16 [4096, 2, 2048], P(('seq', 'head')), may hold values from -6 to 6
- lengths: int32 [2], replicated, may hold values from 1024 to 4096, as said below
- query_weight: bfloat16 [2048, 2048], P(None, 'head'), may hold values from -0.125 to 0.125
- key_weight: bfloat16 [2048, 1024], P(None, 'head'), may hold values from -0.125 to 0.125
- value_weight: bfloat16 [2048, 1024], P(None, 'head'), may hold values from -0.125 to 0.125
- gating_weight: bfloat16 [2048, 2048], P(None, 'head'), may hold values from -0.125 to 0.125
- output_weight: bfloat16 [2048, 2048], P('head'), may hold values from -1.5 to 1.5
- swiglu_gate: bfloat16 [2048, 6144], P(None, 'head'), may hold values from -0.125 to 0.125
- swiglu_lift: bfloat16 [2048, 6144], P(None, 'head'), may hold values from -0.125 to 0.125
- swiglu_down: bfloat16 [6144, 2048], P('head'), may hold values from -0.078125 to 0.078125
- input_gain: float32 [2048], replicated, may hold values from 0.25 to 1.75
- middle_gain: float32 [2048], replicated, may hold values from 0.25 to 1.75
- query_gain: float32 [128], replicated, may hold values from 0.25 to 1.75
- key_gain: float32 [128], replicated, may hold values from 0.25 to 1.75
Outputs:
- output: bfloat16 [4096, 2, 2048], P(('seq', 'head'))
- input_grad: float32 [4096, 2, 2048], P(('seq', 'head'))
- query_weight_grad: float32 [2048, 2048], P(None, 'head')
- key_weight_grad: float32 [2048, 1024], P(None, 'head')
- value_weight_grad: float32 [2048, 1024], P(None, 'head')
- gating_weight_grad: float32 [2048, 2048], P(None, 'head')
- output_weight_grad: float32 [2048, 2048], P('head')
- swiglu_gate_grad: float32 [2048, 6144], P(None, 'head')
- swiglu_lift_grad: float32 [2048, 6144], P(None, 'head')
- swiglu_down_grad: float32 [6144, 2048], P('head')
- input_gain_grad: float32 [2048], P('head')
- middle_gain_grad: float32 [2048], P('head')
- query_gain_grad: float32 [128], P('head')
- key_gain_grad: float32 [128], P('head')
Inputs may be any that keep to these rules, and one draw needn't show every extreme that they name: `lengths`: one sequence, chosen by the seed, has exactly 4096 tokens; the others have 4096 // 4 or more.
All inputs are finite; a program needn't handle non-finite values.
Results may differ from a plain program's by a relative error of at most 0.024.
Values may be sent and summed in bfloat16 or wider, within the bound.
A program may use at most 320 MiB of HBM per device.

v0:
```python
import jax
import jax.numpy as jnp
from jax import lax
from jax.sharding import PartitionSpec as P

EPS = 1e-06
THETA = 1000000.0


def from_behind(value, axis, steps):
    count = lax.axis_size(axis)
    initial, last = (max(0, -steps), min(count, count - steps))
    return lax.ppermute(value, axis, [(source, source + steps) for source in range(initial, last)])


def passed_along(block, axis, distance):
    devices = range(lax.axis_size(axis))
    route = [((i - distance) % len(devices), i) for i in devices]
    return lax.ppermute(block, axis, route)


def norm_rows(values, norm_gain):
    return values * lax.rsqrt(jnp.mean(values * values, axis=-1, keepdims=True) + EPS) * norm_gain


def rotate_norm(raw_part, norm_gain, cosine, sine):
    normed = norm_rows(raw_part, norm_gain)
    half_dim = raw_part.shape[-1] // 2
    first = normed[..., :half_dim]
    second = normed[..., half_dim:]
    return jnp.concatenate(
        [first * cosine - second * sine, second * cosine + first * sine], axis=-1
    )


def turn_tables(positions, head_dim, middle_dims):
    half_dim = head_dim // 2
    inverse = THETA ** (-(jnp.arange(half_dim, dtype=jnp.float32) * 2.0) / head_dim)
    angles = positions.astype(jnp.float32)[:, None] * inverse[None, :]
    table_shape = (positions.shape[0],) + (1,) * middle_dims + (half_dim,)
    return (jnp.cos(angles).reshape(table_shape), jnp.sin(angles).reshape(table_shape))


def block_weights(queries, keys_now, key_start, query_start, lengths, scale_factor):
    raw_scores = jnp.einsum(
        "qbcgd,kbcd->bcgqk", queries, keys_now, preferred_element_type=jnp.float32
    )
    key_pos = key_start + jnp.arange(keys_now.shape[0], dtype=jnp.int32)
    query_pos = query_start + jnp.arange(queries.shape[0], dtype=jnp.int32)
    causal = key_pos[None, :] <= query_pos[:, None]
    live_keys = key_pos[None, :] < lengths[:, None]
    allowed = causal[None, None, None, :, :] & live_keys[:, None, None, None, :]
    return jnp.where(allowed, jnp.exp(raw_scores * scale_factor), 0.0)


def on_device(
    tokens,
    cotangent,
    lengths,
    query_weight,
    key_weight,
    value_weight,
    gating_weight,
    output_weight,
    swiglu_gate,
    swiglu_lift,
    swiglu_down,
    input_gain,
    middle_gain,
    query_gain,
    key_gain,
):
    block_count = lax.axis_size("seq")
    block_index = lax.axis_index("seq")
    part_index = lax.axis_index("head")
    local_rows = tokens.shape[0]
    batch_size = tokens.shape[1]
    model_dim = tokens.shape[2]
    head_dim = query_gain.shape[0]
    block_rows = local_rows * lax.axis_size("head")
    flat_rows = block_rows * batch_size
    key_heads = key_weight.shape[1] // head_dim
    group_size = query_weight.shape[1] // head_dim // key_heads
    scale_factor = head_dim ** (-0.5)
    query_start = block_index * block_rows
    query_last = query_start + block_rows - 1
    positions = query_start + jnp.arange(block_rows, dtype=jnp.int32)
    query_cos, query_sin = turn_tables(positions, head_dim, 3)
    key_cos, key_sin = turn_tables(positions, head_dim, 2)
    gathered = lax.all_gather(tokens, "head", axis=0, tiled=True)
    inputs = gathered.astype(jnp.float32)
    normed_full, input_pull = jax.vjp(norm_rows, inputs, input_gain)
    normed = normed_full.astype(jnp.bfloat16).reshape(flat_rows, model_dim)
    query_raw = jnp.dot(normed, query_weight, preferred_element_type=jnp.float32).reshape(
        block_rows, batch_size, key_heads, group_size, head_dim
    )
    key_raw = jnp.dot(normed, key_weight, preferred_element_type=jnp.float32).reshape(
        block_rows, batch_size, key_heads, head_dim
    )
    value_low = (
        jnp.dot(normed, value_weight, preferred_element_type=jnp.float32)
        .astype(jnp.bfloat16)
        .reshape(block_rows, batch_size, key_heads, head_dim)
    )
    gate_raw = jnp.dot(normed, gating_weight, preferred_element_type=jnp.float32)
    query_rot, query_pull = jax.vjp(
        lambda raw_part, norm_gain: rotate_norm(raw_part, norm_gain, query_cos, query_sin),
        query_raw,
        query_gain,
    )
    key_rot, key_pull = jax.vjp(
        lambda raw_part, norm_gain: rotate_norm(raw_part, norm_gain, key_cos, key_sin),
        key_raw,
        key_gain,
    )
    query_low = query_rot.astype(jnp.bfloat16)
    key_low = key_rot.astype(jnp.bfloat16)

    def attend_block(accum_state, keys_now, values_now, key_start):
        weights_now = block_weights(
            query_low, keys_now, key_start, query_start, lengths, scale_factor
        )
        unscaled = accum_state[0] + jnp.einsum(
            "bcgqk,kbcd->qbcgd",
            weights_now.astype(jnp.bfloat16),
            values_now,
            preferred_element_type=jnp.float32,
        )
        return (unscaled, accum_state[1] + jnp.sum(weights_now, axis=-1))

    def maybe_attend(accum_state, keys_now, values_now, key_start):
        usable = (key_start >= 0) & (key_start <= query_last)
        return lax.cond(
            usable,
            lambda inner_state: attend_block(inner_state, keys_now, values_now, key_start),
            lambda inner_state: inner_state,
            accum_state,
        )

    zero_accum = (
        jnp.zeros((block_rows, batch_size, key_heads, group_size, head_dim), jnp.float32),
        jnp.zeros((batch_size, key_heads, group_size, block_rows), jnp.float32),
    )
    first_state = maybe_attend(zero_accum, key_low, value_low, query_start)

    def forward_turn(step_now, state_now):
        keys_now, values_now, accum_state = state_now
        keys_now, values_now = from_behind((keys_now, values_now), "seq", 1)
        source = block_index - step_now
        return (
            keys_now,
            values_now,
            maybe_attend(accum_state, keys_now, values_now, source * block_rows),
        )

    final_state = lax.fori_loop(1, block_count, forward_turn, (key_low, value_low, first_state))
    accum_state = final_state[2]
    unscaled, summed = accum_state
    inverse_sum = jnp.transpose(1.0 / summed, (3, 0, 1, 2))
    attended = unscaled * inverse_sum[..., None]
    attended_flat = attended.reshape(flat_rows, key_heads * group_size * head_dim)
    acted_full, gate_pull = jax.vjp(
        lambda att_part, gate_part: att_part * jax.nn.sigmoid(gate_part), attended_flat, gate_raw
    )
    acted = acted_full.astype(jnp.bfloat16)
    rows_now = acted
    attention_out = lax.psum_scatter(
        jnp.dot(rows_now, output_weight, preferred_element_type=jnp.float32).reshape(
            lax.axis_size("head") * local_rows, batch_size, model_dim
        ),
        "head",
        scatter_dimension=0,
        tiled=True,
    )
    middle = tokens.astype(jnp.float32) + attention_out
    mid_rows = lax.all_gather(middle.astype(jnp.bfloat16), "head", axis=0, tiled=True)
    normed_mid_full, mid_pull = jax.vjp(norm_rows, mid_rows.astype(jnp.float32), middle_gain)
    normed_mid = normed_mid_full.astype(jnp.bfloat16).reshape(flat_rows, model_dim)
    gate_units = jnp.dot(normed_mid, swiglu_gate, preferred_element_type=jnp.float32)
    lift_units = jnp.dot(normed_mid, swiglu_lift, preferred_element_type=jnp.float32)
    hidden_full, unit_pull = jax.vjp(
        lambda gate_part, lift_part: jax.nn.silu(gate_part) * lift_part, gate_units, lift_units
    )
    hidden = hidden_full.astype(jnp.bfloat16)
    rows_now = hidden
    units_out = lax.psum_scatter(
        jnp.dot(rows_now, swiglu_down, preferred_element_type=jnp.float32)
        .reshape(local_rows * lax.axis_size("head"), batch_size, model_dim)
        .astype(jnp.bfloat16),
        "head",
        scatter_dimension=0,
        tiled=True,
    ).astype(jnp.float32)
    local_pos = query_start + part_index * local_rows + jnp.arange(local_rows, dtype=jnp.int32)
    valid = (local_pos[:, None] < lengths[None, :]).astype(jnp.float32)[..., None]
    output = (valid * (middle + units_out)).astype(jnp.bfloat16)
    masked_grad = valid * cotangent.astype(jnp.float32)
    down_rows = lax.all_gather(
        masked_grad.astype(jnp.bfloat16), "head", axis=0, tiled=True
    ).reshape(flat_rows, model_dim)
    down_weight_grad = jnp.dot(hidden.T, down_rows, preferred_element_type=jnp.float32)
    hidden_grad = jnp.dot(down_rows, swiglu_down.T, preferred_element_type=jnp.float32)
    gate_units_grad, lift_units_grad = unit_pull(hidden_grad)
    gate_units_low = gate_units_grad.astype(jnp.bfloat16)
    lift_units_low = lift_units_grad.astype(jnp.bfloat16)
    gate_weight_grad = jnp.dot(normed_mid.T, gate_units_low, preferred_element_type=jnp.float32)
    lift_weight_grad = jnp.dot(normed_mid.T, lift_units_low, preferred_element_type=jnp.float32)
    normed_mid_grad = jnp.dot(
        gate_units_low, swiglu_gate.T, preferred_element_type=jnp.float32
    ) + jnp.dot(lift_units_low, swiglu_lift.T, preferred_element_type=jnp.float32)
    mid_input_grad, middle_gain_part = mid_pull(
        normed_mid_grad.reshape(block_rows, batch_size, model_dim)
    )
    middle_backward, middle_gain_slice = (
        lax.psum_scatter(mid_input_grad, "head", scatter_dimension=0, tiled=True),
        lax.psum_scatter(middle_gain_part, "head", scatter_dimension=0, tiled=True),
    )
    residual_grad = masked_grad + middle_backward
    residual_full = lax.all_gather(
        residual_grad.astype(jnp.bfloat16), "head", axis=0, tiled=True
    ).reshape(flat_rows, model_dim)
    output_weight_grad = jnp.dot(acted.T, residual_full, preferred_element_type=jnp.float32)
    acted_grad = jnp.dot(residual_full, output_weight.T, preferred_element_type=jnp.float32)
    attended_grad, gate_raw_grad = gate_pull(acted_grad)
    gate_raw_low = gate_raw_grad.astype(jnp.bfloat16)
    attended_grad_heads = attended_grad.reshape(
        block_rows, batch_size, key_heads, group_size, head_dim
    )
    scaled_low = (attended_grad_heads * inverse_sum[..., None]).astype(jnp.bfloat16)
    correction = jnp.transpose(
        jnp.sum(attended_grad_heads * attended, axis=-1) * inverse_sum, (1, 2, 3, 0)
    )

    def grad_block(state_now, keys_now, values_now, key_start):
        query_acc, key_acc, value_acc = state_now
        weights_now = block_weights(
            query_low, keys_now, key_start, query_start, lengths, scale_factor
        )
        prob_grad = jnp.einsum(
            "qbcgd,kbcd->bcgqk", scaled_low, values_now, preferred_element_type=jnp.float32
        )
        score_low = (scale_factor * weights_now * (prob_grad - correction[..., None])).astype(
            jnp.bfloat16
        )
        query_acc = query_acc + jnp.einsum(
            "bcgqk,kbcd->qbcgd", score_low, keys_now, preferred_element_type=jnp.float32
        )
        key_acc = key_acc + jnp.einsum(
            "bcgqk,qbcgd->kbcd", score_low, query_low, preferred_element_type=jnp.float32
        )
        value_acc = value_acc + jnp.einsum(
            "bcgqk,qbcgd->kbcd",
            weights_now.astype(jnp.bfloat16),
            scaled_low,
            preferred_element_type=jnp.float32,
        )
        return (query_acc, key_acc, value_acc)

    def maybe_grad(state_now, keys_now, values_now, key_start):
        return lax.cond(
            key_start <= query_last,
            lambda inner_state: grad_block(inner_state, keys_now, values_now, key_start),
            lambda inner_state: inner_state,
            state_now,
        )

    zero_query = jnp.zeros((block_rows, batch_size, key_heads, group_size, head_dim), jnp.float32)
    zero_keys = jnp.zeros((block_rows, batch_size, key_heads, head_dim), jnp.float32)

    def backward_turn(step_now, state_now):
        keys_now, values_now, key_acc, value_acc, query_acc = state_now
        source = (block_index - step_now) % block_count
        query_acc, key_acc, value_acc = maybe_grad(
            (query_acc, key_acc, value_acc), keys_now, values_now, source * block_rows
        )
        keys_now, values_now, key_acc, value_acc = (
            passed_along(keys_now, "seq", 1),
            passed_along(values_now, "seq", 1),
            passed_along(key_acc.astype(jnp.bfloat16), "seq", 1).astype(key_acc.dtype),
            passed_along(value_acc.astype(jnp.bfloat16), "seq", 1).astype(value_acc.dtype),
        )
        return (keys_now, values_now, key_acc, value_acc, query_acc)

    final_back = lax.fori_loop(
        0, block_count, backward_turn, (key_low, value_low, zero_keys, zero_keys, zero_query)
    )
    key_rot_grad = final_back[2]
    value_grad = final_back[3]
    query_rot_grad = final_back[4]
    query_raw_grad, query_gain_part = query_pull(query_rot_grad)
    key_raw_grad, key_gain_part = key_pull(key_rot_grad)
    query_grad_low = query_raw_grad.reshape(flat_rows, -1).astype(jnp.bfloat16)
    key_grad_low = key_raw_grad.reshape(flat_rows, -1).astype(jnp.bfloat16)
    value_grad_low = value_grad.reshape(flat_rows, -1).astype(jnp.bfloat16)
    query_weight_grad = jnp.dot(normed.T, query_grad_low, preferred_element_type=jnp.float32)
    key_weight_grad = jnp.dot(normed.T, key_grad_low, preferred_element_type=jnp.float32)
    value_weight_grad = jnp.dot(normed.T, value_grad_low, preferred_element_type=jnp.float32)
    gating_weight_grad = jnp.dot(normed.T, gate_raw_low, preferred_element_type=jnp.float32)
    normed_grad = jnp.dot(query_grad_low, query_weight.T, preferred_element_type=jnp.float32)
    normed_grad = normed_grad + jnp.dot(
        key_grad_low, key_weight.T, preferred_element_type=jnp.float32
    )
    normed_grad = normed_grad + jnp.dot(
        value_grad_low, value_weight.T, preferred_element_type=jnp.float32
    )
    normed_grad = normed_grad + jnp.dot(
        gate_raw_low, gating_weight.T, preferred_element_type=jnp.float32
    )
    input_part, input_gain_part = input_pull(normed_grad.reshape(block_rows, batch_size, model_dim))
    input_backward, input_gain_slice, query_gain_slice, key_gain_slice = (
        lax.psum_scatter(
            input_part.astype(jnp.bfloat16), "head", scatter_dimension=0, tiled=True
        ).astype(jnp.float32),
        lax.psum_scatter(
            input_gain_part.astype(jnp.bfloat16), "head", scatter_dimension=0, tiled=True
        ).astype(jnp.float32),
        lax.psum_scatter(
            query_gain_part.astype(jnp.bfloat16), "head", scatter_dimension=0, tiled=True
        ).astype(jnp.float32),
        lax.psum_scatter(
            key_gain_part.astype(jnp.bfloat16), "head", scatter_dimension=0, tiled=True
        ).astype(jnp.float32),
    )
    input_grad = residual_grad + input_backward
    summed_grads = (
        lax.psum(query_weight_grad.astype(jnp.bfloat16), "seq").astype(jnp.float32),
        lax.psum(key_weight_grad.astype(jnp.bfloat16), "seq").astype(jnp.float32),
        lax.psum(value_weight_grad.astype(jnp.bfloat16), "seq").astype(jnp.float32),
        lax.psum(gating_weight_grad.astype(jnp.bfloat16), "seq").astype(jnp.float32),
        lax.psum(output_weight_grad.astype(jnp.bfloat16), "seq").astype(jnp.float32),
        lax.psum(gate_weight_grad.astype(jnp.bfloat16), "seq").astype(jnp.float32),
        lax.psum(lift_weight_grad.astype(jnp.bfloat16), "seq").astype(jnp.float32),
        lax.psum(down_weight_grad.astype(jnp.bfloat16), "seq").astype(jnp.float32),
        lax.psum(input_gain_slice.astype(jnp.bfloat16), "seq").astype(jnp.float32),
        lax.psum(middle_gain_slice.astype(jnp.bfloat16), "seq").astype(jnp.float32),
        lax.psum(query_gain_slice.astype(jnp.bfloat16), "seq").astype(jnp.float32),
        lax.psum(key_gain_slice.astype(jnp.bfloat16), "seq").astype(jnp.float32),
    )
    return (output, input_grad) + tuple(summed_grads)


def solution(mesh):
    return jax.shard_map(
        on_device,
        mesh=mesh,
        in_specs=(
            P(("seq", "head"), None, None),
            P(("seq", "head"), None, None),
            P(),
            P(None, "head"),
            P(None, "head"),
            P(None, "head"),
            P(None, "head"),
            P("head", None),
            P(None, "head"),
            P(None, "head"),
            P("head", None),
            P(),
            P(),
            P(),
            P(),
        ),
        out_specs=(
            P(("seq", "head"), None, None),
            P(("seq", "head"), None, None),
            P(None, "head"),
            P(None, "head"),
            P(None, "head"),
            P(None, "head"),
            P("head", None),
            P(None, "head"),
            P(None, "head"),
            P("head", None),
            P("head"),
            P("head"),
            P("head"),
            P("head"),
        ),
        check_vma=False,
    )
```

profile of v0, /device:TPU:0, one launch (start us, length us, event | category | flops | bytes accessed | tf_op | source)
XLA Modules:
  0.0 2488.7 jit_solution(14870737787049169619)
XLA Ops:
  14.8 78.3 %all-gather.5.cloned.1.call-done = bf16[512,2,2048]{2,1,0:T(2,128)(2,1)} async-done(((bf16[128,2,2048]{2,1,0:T(2,128)(2,1)}), bf16[512,2,2048]{2,1,0:T(2,128)(2,1)}) %all-gather.5.cloned.1.call-update) | async-done | bytes 4194320 | tf_op jit(solution)/shard_map/all_gather | solution.py:90
  100.0 8.8 fusion.150
  137.4 8.7 fusion.56
  169.9 169.5 %while.43 = (s32[]{:T(128)}, bf16[512,2,2,128]{3,0,2,1:T(8,128)(2,1)}, bf16[512,2,2,128]{3,0,2,1:T(8,128)(2,1)}, f32[512,2,2,2,128]{4,0,3,2,1:T(8,128)}, f32[2,2...) while((s32[]{:T(128)}, ...), condition=%wide.region_10.11_spmd, body=%wide.region_6.10_spmd.sunk | while | flops 1087637504 | bytes 48312752 | solution.py:156
  181.4 20.5 collective-permute-start.1
  211.1 11.0 collective-permute-start.1
  222.0 13.9 collective-permute-start
  240.7 11.0 collective-permute-start.1
  260.9 17.7 collective-permute-start.1
  287.8 11.9 collective-permute-start.1
  299.7 10.3 collective-permute-start
  314.7 15.5 collective-permute-start.1
  362.8 10.5 reshape.495
  378.0 314.0 %all-reduce.21.cloned.1.call-done = f32[512,2,2048]{2,1,0:T(2,128)} async-done(((f32[512,2,2048]{2,1,0:T(2,128)}), f32[512,2,2048]{2,1,0:T(2,128)}) %all-reduce.21.cloned.1.call-update) | async-done | bytes 8388624
  696.0 77.9 %all-gather.9.cloned.1.call-done = bf16[512,2,2048]{2,1,0:T(2,128)(2,1)} async-done(((bf16[128,2,2048]{2,1,0:T(2,128)(2,1)}), bf16[512,2,2048]{2,1,0:T(2,128)(2,1)}) %all-gather.9.cloned.1.call-update) | async-done | bytes 4194320 | tf_op jit(solution)/shard_map/all_gather | solution.py:198
  781.3 74.0 %all-gather.7.cloned.1.call-done = bf16[512,2,2048]{2,1,0:T(2,128)(2,1)} async-done(((bf16[128,2,2048]{2,1,0:T(2,128)(2,1)}), bf16[512,2,2048]{2,1,0:T(2,128)(2,1)}) %all-gather.7.cloned.1.call-update) | async-done | bytes 4194320 | tf_op jit(solution)/shard_map/all_gather | solution.py:176
  878.1 12.7 fusion.95
  890.8 10.5 fusion.94
  901.3 15.3 multiply_convert_fusion
  916.7 10.0 fusion.96
  926.7 11.0 convolution_add_fusion
  937.7 10.5 reshape.498
  948.3 13.8 fusion.55
  964.1 10.3 add_add_fusion.1
  974.4 289.5 %all-reduce.23.cloned.1.call-done = f32[512,2,2048]{2,1,0:T(2,128)} async-done(((f32[512,2,2048]{2,1,0:T(2,128)}), f32[512,2,2048]{2,1,0:T(2,128)}) %all-reduce.23.cloned.1.call-update) | async-done | bytes 8388624
  1268.0 11.0 convolution_convert_fusion.3
  1286.6 61.2 %all-gather.11.cloned.1.call-done = bf16[512,2,2048]{2,1,0:T(2,128)(2,1)} async-done(((bf16[128,2,2048]{2,1,0:T(2,128)(2,1)}), bf16[512,2,2048]{2,1,0:T(2,128)(2,1)}) %all-gather.11.cloned.1.call-update) | async-done | bytes 4194320 | tf_op jit(solution)/shard_map/all_gather | solution.py:219
  1371.0 373.8 %while.44 = (s32[]{:T(128)}, bf16[512,2,2,128]{3,0,2,1:T(8,128)(2,1)}, bf16[512,2,2,128]{3,0,2,1:T(8,128)(2,1)}, f32[512,2,2,128]{3,0,2,1:T(8,128)}, f32[512,2,2...) while((s32[]{:T(128)}, ...), condition=%wide.region_20.21_spmd.clone, body=%wide.region_17.20_spmd.clone.sunk | while | flops 2706638848 | bytes 85488368 | solution.py:284
  1375.3 14.7 conditional.8
  1427.2 13.0 collective-permute-start.5
  1475.2 17.1 collective-permute-start.4
  1526.4 15.7 collective-permute-start.2
  1577.2 18.0 collective-permute-start.3
  1670.0 10.9 collective-permute-done.5
  1715.4 11.9 collective-permute-done.5
  1770.3 9.0 add_add_fusion.2
  1779.2 10.6 reshape.501
  1789.8 13.1 fusion.57
  1803.3 10.8 fusion.58
  1814.1 11.9 convolution_convert_fusion.1
  1826.1 8.8 convolution_convert_fusion.2
  1834.9 9.0 convolution_convert_fusion
  1862.0 10.0 all-reduce.9
  1872.1 13.0 all-reduce.14
  1885.3 12.8 all-reduce.12
  1900.3 206.0 %all-reduce.27.cloned.1.call-done = (bf16[512,2,2048]{2,1,0:T(2,128)(2,1)}, bf16[512,2,2048]{2,1,0:T(2,128)(2,1)}) async-done(((bf16[512,2,2048]{2,1,0:T(2,128)(2,1)}, bf16[512,2,2048]{2,1,0:T(2,128)(2,1)}), (bf16[512,2,2048]{2,1,0:T(2,128)(2,1)}, bf16[512,2,2048]{2,1,0:T(2,128)(2,1)})) %all-reduce.27.cloned.1.call-update) | async-done | bytes 8388624
  2112.7 333.7 %all-reduce.25.cloned.1.call-done = (bf16[2048,512]{1,0:T(8,128)(2,1)}, bf16[2048,256]{1,0:T(8,128)(2,1)}, bf16[2048,256]{1,0:T(8,128)(2,1)}, bf16[2048,512]{1,0...) async-done(((bf16[2048,512]{1,0:T(8,128)(2,1)}, bf16[2048,256]{1,0:T(8,128)(2,1)}, ...) | async-done | bytes 27262992 | tf_op jit(solution)/shard_map/psum | solution.py:326
  2459.1 9.5 convert_element_type.296
  (474 shorter events, 592.3 us)
Async XLA Ops:
  7.2 85.9 %all-gather.5.cloned.1.call-start = ((), (), s32[]{:S(2)}) async-start(), calls=%async_computation | async-start | bytes 5242880 | tf_op jit(solution)/shard_map/all_gather | solution.py:90
  7.9 684.0 %all-reduce.21.cloned.1.call-start = ((), (), s32[]{:S(2)}) async-start(), calls=%async_computation.4 | async-start | bytes 16777216
  181.4 24.9 %collective-permute-start.1 = (bf16[512,2,2,128]{3,0,2,1:T(8,128)(2,1)}, bf16[512,2,2,128]{3,0,2,1:T(8,128)(2,1)}, u32[]{:S(2)}, u32[]{:S(2)}) collective-permute-start(bf16[512,2,2,128]{3,0,2,1:T(8,128)(2,1)} %get-tuple-element.1074), channel_id=1, source_target_pairs={{0,4},{4,8},{8,12},{12,16},{16,20},{20,24},{24,28},{1,5},{5,9},{9,... | collective-permute-start | bytes 1572872 | tf_op jit(solution)/shard_map/while/body/eval_jaxpr/ppermute | solution.py:13
  211.1 24.9 %collective-permute-start.1 = (bf16[512,2,2,128]{3,0,2,1:T(8,128)(2,1)}, bf16[512,2,2,128]{3,0,2,1:T(8,128)(2,1)}, u32[]{:S(2)}, u32[]{:S(2)}) collective-permute-start(bf16[512,2,2,128]{3,0,2,1:T(8,128)(2,1)} %get-tuple-element.1074), channel_id=1, source_target_pairs={{0,4},{4,8},{8,12},{12,16},{16,20},{20,24},{24,28},{1,5},{5,9},{9,... | collective-permute-start | bytes 1572872 | tf_op jit(solution)/shard_map/while/body/eval_jaxpr/ppermute | solution.py:13
  222.0 15.0 collective-permute-start
  240.7 15.4 collective-permute-start.1
  260.9 22.1 collective-permute-start.1
  287.8 22.1 collective-permute-start.1
  299.7 11.3 collective-permute-start
  314.7 19.9 collective-permute-start.1
  373.3 400.6 %all-gather.9.cloned.1.call-start = ((), (), s32[]{:S(2)}) async-start(), calls=%async_computation.2 | async-start | bytes 5242880 | tf_op jit(solution)/shard_map/all_gather | solution.py:198
  376.7 478.5 %all-gather.7.cloned.1.call-start = ((), (), s32[]{:S(2)}) async-start(), calls=%async_computation.1 | async-start | bytes 5242880 | tf_op jit(solution)/shard_map/all_gather | solution.py:176
  696.0 567.9 %all-reduce.23.cloned.1.call-start = ((), (), s32[]{:S(2)}) async-start(), calls=%async_computation.5 | async-start | bytes 16777216
  974.4 373.5 %all-gather.11.cloned.1.call-start = ((), (), s32[]{:S(2)}) async-start(), calls=%async_computation.3 | async-start | bytes 5242880 | tf_op jit(solution)/shard_map/all_gather | solution.py:219
  1267.9 838.4 %all-reduce.27.cloned.1.call-start = ((), (), s32[]{:S(2)}) async-start(), calls=%async_computation.7 | async-start | bytes 16777216
  1392.1 9.8 collective-permute-start.5
  1393.0 14.5 collective-permute-start.4
  1394.6 18.5 collective-permute-start.2
  1394.6 24.1 collective-permute-start.3
  1427.2 21.2 collective-permute-start.5
  1441.1 12.8 collective-permute-start.4
  1443.4 16.1 collective-permute-start.2
  1443.4 21.7 collective-permute-start.3
  1473.6 22.0 collective-permute-start.5
  1475.2 25.2 %collective-permute-start.4 = (bf16[512,2,2,128]{3,0,2,1:T(8,128)(2,1)}, bf16[512,2,2,128]{3,0,2,1:T(8,128)(2,1)S(1)}, u32[]{:S(2)}, u32[]{:S(2)}) collective-permute-start(bf16[512,2,2,128]{3,0,2,1:T(8,128)(2,1)} %convert_element_type.425), channel_id=1, source_target_pairs={{28,0},{0,4},{4,8},{8,12},{12,16},{16,20},{20,24},{24,28},{29,1},{... | collective-permute-start | bytes 1572872 | tf_op jit(solution)/shard_map/while/body/eval_jaxpr/ppermute | solution.py:19
  1492.3 13.7 collective-permute-start.2
  1492.4 19.2 collective-permute-start.3
  1520.1 25.3 %collective-permute-start.5 = (bf16[512,2,2,128]{3,0,2,1:T(8,128)(2,1)}, bf16[512,2,2,128]{3,0,2,1:T(8,128)(2,1)}, u32[]{:S(2)}, u32[]{:S(2)}) collective-permute-start(bf16[512,2,2,128]{3,0,2,1:T(8,128)(2,1)} %convert_element_type.427), channel_id=1, source_target_pairs={{28,0},{0,4},{4,8},{8,12},{12,16},{16,20},{20,24},{24,28},{29,1},{... | collective-permute-start | bytes 1572872 | tf_op jit(solution)/shard_map/while/body/eval_jaxpr/ppermute | solution.py:19
  1524.1 23.4 collective-permute-start.4
  1526.4 26.0 %collective-permute-start.2 = (bf16[512,2,2,128]{3,0,2,1:T(8,128)(2,1)S(1)}, bf16[512,2,2,128]{3,0,2,1:T(8,128)(2,1)S(1)}, u32[]{:S(2)}, u32[]{:S(2)}) collective-permute-start(bf16[512,2,2,128]{3,0,2,1:T(8,128)(2,1)S(1)} %copy.262), channel_id=1, source_target_pairs={{28,0},{0,4},{4,8},{8,12},{12,16},{16,20},{20,24},{24,28},{29,1},{... | collective-permute-start | bytes 1572872 | tf_op jit(solution)/shard_map/while/body/eval_jaxpr/ppermute | solution.py:19
  1542.2 16.0 collective-permute-start.3
  1566.6 28.6 %collective-permute-start.5 = (bf16[512,2,2,128]{3,0,2,1:T(8,128)(2,1)}, bf16[512,2,2,128]{3,0,2,1:T(8,128)(2,1)}, u32[]{:S(2)}, u32[]{:S(2)}) collective-permute-start(bf16[512,2,2,128]{3,0,2,1:T(8,128)(2,1)} %convert_element_type.427), channel_id=1, source_target_pairs={{28,0},{0,4},{4,8},{8,12},{12,16},{16,20},{20,24},{24,28},{29,1},{... | collective-permute-start | bytes 1572872 | tf_op jit(solution)/shard_map/while/body/eval_jaxpr/ppermute | solution.py:19
  1569.2 28.1 %collective-permute-start.4 = (bf16[512,2,2,128]{3,0,2,1:T(8,128)(2,1)}, bf16[512,2,2,128]{3,0,2,1:T(8,128)(2,1)S(1)}, u32[]{:S(2)}, u32[]{:S(2)}) collective-permute-start(bf16[512,2,2,128]{3,0,2,1:T(8,128)(2,1)} %convert_element_type.425), channel_id=1, source_target_pairs={{28,0},{0,4},{4,8},{8,12},{12,16},{16,20},{20,24},{24,28},{29,1},{... | collective-permute-start | bytes 1572872 | tf_op jit(solution)/shard_map/while/body/eval_jaxpr/ppermute | solution.py:19
  1571.6 27.4 %collective-permute-start.2 = (bf16[512,2,2,128]{3,0,2,1:T(8,128)(2,1)S(1)}, bf16[512,2,2,128]{3,0,2,1:T(8,128)(2,1)S(1)}, u32[]{:S(2)}, u32[]{:S(2)}) collective-permute-start(bf16[512,2,2,128]{3,0,2,1:T(8,128)(2,1)S(1)} %copy.262), channel_id=1, source_target_pairs={{28,0},{0,4},{4,8},{8,12},{12,16},{16,20},{20,24},{24,28},{29,1},{... | collective-permute-start | bytes 1572872 | tf_op jit(solution)/shard_map/while/body/eval_jaxpr/ppermute | solution.py:19
  1577.2 27.4 %collective-permute-start.3 = (bf16[512,2,2,128]{3,0,2,1:T(8,128)(2,1)}, bf16[512,2,2,128]{3,0,2,1:T(8,128)(2,1)S(1)}, u32[]{:S(2)}, u32[]{:S(2)}) collective-permute-start(bf16[512,2,2,128]{3,0,2,1:T(8,128)(2,1)} %copy.263), channel_id=1, source_target_pairs={{28,0},{0,4},{4,8},{8,12},{12,16},{16,20},{20,24},{24,28},{29,1},{... | collective-permute-start | bytes 1572872 | tf_op jit(solution)/shard_map/while/body/eval_jaxpr/ppermute | solution.py:19
  1613.1 21.3 collective-permute-start.5
  1616.4 23.5 collective-permute-start.4
  1618.7 26.7 %collective-permute-start.2 = (bf16[512,2,2,128]{3,0,2,1:T(8,128)(2,1)S(1)}, bf16[512,2,2,128]{3,0,2,1:T(8,128)(2,1)S(1)}, u32[]{:S(2)}, u32[]{:S(2)}) collective-permute-start(bf16[512,2,2,128]{3,0,2,1:T(8,128)(2,1)S(1)} %copy.262), channel_id=1, source_target_pairs={{28,0},{0,4},{4,8},{8,12},{12,16},{16,20},{20,24},{24,28},{29,1},{... | collective-permute-start | bytes 1572872 | tf_op jit(solution)/shard_map/while/body/eval_jaxpr/ppermute | solution.py:19
  1627.0 24.1 collective-permute-start.3
  1659.6 21.3 collective-permute-start.5
  1660.4 25.9 %collective-permute-start.4 = (bf16[512,2,2,128]{3,0,2,1:T(8,128)(2,1)}, bf16[512,2,2,128]{3,0,2,1:T(8,128)(2,1)S(1)}, u32[]{:S(2)}, u32[]{:S(2)}) collective-permute-start(bf16[512,2,2,128]{3,0,2,1:T(8,128)(2,1)} %convert_element_type.425), channel_id=1, source_target_pairs={{28,0},{0,4},{4,8},{8,12},{12,16},{16,20},{20,24},{24,28},{29,1},{... | collective-permute-start | bytes 1572872 | tf_op jit(solution)/shard_map/while/body/eval_jaxpr/ppermute | solution.py:19
  1660.4 31.5 %collective-permute-start.2 = (bf16[512,2,2,128]{3,0,2,1:T(8,128)(2,1)S(1)}, bf16[512,2,2,128]{3,0,2,1:T(8,128)(2,1)S(1)}, u32[]{:S(2)}, u32[]{:S(2)}) collective-permute-start(bf16[512,2,2,128]{3,0,2,1:T(8,128)(2,1)S(1)} %copy.262), channel_id=1, source_target_pairs={{28,0},{0,4},{4,8},{8,12},{12,16},{16,20},{20,24},{24,28},{29,1},{... | collective-permute-start | bytes 1572872 | tf_op jit(solution)/shard_map/while/body/eval_jaxpr/ppermute | solution.py:19
  1666.7 30.9 %collective-permute-start.3 = (bf16[512,2,2,128]{3,0,2,1:T(8,128)(2,1)}, bf16[512,2,2,128]{3,0,2,1:T(8,128)(2,1)S(1)}, u32[]{:S(2)}, u32[]{:S(2)}) collective-permute-start(bf16[512,2,2,128]{3,0,2,1:T(8,128)(2,1)} %copy.263), channel_id=1, source_target_pairs={{28,0},{0,4},{4,8},{8,12},{12,16},{16,20},{20,24},{24,28},{29,1},{... | collective-permute-start | bytes 1572872 | tf_op jit(solution)/shard_map/while/body/eval_jaxpr/ppermute | solution.py:19
  1706.1 21.3 collective-permute-start.5
  1706.9 25.9 %collective-permute-start.4 = (bf16[512,2,2,128]{3,0,2,1:T(8,128)(2,1)}, bf16[512,2,2,128]{3,0,2,1:T(8,128)(2,1)S(1)}, u32[]{:S(2)}, u32[]{:S(2)}) collective-permute-start(bf16[512,2,2,128]{3,0,2,1:T(8,128)(2,1)} %convert_element_type.425), channel_id=1, source_target_pairs={{28,0},{0,4},{4,8},{8,12},{12,16},{16,20},{20,24},{24,28},{29,1},{... | collective-permute-start | bytes 1572872 | tf_op jit(solution)/shard_map/while/body/eval_jaxpr/ppermute | solution.py:19
  1706.9 31.5 %collective-permute-start.2 = (bf16[512,2,2,128]{3,0,2,1:T(8,128)(2,1)S(1)}, bf16[512,2,2,128]{3,0,2,1:T(8,128)(2,1)S(1)}, u32[]{:S(2)}, u32[]{:S(2)}) collective-permute-start(bf16[512,2,2,128]{3,0,2,1:T(8,128)(2,1)S(1)} %copy.262), channel_id=1, source_target_pairs={{28,0},{0,4},{4,8},{8,12},{12,16},{16,20},{20,24},{24,28},{29,1},{... | collective-permute-start | bytes 1572872 | tf_op jit(solution)/shard_map/while/body/eval_jaxpr/ppermute | solution.py:19
  1712.1 32.0 %collective-permute-start.3 = (bf16[512,2,2,128]{3,0,2,1:T(8,128)(2,1)}, bf16[512,2,2,128]{3,0,2,1:T(8,128)(2,1)S(1)}, u32[]{:S(2)}, u32[]{:S(2)}) collective-permute-start(bf16[512,2,2,128]{3,0,2,1:T(8,128)(2,1)} %copy.263), channel_id=1, source_target_pairs={{28,0},{0,4},{4,8},{8,12},{12,16},{16,20},{20,24},{24,28},{29,1},{... | collective-permute-start | bytes 1572872 | tf_op jit(solution)/shard_map/while/body/eval_jaxpr/ppermute | solution.py:19
  1814.1 632.4 %all-reduce.25.cloned.1.call-start = ((), (), s32[]{:S(2)}) async-start(), calls=%async_computation.6 | async-start | bytes 54525952 | tf_op jit(solution)/shard_map/psum | solution.py:326
  (94 other events, 3590.4 us)
Sparse Core Ops, SparseCore 0:
  9.6 83.4 all-gather.4
  373.4 318.4 all-reduce.20
  694.1 79.7 all-gather.8
  775.9 79.2 all-gather.6
  974.5 289.3 all-reduce.22
  1268.0 79.7 all-gather.10
  1814.2 292.0 all-reduce.26
  2112.5 333.8 all-reduce.24
where the time goes:
time: 2500 us; the launch traced here: 2490 us
  waiting for transfers between devices  1570 us (63%)
  starting transfers between devices  265 us (11%)
  other arithmetic  234 us (9%)
  matrix products  193 us (8%)
  local copies, waits for them, and re-layouts  168 us (7%)
  blocking collectives  35.8 us (1%)
    unnamed x11, waiting for transfers between devices  810 us
    psum x1, waiting for transfers between devices, on_device(): lax.psum(query_weight_grad.astype(jnp.bfloat16), 'seq').astype(jnp.float32)  334 us
    ppermute x14, starting transfers between devices, from_behind(): lax.ppermute(value, axis, [(source, source + steps) for source in range(i...  136 us
    ppermute x32, waiting for transfers between devices, passed_along(): return lax.ppermute(block, axis, route)  132 us
    ppermute x32, starting transfers between devices, passed_along(): return lax.ppermute(block, axis, route)  129 us
    all_gather x1, waiting for transfers between devices, on_device(): gathered = lax.all_gather(tokens, 'head', axis=0, tiled=True)  78.3 us
    all_gather x1, waiting for transfers between devices, on_device(): lax.all_gather(masked_grad.astype(jnp.bfloat16), 'head', axis=0, tiled=True)  77.9 us
    all_gather x1, waiting for transfers between devices, on_device(): lax.all_gather(middle.astype(jnp.bfloat16), 'head', axis=0, tiled=True)  74 us
  transfers between devices with their start and end apart: 54, of which 42 were waited for; matrix products, arithmetic and copies ran while one was open for 5% of the time, Pallas kernels for 0%

commit v1 on v0

v1 whole, which is shorter than its diff:
```python
import functools

import jax
import jax.numpy as jnp
from jax import lax
from jax.experimental import pallas as pl
from jax.experimental.pallas import tpu as pltpu
from jax.sharding import PartitionSpec as P

EPS = 1e-06
THETA = 1000000.0
LOG2E = 1.4426950408889634
VMEM_LIMIT = 58 * 1024 * 1024
LOW = jnp.bfloat16
F32 = jnp.float32


def mm(left, right):
    return jnp.dot(left, right, preferred_element_type=F32)


def mm_t(left, right):
    return lax.dot_general(left, right, (((1,), (1,)), ((), ())), preferred_element_type=F32)


def t_mm(left, right):
    return lax.dot_general(left, right, (((0,), (0,)), ((), ())), preferred_element_type=F32)


def shape_of(rows, columns, kind):
    return jax.ShapeDtypeStruct((rows, columns), kind)


def params(**extra):
    return pltpu.CompilerParams(vmem_limit_bytes=VMEM_LIMIT, **extra)


def cost(flops, moved, exps=0):
    return pl.CostEstimate(flops=int(flops), bytes_accessed=int(moved), transcendentals=int(exps))


WHOLE = pl.BlockSpec(memory_space=pltpu.VMEM)
SCALARS = pl.BlockSpec(memory_space=pltpu.SMEM)


def full_block(array):
    return pl.BlockSpec(array.shape, lambda i: (0,) * len(array.shape))


def inverse_rms(values):
    return lax.rsqrt(jnp.mean(values * values, axis=-1, keepdims=True) + EPS)


def turn(values, cosine, sine):
    return values * cosine + pltpu.roll(values, values.shape[-1] // 2, 1) * sine


def turn_back(grads, cosine, sine):
    return grads * cosine + pltpu.roll(grads * sine, grads.shape[-1] // 2, 1)


def project_kernel(
    head_dim,
    x_ref, gain_ref, cos_ref, sin_ref, qgain_ref, kgain_ref, wq_ref, wk_ref, wv_ref, wg_ref,
    normed_ref, qraw_ref, q_ref, kraw_ref, kv_ref, gate_ref,
):
    x = x_ref[...].astype(F32)
    normed = (x * inverse_rms(x) * gain_ref[...]).astype(LOW)
    normed_ref[...] = normed
    cosine, sine = cos_ref[...], sin_ref[...]
    raw = mm(normed, wk_ref[...])
    kraw_ref[...] = raw
    for h in range(raw.shape[1] // head_dim):
        part = raw[:, h * head_dim : (h + 1) * head_dim]
        part = part * inverse_rms(part) * kgain_ref[...]
        kv_ref[:, h * head_dim : (h + 1) * head_dim] = turn(part, cosine, sine).astype(LOW)
    kv_ref[:, raw.shape[1] :] = mm(normed, wv_ref[...]).astype(LOW)
    raw = mm(normed, wq_ref[...])
    qraw_ref[...] = raw
    for h in range(raw.shape[1] // head_dim):
        part = raw[:, h * head_dim : (h + 1) * head_dim]
        part = part * inverse_rms(part) * qgain_ref[...]
        q_ref[:, h * head_dim : (h + 1) * head_dim] = turn(part, cosine, sine).astype(LOW)
    gate_ref[...] = mm(normed, wg_ref[...])


def project(x, gain, cosine, sine, qgain, kgain, wq, wk, wv, wg):
    rows, model = x.shape
    head_dim = qgain.shape[1]
    tile = min(rows, 256)
    nq, nk = wq.shape[1], wk.shape[1]

    def by_row(columns):
        return pl.BlockSpec((tile, columns), lambda i: (i, 0))

    return pl.pallas_call(
        functools.partial(project_kernel, head_dim),
        grid=(rows // tile,),
        in_specs=[
            by_row(model), full_block(gain), by_row(head_dim), by_row(head_dim),
            full_block(qgain), full_block(kgain),
            full_block(wq), full_block(wk), full_block(wv), full_block(wg),
        ],
        out_specs=[by_row(model), by_row(nq), by_row(nq), by_row(nk), by_row(2 * nk), by_row(nq)],
        out_shape=[
            shape_of(rows, model, LOW), shape_of(rows, nq, F32), shape_of(rows, nq, LOW),
            shape_of(rows, nk, F32), shape_of(rows, 2 * nk, LOW), shape_of(rows, nq, F32),
        ],
        compiler_params=params(),
        cost_estimate=cost(2 * rows * model * 2 * (nq + nk), model * 2 * (nq + nk) * 2),
        name="project",
    )(x, gain, cosine, sine, qgain, kgain, wq, wk, wv, wg)


def live_blocks(place_ref, rows):
    start, length = place_ref[0], place_ref[1]
    whole = jnp.minimum(start // rows, length // rows)
    end = jnp.minimum(start // rows + 1, (length + rows - 1) // rows)
    end = jnp.where(start < length, end, 0)
    return jnp.minimum(whole, end), end


def attend_kernel(
    group, head_dim, place_ref, q_ref, kv_ref, gate_ref, att_ref, acted_ref, inv_ref, acc_ref, sum_ref
):
    rows = q_ref.shape[0]
    heads = q_ref.shape[1] // head_dim
    kv_heads = heads // group
    factor = head_dim ** (-0.5) * LOG2E
    start, length = place_ref[0], place_ref[1]
    acc_ref[...] = jnp.zeros_like(acc_ref)
    sum_ref[...] = jnp.zeros_like(sum_ref)
    whole, end = live_blocks(place_ref, rows)

    def one_block(j, masked):
        span = pl.ds(pl.multiple_of(j * rows, rows), rows)
        if masked:
            key_pos = j * rows + lax.broadcasted_iota(jnp.int32, (rows, rows), 1)
            query_pos = start + lax.broadcasted_iota(jnp.int32, (rows, rows), 0)
            allowed = (key_pos <= query_pos) & (key_pos < length)
        for h in range(heads):
            c = h // group
            keys = kv_ref[span, c * head_dim : (c + 1) * head_dim]
            values = kv_ref[span, (kv_heads + c) * head_dim : (kv_heads + c + 1) * head_dim]
            weights = jnp.exp2(mm_t(q_ref[:, h * head_dim : (h + 1) * head_dim], keys) * factor)
            if masked:
                weights = jnp.where(allowed, weights, 0.0)
            total = weights[:, :128]
            for piece in range(1, rows // 128):
                total = total + weights[:, piece * 128 : (piece + 1) * 128]
            sum_ref[h] = sum_ref[h] + total
            acc_ref[h] = acc_ref[h] + mm(weights.astype(LOW), values)

    def plain(j, carry):
        one_block(j, False)
        return carry

    def edge(j, carry):
        one_block(j, True)
        return carry

    lax.fori_loop(0, whole, plain, 0)
    lax.fori_loop(whole, end, edge, 0)
    lane = lax.broadcasted_iota(jnp.int32, inv_ref.shape, 1)
    kept = jnp.zeros(inv_ref.shape, F32)
    for h in range(heads):
        total = jnp.sum(sum_ref[h], axis=1, keepdims=True)
        inverse = 1.0 / jnp.where(total > 0.0, total, 1.0)
        attended = acc_ref[h] * inverse
        columns = slice(h * head_dim, (h + 1) * head_dim)
        att_ref[:, columns] = attended
        acted_ref[:, columns] = (attended * jax.nn.sigmoid(gate_ref[:, columns])).astype(LOW)
        kept = jnp.where(lane == h, inverse, kept)
    inv_ref[...] = kept


def attend(place, q, kv, gate, group, head_dim):
    rows, width = q.shape
    heads = width // head_dim
    return pl.pallas_call(
        functools.partial(attend_kernel, group, head_dim),
        in_specs=[SCALARS, WHOLE, WHOLE, WHOLE],
        out_specs=[WHOLE, WHOLE, WHOLE],
        out_shape=[shape_of(rows, width, F32), shape_of(rows, width, LOW), shape_of(rows, 128, F32)],
        scratch_shapes=[
            pltpu.VMEM((heads, rows, head_dim), F32),
            pltpu.VMEM((heads, rows, 128), F32),
        ],
        compiler_params=params(),
        cost_estimate=cost(4 * rows * kv.shape[0] * width, kv.size * 2, rows * kv.shape[0] * heads),
        name="attend",
    )(place, q, kv, gate)


def attend_back_kernel(
    group, head_dim,
    place_ref, q_ref, kv_ref, r_ref, wo_ref, att_ref, gate_ref, inv_ref,
    dq_ref, dkv_ref, dgate_ref,
    scaled_ref, corr_ref, acc_ref,
):
    rows = q_ref.shape[0]
    heads = q_ref.shape[1] // head_dim
    kv_heads = heads // group
    scale = head_dim ** (-0.5)
    start, length = place_ref[0], place_ref[1]
    acted_grad = mm_t(r_ref[...], wo_ref[...])
    lane = lax.broadcasted_iota(jnp.int32, inv_ref.shape, 1)
    kept = jnp.zeros(inv_ref.shape, F32)
    for h in range(heads):
        columns = slice(h * head_dim, (h + 1) * head_dim)
        sigmoid = jax.nn.sigmoid(gate_ref[:, columns])
        attended = att_ref[:, columns]
        grad = acted_grad[:, columns]
        dgate_ref[:, columns] = (grad * attended * sigmoid * (1.0 - sigmoid)).astype(LOW)
        grad = grad * sigmoid
        inverse = inv_ref[:, h : h + 1]
        scaled_ref[:, columns] = (grad * inverse).astype(LOW)
        kept = jnp.where(
            lane == h, jnp.sum(grad * attended, axis=1, keepdims=True) * inverse, kept
        )
    corr_ref[...] = kept.T
    acc_ref[...] = jnp.zeros_like(acc_ref)
    whole, end = live_blocks(place_ref, rows)

    def one_block(j, masked):
        span = pl.ds(pl.multiple_of(j * rows, rows), rows)
        if masked:
            key_pos = j * rows + lax.broadcasted_iota(jnp.int32, (rows, rows), 0)
            query_pos = start + lax.broadcasted_iota(jnp.int32, (rows, rows), 1)
            allowed = (key_pos <= query_pos) & (key_pos < length)
        for c in range(kv_heads):
            key_columns = slice(c * head_dim, (c + 1) * head_dim)
            value_columns = slice((kv_heads + c) * head_dim, (kv_heads + c + 1) * head_dim)
            keys = kv_ref[span, key_columns]
            values = kv_ref[span, value_columns]
            dk = jnp.zeros((rows, head_dim), F32)
            dv = jnp.zeros((rows, head_dim), F32)
            for h in range(c * group, (c + 1) * group):
                columns = slice(h * head_dim, (h + 1) * head_dim)
                queries = q_ref[:, columns]
                scaled = scaled_ref[:, columns]
                weights = jnp.exp2(mm_t(keys, queries) * (scale * LOG2E))
                if masked:
                    weights = jnp.where(allowed, weights, 0.0)
                dv = dv + mm(weights.astype(LOW), scaled)
                score = (weights * (mm_t(values, scaled) - corr_ref[h : h + 1, :])).astype(LOW)
                dk = dk + mm(score, queries)
                acc_ref[h] = acc_ref[h] + t_mm(score, keys)
            dkv_ref[span, key_columns] = (dk * scale).astype(LOW)
            dkv_ref[span, value_columns] = dv.astype(LOW)

    def plain(j, carry):
        one_block(j, False)
        return carry

    def edge(j, carry):
        one_block(j, True)
        return carry

    def empty(j, carry):
        span = pl.ds(pl.multiple_of(j * rows, rows), rows)
        dkv_ref[span, :] = jnp.zeros((rows, dkv_ref.shape[1]), LOW)
        return carry

    lax.fori_loop(0, whole, plain, 0)
    lax.fori_loop(whole, end, edge, 0)
    lax.fori_loop(end, dkv_ref.shape[0] // rows, empty, 0)
    for h in range(heads):
        dq_ref[:, h * head_dim : (h + 1) * head_dim] = acc_ref[h] * scale


def attend_back(place, q, kv, r, wo, att, gate, inv, group, head_dim):
    rows, width = q.shape
    heads = width // head_dim
    return pl.pallas_call(
        functools.partial(attend_back_kernel, group, head_dim),
        in_specs=[SCALARS] + [WHOLE] * 7,
        out_specs=[WHOLE] * 3,
        out_shape=[
            shape_of(rows, width, F32), shape_of(kv.shape[0], kv.shape[1], LOW), shape_of(rows, width, LOW)
        ],
        scratch_shapes=[
            pltpu.VMEM((rows, width), LOW),
            pltpu.VMEM((128, rows), F32),
            pltpu.VMEM((heads, rows, head_dim), F32),
        ],
        compiler_params=params(),
        cost_estimate=cost(10 * rows * kv.shape[0] * width, kv.size * 4, rows * kv.shape[0] * heads),
        name="attend_back",
    )(place, q, kv, r, wo, att, gate, inv)


def units_kernel(
    mid_ref, masked_ref, gain_ref, wg_ref, wl_ref, wd_ref,
    normed_ref, hidden_ref, dg_ref, dl_ref, dn_ref, dgain_ref,
    acc_ref,
):
    step = pl.program_id(0)

    @pl.when(step == 0)
    def _():
        x = mid_ref[...].astype(F32)
        normed_ref[...] = (x * inverse_rms(x) * gain_ref[...]).astype(LOW)

    normed = normed_ref[...]
    gate = mm(normed, wg_ref[...])
    lift = mm(normed, wl_ref[...])
    grad = mm_t(masked_ref[...], wd_ref[...])
    sigmoid = jax.nn.sigmoid(gate)
    silu = gate * sigmoid
    hidden_ref[...] = (silu * lift).astype(LOW)
    lift_grad = (grad * silu).astype(LOW)
    gate_grad = (grad * lift * (sigmoid + silu * (1.0 - sigmoid))).astype(LOW)
    dg_ref[...] = gate_grad
    dl_ref[...] = lift_grad
    part = mm_t(gate_grad, wg_ref[...]) + mm_t(lift_grad, wl_ref[...])

    @pl.when(step == 0)
    def _():
        acc_ref[...] = part

    @pl.when(step > 0)
    def _():
        acc_ref[...] = acc_ref[...] + part

    @pl.when(step == pl.num_programs(0) - 1)
    def _():
        total = acc_ref[...]
        dn_ref[...] = total.astype(LOW)
        x = mid_ref[...].astype(F32)
        dgain_ref[...] = jnp.sum(total * x * inverse_rms(x), axis=0, keepdims=True)


def units(mid, masked, gain, wg, wl, wd):
    rows, model = mid.shape
    hidden = wg.shape[1]
    tile = 256
    whole = pl.BlockSpec((rows, model), lambda i: (0, 0))
    tall = pl.BlockSpec((model, tile), lambda i: (0, i))
    wide = pl.BlockSpec((tile, model), lambda i: (i, 0))
    part = pl.BlockSpec((rows, tile), lambda i: (0, i))
    return pl.pallas_call(
        units_kernel,
        grid=(hidden // tile,),
        in_specs=[whole, whole, full_block(gain), tall, tall, wide],
        out_specs=[whole, part, part, part, whole, pl.BlockSpec((1, model), lambda i: (0, 0))],
        out_shape=[
            shape_of(rows, model, LOW), shape_of(rows, hidden, LOW), shape_of(rows, hidden, LOW),
            shape_of(rows, hidden, LOW), shape_of(rows, model, LOW), shape_of(1, model, F32),
        ],
        scratch_shapes=[pltpu.VMEM((rows, model), F32)],
        compiler_params=params(),
        cost_estimate=cost(10 * rows * model * hidden, 6 * model * hidden),
        name="units",
    )(mid, masked, gain, wg, wl, wd)


def unproject_kernel(
    head_dim,
    x_ref, gain_ref, cos_ref, sin_ref, qgain_ref, kgain_ref, wq_ref, wk_ref, wv_ref, wg_ref,
    dq_ref, qraw_ref, dkv_ref, kraw_ref, dgate_ref,
    dall_ref, dn_ref, dgain_ref, dqgain_ref, dkgain_ref,
):
    step = pl.program_id(0)
    cosine, sine = cos_ref[...], sin_ref[...]
    nq, nk = qraw_ref.shape[1], kraw_ref.shape[1]

    def heads_back(grad_ref, raw_ref, head_gain, count, place):
        gain_total = jnp.zeros((1, head_dim), F32)
        for h in range(count):
            columns = slice(h * head_dim, (h + 1) * head_dim)
            grad = turn_back(grad_ref[:, columns].astype(F32), cosine, sine)
            raw = raw_ref[:, columns]
            inverse = inverse_rms(raw)
            gain_total = gain_total + jnp.sum(grad * raw * inverse, axis=0, keepdims=True)
            grad = grad * head_gain
            mean = jnp.mean(grad * raw, axis=-1, keepdims=True)
            grad = inverse * (grad - raw * (inverse * inverse * mean))
            dall_ref[:, place + h * head_dim : place + (h + 1) * head_dim] = grad.astype(LOW)
        return gain_total

    dqgain = heads_back(dq_ref, qraw_ref, qgain_ref[...], nq // head_dim, 0)
    dkgain = heads_back(dkv_ref, kraw_ref, kgain_ref[...], nk // head_dim, nq)
    dall_ref[:, nq + nk : nq + 2 * nk] = dkv_ref[:, nk:]
    dall_ref[:, nq + 2 * nk :] = dgate_ref[...]
    total = (
        mm_t(dall_ref[:, :nq], wq_ref[...])
        + mm_t(dall_ref[:, nq : nq + nk], wk_ref[...])
        + mm_t(dall_ref[:, nq + nk : nq + 2 * nk], wv_ref[...])
        + mm_t(dall_ref[:, nq + 2 * nk :], wg_ref[...])
    )
    dn_ref[...] = total.astype(LOW)
    x = x_ref[...].astype(F32)
    dgain = jnp.sum(total * x * inverse_rms(x), axis=0, keepdims=True)

    @pl.when(step == 0)
    def _():
        dgain_ref[...] = dgain
        dqgain_ref[...] = dqgain
        dkgain_ref[...] = dkgain

    @pl.when(step > 0)
    def _():
        dgain_ref[...] = dgain_ref[...] + dgain
        dqgain_ref[...] = dqgain_ref[...] + dqgain
        dkgain_ref[...] = dkgain_ref[...] + dkgain


def unproject(x, gain, cosine, sine, qgain, kgain, wq, wk, wv, wg, dq, qraw, dkv, kraw, dgate):
    rows, model = x.shape
    head_dim = qgain.shape[1]
    tile = min(rows, 256)
    nq, nk = wq.shape[1], wk.shape[1]

    def by_row(columns):
        return pl.BlockSpec((tile, columns), lambda i: (i, 0))

    def line(columns):
        return pl.BlockSpec((1, columns), lambda i: (0, 0))

    return pl.pallas_call(
        functools.partial(unproject_kernel, head_dim),
        grid=(rows // tile,),
        in_specs=[
            by_row(model), full_block(gain), by_row(head_dim), by_row(head_dim),
            full_block(qgain), full_block(kgain),
            full_block(wq), full_block(wk), full_block(wv), full_block(wg),
            by_row(nq), by_row(nq), by_row(2 * nk), by_row(nk), by_row(nq),
        ],
        out_specs=[by_row(2 * nq + 2 * nk), by_row(model), line(model), line(head_dim), line(head_dim)],
        out_shape=[
            shape_of(rows, 2 * nq + 2 * nk, LOW), shape_of(rows, model, LOW),
            shape_of(1, model, F32), shape_of(1, head_dim, F32), shape_of(1, head_dim, F32),
        ],
        compiler_params=params(),
        cost_estimate=cost(2 * rows * model * 2 * (nq + nk), model * 2 * (nq + nk) * 2),
        name="unproject",
    )(x, gain, cosine, sine, qgain, kgain, wq, wk, wv, wg, dq, qraw, dkv, kraw, dgate)


def turn_tables(positions, head_dim):
    half_dim = head_dim // 2
    inverse = THETA ** (-(jnp.arange(half_dim, dtype=F32) * 2.0) / head_dim)
    angles = positions.astype(F32)[:, None] * inverse[None, :]
    cosine, sine = jnp.cos(angles), jnp.sin(angles)
    return jnp.concatenate([cosine, cosine], axis=1), jnp.concatenate([-sine, sine], axis=1)


def norm_back(grad, values, gain):
    inverse = inverse_rms(values)
    grad = grad * gain
    mean = jnp.mean(grad * values, axis=-1, keepdims=True)
    return inverse * (grad - values * (inverse * inverse * mean))


def gather(value, axis):
    return lax.all_gather(value, axis, axis=0, tiled=True)


def scatter(value, axis):
    return lax.psum_scatter(value, axis, scatter_dimension=0, tiled=True)


def on_device(
    tokens, cotangent, lengths,
    query_weight, key_weight, value_weight, gating_weight, output_weight,
    swiglu_gate, swiglu_lift, swiglu_down,
    input_gain, middle_gain, query_gain, key_gain,
):
    block_index = lax.axis_index("seq")
    part_index = lax.axis_index("head")
    parts = lax.axis_size("head")
    local_rows, batch, model = tokens.shape
    head_dim = query_gain.shape[0]
    block_rows = local_rows * parts
    group = query_weight.shape[1] // key_weight.shape[1]
    nq, nk = query_weight.shape[1], key_weight.shape[1]
    query_start = block_index * block_rows
    positions = query_start + jnp.arange(block_rows, dtype=jnp.int32)
    cosine, sine = turn_tables(positions, head_dim)
    gain_in, gain_mid = input_gain[None, :], middle_gain[None, :]
    gain_q, gain_k = query_gain[None, :], key_gain[None, :]
    local_pos = query_start + part_index * local_rows + jnp.arange(local_rows, dtype=jnp.int32)
    seqs = range(batch)
    places = [jnp.stack([query_start, lengths[b]]).astype(jnp.int32) for b in seqs]
    valid = [(local_pos < lengths[b]).astype(F32)[:, None] for b in seqs]
    own = [tokens[:, b, :] for b in seqs]
    own_masked = [valid[b] * cotangent[:, b, :].astype(F32) for b in seqs]

    rows_in = [gather(own[b], "head") for b in seqs]
    projected = [
        project(
            rows_in[b], gain_in, cosine, sine, gain_q, gain_k,
            query_weight, key_weight, value_weight, gating_weight,
        )
        for b in seqs
    ]
    normed, qraw, q, kraw, kv_own, gate = [list(x) for x in zip(*projected)]
    kv = [gather(kv_own[b], "seq") for b in seqs]
    masked = [gather(own_masked[b].astype(LOW), "head") for b in seqs]
    attended = [attend(places[b], q[b], kv[b], gate[b], group, head_dim) for b in seqs]
    att, acted, inv = [list(x) for x in zip(*attended)]
    middle = [
        own[b].astype(F32)
        + scatter(mm(acted[b], output_weight).astype(LOW), "head").astype(F32)
        for b in seqs
    ]
    mid = [gather(middle[b].astype(LOW), "head") for b in seqs]
    forward = [units(mid[b], masked[b], gain_mid, swiglu_gate, swiglu_lift, swiglu_down) for b in seqs]
    normed_mid, hidden, dg, dl, dn_mid, dgain_mid = [list(x) for x in zip(*forward)]
    residual = [
        own_masked[b]
        + norm_back(
            scatter(dn_mid[b], "head").astype(F32), middle[b].astype(LOW).astype(F32), gain_mid
        )
        for b in seqs
    ]
    r = [gather(residual[b].astype(LOW), "head") for b in seqs]

    def both(pair):
        return jnp.concatenate(pair, axis=0)

    normed_mid_all, masked_all = both(normed_mid), both(masked)
    ff_grads = (
        t_mm(normed_mid_all, both(dg)).astype(LOW),
        t_mm(normed_mid_all, both(dl)).astype(LOW),
        t_mm(both(hidden), masked_all).astype(LOW),
    )
    ff_grads = [x.astype(F32) for x in lax.psum(ff_grads, "seq")]
    units_out = [scatter(mm(hidden[b], swiglu_down).astype(LOW), "head").astype(F32) for b in seqs]
    output = jnp.stack(
        [(valid[b] * (middle[b] + units_out[b])).astype(LOW) for b in seqs], axis=1
    )

    back = [
        attend_back(places[b], q[b], kv[b], r[b], output_weight, att[b], gate[b], inv[b], group, head_dim)
        for b in seqs
    ]
    dq, dkv_all, dgate = [list(x) for x in zip(*back)]
    dkv = [scatter(dkv_all[b], "seq") for b in seqs]
    last = [
        unproject(
            rows_in[b], gain_in, cosine, sine, gain_q, gain_k,
            query_weight, key_weight, value_weight, gating_weight,
            dq[b], qraw[b], dkv[b], kraw[b], dgate[b],
        )
        for b in seqs
    ]
    dall, dn_in, dgain_in, dgain_q, dgain_k = [list(x) for x in zip(*last)]
    input_grad = jnp.stack(
        [
            residual[b] + norm_back(scatter(dn_in[b], "head").astype(F32), own[b].astype(F32), gain_in)
            for b in seqs
        ],
        axis=1,
    )
    out_grad = t_mm(both(acted), both(r)).astype(LOW)
    proj_grad = t_mm(both(normed), both(dall)).astype(LOW)
    out_grad = gather(scatter(out_grad, "seq"), "seq").astype(F32)
    proj_grad = gather(scatter(proj_grad, "seq"), "seq")
    gains = jnp.concatenate(
        [sum(dgain_in)[0], sum(dgain_mid)[0], sum(dgain_q)[0], sum(dgain_k)[0]]
    )
    gains = lax.psum(gains, ("seq", "head"))

    def share(start, width):
        piece = width // parts
        return lax.dynamic_slice(gains, (start + part_index * piece,), (piece,))

    return (
        output,
        input_grad,
        proj_grad[:, :nq].astype(F32),
        proj_grad[:, nq : nq + nk].astype(F32),
        proj_grad[:, nq + nk : nq + 2 * nk].astype(F32),
        proj_grad[:, nq + 2 * nk :].astype(F32),
        out_grad,
        ff_grads[0],
        ff_grads[1],
        ff_grads[2],
        share(0, model),
        share(model, model),
        share(2 * model, head_dim),
        share(2 * model + head_dim, head_dim),
    )


def solution(mesh):
    return jax.shard_map(
        on_device,
        mesh=mesh,
        in_specs=(
            P(("seq", "head"), None, None),
            P(("seq", "head"), None, None),
            P(),
            P(None, "head"),
            P(None, "head"),
            P(None, "head"),
            P(None, "head"),
            P("head", None),
            P(None, "head"),
            P(None, "head"),
            P("head", None),
            P(),
            P(),
            P(),
            P(),
        ),
        out_specs=(
            P(("seq", "head"), None, None),
            P(("seq", "head"), None, None),
            P(None, "head"),
            P(None, "head"),
            P(None, "head"),
            P(None, "head"),
            P("head", None),
            P(None, "head"),
            P(None, "head"),
            P("head", None),
            P("head"),
            P("head"),
            P("head"),
            P("head"),
        ),
        check_vma=False,
    )
```

time: 2500 us -> 1450 us (0.58)
  waiting for transfers between devices: 1570 us -> 1070 us
  starting transfers between devices: 265 us -> 1.77 us
  other arithmetic: 234 us -> 64.5 us
  Pallas kernels: 0 us -> 164 us
  local copies, waits for them, and re-layouts: 168 us -> 22.9 us
  matrix products: 193 us -> 68.9 us
    unnamed x11 -> x25, waiting for transfers between devices: 810 us -> 1.73 us
    reduce_scatter x0 -> x12, waiting for transfers between devices: none -> 422 us  [scatter(): return lax.psum_scatter(value, axis, scatter_dimension=0, tiled=True)]
    ppermute x46 -> x0, starting transfers between devices: 264 us -> none  [the longest x14 136 us: from_behind(): lax.ppermute(value, axis, [(source, source + steps) for source in range(i...]
    pallas_call x0 -> x10, Pallas kernels: none -> 164 us  [the longest x2 82.2 us: units(): pl.pallas_call(units_kernel, grid=(hidden // tile,), in_specs=[whole, who...]
    ppermute x46 -> x0, waiting for transfers between devices: 139 us -> none  [the longest x32 132 us: passed_along(): return lax.ppermute(block, axis, route)]
    dot_general x31 -> x9, matrix products: 193 us -> 68.9 us  [the longest x5 44.6 us: t_mm(): lax.dot_general(left, right, (((0,), (0,)), ((), ())), preferred_element_...]
    all_gather x4 -> x12, waiting for transfers between devices: 291 us -> 404 us  [gather(): return lax.all_gather(value, axis, axis=0, tiled=True)]
    convert_element_type x57 -> x15, other arithmetic: 144 us -> 47.4 us  [the longest x3 22.3 us: on_device(): ff_grads = [x.astype(F32) for x in lax.psum(ff_grads, 'seq')]]
  transfers between devices with their start and end apart: 54 -> 25, of which waited for: 42 -> 23; matrix products, arithmetic and copies ran while one was open for 5% -> 9% of each run, Pallas kernels for 0% -> 9%
where the time goes in v1:
time: 1450 us
  waiting for transfers between devices  1070 us (74%)
  Pallas kernels  164 us (11%)
  matrix products  68.9 us (5%)
  other arithmetic  64.5 us (4%)
  blocking collectives  41.6 us (3%)
  local copies, waits for them, and re-layouts  22.9 us (2%)
  between operations  14.8 us (1%)
    reduce_scatter x12, waiting for transfers between devices, scatter(): return lax.psum_scatter(value, axis, scatter_dimension=0, tiled=True)  422 us
    all_gather x12, waiting for transfers between devices, gather(): return lax.all_gather(value, axis, axis=0, tiled=True)  404 us
    psum x1, waiting for transfers between devices, on_device(): ff_grads = [x.astype(F32) for x in lax.psum(ff_grads, 'seq')]  246 us
    pallas_call x2, Pallas kernels, units(): pl.pallas_call(units_kernel, grid=(hidden // tile,), in_specs=[whole, who...  82.2 us
    dot_general x5, matrix products, t_mm(): lax.dot_general(left, right, (((0,), (0,)), ((), ())), preferred_element_...  44.6 us
    psum x1, blocking collectives, on_device(): gains = lax.psum(gains, ('seq', 'head'))  41.6 us
  transfers between devices with their start and end apart: 25, of which 23 were waited for; matrix products, arithmetic and copies ran while one was open for 9% of the time, Pallas kernels for 9%

profile of v1, /device:TPU:0, one launch (start us, length us, event | category | flops | bytes accessed | tf_op | source)
XLA Modules:
  0.0 1451.8 jit_solution(9859390600835746525)
XLA Ops:
  13.8 46.7 %all-gather.35.cloned.1.call-done = bf16[512,1,2048]{2,0,1:T(8,128)(2,1)} async-done(((bf16[128,1,2048]{2,0,1:T(8,128)(2,1)}), bf16[512,1,2048]{2,0,1:T(8,128)(2,1)}) %all-gather.35.cloned.1.call-update) | async-done | bytes 2097168 | tf_op jit(solution)/shard_map/all_gather | solution.py:457
  60.5 8.6 project.2
  71.0 33.7 %all-gather.15.cloned.1.call-done.kv_ref = bf16[4096,512]{1,0:T(8,128)(2,1)} async-done(((bf16[512,512]{1,0:T(8,128)(2,1)}), bf16[4096,512]{1,0:T(8,128)(2,1)}) %all-gather.15.cloned.1.call-update) | async-done | bytes 4194320 | tf_op jit(solution)/shard_map/all_gather | solution.py:457
  104.7 6.2 attend.2
  120.8 46.4 %reduce-scatter.13.cloned.1.call-done = bf16[128,2048]{1,0:T(8,128)(2,1)} async-done(((bf16[512,2048]{1,0:T(8,128)(2,1)}), bf16[128,2048]{1,0:T(8,128)(2,1)}) %reduce-scatter.13.cloned.1.call-update) | async-done | bytes 524304 | tf_op jit(solution)/shard_map/reduce_scatter | solution.py:461
  170.9 43.8 %all-gather.19.cloned.1.call-done.masked_ref = bf16[512,2048]{1,0:T(8,128)(2,1)} async-done(((bf16[128,2048]{1,0:T(8,128)(2,1)}), bf16[512,2048]{1,0:T(8,128)(2,1)}) %all-gather.19.cloned.1.call-update) | async-done | bytes 2097168 | tf_op jit(solution)/shard_map/all_gather | solution.py:457
  214.6 46.2 %all-gather.17.cloned.1.call-done.mid_ref = bf16[512,2048]{1,0:T(8,128)(2,1)} async-done(((bf16[128,2048]{1,0:T(8,128)(2,1)}), bf16[512,2048]{1,0:T(8,128)(2,1)}) %all-gather.17.cloned.1.call-update) | async-done | bytes 2097168 | tf_op jit(solution)/shard_map/all_gather | solution.py:457
  260.8 41.1 %units.2 = (bf16[512,2048]{1,0:T(8,128)(2,1)}, bf16[512,1536]{1,0:T(8,128)(2,1)}, bf16[512,1536]{1,0:T(8,128)(2,1)}, bf16[512,1536]{1,0:T(8,128)(2,1)}, bf16[512,2048]{1,0:T(8,128)(2,1)}, /*index=5*/f32[1,2048]{1,0:T(1,128)}) custom-call(bf16[512,2048]{1,0:T(8,128)(2,1)} %all-gather.17.cloned.1.call-done.mid_ref, ...), custom_call_target="tpu_custom_call" | custom-call | flops 16106127360 | bytes 18874368 | tf_op jit(solution)/shard_map/units/pallas_call | solution.py:342
  301.9 5.6 all-gather.37.cloned.1.call-done
  307.6 8.6 project.3
  316.3 36.9 %reduce-scatter.21.cloned.1.call-done = bf16[128,2048]{1,0:T(8,128)(2,1)} async-done(((bf16[512,2048]{1,0:T(8,128)(2,1)}), bf16[128,2048]{1,0:T(8,128)(2,1)}) %reduce-scatter.21.cloned.1.call-update) | async-done | bytes 524304 | tf_op jit(solution)/shard_map/reduce_scatter | solution.py:461
  358.9 32.8 %all-gather.21.cloned.1.call-done.kv_ref = bf16[4096,512]{1,0:T(8,128)(2,1)} async-done(((bf16[512,512]{1,0:T(8,128)(2,1)}), bf16[4096,512]{1,0:T(8,128)(2,1)}) %all-gather.21.cloned.1.call-update) | async-done | bytes 4194320 | tf_op jit(solution)/shard_map/all_gather | solution.py:457
  391.7 6.6 attend.3
  402.0 37.8 %all-gather.27.cloned.1.call-done.r_ref = bf16[512,2048]{1,0:T(8,128)(2,1)} async-done(((bf16[128,2048]{1,0:T(8,128)(2,1)}), bf16[512,2048]{1,0:T(8,128)(2,1)}) %all-gather.27.cloned.1.call-update) | async-done | bytes 2097168 | tf_op jit(solution)/shard_map/all_gather | solution.py:457
  439.8 13.0 attend_back.2
  454.9 30.2 %reduce-scatter.17.cloned.1.call-done = bf16[128,2048]{1,0:T(8,128)(2,1)} async-done(((bf16[512,2048]{1,0:T(8,128)(2,1)}), bf16[128,2048]{1,0:T(8,128)(2,1)}) %reduce-scatter.17.cloned.1.call-update) | async-done | bytes 524304 | tf_op jit(solution)/shard_map/reduce_scatter | solution.py:461
  487.4 52.7 %reduce-scatter.23.cloned.1.call-done.dkv_ref = bf16[512,512]{1,0:T(8,128)(2,1)} async-done(((bf16[4096,512]{1,0:T(8,128)(2,1)}), bf16[512,512]{1,0:T(8,128)(2,1)}) %reduce-scatter.23.cloned.1.call-update) | async-done | bytes 524304 | tf_op jit(solution)/shard_map/reduce_scatter | solution.py:461
  540.1 12.6 unproject.2
  552.8 8.0 convolution_convert_fusion.6
  560.9 27.1 %all-gather.25.cloned.1.call-done.masked_ref = bf16[512,2048]{1,0:T(8,128)(2,1)} async-done(((bf16[128,2048]{1,0:T(8,128)(2,1)}), bf16[512,2048]{1,0:T(8,128)(2,1)}) %all-gather.25.cloned.1.call-update) | async-done | bytes 2097168 | tf_op jit(solution)/shard_map/all_gather | solution.py:457
  588.0 46.3 %all-gather.23.cloned.1.call-done.mid_ref = bf16[512,2048]{1,0:T(8,128)(2,1)} async-done(((bf16[128,2048]{1,0:T(8,128)(2,1)}), bf16[512,2048]{1,0:T(8,128)(2,1)}) %all-gather.23.cloned.1.call-update) | async-done | bytes 2097168 | tf_op jit(solution)/shard_map/all_gather | solution.py:457
  634.3 41.1 %units.3 = (bf16[512,2048]{1,0:T(8,128)(2,1)}, bf16[512,1536]{1,0:T(8,128)(2,1)}, bf16[512,1536]{1,0:T(8,128)(2,1)}, bf16[512,1536]{1,0:T(8,128)(2,1)}, bf16[512,2048]{1,0:T(8,128)(2,1)}, /*index=5*/f32[1,2048]{1,0:T(1,128)}) custom-call(bf16[512,2048]{1,0:T(8,128)(2,1)} %all-gather.23.cloned.1.call-done.mid_ref, ...), custom_call_target="tpu_custom_call" | custom-call | flops 16106127360 | bytes 18874368 | tf_op jit(solution)/shard_map/units/pallas_call | solution.py:342
  675.5 4.2 reduce-scatter.25.cloned.1.call-done
  681.1 44.6 %reduce-scatter.15.cloned.1.call-done = bf16[128,2048]{1,0:T(8,128)(2,1)} async-done(((bf16[512,2048]{1,0:T(8,128)(2,1)}), bf16[128,2048]{1,0:T(8,128)(2,1)}) %reduce-scatter.15.cloned.1.call-update) | async-done | bytes 524304 | tf_op jit(solution)/shard_map/reduce_scatter | solution.py:461
  725.7 46.0 %reduce-scatter.27.cloned.1.call-done = bf16[128,2048]{1,0:T(8,128)(2,1)} async-done(((bf16[512,2048]{1,0:T(8,128)(2,1)}), bf16[128,2048]{1,0:T(8,128)(2,1)}) %reduce-scatter.27.cloned.1.call-update) | async-done | bytes 524304 | tf_op jit(solution)/shard_map/reduce_scatter | solution.py:461
  771.6 4.9 fusion.40
  778.0 45.3 %all-gather.29.cloned.1.call-done.r_ref = bf16[512,2048]{1,0:T(8,128)(2,1)} async-done(((bf16[128,2048]{1,0:T(8,128)(2,1)}), bf16[512,2048]{1,0:T(8,128)(2,1)}) %all-gather.29.cloned.1.call-update) | async-done | bytes 2097168 | tf_op jit(solution)/shard_map/all_gather | solution.py:457
  823.3 13.4 attend_back.3
  838.0 5.9 fusion.22
  843.9 64.9 %reduce-scatter.29.cloned.1.call-done.dkv_ref = bf16[512,512]{1,0:T(8,128)(2,1)} async-done(((bf16[4096,512]{1,0:T(8,128)(2,1)}), bf16[512,512]{1,0:T(8,128)(2,1)}) %reduce-scatter.29.cloned.1.call-update) | async-done | bytes 524304 | tf_op jit(solution)/shard_map/reduce_scatter | solution.py:461
  908.8 12.7 unproject.3
  921.5 10.9 convolution_convert_fusion.3
  937.2 10.3 convolution_convert_fusion
  947.4 8.8 convolution_convert_fusion.1
  956.2 8.8 convolution_convert_fusion.2
  966.8 9.1 convolution_convert_fusion.4
  975.9 43.4 %reduce-scatter.33.cloned.1.call-done = bf16[256,1536]{1,0:T(8,128)(2,1)} async-done(((bf16[2048,1536]{1,0:T(8,128)(2,1)}), bf16[256,1536]{1,0:T(8,128)(2,1)}) %reduce-scatter.33.cloned.1.call-update) | async-done | bytes 786448 | tf_op jit(solution)/shard_map/reduce_scatter | solution.py:461
  1019.4 245.7 %all-reduce.3.cloned.1.call-done = (bf16[2048,1536]{1,0:T(8,128)(2,1)}, bf16[2048,1536]{1,0:T(8,128)(2,1)}, bf16[1536,2048]{1,0:T(8,128)(2,1)}) async-done(((bf16[2048,1536]{1,0:T(8,128)(2,1)}, bf16[2048,1536]{1,0:T(8,128)(2,1)}, bf16[1536,2048]{1,0:T(8,128)(2,1)}), (bf16[2048,1536]{1,0:T(8,128)(2,1)}, bf16[2048,1536]{1,0:T(8,128)(2,1)}, bf16[1536,2048]{1,0:T(8,128)(2,1)})) %all-reduce.3.cloned.1.call-update) | async-done | bytes 18874384 | tf_op jit(solution)/shard_map/psum | solution.py:529
  1265.1 9.5 convert_element_type.187
  1274.6 6.6 convert_element_type.189
  1281.2 6.3 convert_element_type.191
  1287.6 41.6 %psum.31 = f32[4352]{0:T(1024)S(1)} all-reduce(f32[4352]{0:T(1024)S(1)} %pad_maximum_fusion.4), channel_id=1, replica_groups=mesh['seq'=8,'head'=4] {'seq','head'}, use_global_device_ids=true, to_apply=%region_23.0 | all-reduce | flops 4352 | bytes 34816 | tf_op jit(solution)/shard_map/psum | solution.py:564
  1330.5 4.2 convert_element_type.185
  1334.7 8.4 reduce-scatter.31.cloned.1.call-done
  1344.6 44.4 %reduce-scatter.19.cloned.1.call-done = bf16[128,2048]{1,0:T(8,128)(2,1)} async-done(((bf16[512,2048]{1,0:T(8,128)(2,1)}), bf16[128,2048]{1,0:T(8,128)(2,1)}) %reduce-scatter.19.cloned.1.call-update) | async-done | bytes 524304 | tf_op jit(solution)/shard_map/reduce_scatter | solution.py:461
  1397.2 38.7 %all-gather.31.cloned.1.call-done = bf16[2048,1536]{1,0:T(8,128)(2,1)} async-done(((bf16[256,1536]{1,0:T(8,128)(2,1)}), bf16[2048,1536]{1,0:T(8,128)(2,1)}) %all-gather.31.cloned.1.call-update) | async-done | bytes 6291472 | tf_op jit(solution)/shard_map/all_gather | solution.py:457
  1435.9 4.0 slice_convert_fusion.2
  1440.4 4.6 slice_convert_fusion
  (169 shorter events, 58.1 us)
Async XLA Ops:
  7.2 53.3 %all-gather.35.cloned.1.call-start = ((), (), s32[]{:S(2)}) async-start(), calls=%async_computation.34 | async-start | bytes 2621440 | tf_op jit(solution)/shard_map/all_gather | solution.py:457
  11.7 93.0 %all-gather.15.cloned.1.call-start = ((), (), s32[]{:S(2)}) async-start(), calls=%async_computation.12 | async-start | bytes 4718592 | tf_op jit(solution)/shard_map/all_gather | solution.py:457
  60.5 8.7 copy-start.18
  69.1 98.1 %reduce-scatter.13.cloned.1.call-start = ((), (), s32[]{:S(2)}) async-start(), calls=%async_computation.13 | async-start | bytes 2621440 | tf_op jit(solution)/shard_map/reduce_scatter | solution.py:461
  114.5 100.1 %all-gather.19.cloned.1.call-start = ((), (), s32[]{:S(2)}) async-start(), calls=%async_computation.15 | async-start | bytes 2621440 | tf_op jit(solution)/shard_map/all_gather | solution.py:457
  120.8 140.0 %all-gather.17.cloned.1.call-start = ((), (), s32[]{:S(2)}) async-start(), calls=%async_computation.14 | async-start | bytes 2621440 | tf_op jit(solution)/shard_map/all_gather | solution.py:457
  169.5 138.1 %all-gather.37.cloned.1.call-start = ((), (), s32[]{:S(2)}) async-start(), calls=%async_computation.35 | async-start | bytes 2621440 | tf_op jit(solution)/shard_map/all_gather | solution.py:457
  170.7 182.5 %reduce-scatter.21.cloned.1.call-start = ((), (), s32[]{:S(2)}) async-start(), calls=%async_computation.22 | async-start | bytes 2621440 | tf_op jit(solution)/shard_map/reduce_scatter | solution.py:461
  301.9 89.8 %all-gather.21.cloned.1.call-start = ((), (), s32[]{:S(2)}) async-start(), calls=%async_computation.17 | async-start | bytes 4718592 | tf_op jit(solution)/shard_map/all_gather | solution.py:457
  307.6 45.6 %copy-start.12 = (f32[2048]{0:T(1024)S(1)}, f32[2048]{0:T(1024)}, u32[]{:S(2)}) copy-start(f32[2048]{0:T(1024)} %param.27) | copy-start | bytes 24580
  316.2 123.6 %all-gather.27.cloned.1.call-start = ((), (), s32[]{:S(2)}) async-start(), calls=%async_computation.23 | async-start | bytes 2621440 | tf_op jit(solution)/shard_map/all_gather | solution.py:457
  357.6 127.6 %reduce-scatter.17.cloned.1.call-start = ((), (), s32[]{:S(2)}) async-start(), calls=%async_computation.18 | async-start | bytes 2621440 | tf_op jit(solution)/shard_map/reduce_scatter | solution.py:461
  391.7 6.6 copy-start.20
  401.9 138.2 %reduce-scatter.23.cloned.1.call-start = ((), (), s32[]{:S(2)}) async-start(), calls=%async_computation.24 | async-start | bytes 4718592 | tf_op jit(solution)/shard_map/reduce_scatter | solution.py:461
  452.8 135.2 %all-gather.25.cloned.1.call-start = ((), (), s32[]{:S(2)}) async-start(), calls=%async_computation.20 | async-start | bytes 2621440 | tf_op jit(solution)/shard_map/all_gather | solution.py:457
  454.7 179.6 %all-gather.23.cloned.1.call-start = ((), (), s32[]{:S(2)}) async-start(), calls=%async_computation.19 | async-start | bytes 2621440 | tf_op jit(solution)/shard_map/all_gather | solution.py:457
  487.3 192.3 %reduce-scatter.25.cloned.1.call-start = ((), (), s32[]{:S(2)}) async-start(), calls=%async_computation.25 | async-start | bytes 2621440 | tf_op jit(solution)/shard_map/reduce_scatter | solution.py:461
  552.8 172.9 %reduce-scatter.15.cloned.1.call-start = ((), (), s32[]{:S(2)}) async-start(), calls=%async_computation.16 | async-start | bytes 2621440 | tf_op jit(solution)/shard_map/reduce_scatter | solution.py:461
  560.9 118.8 %copy-start.10 = (f32[2048]{0:T(1024)S(1)}, f32[2048]{0:T(1024)}, u32[]{:S(2)}) copy-start(f32[2048]{0:T(1024)} %param.26) | copy-start | bytes 24580
  560.9 210.8 %reduce-scatter.27.cloned.1.call-start = ((), (), s32[]{:S(2)}) async-start(), calls=%async_computation.26 | async-start | bytes 2621440 | tf_op jit(solution)/shard_map/reduce_scatter | solution.py:461
  675.4 96.2 %copy-start.13 = (f32[2048]{0:T(1024)S(1)}, f32[2048]{0:T(1024)}, u32[]{:S(2)}) copy-start(f32[2048]{0:T(1024)} %param.27) | copy-start | bytes 24580
  675.4 147.9 %all-gather.29.cloned.1.call-start = ((), (), s32[]{:S(2)}) async-start(), calls=%async_computation.27 | async-start | bytes 2621440 | tf_op jit(solution)/shard_map/all_gather | solution.py:457
  777.9 130.8 %reduce-scatter.29.cloned.1.call-start = ((), (), s32[]{:S(2)}) async-start(), calls=%async_computation.28 | async-start | bytes 4718592 | tf_op jit(solution)/shard_map/reduce_scatter | solution.py:461
  836.8 128.3 %reduce-scatter.35.cloned.1.call-start = ((), (), s32[]{:S(2)}) async-start(), calls=%async_computation.32 | async-start | bytes 2359296 | tf_op jit(solution)/shard_map/reduce_scatter | solution.py:461
  843.9 175.4 %reduce-scatter.33.cloned.1.call-start = ((), (), s32[]{:S(2)}) async-start(), calls=%async_computation.30 | async-start | bytes 7077888 | tf_op jit(solution)/shard_map/reduce_scatter | solution.py:461
  908.8 12.7 copy-start.23
  932.4 332.7 %all-reduce.3.cloned.1.call-start = ((), (), s32[]{:S(2)}) async-start(), calls=%async_computation.36 | async-start | bytes 37748736 | tf_op jit(solution)/shard_map/psum | solution.py:529
  937.2 10.3 copy-start.32
  937.2 10.3 copy-start.34
  947.4 8.8 copy-start.31
  947.4 8.8 copy-start.33
  965.0 365.5 %all-gather.33.cloned.1.call-start = ((), (), s32[]{:S(2)}) async-start(), calls=%async_computation.33 | async-start | bytes 2359296 | tf_op jit(solution)/shard_map/all_gather | solution.py:457
  965.8 377.3 %reduce-scatter.31.cloned.1.call-start = ((), (), s32[]{:S(2)}) async-start(), calls=%async_computation.29 | async-start | bytes 2621440 | tf_op jit(solution)/shard_map/reduce_scatter | solution.py:461
  966.5 52.8 %copy-start.14 = (f32[1,2048]{1,0:T(1,128)S(1)}, f32[1,2048]{1,0:T(1,128)}, u32[]{:S(2)}) copy-start(f32[1,2048]{1,0:T(1,128)} %get-tuple-element.100) | copy-start | bytes 24580
  966.5 52.8 %copy-start.16 = (f32[1,2048]{1,0:T(1,128)S(1)}, f32[1,2048]{1,0:T(1,128)}, u32[]{:S(2)}) copy-start(f32[1,2048]{1,0:T(1,128)} %get-tuple-element.101) | copy-start | bytes 24580
  966.5 422.5 %reduce-scatter.19.cloned.1.call-start = ((), (), s32[]{:S(2)}) async-start(), calls=%async_computation.21 | async-start | bytes 2621440 | tf_op jit(solution)/shard_map/reduce_scatter | solution.py:461
  975.9 460.1 %all-gather.31.cloned.1.call-start = ((), (), s32[]{:S(2)}) async-start(), calls=%async_computation.31 | async-start | bytes 7077888 | tf_op jit(solution)/shard_map/all_gather | solution.py:457
  1265.1 9.5 copy-start.4
  1265.1 16.1 %slice-start = ((s8[6291456]{0:T(1024)(128)(4,1)}), s8[4194304]{0:T(1024)(128)(4,1)S(1)}, s32[]{:S(2)}) async-start(s8[6291456]{0:T(1024)(128)(4,1)} %bitcast.69), calls=%async_computation.37 | async-start | bytes 8388608
  1274.6 6.6 slice-start.1
  1281.2 6.4 copy-start.15
  1281.2 6.4 copy-start.25
  1281.2 6.4 copy-start.27
  1281.2 6.4 copy-start.24
  1281.2 6.4 copy-start.26
  1330.5 12.6 copy-start.11
  1330.5 58.5 %copy-start.2 = (bf16[128,2048]{1,0:T(8,128)(2,1)S(1)}, bf16[128,2048]{1,0:T(8,128)(2,1)}, u32[]{:S(2)}) copy-start(bf16[128,2048]{1,0:T(8,128)(2,1)} %fusion.53) | copy-start | bytes 1572868
  1330.5 58.5 %copy-start.6 = (bf16[128,2048]{1,0:T(8,128)(2,1)S(1)}, bf16[128,2048]{1,0:T(8,128)(2,1)}, u32[]{:S(2)}) copy-start(bf16[128,2048]{1,0:T(8,128)(2,1)} %reduce-scatter.27.cloned.1.call-done) | copy-start | bytes 1572868
  (14 other events, 45.4 us)
Sparse Core Ops, SparseCore 0:
  11.8 48.6 all-gather.34
  69.2 35.4 all-gather.14
  114.6 52.5 reduce-scatter.12
  169.3 45.2 all-gather.18
  216.1 44.6 all-gather.16
  262.9 44.6 all-gather.36
  310.5 42.5 reduce-scatter.20
  355.6 36.0 all-gather.20
  393.8 45.9 all-gather.26
  442.5 42.5 reduce-scatter.16
  489.4 50.6 reduce-scatter.22
  542.1 45.8 all-gather.24
  589.6 44.6 all-gather.22
  637.0 42.5 reduce-scatter.24
  682.4 43.1 reduce-scatter.14
  728.4 43.1 reduce-scatter.26
  778.1 45.2 all-gather.28
  836.9 71.8 reduce-scatter.28
  912.1 41.1 reduce-scatter.34
  957.5 61.7 reduce-scatter.32
  1024.6 240.4 all-reduce.2
  1267.2 27.9 all-gather.32
  1298.2 44.8 reduce-scatter.30
  1345.8 43.1 reduce-scatter.18
  1391.1 44.8 all-gather.30

commit v2 on v1

--- a/solution.py
+++ b/solution.py
@@ -13,6 +13,7 @@
 VMEM_LIMIT = 58 * 1024 * 1024
 LOW = jnp.bfloat16
 F32 = jnp.float32
+MESH = pl.DeviceIdType.MESH
 
 
 def mm(left, right):
@@ -35,8 +36,10 @@
     return pltpu.CompilerParams(vmem_limit_bytes=VMEM_LIMIT, **extra)
 
 
-def cost(flops, moved, exps=0):
-    return pl.CostEstimate(flops=int(flops), bytes_accessed=int(moved), transcendentals=int(exps))
+def takes(microseconds):
+    return pl.CostEstimate(
+        flops=int(microseconds * 1.15e9), bytes_accessed=int(microseconds * 3.69e6), transcendentals=0
+    )
 
 
 WHOLE = pl.BlockSpec(memory_space=pltpu.VMEM)
@@ -107,7 +110,7 @@
             shape_of(rows, nk, F32), shape_of(rows, 2 * nk, LOW), shape_of(rows, nq, F32),
         ],
         compiler_params=params(),
-        cost_estimate=cost(2 * rows * model * 2 * (nq + nk), model * 2 * (nq + nk) * 2),
+        cost_estimate=takes(9),
         name="project",
     )(x, gain, cosine, sine, qgain, kgain, wq, wk, wv, wg)
 
@@ -187,7 +190,7 @@
             pltpu.VMEM((heads, rows, 128), F32),
         ],
         compiler_params=params(),
-        cost_estimate=cost(4 * rows * kv.shape[0] * width, kv.size * 2, rows * kv.shape[0] * heads),
+        cost_estimate=takes(9),
         name="attend",
     )(place, q, kv, gate)
 
@@ -285,74 +288,9 @@
             pltpu.VMEM((heads, rows, head_dim), F32),
         ],
         compiler_params=params(),
-        cost_estimate=cost(10 * rows * kv.shape[0] * width, kv.size * 4, rows * kv.shape[0] * heads),
+        cost_estimate=takes(20),
         name="attend_back",
     )(place, q, kv, r, wo, att, gate, inv)
-
-
-def units_kernel(
-    mid_ref, masked_ref, gain_ref, wg_ref, wl_ref, wd_ref,
-    normed_ref, hidden_ref, dg_ref, dl_ref, dn_ref, dgain_ref,
-    acc_ref,
-):
-    step = pl.program_id(0)
-
-    @pl.when(step == 0)
-    def _():
-        x = mid_ref[...].astype(F32)
-        normed_ref[...] = (x * inverse_rms(x) * gain_ref[...]).astype(LOW)
-
-    normed = normed_ref[...]
-    gate = mm(normed, wg_ref[...])
-    lift = mm(normed, wl_ref[...])
-    grad = mm_t(masked_ref[...], wd_ref[...])
-    sigmoid = jax.nn.sigmoid(gate)
-    silu = gate * sigmoid
-    hidden_ref[...] = (silu * lift).astype(LOW)
-    lift_grad = (grad * silu).astype(LOW)
-    gate_grad = (grad * lift * (sigmoid + silu * (1.0 - sigmoid))).astype(LOW)
-    dg_ref[...] = gate_grad
-    dl_ref[...] = lift_grad
-    part = mm_t(gate_grad, wg_ref[...]) + mm_t(lift_grad, wl_ref[...])
-
-    @pl.when(step == 0)
-    def _():
-        acc_ref[...] = part
-
-    @pl.when(step > 0)
-    def _():
-        acc_ref[...] = acc_ref[...] + part
-
-    @pl.when(step == pl.num_programs(0) - 1)
-    def _():
-        total = acc_ref[...]
-        dn_ref[...] = total.astype(LOW)
-        x = mid_ref[...].astype(F32)
-        dgain_ref[...] = jnp.sum(total * x * inverse_rms(x), axis=0, keepdims=True)
-
-
-def units(mid, masked, gain, wg, wl, wd):
-    rows, model = mid.shape
-    hidden = wg.shape[1]
-    tile = 256
-    whole = pl.BlockSpec((rows, model), lambda i: (0, 0))
-    tall = pl.BlockSpec((model, tile), lambda i: (0, i))
-    wide = pl.BlockSpec((tile, model), lambda i: (i, 0))
-    part = pl.BlockSpec((rows, tile), lambda i: (0, i))
-    return pl.pallas_call(
-        units_kernel,
-        grid=(hidden // tile,),
-        in_specs=[whole, whole, full_block(gain), tall, tall, wide],
-        out_specs=[whole, part, part, part, whole, pl.BlockSpec((1, model), lambda i: (0, 0))],
-        out_shape=[
-            shape_of(rows, model, LOW), shape_of(rows, hidden, LOW), shape_of(rows, hidden, LOW),
-            shape_of(rows, hidden, LOW), shape_of(rows, model, LOW), shape_of(1, model, F32),
-        ],
-        scratch_shapes=[pltpu.VMEM((rows, model), F32)],
-        compiler_params=params(),
-        cost_estimate=cost(10 * rows * model * hidden, 6 * model * hidden),
-        name="units",
-    )(mid, masked, gain, wg, wl, wd)
 
 
 def unproject_kernel(
@@ -433,9 +371,599 @@
             shape_of(1, model, F32), shape_of(1, head_dim, F32), shape_of(1, head_dim, F32),
         ],
         compiler_params=params(),
-        cost_estimate=cost(2 * rows * model * 2 * (nq + nk), model * 2 * (nq + nk) * 2),
+        cost_estimate=takes(13),
         name="unproject",
     )(x, gain, cosine, sine, qgain, kgain, wq, wk, wv, wg, dq, qraw, dkv, kraw, dgate)
+
+
+class Line:
+    def __init__(self, pieces, count, part_ref, own_ref, right_ref, left_ref, sems, spread=None):
+        self.pieces, self.count = pieces, count
+        self.place = lax.axis_index("head")
+        self.part_ref, self.own_ref = part_ref, own_ref
+        self.right_ref, self.left_ref = right_ref, left_ref
+        self.sems = sems
+        self.spread = spread
+
+    def barrier(self):
+        sem = pltpu.get_barrier_semaphore()
+        place, count = self.place, self.count
+
+        @pl.when(place > 0)
+        def _():
+            pl.semaphore_signal(sem, inc=1, device_id={"head": place - 1}, device_id_type=MESH)
+
+        @pl.when(place < count - 1)
+        def _():
+            pl.semaphore_signal(sem, inc=1, device_id={"head": place + 1}, device_id_type=MESH)
+
+        inside = (place > 0) & (place < count - 1)
+
+        @pl.when(inside)
+        def _():
+            pl.semaphore_wait(sem, 2)
+
+        @pl.when(jnp.logical_not(inside))
+        def _():
+            pl.semaphore_wait(sem, 1)
+
+    def copy(self, ref, send, receive, p, t, step):
+        return pltpu.make_async_remote_copy(
+            src_ref=ref,
+            dst_ref=ref,
+            send_sem=self.sems[send].at[p, t],
+            recv_sem=self.sems[receive].at[p, t],
+            device_id={"head": jnp.clip(self.place + step, 0, self.count - 1)},
+            device_id_type=MESH,
+        )
+
+    def sum_copy(self, p, t, step):
+        ref = self.right_ref if step > 0 else self.left_ref
+        base = 0 if step > 0 else 2
+        return self.copy(ref.at[p, t], base, base + 1, p, t, step)
+
+    def spread_copy(self, p, t, step):
+        return self.copy(self.spread(p, t), 4 if step > 0 else 5, 6, p, t, step)
+
+    def send_sums(self, p, distance):
+        place, count = self.place, self.count
+        for step, ref in ((1, self.right_ref), (-1, self.left_ref)):
+            t = place + step * distance
+            first = place == (0 if step > 0 else count - 1)
+
+            @pl.when((t >= 0) & (t < count))
+            def _(t=t, step=step, ref=ref, first=first):
+                @pl.when(first)
+                def _():
+                    ref[p, t] = self.part_ref[t].astype(LOW)
+
+                @pl.when(jnp.logical_not(first))
+                def _():
+                    self.sum_copy(p, t, step).wait_recv()
+                    ref[p, t] = (ref[p, t].astype(F32) + self.part_ref[t].astype(F32)).astype(LOW)
+
+                self.sum_copy(p, t, step).start()
+
+    def keep_own(self, p):
+        self.own_ref[p] = self.part_ref[self.place].astype(F32)
+
+    def finish_own(self, p):
+        place, count = self.place, self.count
+        for step, ref, inner in ((1, self.right_ref, place > 0), (-1, self.left_ref, place < count - 1)):
+
+            @pl.when(inner)
+            def _(step=step, ref=ref):
+                self.sum_copy(p, place, step).wait_recv()
+                self.own_ref[p] = self.own_ref[p] + ref[p, place].astype(F32)
+
+    def hand_out(self, p):
+        place, count = self.place, self.count
+
+        @pl.when(place < count - 1)
+        def _():
+            self.spread_copy(p, place, 1).start()
+
+        @pl.when(place > 0)
+        def _():
+            self.spread_copy(p, place, -1).start()
+
+    def hand_on(self, p, distance):
+        place, count = self.place, self.count
+        for step, more in ((1, place < count - 1), (-1, place > 0)):
+            t = place - step * distance
+
+            @pl.when((t >= 0) & (t < count))
+            def _(t=t, step=step, more=more):
+                self.spread_copy(p, t, step).wait_recv()
+
+                @pl.when(more)
+                def _():
+                    self.spread_copy(p, t, step).start()
+
+    def drain(self):
+        place, count = self.place, self.count
+
+        def one(p, carry):
+            for t in range(count):
+
+                @pl.when(t > place)
+                def _(t=t):
+                    self.sum_copy(p, t, 1).wait_send()
+
+                @pl.when(t < place)
+                def _(t=t):
+                    self.sum_copy(p, t, -1).wait_send()
+
+                if self.spread is not None:
+
+                    @pl.when((t <= place) & (place < count - 1))
+                    def _(t=t):
+                        self.spread_copy(p, t, 1).wait_send()
+
+                    @pl.when((t >= place) & (place > 0))
+                    def _(t=t):
+                        self.spread_copy(p, t, -1).wait_send()
+
+            return carry
+
+        lax.fori_loop(0, self.pieces, one, 0)
+
+
+def line_scratch(pieces, count, rows, model, part_kind, spread):
+    slots = (pieces, count)
+    scratch = [
+        pltpu.VMEM((pieces, rows, model), F32),
+        pltpu.VMEM((pieces, count, rows, model), LOW),
+        pltpu.VMEM((pieces, count, rows, model), LOW),
+    ] + [pltpu.SemaphoreType.DMA(slots)] * (7 if spread else 4)
+    if part_kind is not None:
+        scratch = [pltpu.VMEM((count, rows, model), part_kind)] + scratch
+    return scratch
+
+
+def both_ways(index, limit, body):
+    @pl.when((index >= 0) & (index < limit))
+    def _():
+        body(index)
+
+
+def middle_kernel(
+    pieces, count,
+    acted_ref, tok_ref, gain_ref, wo_ref, masked_hbm, wg_hbm, wl_hbm, wd_hbm,
+    middle_ref, dgain_ref, normed_hbm, hidden_hbm, dg_hbm, dl_hbm, dn_hbm,
+    mid_ref, wg_ref, wl_ref, wd_ref, masked_ref, normed_ref, hidden_ref, dg_ref, dl_ref, dn_ref, acc_ref,
+    load_sem, masked_sem, store_sem,
+    part_ref, own_ref, right_ref, left_ref, *sems,
+):
+    rows, model = own_ref.shape[1], own_ref.shape[2]
+    tall = count * rows
+    hidden = wg_ref.shape[1]
+    line = Line(
+        pieces, count, part_ref, own_ref, right_ref, left_ref, sems, spread=lambda p, t: mid_ref.at[p, t]
+    )
+    place = line.place
+    loads = [
+        pltpu.make_async_copy(source, target, load_sem.at[i])
+        for i, (source, target) in enumerate(((wg_hbm, wg_ref), (wl_hbm, wl_ref), (wd_hbm, wd_ref)))
+    ]
+    line.barrier()
+    for load in loads:
+        load.start()
+    dgain_ref[...] = jnp.zeros_like(dgain_ref)
+    tiles = 3
+    tile = hidden // tiles
+
+    def masked_copy(p):
+        return pltpu.make_async_copy(masked_hbm.at[:, p], masked_ref, masked_sem)
+
+    def stores(p):
+        pairs = (
+            (normed_ref, normed_hbm), (hidden_ref, hidden_hbm), (dg_ref, dg_hbm), (dl_ref, dl_hbm),
+            (dn_ref, dn_hbm),
+        )
+        return [
+            pltpu.make_async_copy(source, target.at[:, p], store_sem.at[i])
+            for i, (source, target) in enumerate(pairs)
+        ]
+
+    def begin(p):
+        acted = acted_ref[p // 2, :, p % 2].reshape(tall, acted_ref.shape[-1])
+        part_ref[...] = mm(acted, wo_ref[...]).reshape(count, rows, model)
+        line.keep_own(p)
+
+    def own(p):
+        line.finish_own(p)
+        middle = own_ref[p] + tok_ref[p].astype(F32)
+        middle_ref[p] = middle
+        mid_ref[p, place] = middle.astype(LOW)
+        line.hand_out(p)
+
+    def units_begin(p):
+        line.hand_on(p, count - 1)
+
+        @pl.when(p > 0)
+        def _():
+            for store in stores(p - 1):
+                store.wait()
+
+        x = mid_ref[p].reshape(tall, model).astype(F32)
+        normed = (x * inverse_rms(x) * gain_ref[...]).astype(LOW)
+        normed_ref[...] = normed.reshape(count, rows, model)
+        masked_copy(p).wait()
+
+        @pl.when(p == 0)
+        def _():
+            for load in loads:
+                load.wait()
+
+    def units_tile(i):
+        span = slice(i * tile, (i + 1) * tile)
+        normed = normed_ref[...].reshape(tall, model)
+        gate = mm(normed, wg_ref[:, span])
+        lift = mm(normed, wl_ref[:, span])
+        grad = mm_t(masked_ref[...].reshape(tall, model), wd_ref[span, :])
+        sigmoid = jax.nn.sigmoid(gate)
+        silu = gate * sigmoid
+        lift_grad = (grad * silu).astype(LOW)
+        gate_grad = (grad * lift * (sigmoid + silu * (1.0 - sigmoid))).astype(LOW)
+        hidden_ref[:, :, span] = (silu * lift).astype(LOW).reshape(count, rows, tile)
+        dg_ref[:, :, span] = gate_grad.reshape(count, rows, tile)
+        dl_ref[:, :, span] = lift_grad.reshape(count, rows, tile)
+        part = mm_t(gate_grad, wg_ref[:, span]) + mm_t(lift_grad, wl_ref[:, span])
+        if i == 0:
+            acc_ref[...] = part
+        else:
+            acc_ref[...] = acc_ref[...] + part
+
+    def units_end(p):
+        total = acc_ref[...]
+        dn_ref[...] = total.astype(LOW).reshape(count, rows, model)
+        x = mid_ref[p].reshape(tall, model).astype(F32)
+        dgain_ref[...] = dgain_ref[...] + jnp.sum(total * x * inverse_rms(x), axis=0, keepdims=True)
+        for store in stores(p):
+            store.start()
+
+        @pl.when(p < pieces - 1)
+        def _():
+            masked_copy(p + 1).start()
+
+    masked_copy(0).start()
+
+    def turn_once(k, carry):
+        both_ways(k, pieces, begin)
+        for i in range(max(tiles, count - 1)):
+            if i < count - 1:
+                both_ways(k, pieces, lambda p, i=i: line.send_sums(p, count - 1 - i))
+            if i == 0:
+                both_ways(k - 1, pieces, own)
+                both_ways(k - 2, pieces, units_begin)
+            elif i < count - 1:
+                both_ways(k - 1, pieces, lambda p, i=i: line.hand_on(p, i))
+            if i < tiles:
+                both_ways(k - 2, pieces, lambda p, i=i: units_tile(i))
+        both_ways(k - 2, pieces, units_end)
+        return carry
+
+    lax.fori_loop(0, pieces + 2, turn_once, 0)
+    for store in stores(pieces - 1):
+        store.wait()
+    line.drain()
+
+
+def middle_step(acted, tok, gain, wo, masked, wg, wl, wd, count):
+    pieces, rows, model = tok.shape
+    hidden = wg.shape[1]
+    any_place = pl.BlockSpec(memory_space=pl.ANY)
+
+    def wide(columns, kind=LOW):
+        return jax.ShapeDtypeStruct((count, pieces, rows, columns), kind)
+
+    def room(columns, kind=LOW):
+        return pltpu.VMEM((count, rows, columns), kind)
+
+    return pl.pallas_call(
+        functools.partial(middle_kernel, pieces, count),
+        in_specs=[WHOLE] * 4 + [any_place] * 4,
+        out_specs=[WHOLE] * 2 + [any_place] * 5,
+        out_shape=[
+            jax.ShapeDtypeStruct((pieces, rows, model), F32), shape_of(1, model, F32),
+            wide(model), wide(hidden), wide(hidden), wide(hidden), wide(model),
+        ],
+        scratch_shapes=[
+            pltpu.VMEM((pieces, count, rows, model), LOW),
+            pltpu.VMEM(wg.shape, LOW), pltpu.VMEM(wl.shape, LOW), pltpu.VMEM(wd.shape, LOW),
+            room(model), room(model), room(hidden), room(hidden), room(hidden), room(model),
+            pltpu.VMEM((count * rows, model), F32),
+            pltpu.SemaphoreType.DMA((3,)), pltpu.SemaphoreType.DMA, pltpu.SemaphoreType.DMA((5,)),
+        ]
+        + line_scratch(pieces, count, rows, model, F32, True),
+        compiler_params=params(collective_id=0, has_side_effects=True),
+        cost_estimate=takes(128),
+        name="middle",
+    )(acted, tok, gain, wo, masked, wg, wl, wd)
+
+
+def residual_kernel(
+    pieces, count,
+    dn_ref, middle_ref, masked_ref, gain_ref, residual_ref, r_ref,
+    part_ref, own_ref, right_ref, left_ref, *sems,
+):
+    line = Line(
+        pieces, count, part_ref, own_ref, right_ref, left_ref, sems,
+        spread=lambda p, t: r_ref.at[p // 2, t, p % 2],
+    )
+    line.barrier()
+
+    def begin(p):
+        part_ref[...] = dn_ref[:, p]
+        line.keep_own(p)
+
+    def own(p):
+        line.finish_own(p)
+        x = middle_ref[p].astype(LOW).astype(F32)
+        residual = masked_ref[p] + norm_back(own_ref[p], x, gain_ref[...])
+        residual_ref[p] = residual
+        r_ref[p // 2, line.place, p % 2] = residual.astype(LOW)
+        line.hand_out(p)
+
+    def turn_once(k, carry):
+        both_ways(k, pieces, begin)
+        for i in range(count - 1):
+            both_ways(k, pieces, lambda p, i=i: line.send_sums(p, count - 1 - i))
+            if i == 0:
+                both_ways(k - 1, pieces, own)
+            else:
+                both_ways(k - 1, pieces, lambda p, i=i: line.hand_on(p, i))
+        both_ways(k - 1, pieces, lambda p: line.hand_on(p, count - 1))
+        return carry
+
+    lax.fori_loop(0, pieces + 1, turn_once, 0)
+    line.drain()
+
+
+def residual_step(dn, middle, masked, gain):
+    count, pieces, rows, model = dn.shape
+    return pl.pallas_call(
+        functools.partial(residual_kernel, pieces, count),
+        in_specs=[WHOLE] * 4,
+        out_specs=[WHOLE] * 2,
+        out_shape=[
+            jax.ShapeDtypeStruct((pieces, rows, model), F32),
+            jax.ShapeDtypeStruct((pieces // 2, count, 2, rows, model), LOW),
+        ],
+        scratch_shapes=line_scratch(pieces, count, rows, model, LOW, True),
+        compiler_params=params(collective_id=1, has_side_effects=True),
+        cost_estimate=takes(120),
+        name="residual",
+    )(dn, middle, masked, gain)
+
+
+def input_kernel(
+    pieces, count,
+    dn_ref, tok_ref, residual_ref, gain_ref, grad_ref,
+    part_ref, own_ref, right_ref, left_ref, *sems,
+):
+    line = Line(pieces, count, part_ref, own_ref, right_ref, left_ref, sems)
+    line.barrier()
+
+    def begin(p):
+        part_ref[...] = dn_ref[p // 2, :, p % 2]
+        line.keep_own(p)
+
+    def own(p):
+        line.finish_own(p)
+        x = tok_ref[p].astype(F32)
+        grad_ref[p] = residual_ref[p] + norm_back(own_ref[p], x, gain_ref[...])
+
+    def turn_once(k, carry):
+        both_ways(k, pieces, begin)
+        for i in range(count - 1):
+            both_ways(k, pieces, lambda p, i=i: line.send_sums(p, count - 1 - i))
+            if i == 0:
+                both_ways(k - 1, pieces, own)
+        return carry
+
+    lax.fori_loop(0, pieces + 1, turn_once, 0)
+    line.drain()
+
+
+def input_step(dn, tok, residual, gain):
+    batch, count, halves, rows, model = dn.shape
+    pieces = batch * halves
+    return pl.pallas_call(
+        functools.partial(input_kernel, pieces, count),
+        in_specs=[WHOLE] * 4,
+        out_specs=WHOLE,
+        out_shape=jax.ShapeDtypeStruct((pieces, rows, model), F32),
+        scratch_shapes=line_scratch(pieces, count, rows, model, LOW, False),
+        compiler_params=params(collective_id=2, has_side_effects=True),
+        cost_estimate=takes(110),
+        name="input_grad",
+    )(dn, tok, residual, gain)
+
+
+def flipped(place, mask):
+    bit = 1
+    while bit <= mask:
+        if mask & bit:
+            place = place + (1 - 2 * (place // bit % 2)) * bit
+        bit *= 2
+    return place
+
+
+def digit_orders(count, batch):
+    upper = [1 << i for i in range(1, count.bit_length() - 1)]
+    return [(upper if b % 2 == 0 else upper[::-1]) + [1] for b in range(batch)]
+
+
+def greet(place, digits):
+    sem = pltpu.get_barrier_semaphore()
+    for digit in digits:
+        pl.semaphore_signal(sem, inc=1, device_id={"seq": flipped(place, digit)}, device_id_type=MESH)
+    pl.semaphore_wait(sem, len(digits))
+
+
+def gather_kernel(count, batch, *refs):
+    own, out = refs[:batch], refs[batch : 2 * batch]
+    local_sem, send_sem, receive_sem = refs[2 * batch :]
+    place = lax.axis_index("seq")
+    orders = digit_orders(count, batch)
+    greet(place, orders[0])
+    local = [pltpu.make_async_copy(own[b], out[b].at[place], local_sem.at[b]) for b in range(batch)]
+    for copy in local:
+        copy.start()
+
+    def block(b, mask):
+        return out[b].at[flipped(place, mask)]
+
+    def send(b, mask, step):
+        digit = orders[b][step]
+        return pltpu.make_async_remote_copy(
+            src_ref=own[b] if mask == 0 else block(b, mask),
+            dst_ref=block(b, mask),
+            send_sem=send_sem.at[b, step, mask],
+            recv_sem=receive_sem.at[b, mask | digit],
+            device_id={"seq": flipped(place, digit)},
+            device_id_type=MESH,
+        )
+
+    def arrival(b, mask):
+        return pltpu.make_async_remote_copy(
+            src_ref=block(b, mask),
+            dst_ref=block(b, mask),
+            send_sem=send_sem.at[b, 0, mask],
+            recv_sem=receive_sem.at[b, mask],
+            device_id={"seq": flipped(place, mask)},
+            device_id_type=MESH,
+        )
+
+    steps = len(orders[0])
+    started = []
+    for level in range(-1, steps):
+        masks = [0] if level < 0 else range(1 << level)
+        for turn in masks:
+            for b in range(batch):
+                mask = 0
+                if level >= 0:
+                    mask = orders[b][level]
+                    for i in range(level):
+                        if turn >> i & 1:
+                            mask |= orders[b][i]
+                    arrival(b, mask).wait_recv()
+                for step in range(level + 1, steps):
+                    copy = send(b, mask, step)
+                    copy.start()
+                    started.append(copy)
+    for copy in started:
+        copy.wait_send()
+    for copy in local:
+        copy.wait()
+
+
+def gather_blocks(own):
+    count, batch = lax.axis_size("seq"), len(own)
+    rows, columns = own[0].shape
+    steps = count.bit_length() - 1
+    any_place = pl.BlockSpec(memory_space=pl.ANY)
+    return pl.pallas_call(
+        functools.partial(gather_kernel, count, batch),
+        in_specs=[any_place] * batch,
+        out_specs=[any_place] * batch,
+        out_shape=[jax.ShapeDtypeStruct((count, rows, columns), LOW)] * batch,
+        scratch_shapes=[
+            pltpu.SemaphoreType.DMA((batch,)),
+            pltpu.SemaphoreType.DMA((batch, steps, count)),
+            pltpu.SemaphoreType.DMA((batch, count)),
+        ],
+        compiler_params=params(collective_id=3, has_side_effects=True),
+        cost_estimate=takes(41),
+        name="gather_blocks",
+    )(*own)
+
+
+def scatter_kernel(count, batch, *refs):
+    parts, out = refs[:batch], refs[batch : 2 * batch]
+    slots, send_sem, receive_sem = refs[2 * batch :]
+    place = lax.axis_index("seq")
+    orders = [order[::-1] for order in digit_orders(count, batch)]
+    steps = len(orders[0])
+    greet(place, orders[0])
+
+    def masks_at(b, step):
+        found = [0]
+        for digit in orders[b][step + 1 :][::-1]:
+            found = [mask | digit for mask in found] + found
+        return found
+
+    numbers = {}
+    for b in range(batch):
+        place_in = 0
+        for step in range(steps):
+            for mask in masks_at(b, step):
+                numbers[b, step, mask] = place_in
+                place_in += 1
+
+    def slot(b, step, mask):
+        return slots.at[b, numbers[b, step, mask]]
+
+    def transfer(b, step, mask):
+        digit = orders[b][step]
+        number = numbers[b, step, mask]
+        if step == 0:
+            source = parts[b].at[flipped(place, mask | digit)]
+        else:
+            source = slot(b, step - 1, mask | digit)
+        return pltpu.make_async_remote_copy(
+            src_ref=source,
+            dst_ref=slots.at[b, number],
+            send_sem=send_sem.at[b, number],
+            recv_sem=receive_sem.at[b, number],
+            device_id={"seq": flipped(place, digit)},
+            device_id_type=MESH,
+        )
+
+    started = []
+    for turn in range(count // 2):
+        for b in range(batch):
+            copy = transfer(b, 0, masks_at(b, 0)[turn])
+            copy.start()
+            started.append(copy)
+    for step in range(steps):
+        for turn in range(len(masks_at(0, step))):
+            for b in range(batch):
+                mask = masks_at(b, step)[turn]
+                transfer(b, step, mask).wait_recv()
+                held = parts[b].at[flipped(place, mask)] if step == 0 else slot(b, step - 1, mask)
+                total = held[...].astype(F32) + slot(b, step, mask)[...].astype(F32)
+                if step == steps - 1:
+                    out[b][...] = total.astype(LOW)
+                else:
+                    slot(b, step, mask)[...] = total.astype(LOW)
+                    if mask & orders[b][step + 1]:
+                        copy = transfer(b, step + 1, mask & ~orders[b][step + 1])
+                        copy.start()
+                        started.append(copy)
+    for copy in started:
+        copy.wait_send()
+
+
+def scatter_blocks(parts):
+    count, batch = lax.axis_size("seq"), len(parts)
+    rows, columns = parts[0].shape[0] // count, parts[0].shape[1]
+    return pl.pallas_call(
+        functools.partial(scatter_kernel, count, batch),
+        in_specs=[WHOLE] * batch,
+        out_specs=[WHOLE] * batch,
+        out_shape=[shape_of(rows, columns, LOW)] * batch,
+        scratch_shapes=[
+            pltpu.VMEM((batch, count - 1, rows, columns), LOW),
+            pltpu.SemaphoreType.DMA((batch, count - 1)),
+            pltpu.SemaphoreType.DMA((batch, count - 1)),
+        ],
+        compiler_params=params(collective_id=4, has_side_effects=True),
+        cost_estimate=takes(52),
+        name="scatter_blocks",
+    )(*[part.reshape(count, rows, columns) for part in parts])
 
 
 def turn_tables(positions, head_dim):
@@ -496,38 +1024,40 @@
         for b in seqs
     ]
     normed, qraw, q, kraw, kv_own, gate = [list(x) for x in zip(*projected)]
-    kv = [gather(kv_own[b], "seq") for b in seqs]
-    masked = [gather(own_masked[b].astype(LOW), "head") for b in seqs]
+    kv = [x.reshape(-1, 2 * nk) for x in gather_blocks(kv_own)]
+    masked = gather(jnp.concatenate([x.astype(LOW) for x in own_masked], axis=0), "head")
     attended = [attend(places[b], q[b], kv[b], gate[b], group, head_dim) for b in seqs]
     att, acted, inv = [list(x) for x in zip(*attended)]
-    middle = [
-        own[b].astype(F32)
-        + scatter(mm(acted[b], output_weight).astype(LOW), "head").astype(F32)
-        for b in seqs
-    ]
-    mid = [gather(middle[b].astype(LOW), "head") for b in seqs]
-    forward = [units(mid[b], masked[b], gain_mid, swiglu_gate, swiglu_lift, swiglu_down) for b in seqs]
-    normed_mid, hidden, dg, dl, dn_mid, dgain_mid = [list(x) for x in zip(*forward)]
-    residual = [
-        own_masked[b]
-        + norm_back(
-            scatter(dn_mid[b], "head").astype(F32), middle[b].astype(LOW).astype(F32), gain_mid
-        )
-        for b in seqs
-    ]
-    r = [gather(residual[b].astype(LOW), "head") for b in seqs]
-
-    def both(pair):
-        return jnp.concatenate(pair, axis=0)
-
-    normed_mid_all, masked_all = both(normed_mid), both(masked)
+    halves = 2
+    rows = local_rows // halves
+    pieces = batch * halves
+    acted_all = jnp.stack(acted).reshape(batch, parts, halves, rows, nq)
+    tok = jnp.stack(own).reshape(pieces, rows, model)
+    masked_own = jnp.stack(own_masked).reshape(pieces, rows, model)
+    middle, dgain_mid, normed_mid, hidden, dg, dl, dn_mid = middle_step(
+        acted_all, tok, gain_mid, output_weight,
+        masked.reshape(parts, pieces, rows, model), swiglu_gate, swiglu_lift, swiglu_down, parts,
+    )
+    flat_rows = block_rows * batch
+
+    def flat(array):
+        return array.reshape(flat_rows, array.shape[-1])
+
+    normed_mid, hidden, dg, dl = flat(normed_mid), flat(hidden), flat(dg), flat(dl)
     ff_grads = (
-        t_mm(normed_mid_all, both(dg)).astype(LOW),
-        t_mm(normed_mid_all, both(dl)).astype(LOW),
-        t_mm(both(hidden), masked_all).astype(LOW),
+        t_mm(normed_mid, dg).astype(LOW),
+        t_mm(normed_mid, dl).astype(LOW),
+        t_mm(hidden, masked).astype(LOW),
     )
-    ff_grads = [x.astype(F32) for x in lax.psum(ff_grads, "seq")]
-    units_out = [scatter(mm(hidden[b], swiglu_down).astype(LOW), "head").astype(F32) for b in seqs]
+    dn_mid, ff_grads = lax.optimization_barrier((dn_mid, ff_grads))
+    ff_grads = lax.psum(ff_grads, "seq")
+    residual, r_all = residual_step(dn_mid, middle, masked_own, gain_mid)
+    r_all, hidden = lax.optimization_barrier((r_all, hidden))
+    r_all = r_all.reshape(batch, block_rows, model)
+    r = [r_all[b] for b in seqs]
+    units_out = scatter(mm(hidden, swiglu_down).astype(LOW), "head").astype(F32)
+    units_out = units_out.reshape(batch, local_rows, model)
+    middle = middle.reshape(batch, local_rows, model)
     output = jnp.stack(
         [(valid[b] * (middle[b] + units_out[b])).astype(LOW) for b in seqs], axis=1
     )
@@ -537,7 +1067,7 @@
         for b in seqs
     ]
     dq, dkv_all, dgate = [list(x) for x in zip(*back)]
-    dkv = [scatter(dkv_all[b], "seq") for b in seqs]
+    dkv = scatter_blocks(dkv_all)
     last = [
         unproject(
             rows_in[b], gain_in, cosine, sine, gain_q, gain_k,
@@ -547,19 +1077,20 @@
         for b in seqs
     ]
     dall, dn_in, dgain_in, dgain_q, dgain_k = [list(x) for x in zip(*last)]
-    input_grad = jnp.stack(
-        [
-            residual[b] + norm_back(scatter(dn_in[b], "head").astype(F32), own[b].astype(F32), gain_in)
-            for b in seqs
-        ],
-        axis=1,
+    input_grad = input_step(
+        jnp.stack(dn_in).reshape(batch, parts, halves, rows, model), tok, residual, gain_in
     )
-    out_grad = t_mm(both(acted), both(r)).astype(LOW)
+    input_grad = jnp.transpose(input_grad.reshape(batch, local_rows, model), (1, 0, 2))
+
+    def both(pair):
+        return jnp.concatenate(pair, axis=0)
+
+    ff_grads, dall = lax.optimization_barrier((ff_grads, dall))
+    out_grad = t_mm(both(acted), r_all.reshape(flat_rows, model)).astype(LOW)
     proj_grad = t_mm(both(normed), both(dall)).astype(LOW)
-    out_grad = gather(scatter(out_grad, "seq"), "seq").astype(F32)
-    proj_grad = gather(scatter(proj_grad, "seq"), "seq")
+    out_grad, proj_grad = lax.psum((out_grad, proj_grad), "seq")
     gains = jnp.concatenate(
-        [sum(dgain_in)[0], sum(dgain_mid)[0], sum(dgain_q)[0], sum(dgain_k)[0]]
+        [sum(dgain_in)[0], dgain_mid[0], sum(dgain_q)[0], sum(dgain_k)[0]]
     )
     gains = lax.psum(gains, ("seq", "head"))
 
@@ -574,10 +1105,10 @@
         proj_grad[:, nq : nq + nk].astype(F32),
         proj_grad[:, nq + nk : nq + 2 * nk].astype(F32),
         proj_grad[:, nq + 2 * nk :].astype(F32),
-        out_grad,
-        ff_grads[0],
-        ff_grads[1],
-        ff_grads[2],
+        out_grad.astype(F32),
+        ff_grads[0].astype(F32),
+        ff_grads[1].astype(F32),
+        ff_grads[2].astype(F32),
         share(0, model),
         share(model, model),
         share(2 * model, head_dim),

time: 1450 us -> 906 us (0.62)
  waiting for transfers between devices: 1070 us -> 119 us
  Pallas kernels: 164 us -> 592 us
  matrix products: 68.9 us -> 52.3 us
    pallas_call x2 -> x5, Pallas kernels: 82.2 us -> 510 us  [the longest x1 130 us: input_step(): pl.pallas_call(functools.partial(input_kernel, pieces, count), in_specs=[...]
    reduce_scatter x12 -> x1, waiting for transfers between devices: 422 us -> 0.02 us  [scatter(): return lax.psum_scatter(value, axis, scatter_dimension=0, tiled=True)]
    all_gather x12 -> x3, waiting for transfers between devices: 404 us -> 82.4 us  [gather(): return lax.all_gather(value, axis, axis=0, tiled=True)]
    psum x1 -> x2, waiting for transfers between devices: 246 us -> 36.7 us  [the longest x1 36.7 us: on_device(): out_grad, proj_grad = lax.psum((out_grad, proj_grad), 'seq')]
    dot_general x4 -> x1, matrix products: 24.3 us -> 8.22 us  [mm(): return jnp.dot(left, right, preferred_element_type=F32)]
    convert_element_type x10 -> x8, other arithmetic: 37.5 us -> 24.9 us  [the longest x1 6.9 us: on_device(): ff_grads[0].astype(F32)]
  transfers between devices with their start and end apart: 25 -> 6, of which waited for: 23 -> 4; matrix products, arithmetic and copies ran while one was open for 9% -> 9% of each run, Pallas kernels for 9% -> 51%
where the time goes in v2:
time: 906 us; the launch traced here: 903 us
  Pallas kernels  592 us (65%)
  waiting for transfers between devices  119 us (13%)
  other arithmetic  54.2 us (6%)
  matrix products  52.3 us (6%)
  blocking collectives  40.1 us (4%)
  local copies, waits for them, and re-layouts  29.2 us (3%)
  between operations  15 us (2%)
    pallas_call x1, Pallas kernels, input_step(): pl.pallas_call(functools.partial(input_kernel, pieces, count), in_specs=[...  130 us
    pallas_call x1, Pallas kernels, middle_step(): pl.pallas_call(functools.partial(middle_kernel, pieces, count), in_specs=...  129 us
    pallas_call x1, Pallas kernels, residual_step(): pl.pallas_call(functools.partial(residual_kernel, pieces, count), in_spec...  121 us
    pallas_call x1, Pallas kernels, scatter_blocks(): pl.pallas_call(functools.partial(scatter_kernel, count, batch), in_specs=...  88.8 us
    all_gather x3, waiting for transfers between devices, gather(): return lax.all_gather(value, axis, axis=0, tiled=True)  82.4 us
    dot_general x5, matrix products, t_mm(): lax.dot_general(left, right, (((0,), (0,)), ((), ())), preferred_element_...  44.1 us
    pallas_call x1, Pallas kernels, gather_blocks(): pl.pallas_call(functools.partial(gather_kernel, count, batch), in_specs=[...  41.5 us
    psum x1, blocking collectives, on_device(): gains = lax.psum(gains, ('seq', 'head'))  40.1 us
  transfers between devices with their start and end apart: 6, of which 4 were waited for; matrix products, arithmetic and copies ran while one was open for 9% of the time, Pallas kernels for 51%

profile of v2, /device:TPU:0, one launch (start us, length us, event | category | flops | bytes accessed | tf_op | source)
XLA Modules:
  0.0 902.6 jit_solution(4684586345950124265)
XLA Ops:
  7.2 3.4 fusion.25
  10.6 1.1 copy.38
  11.8 1.1 copy.37
  13.6 1.3 compare_convert_fusion
  14.9 3.4 fusion.24
  21.3 1.1 copy.50
  22.4 1.1 copy.49
  23.5 1.6 fusion.11
  25.5 1.9 pad_add_fusion
  28.4 2.3 pad_maximum_fusion.3
  30.7 1.5 pad_maximum_fusion.1
  33.2 27.3 %all-gather.10.cloned.1.call-done = bf16[512,1,2048]{2,0,1:T(8,128)(2,1)} async-done(((bf16[128,1,2048]{2,0,1:T(8,128)(2,1)}), bf16[512,1,2048]{2,0,1:T(8,128)(2,1)}) %all-gather.10.cloned.1.call-update) | async-done | bytes 2097168 | tf_op jit(solution)/shard_map/all_gather | solution.py:985
  60.6 8.6 project.3
  69.2 38.2 %all-gather.8.cloned.1.call-done = bf16[512,1,2048]{2,0,1:T(8,128)(2,1)} async-done(((bf16[128,1,2048]{2,0,1:T(8,128)(2,1)}), bf16[512,1,2048]{2,0,1:T(8,128)(2,1)}) %all-gather.8.cloned.1.call-update) | async-done | bytes 2097168 | tf_op jit(solution)/shard_map/all_gather | solution.py:985
  107.4 8.6 project.2
  116.0 41.5 %gather_blocks.1 = (bf16[8,512,512]{2,1,0:T(8,128)(2,1)}, bf16[8,512,512]{2,1,0:T(8,128)(2,1)}) custom-call(bf16[512,512]{1,0:T(8,128)(2,1)} %get-tuple-element.73.refs_0_, bf16[512,512]{1,0:T(8,128)(2,1)} %get-tuple-element.74.refs_1_), custom_call_target="tpu_custom_call" | custom-call | flops 47149998080 | bytes 151290000 | tf_op jit(solution)/shard_map/gather_blocks/pallas_call | solution.py:868
  157.5 6.5 attend.3
  164.0 6.1 attend.2
  170.1 2.1 pad_maximum_fusion.2.acted_ref
  172.2 16.8 %all-gather.6.cloned.1.call-done = bf16[1024,2048]{1,0:T(8,128)(2,1)} async-done(((bf16[256,2048]{1,0:T(8,128)(2,1)}), bf16[1024,2048]{1,0:T(8,128)(2,1)}) %all-gather.6.cloned.1.call-update) | async-done | bytes 4194320 | tf_op jit(solution)/shard_map/all_gather | solution.py:985
  189.0 129.0 %middle.1 = (f32[4,64,2048]{2,1,0:T(8,128)}, f32[1,2048]{1,0:T(1,128)}, bf16[4,4,64,2048]{3,2,1,0:T(8,128)(2,1)}, bf16[4,4,64,1536]{3,2,1,0:T(8,128)(2,1)}, bf16...) custom-call(bf16[2,4,2,64,512]{4,3,2,1,0:T(8,128)(2,1)} %pad_maximum_fusion.2.acted_, ...), custom_call_target="tpu_custom_call" | custom-call | flops 147200000000 | bytes 472320000 | tf_op jit(solution)/shard_map/middle/pallas_call | solution.py:664
  318.1 11.9 %bitcast_convert_fusion.1 = bf16[2048,1536]{1,0:T(8,128)(2,1)} fusion(bf16[4,4,64,2048]{3,2,1,0:T(8,128)(2,1)} %get-tuple-element.84, bf16[4,4,64,1536]{3,2,1,0:T(8,128)(2,1)} %get-tuple-element.85), kind=kOutput, calls=%fused_computation.1 | convolution fusion | flops 6445596672 | bytes 13631488 | tf_op jit(solution)/shard_map/dot_general | solution.py:28
  330.0 8.8 bitcast_convert_fusion
  338.8 8.8 convolution_convert_fusion.1
  347.6 120.9 %residual.1 = (f32[4,64,2048]{2,1,0:T(8,128)}, bf16[2,4,2,64,2048]{4,3,2,1,0:T(8,128)(2,1)}) custom-call(bf16[4,4,64,2048]{3,2,1,0:T(8,128)(2,1)} %get-tuple-element.88.dn_ref, f32[4,64,2048]{2,1,0:T(8,128)} %get-tuple-element.82.middle_ref, f32[4,64,2048]{2,1,0:T(8,128)} %bitcast.88, f32[1,2048]{1,0:T(1,128)} %bitcast.111), custom_call_target="tpu_custom_call" | custom-call | flops 138000007168 | bytes 442800000 | tf_op jit(solution)/shard_map/residual/pallas_call | solution.py:726
  468.5 5.2 fusion.22
  474.2 8.2 convolution_convert_fusion.2
  482.5 13.5 %attend_back.3 = (f32[512,512]{1,0:T(8,128)}, bf16[4096,512]{1,0:T(8,128)(2,1)}, bf16[512,512]{1,0:T(8,128)(2,1)}) custom-call(s32[2]{0:T(128)} %get-tuple-element.173.place_ref, bf16[512,512]{1,0:T(8,128)(2,1)} %get-tuple-element.78.q_ref, bf16[4096,512]{1,0:T(8,128)(2,1)} %bitcast.128, bf16[512,2048]{1,0:T(8,128)(2,1)} %bitcast.95, ...), custom_call_target="tpu_custom_call" | custom-call | flops 23000000512 | bytes 73800000 | tf_op jit(solution)/shard_map/attend_back/pallas_call | solution.py:278
  496.0 13.2 %attend_back.2 = (f32[512,512]{1,0:T(8,128)}, bf16[4096,512]{1,0:T(8,128)(2,1)}, bf16[512,512]{1,0:T(8,128)(2,1)}) custom-call(s32[2]{0:T(128)} %get-tuple-element.172.place_ref, bf16[512,512]{1,0:T(8,128)(2,1)} %get-tuple-element.72.q_ref, bf16[4096,512]{1,0:T(8,128)(2,1)} %bitcast.126, bf16[512,2048]{1,0:T(8,128)(2,1)} %bitcast.93, ...), custom_call_target="tpu_custom_call" | custom-call | flops 23000000512 | bytes 73800000 | tf_op jit(solution)/shard_map/attend_back/pallas_call | solution.py:278
  509.2 88.8 %scatter_blocks.1 = (bf16[512,512]{1,0:T(8,128)(2,1)}, bf16[512,512]{1,0:T(8,128)(2,1)}) custom-call(bf16[8,512,512]{2,1,0:T(8,128)(2,1)} %bitcast.130, bf16[8,512,512]{2,1,0:T(8,128)(2,1)} %bitcast.129), custom_call_target="tpu_custom_call" | custom-call | flops 59799998464 | bytes 191880000 | tf_op jit(solution)/shard_map/scatter_blocks/pallas_call | solution.py:953
  598.0 13.1 %unproject.3 = (bf16[512,1536]{1,0:T(8,128)(2,1)}, bf16[512,2048]{1,0:T(8,128)(2,1)}, f32[1,2048]{1,0:T(1,128)}, f32[1,128]{1,0:T(1,128)}, f32[1,128]{1,0:T(1,128)}) custom-call(bf16[512,2048]{1,0:T(8,128)(2,1)} %bitcast.109, f32[1,2048]{1,0:T(1,128)} %bitcast.114, f32[512,128]{1,0:T(8,128)} %get-tuple-element.174.cos_ref, ...), custom_call_target="tpu_custom_call" | custom-call | flops 14949999616 | bytes 47970000 | tf_op jit(solution)/shard_map/unproject/pallas_call | solution.py:359
  611.2 12.9 %unproject.2 = (bf16[512,1536]{1,0:T(8,128)(2,1)}, bf16[512,2048]{1,0:T(8,128)(2,1)}, f32[1,2048]{1,0:T(1,128)}, f32[1,128]{1,0:T(1,128)}, f32[1,128]{1,0:T(1,128)}) custom-call(bf16[512,2048]{1,0:T(8,128)(2,1)} %bitcast.107, f32[1,2048]{1,0:T(1,128)} %bitcast.115, f32[512,128]{1,0:T(8,128)} %get-tuple-element.174.cos_ref, ...), custom_call_target="tpu_custom_call" | custom-call | flops 14949999616 | bytes 47970000 | tf_op jit(solution)/shard_map/unproject/pallas_call | solution.py:359
  624.1 4.1 pad_maximum_fusion.dn_ref
  628.3 3.8 convolution_convert_fusion.3
  632.0 10.9 %convolution_convert_fusion = bf16[2048,1536]{1,0:T(8,128)(2,1)} fusion(bf16[512,2048]{1,0:T(8,128)(2,1)S(1)} %copy-done.24, bf16[512,2048]{1,0:T(8,128)(2,1)} %get-tuple-element.111, bf16[512,1536]{1,0:T(8,128)(2,1)} %get-tuple-element.119, bf16[512,1536]{1,0:T(8,128)(2,1)} %get-tuple-element.118), kind=kOutput, calls=%fused_computation.2 | convolution fusion | flops 6460276736 | bytes 13631488 | tf_op jit(solution)/shard_map/dot_general | solution.py:28
  642.9 129.6 %input_grad.1 = f32[4,64,2048]{2,1,0:T(8,128)} custom-call(bf16[2,4,2,64,2048]{4,3,2,1,0:T(8,128)(2,1)} %pad_maximum_fusion.dn_ref, bf16[4,64,2048]{2,1,0:T(8,128)(2,1)} %bitcast.100, f32[4,64,2048]{2,1,0:T(8,128)} %get-tuple-element.110.residual_ref, f32[1,2048]{1,0:T(1,128)} %bitcast.116), custom_call_target="tpu_custom_call" | custom-call | flops 126500003840 | bytes 405900000 | tf_op jit(solution)/shard_map/input_grad/pallas_call | solution.py:773
  772.6 4.6 copy.48
  777.3 40.1 %psum.47 = f32[4352]{0:T(1024)S(1)} all-reduce(f32[4352]{0:T(1024)S(1)} %pad_maximum_fusion.8), channel_id=1, replica_groups=mesh['seq'=8,'head'=4] {'seq','head'}, use_global_device_ids=true, to_apply=%region_6.0 | all-reduce | flops 4352 | bytes 34816 | tf_op jit(solution)/shard_map/psum | solution.py:1095
  818.7 1.7 fusion.23
  820.4 1.4 convert_element_type.139
  822.3 2.0 copy.34
  825.5 6.9 convert_element_type.151
  832.4 6.6 convert_element_type.152
  838.9 6.3 convert_element_type.153
  845.2 36.7 %all-reduce.5.cloned.1.call-done = (bf16[2048,1536]{1,0:T(8,128)(2,1)}, bf16[512,2048]{1,0:T(8,128)(2,1)}) async-done(((bf16[2048,1536]{1,0:T(8,128)(2,1)}, bf16[512,2048]{1,0:T(8,128)(2,1)}), (bf16[2048,1536]{1,0:T(8,128)(2,1)}, bf16[512,2048]{1,0:T(8,128)(2,1)})) %all-reduce.5.cloned.1.call-update) | async-done | bytes 8388624 | tf_op jit(solution)/shard_map/psum | solution.py:1091
  881.9 6.8 slice_convert_fusion
  888.7 4.0 slice_convert_fusion.2
  892.8 2.5 convert_element_type.150
  (95 shorter events, 9.6 us)
Async XLA Ops:
  7.2 5.8 copy-start.15
  7.2 53.4 %all-gather.10.cloned.1.call-start = ((), (), s32[]{:S(2)}) async-start(), calls=%async_computation.4 | async-start | bytes 2621440 | tf_op jit(solution)/shard_map/all_gather | solution.py:985
  11.8 95.6 %all-gather.8.cloned.1.call-start = ((), (), s32[]{:S(2)}) async-start(), calls=%async_computation.3 | async-start | bytes 2621440 | tf_op jit(solution)/shard_map/all_gather | solution.py:985
  12.9 176.1 %all-gather.6.cloned.1.call-start = ((), (), s32[]{:S(2)}) async-start(), calls=%async_computation.1 | async-start | bytes 5242880 | tf_op jit(solution)/shard_map/all_gather | solution.py:985
  14.9 8.6 copy-start.8
  14.9 10.2 %copy-start.10 = (f32[128]{0:T(128)}, f32[128]{0:T(128)S(1)}, u32[]{:S(2)}) copy-start(f32[128]{0:T(128)S(1)} %get-tuple-element.177) | copy-start | bytes 1540
  18.3 1.0 copy-start
  21.2 610.8 %all-reduce.7.cloned.1.call-start = ((), (), s32[]{:S(2)}) async-start(), calls=%async_computation.6 | async-start | bytes 37748736 | tf_op jit(solution)/shard_map/psum | solution.py:1053
  164.0 6.1 copy-start.5
  318.1 11.9 %copy-start.25 = (bf16[4,4,64,2048]{3,2,1,0:T(8,128)(2,1)S(1)}, bf16[4,4,64,2048]{3,2,1,0:T(8,128)(2,1)}, u32[]{:S(2)}) copy-start(bf16[4,4,64,2048]{3,2,1,0:T(8,128)(2,1)} %get-tuple-element.84) | copy-start | bytes 12582916
  318.1 11.9 %copy-start.26 = (bf16[4,4,64,1536]{3,2,1,0:T(8,128)(2,1)S(1)}, bf16[4,4,64,1536]{3,2,1,0:T(8,128)(2,1)}, u32[]{:S(2)}) copy-start(bf16[4,4,64,1536]{3,2,1,0:T(8,128)(2,1)} %get-tuple-element.86) | copy-start | bytes 9437188
  330.0 8.8 copy-start.17
  330.0 8.8 copy-start.18
  347.6 472.8 %reduce-scatter.2.cloned.1.call-start = ((), (), s32[]{:S(2)}) async-start(), calls=%async_computation.2 | async-start | bytes 5242880 | tf_op jit(solution)/shard_map/reduce_scatter | solution.py:989
  347.6 126.1 %copy-start.19 = (bf16[4,4,64,1536]{3,2,1,0:T(8,128)(2,1)S(1)}, bf16[4,4,64,1536]{3,2,1,0:T(8,128)(2,1)}, u32[]{:S(2)}) copy-start(bf16[4,4,64,1536]{3,2,1,0:T(8,128)(2,1)} %get-tuple-element.87) | copy-start | bytes 9437188
  468.5 5.7 copy-start.16
  482.5 399.4 %all-reduce.5.cloned.1.call-start = ((), (), s32[]{:S(2)}) async-start(), calls=%async_computation.5 | async-start | bytes 16777216 | tf_op jit(solution)/shard_map/psum | solution.py:1091
  611.2 12.9 %copy-start.4 = (bf16[512,2048]{1,0:T(8,128)(2,1)S(1)}, bf16[512,2048]{1,0:T(8,128)(2,1)}, u32[]{:S(2)}) copy-start(bf16[512,2048]{1,0:T(8,128)(2,1)} %get-tuple-element.109) | copy-start | bytes 6291460
  624.1 4.2 copy-start.2
  624.1 4.2 copy-start.6
  624.1 4.2 copy-start.7
  628.2 3.8 copy-start.24
  772.5 4.7 copy-start.13
  772.5 4.7 copy-start.14
  772.6 4.7 copy-start.21
  772.6 4.7 copy-start.23
  772.6 4.7 copy-start.20
  772.6 4.7 copy-start.22
  772.6 4.7 copy-start.12
  777.2 44.7 %copy-start.9 = (f32[128]{0:T(128)S(1)}, f32[128]{0:T(128)}, u32[]{:S(2)}) copy-start(f32[128]{0:T(128)} %copy-done.8) | copy-start | bytes 1540
  777.2 44.7 %copy-start.11 = (f32[128]{0:T(128)S(1)}, f32[128]{0:T(128)}, u32[]{:S(2)}) copy-start(f32[128]{0:T(128)} %copy-done.10) | copy-start | bytes 1540
  821.9 3.6 copy-start.1
  821.9 10.5 %slice-start.2 = ((s8[6291456]{0:T(1024)(128)(4,1)}), s8[4194304]{0:T(1024)(128)(4,1)S(1)}, s32[]{:S(2)}) async-start(s8[6291456]{0:T(1024)(128)(4,1)} %bitcast.85), calls=%async_computation.9 | async-start | bytes 8388608
  825.5 6.9 slice-start.3
  825.5 13.5 %slice-start = ((s8[6291456]{0:T(1024)(128)(4,1)}), s8[4194304]{0:T(1024)(128)(4,1)S(1)}, s32[]{:S(2)}) async-start(s8[6291456]{0:T(1024)(128)(4,1)} %bitcast.83), calls=%async_computation.7 | async-start | bytes 8388608
  832.4 6.6 slice-start.1
  888.7 4.1 copy-start.3
Sparse Core Ops, SparseCore 0:
  11.9 48.6 all-gather.9
  62.7 44.6 all-gather.7
  109.5 79.4 all-gather.5
  347.7 272.1 all-reduce.6
  622.8 123.0 reduce-scatter.1
  750.0 131.8 all-reduce.4

commit v3 on v2

--- a/solution.py
+++ b/solution.py
@@ -288,7 +288,7 @@
             pltpu.VMEM((heads, rows, head_dim), F32),
         ],
         compiler_params=params(),
-        cost_estimate=takes(20),
+        cost_estimate=takes(3),
         name="attend_back",
     )(place, q, kv, r, wo, att, gate, inv)
 
@@ -371,7 +371,7 @@
             shape_of(1, model, F32), shape_of(1, head_dim, F32), shape_of(1, head_dim, F32),
         ],
         compiler_params=params(),
-        cost_estimate=takes(13),
+        cost_estimate=takes(3),
         name="unproject",
     )(x, gain, cosine, sine, qgain, kgain, wq, wk, wv, wg, dq, qraw, dkv, kraw, dgate)
 
@@ -385,9 +385,12 @@
         self.sems = sems
         self.spread = spread
 
-    def barrier(self):
+    def barrier(self, digits=()):
         sem = pltpu.get_barrier_semaphore()
         place, count = self.place, self.count
+        for digit in digits:
+            partner = flipped(lax.axis_index("seq"), digit)
+            pl.semaphore_signal(sem, inc=1, device_id={"seq": partner}, device_id_type=MESH)
 
         @pl.when(place > 0)
         def _():
@@ -401,11 +404,11 @@
 
         @pl.when(inside)
         def _():
-            pl.semaphore_wait(sem, 2)
+            pl.semaphore_wait(sem, 2 + len(digits))
 
         @pl.when(jnp.logical_not(inside))
         def _():
-            pl.semaphore_wait(sem, 1)
+            pl.semaphore_wait(sem, 1 + len(digits))
 
     def copy(self, ref, send, receive, p, t, step):
         return pltpu.make_async_remote_copy(
@@ -733,7 +736,7 @@
         ],
         scratch_shapes=line_scratch(pieces, count, rows, model, LOW, True),
         compiler_params=params(collective_id=1, has_side_effects=True),
-        cost_estimate=takes(120),
+        cost_estimate=takes(10),
         name="residual",
     )(dn, middle, masked, gain)
 
@@ -881,13 +884,10 @@
     )(*own)
 
 
-def scatter_kernel(count, batch, *refs):
-    parts, out = refs[:batch], refs[batch : 2 * batch]
-    slots, send_sem, receive_sem = refs[2 * batch :]
+def block_sums(count, batch, parts, out, slots, send_sem, receive_sem):
     place = lax.axis_index("seq")
     orders = [order[::-1] for order in digit_orders(count, batch)]
     steps = len(orders[0])
-    greet(place, orders[0])
 
     def masks_at(b, step):
         found = [0]
@@ -923,47 +923,127 @@
         )
 
     started = []
-    for turn in range(count // 2):
-        for b in range(batch):
-            copy = transfer(b, 0, masks_at(b, 0)[turn])
-            copy.start()
-            started.append(copy)
+
+    def begin():
+        for turn in range(count // 2):
+            for b in range(batch):
+                copy = transfer(b, 0, masks_at(b, 0)[turn])
+                copy.start()
+                started.append(copy)
+
+    def take(b, step, mask):
+        transfer(b, step, mask).wait_recv()
+        held = parts[b].at[flipped(place, mask)] if step == 0 else slot(b, step - 1, mask)
+        total = held[...].astype(F32) + slot(b, step, mask)[...].astype(F32)
+        if step == steps - 1:
+            out[b][...] = total.astype(LOW)
+        else:
+            slot(b, step, mask)[...] = total.astype(LOW)
+            if mask & orders[b][step + 1]:
+                copy = transfer(b, step + 1, mask & ~orders[b][step + 1])
+                copy.start()
+                started.append(copy)
+
+    events = [begin]
     for step in range(steps):
         for turn in range(len(masks_at(0, step))):
             for b in range(batch):
-                mask = masks_at(b, step)[turn]
-                transfer(b, step, mask).wait_recv()
-                held = parts[b].at[flipped(place, mask)] if step == 0 else slot(b, step - 1, mask)
-                total = held[...].astype(F32) + slot(b, step, mask)[...].astype(F32)
-                if step == steps - 1:
-                    out[b][...] = total.astype(LOW)
-                else:
-                    slot(b, step, mask)[...] = total.astype(LOW)
-                    if mask & orders[b][step + 1]:
-                        copy = transfer(b, step + 1, mask & ~orders[b][step + 1])
-                        copy.start()
-                        started.append(copy)
-    for copy in started:
-        copy.wait_send()
-
-
-def scatter_blocks(parts):
-    count, batch = lax.axis_size("seq"), len(parts)
-    rows, columns = parts[0].shape[0] // count, parts[0].shape[1]
-    return pl.pallas_call(
-        functools.partial(scatter_kernel, count, batch),
-        in_specs=[WHOLE] * batch,
-        out_specs=[WHOLE] * batch,
-        out_shape=[shape_of(rows, columns, LOW)] * batch,
+                events.append(functools.partial(take, b, step, masks_at(b, step)[turn]))
+
+    def drain():
+        for copy in started:
+            copy.wait_send()
+
+    return events, drain
+
+
+def interleaved(first, second):
+    taken = 0
+    for i, call in enumerate(first):
+        call()
+        due = (i + 1) * len(second) // len(first)
+        while taken < due:
+            second[taken]()
+            taken += 1
+
+
+def scatter_kernel(pieces, count, seq_count, batch, *refs):
+    parts, refs = refs[:batch], refs[batch:]
+    hidden_hbm, wd_hbm, middle_ref, valid_ref = refs[:4]
+    out, output_ref = refs[4 : 4 + batch], refs[4 + batch]
+    (
+        wd_ref, hidden_ref, load_sem, hidden_sem, slots, send_sem, receive_sem,
+        part_ref, own_ref, right_ref, left_ref, *sems,
+    ) = refs[5 + batch :]
+    rows, model = own_ref.shape[1], own_ref.shape[2]
+    tall = count * rows
+    line = Line(pieces, count, part_ref, own_ref, right_ref, left_ref, sems)
+    load = pltpu.make_async_copy(wd_hbm, wd_ref, load_sem)
+
+    def hidden_copy(p):
+        return pltpu.make_async_copy(hidden_hbm.at[:, p], hidden_ref.at[p % 2], hidden_sem.at[p % 2])
+
+    load.start()
+    hidden_copy(0).start()
+    line.barrier(digit_orders(seq_count, batch)[0])
+    events, drain = block_sums(seq_count, batch, parts, out, slots, send_sem, receive_sem)
+
+    def begin(p):
+        if p == 0:
+            load.wait()
+        if p + 1 < pieces:
+            hidden_copy(p + 1).start()
+        hidden_copy(p).wait()
+        hidden = hidden_ref[p % 2].reshape(tall, hidden_ref.shape[-1])
+        part_ref[...] = mm(hidden, wd_ref[...]).reshape(count, rows, model)
+        line.keep_own(p)
+
+    def own(p):
+        line.finish_own(p)
+        output_ref[p] = (valid_ref[p] * (middle_ref[p] + own_ref[p])).astype(LOW)
+
+    steps = []
+    for k in range(pieces + 1):
+        for i in range(count - 1):
+            if i == 0 and k < pieces:
+                steps.append(functools.partial(begin, k))
+            if k < pieces:
+                steps.append(functools.partial(line.send_sums, k, count - 1 - i))
+            if i == 0 and k > 0:
+                steps.append(functools.partial(own, k - 1))
+    events[0]()
+    interleaved(steps, events[1:])
+    drain()
+    line.drain()
+
+
+def scatter_blocks(parts, hidden, wd, middle, valid):
+    seq_count, batch = lax.axis_size("seq"), len(parts)
+    rows, columns = parts[0].shape[0] // seq_count, parts[0].shape[1]
+    count, pieces, piece_rows, units = hidden.shape
+    model = wd.shape[1]
+    any_place = pl.BlockSpec(memory_space=pl.ANY)
+    *sums, output = pl.pallas_call(
+        functools.partial(scatter_kernel, pieces, count, seq_count, batch),
+        in_specs=[WHOLE] * batch + [any_place, any_place, WHOLE, WHOLE],
+        out_specs=[WHOLE] * (batch + 1),
+        out_shape=[shape_of(rows, columns, LOW)] * batch
+        + [jax.ShapeDtypeStruct((pieces, piece_rows, model), LOW)],
         scratch_shapes=[
-            pltpu.VMEM((batch, count - 1, rows, columns), LOW),
-            pltpu.SemaphoreType.DMA((batch, count - 1)),
-            pltpu.SemaphoreType.DMA((batch, count - 1)),
-        ],
+            pltpu.VMEM(wd.shape, LOW),
+            pltpu.VMEM((2, count, piece_rows, units), LOW),
+            pltpu.SemaphoreType.DMA,
+            pltpu.SemaphoreType.DMA((2,)),
+            pltpu.VMEM((batch, seq_count - 1, rows, columns), LOW),
+            pltpu.SemaphoreType.DMA((batch, seq_count - 1)),
+            pltpu.SemaphoreType.DMA((batch, seq_count - 1)),
+        ]
+        + line_scratch(pieces, count, piece_rows, model, F32, False),
         compiler_params=params(collective_id=4, has_side_effects=True),
-        cost_estimate=takes(52),
+        cost_estimate=takes(10),
         name="scatter_blocks",
-    )(*[part.reshape(count, rows, columns) for part in parts])
+    )(*[part.reshape(seq_count, rows, columns) for part in parts], hidden, wd, middle, valid)
+    return sums, output
 
 
 def turn_tables(positions, head_dim):
@@ -1052,22 +1132,21 @@
     dn_mid, ff_grads = lax.optimization_barrier((dn_mid, ff_grads))
     ff_grads = lax.psum(ff_grads, "seq")
     residual, r_all = residual_step(dn_mid, middle, masked_own, gain_mid)
-    r_all, hidden = lax.optimization_barrier((r_all, hidden))
     r_all = r_all.reshape(batch, block_rows, model)
     r = [r_all[b] for b in seqs]
-    units_out = scatter(mm(hidden, swiglu_down).astype(LOW), "head").astype(F32)
-    units_out = units_out.reshape(batch, local_rows, model)
-    middle = middle.reshape(batch, local_rows, model)
-    output = jnp.stack(
-        [(valid[b] * (middle[b] + units_out[b])).astype(LOW) for b in seqs], axis=1
-    )
-
     back = [
         attend_back(places[b], q[b], kv[b], r[b], output_weight, att[b], gate[b], inv[b], group, head_dim)
         for b in seqs
     ]
     dq, dkv_all, dgate = [list(x) for x in zip(*back)]
-    dkv = scatter_blocks(dkv_all)
+    dkv, output = scatter_blocks(
+        dkv_all,
+        hidden.reshape(parts, pieces, rows, -1),
+        swiglu_down,
+        middle,
+        jnp.stack(valid).reshape(pieces, rows, 1),
+    )
+    output = jnp.transpose(output.reshape(batch, local_rows, model), (1, 0, 2))
     last = [
         unproject(
             rows_in[b], gain_in, cosine, sine, gain_q, gain_k,
@@ -1077,21 +1156,24 @@
         for b in seqs
     ]
     dall, dn_in, dgain_in, dgain_q, dgain_k = [list(x) for x in zip(*last)]
+    def both(pair):
+        return jnp.concatenate(pair, axis=0)
+
+    ff_sums, dall = lax.optimization_barrier((ff_grads, dall))
+    out_grad = t_mm(both(acted), r_all.reshape(flat_rows, model)).astype(LOW)
+    proj_grad = t_mm(both(normed), both(dall)).astype(LOW)
+    out_grad, proj_grad = lax.psum((out_grad, proj_grad), "seq")
     input_grad = input_step(
         jnp.stack(dn_in).reshape(batch, parts, halves, rows, model), tok, residual, gain_in
     )
+    input_grad, ff_sums = lax.optimization_barrier((input_grad, ff_sums))
+    ff_sums = [x.astype(F32) for x in ff_sums]
     input_grad = jnp.transpose(input_grad.reshape(batch, local_rows, model), (1, 0, 2))
 
-    def both(pair):
-        return jnp.concatenate(pair, axis=0)
-
-    ff_grads, dall = lax.optimization_barrier((ff_grads, dall))
-    out_grad = t_mm(both(acted), r_all.reshape(flat_rows, model)).astype(LOW)
-    proj_grad = t_mm(both(normed), both(dall)).astype(LOW)
-    out_grad, proj_grad = lax.psum((out_grad, proj_grad), "seq")
     gains = jnp.concatenate(
         [sum(dgain_in)[0], dgain_mid[0], sum(dgain_q)[0], sum(dgain_k)[0]]
     )
+    ff_sums, gains = lax.optimization_barrier((ff_sums, gains))
     gains = lax.psum(gains, ("seq", "head"))
 
     def share(start, width):
@@ -1106,9 +1188,9 @@
         proj_grad[:, nq + nk : nq + 2 * nk].astype(F32),
         proj_grad[:, nq + 2 * nk :].astype(F32),
         out_grad.astype(F32),
-        ff_grads[0].astype(F32),
-        ff_grads[1].astype(F32),
-        ff_grads[2].astype(F32),
+        ff_sums[0],
+        ff_sums[1],
+        ff_sums[2],
         share(0, model),
         share(model, model),
         share(2 * model, head_dim),

time: 906 us -> 844 us (0.932)
  Pallas kernels: 592 us -> 559 us
  waiting for transfers between devices: 119 us -> 91 us
    pallas_call x1, Pallas kernels: 130 us -> 79.1 us  [input_step(): pl.pallas_call(functools.partial(input_kernel, pieces, count), in_specs=[...]
    psum x1, waiting for transfers between devices: 36.7 us -> 0.01 us  [on_device(): out_grad, proj_grad = lax.psum((out_grad, proj_grad), 'seq')]
    pallas_call x1, Pallas kernels: 88.8 us -> 108 us  [scatter_blocks(): pl.pallas_call(functools.partial(scatter_kernel, pieces, count, seq_count...]
    convert_element_type x5 -> x3, other arithmetic: 21.5 us -> 22.7 us  [on_device(): ff_sums = [x.astype(F32) for x in ff_sums]]
  transfers between devices with their start and end apart: 6 -> 5, of which waited for: 4 -> 3; matrix products, arithmetic and copies ran while one was open for 9% -> 7% of each run, Pallas kernels for 51% -> 51%
where the time goes in v3:
time: 844 us; the launch traced here: 836 us
  Pallas kernels  559 us (66%)
  waiting for transfers between devices  91 us (11%)
  other arithmetic  54.4 us (6%)
  matrix products  52.2 us (6%)
  blocking collectives  43.1 us (5%)
  local copies, waits for them, and re-layouts  21.4 us (3%)
  between operations  14.7 us (2%)
    pallas_call x1, Pallas kernels, middle_step(): pl.pallas_call(functools.partial(middle_kernel, pieces, count), in_specs=...  129 us
    pallas_call x1, Pallas kernels, residual_step(): pl.pallas_call(functools.partial(residual_kernel, pieces, count), in_spec...  120 us
    pallas_call x1, Pallas kernels, scatter_blocks(): pl.pallas_call(functools.partial(scatter_kernel, pieces, count, seq_count...  108 us
    all_gather x3, waiting for transfers between devices, gather(): return lax.all_gather(value, axis, axis=0, tiled=True)  91 us
    pallas_call x1, Pallas kernels, input_step(): pl.pallas_call(functools.partial(input_kernel, pieces, count), in_specs=[...  79.1 us
    dot_general x5, matrix products, t_mm(): lax.dot_general(left, right, (((0,), (0,)), ((), ())), preferred_element_...  52.2 us
    psum x1, blocking collectives, on_device(): gains = lax.psum(gains, ('seq', 'head'))  43.1 us
    pallas_call x1, Pallas kernels, gather_blocks(): pl.pallas_call(functools.partial(gather_kernel, count, batch), in_specs=[...  41.5 us
  transfers between devices with their start and end apart: 5, of which 3 were waited for; matrix products, arithmetic and copies ran while one was open for 7% of the time, Pallas kernels for 51%

profile of v3, /device:TPU:0, one launch (start us, length us, event | category | flops | bytes accessed | tf_op | source)
XLA Modules:
  0.0 835.9 jit_solution(13790388501209906601)
XLA Ops:
  7.2 3.4 fusion.22
  10.6 1.1 copy.44
  11.8 1.1 copy.43
  13.6 1.3 compare_convert_fusion
  14.9 1.5 fusion.21
  17.8 1.1 pad_maximum_fusion.4
  19.6 1.9 pad_add_fusion
  21.6 1.0 fusion.15
  22.6 1.1 pad_maximum_fusion.3
  23.7 1.0 pad_maximum_fusion.5
  24.7 35.8 %all-gather.10.cloned.1.call-done = bf16[512,1,2048]{2,0,1:T(8,128)(2,1)} async-done(((bf16[128,1,2048]{2,0,1:T(8,128)(2,1)}), bf16[512,1,2048]{2,0,1:T(8,128)(2,1)}) %all-gather.10.cloned.1.call-update) | async-done | bytes 2097168 | tf_op jit(solution)/shard_map/all_gather | solution.py:1065
  60.5 8.6 %project.3 = (bf16[512,2048]{1,0:T(8,128)(2,1)}, f32[512,512]{1,0:T(8,128)}, bf16[512,512]{1,0:T(8,128)(2,1)}, f32[512,256]{1,0:T(8,128)}, bf16[512,512]{1,0:T(8,128)(2,1)}, /*index=5*/f32[512,512]{1,0:T(8,128)}) custom-call(bf16[512,2048]{1,0:T(8,128)(2,1)} %bitcast.102, f32[1,2048]{1,0:T(1,128)} %bitcast.108, f32[512,128]{1,0:T(8,128)} %get-tuple-element.170.cos_ref, ...), custom_call_target="tpu_custom_call" | custom-call | flops 10350000128 | bytes 33210000 | tf_op jit(solution)/shard_map/project/pallas_call | solution.py:99
  69.1 38.1 %all-gather.8.cloned.1.call-done = bf16[512,1,2048]{2,0,1:T(8,128)(2,1)} async-done(((bf16[128,1,2048]{2,0,1:T(8,128)(2,1)}), bf16[512,1,2048]{2,0,1:T(8,128)(2,1)}) %all-gather.8.cloned.1.call-update) | async-done | bytes 2097168 | tf_op jit(solution)/shard_map/all_gather | solution.py:1065
  107.3 8.6 %project.2 = (bf16[512,2048]{1,0:T(8,128)(2,1)}, f32[512,512]{1,0:T(8,128)}, bf16[512,512]{1,0:T(8,128)(2,1)}, f32[512,256]{1,0:T(8,128)}, bf16[512,512]{1,0:T(8,128)(2,1)}, /*index=5*/f32[512,512]{1,0:T(8,128)}) custom-call(bf16[512,2048]{1,0:T(8,128)(2,1)} %bitcast.104, f32[1,2048]{1,0:T(1,128)} %bitcast.109, f32[512,128]{1,0:T(8,128)} %get-tuple-element.170.cos_ref, ...), custom_call_target="tpu_custom_call" | custom-call | flops 10350000128 | bytes 33210000 | tf_op jit(solution)/shard_map/project/pallas_call | solution.py:99
  115.9 41.5 %gather_blocks.1 = (bf16[8,512,512]{2,1,0:T(8,128)(2,1)}, bf16[8,512,512]{2,1,0:T(8,128)(2,1)}) custom-call(bf16[512,512]{1,0:T(8,128)(2,1)} %get-tuple-element.80.refs_0_, bf16[512,512]{1,0:T(8,128)(2,1)} %get-tuple-element.81.refs_1_), custom_call_target="tpu_custom_call" | custom-call | flops 47149998080 | bytes 151290000 | tf_op jit(solution)/shard_map/gather_blocks/pallas_call | solution.py:871
  157.4 6.4 attend.2
  163.8 6.1 attend.3
  169.8 2.1 pad_maximum_fusion.2.acted_ref
  171.9 17.0 %all-gather.6.cloned.1.call-done = bf16[1024,2048]{1,0:T(8,128)(2,1)} async-done(((bf16[256,2048]{1,0:T(8,128)(2,1)}), bf16[1024,2048]{1,0:T(8,128)(2,1)}) %all-gather.6.cloned.1.call-update) | async-done | bytes 4194320 | tf_op jit(solution)/shard_map/all_gather | solution.py:1065
  188.9 128.9 %middle.1 = (f32[4,64,2048]{2,1,0:T(8,128)}, f32[1,2048]{1,0:T(1,128)}, bf16[4,4,64,2048]{3,2,1,0:T(8,128)(2,1)}, bf16[4,4,64,1536]{3,2,1,0:T(8,128)(2,1)}, bf16...) custom-call(bf16[2,4,2,64,512]{4,3,2,1,0:T(8,128)(2,1)} %pad_maximum_fusion.2.acted_, ...), custom_call_target="tpu_custom_call" | custom-call | flops 147200000000 | bytes 472320000 | tf_op jit(solution)/shard_map/middle/pallas_call | solution.py:667
  317.9 19.8 %bitcast_convert_fusion = bf16[2048,1536]{1,0:T(8,128)(2,1)} fusion(bf16[4,4,64,2048]{3,2,1,0:T(8,128)(2,1)} %get-tuple-element.90, bf16[4,4,64,1536]{3,2,1,0:T(8,128)(2,1)} %get-tuple-element.92), kind=kOutput, calls=%fused_computation | convolution fusion | flops 6445596672 | bytes 13631488 | tf_op jit(solution)/shard_map/dot_general | solution.py:28
  337.7 8.8 %bitcast_convert_fusion.1 = bf16[2048,1536]{1,0:T(8,128)(2,1)} fusion(bf16[4,4,64,2048]{3,2,1,0:T(8,128)(2,1)S(1)} %copy-done.30, bf16[4,4,64,1536]{3,2,1,0:T(8,128)(2,1)S(1)} %copy-done.31), kind=kOutput, calls=%fused_computation.1 | convolution fusion | flops 6445596672 | bytes 13631488 | tf_op jit(solution)/shard_map/dot_general | solution.py:28
  346.5 8.8 %convolution_convert_fusion.1 = bf16[1536,2048]{1,0:T(8,128)(2,1)} fusion(bf16[1024,1536]{1,0:T(8,128)(2,1)S(1)} %bitcast.127, bf16[1024,2048]{1,0:T(8,128)(2,1)S(1)} %copy-done.22), kind=kOutput, calls=%fused_computation.3 | convolution fusion | flops 6445596672 | bytes 13631488 | tf_op jit(solution)/shard_map/dot_general | solution.py:28
  355.3 1.4 fusion.16
  356.8 0.9 reshape.217.refs_5_
  358.5 1.5 pad_maximum_fusion.1
  360.0 119.6 %residual.1 = (f32[4,64,2048]{2,1,0:T(8,128)}, bf16[2,4,2,64,2048]{4,3,2,1,0:T(8,128)(2,1)}) custom-call(bf16[4,4,64,2048]{3,2,1,0:T(8,128)(2,1)} %get-tuple-element.94.dn_ref, f32[4,64,2048]{2,1,0:T(8,128)} %get-tuple-element.95.middle_ref.refs_4_, f32[4,64,2048]{2,1,0:T(8,128)} %bitcast.86, f32[1,2048]{1,0:T(1,128)} %bitcast.107), custom_call_target="tpu_custom_call" | custom-call | flops 11500000256 | bytes 36900000 | tf_op jit(solution)/shard_map/residual/pallas_call | solution.py:729
  479.6 5.3 fusion.20
  484.9 13.8 %attend_back.3 = (f32[512,512]{1,0:T(8,128)}, bf16[4096,512]{1,0:T(8,128)(2,1)}, bf16[512,512]{1,0:T(8,128)(2,1)}) custom-call(s32[2]{0:T(128)} %get-tuple-element.169.place_ref, bf16[512,512]{1,0:T(8,128)(2,1)} %get-tuple-element.85.q_ref, bf16[4096,512]{1,0:T(8,128)(2,1)} %bitcast.124, bf16[512,2048]{1,0:T(8,128)(2,1)} %bitcast.92, ...), custom_call_target="tpu_custom_call" | custom-call | flops 3449999872 | bytes 11070000 | tf_op jit(solution)/shard_map/attend_back/pallas_call | solution.py:278
  498.7 13.0 %attend_back.2 = (f32[512,512]{1,0:T(8,128)}, bf16[4096,512]{1,0:T(8,128)(2,1)}, bf16[512,512]{1,0:T(8,128)(2,1)}) custom-call(s32[2]{0:T(128)} %get-tuple-element.168.place_ref, bf16[512,512]{1,0:T(8,128)(2,1)} %get-tuple-element.79.q_ref, bf16[4096,512]{1,0:T(8,128)(2,1)} %bitcast.122, bf16[512,2048]{1,0:T(8,128)(2,1)} %bitcast.90, ...), custom_call_target="tpu_custom_call" | custom-call | flops 3449999872 | bytes 11070000 | tf_op jit(solution)/shard_map/attend_back/pallas_call | solution.py:278
  511.7 107.8 %scatter_blocks.1 = (bf16[512,512]{1,0:T(8,128)(2,1)}, bf16[512,512]{1,0:T(8,128)(2,1)}, bf16[4,64,2048]{2,1,0:T(8,128)(2,1)}) custom-call(bf16[8,512,512]{2,1,0:T(8,128)(2,1)} %bitcast.126, bf16[8,512,512]{2,1,0:T(8,128)(2,1)} %bitcast.125, bf16[4,4,64,1536]{3,2,1,0:T(8,128)(2,1)} %get-tuple-element.93.refs_2_, bf16[1536,2048]{1,0:T(8,128)(2,1)} %refs_3_.1, ...), custom_call_target="tpu_custom_call" | custom-call | flops 11500000256 | bytes 36900000 | tf_op jit(solution)/shard_map/scatter_blocks/pallas_call | solution.py:1026
  619.5 12.7 %unproject.2 = (bf16[512,1536]{1,0:T(8,128)(2,1)}, bf16[512,2048]{1,0:T(8,128)(2,1)}, f32[1,2048]{1,0:T(1,128)}, f32[1,128]{1,0:T(1,128)}, f32[1,128]{1,0:T(1,128)}) custom-call(bf16[512,2048]{1,0:T(8,128)(2,1)} %bitcast.105, f32[1,2048]{1,0:T(1,128)} %bitcast.110, f32[512,128]{1,0:T(8,128)} %get-tuple-element.170.cos_ref, ...), custom_call_target="tpu_custom_call" | custom-call | flops 3449999872 | bytes 11070000 | tf_op jit(solution)/shard_map/unproject/pallas_call | solution.py:359
  632.2 12.8 %unproject.3 = (bf16[512,1536]{1,0:T(8,128)(2,1)}, bf16[512,2048]{1,0:T(8,128)(2,1)}, f32[1,2048]{1,0:T(1,128)}, f32[1,128]{1,0:T(1,128)}, f32[1,128]{1,0:T(1,128)}) custom-call(bf16[512,2048]{1,0:T(8,128)(2,1)} %bitcast.103, f32[1,2048]{1,0:T(1,128)} %bitcast.111, f32[512,128]{1,0:T(8,128)} %get-tuple-element.170.cos_ref, ...), custom_call_target="tpu_custom_call" | custom-call | flops 3449999872 | bytes 11070000 | tf_op jit(solution)/shard_map/unproject/pallas_call | solution.py:359
  645.0 4.1 pad_maximum_fusion.dn_ref
  649.2 3.8 convolution_convert_fusion.2
  652.9 11.1 %convolution_convert_fusion = bf16[2048,1536]{1,0:T(8,128)(2,1)} fusion(bf16[512,2048]{1,0:T(8,128)(2,1)} %get-tuple-element.127, bf16[512,2048]{1,0:T(8,128)(2,1)} %get-tuple-element.126, bf16[512,1536]{1,0:T(8,128)(2,1)S(1)} %copy-done.29, bf16[512,1536]{1,0:T(8,128)(2,1)S(1)} %copy-done.28), kind=kOutput, calls=%fused_computation.2 | convolution fusion | flops 6460276736 | bytes 13631488 | tf_op jit(solution)/shard_map/dot_general | solution.py:28
  664.1 79.1 %input_grad.1 = f32[4,64,2048]{2,1,0:T(8,128)} custom-call(bf16[2,4,2,64,2048]{4,3,2,1,0:T(8,128)(2,1)} %pad_maximum_fusion.dn_ref, bf16[4,64,2048]{2,1,0:T(8,128)(2,1)} %bitcast.94, f32[4,64,2048]{2,1,0:T(8,128)} %get-tuple-element.116.residual_ref, f32[1,2048]{1,0:T(1,128)} %bitcast.112), custom_call_target="tpu_custom_call" | custom-call | flops 126500003840 | bytes 405900000 | tf_op jit(solution)/shard_map/input_grad/pallas_call | solution.py:776
  743.3 2.0 copy.56
  745.5 9.5 %convert_element_type.139 = f32[2048,1536]{1,0:T(8,128)} convert(bf16[2048,1536]{1,0:T(8,128)(2,1)} %get-tuple-element.130) | non-fusion elementwise | flops 3145728 | bytes 18874368 | tf_op jit(solution)/shard_map/convert_element_type | solution.py:1170
  755.0 6.9 convert_element_type.140
  761.9 6.3 convert_element_type.141
  768.2 2.9 copy.55
  771.1 43.1 %psum.47 = f32[4352]{0:T(1024)S(1)} all-reduce(f32[4352]{0:T(1024)S(1)} %pad_maximum_fusion.7), channel_id=1, replica_groups=mesh['seq'=8,'head'=4] {'seq','head'}, use_global_device_ids=true, to_apply=%region_5.0 | all-reduce | flops 4352 | bytes 34816 | tf_op jit(solution)/shard_map/psum | solution.py:1177
  814.3 0.6 fusion.23
  814.9 0.7 fusion.24
  815.5 6.8 slice_convert_fusion
  822.4 4.0 slice_convert_fusion.2
  826.4 2.5 convert_element_type.138
  (95 shorter events, 3.9 us)
Async XLA Ops:
  7.2 5.8 copy-start.21
  7.2 7.7 copy-start.6
  7.2 53.3 %all-gather.10.cloned.1.call-start = ((), (), s32[]{:S(2)}) async-start(), calls=%async_computation.2 | async-start | bytes 2621440 | tf_op jit(solution)/shard_map/all_gather | solution.py:1065
  11.8 95.5 %all-gather.8.cloned.1.call-start = ((), (), s32[]{:S(2)}) async-start(), calls=%async_computation.1 | async-start | bytes 2621440 | tf_op jit(solution)/shard_map/all_gather | solution.py:1065
  12.9 176.0 %all-gather.6.cloned.1.call-start = ((), (), s32[]{:S(2)}) async-start(), calls=%async_computation | async-start | bytes 5242880 | tf_op jit(solution)/shard_map/all_gather | solution.py:1065
  14.9 2.9 copy-start.17
  14.9 2.9 copy-start.19
  16.4 1.0 copy-start
  16.4 1.4 copy-start.2
  18.9 634.0 %all-reduce.7.cloned.1.call-start = ((), (), s32[]{:S(2)}) async-start(), calls=%async_computation.4 | async-start | bytes 37748736 | tf_op jit(solution)/shard_map/psum | solution.py:1133
  163.8 6.1 copy-start.11
  317.9 19.8 %copy-start.30 = (bf16[4,4,64,2048]{3,2,1,0:T(8,128)(2,1)S(1)}, bf16[4,4,64,2048]{3,2,1,0:T(8,128)(2,1)}, u32[]{:S(2)}) copy-start(bf16[4,4,64,2048]{3,2,1,0:T(8,128)(2,1)} %get-tuple-element.90) | copy-start | bytes 12582916
  317.9 19.8 %copy-start.31 = (bf16[4,4,64,1536]{3,2,1,0:T(8,128)(2,1)S(1)}, bf16[4,4,64,1536]{3,2,1,0:T(8,128)(2,1)}, u32[]{:S(2)}) copy-start(bf16[4,4,64,1536]{3,2,1,0:T(8,128)(2,1)} %get-tuple-element.91) | copy-start | bytes 9437188
  337.7 8.8 %copy-start.22 = (bf16[1024,2048]{1,0:T(8,128)(2,1)S(1)}, bf16[1024,2048]{1,0:T(8,128)(2,1)}, u32[]{:S(2)}) copy-start(bf16[1024,2048]{1,0:T(8,128)(2,1)} %all-gather.6.cloned.1.call-done) | copy-start | bytes 12582916
  337.7 8.8 %copy-start.23 = (bf16[4,4,64,1536]{3,2,1,0:T(8,128)(2,1)S(1)}, bf16[4,4,64,1536]{3,2,1,0:T(8,128)(2,1)}, u32[]{:S(2)}) copy-start(bf16[4,4,64,1536]{3,2,1,0:T(8,128)(2,1)} %get-tuple-element.93.refs_2_) | copy-start | bytes 9437188
  355.3 2.4 copy-start.3
  355.3 2.4 copy-start.20
  355.3 2.8 copy-start.1
  355.3 2.8 copy-start.18
  355.3 460.2 %all-reduce.5.cloned.1.call-start = ((), (), s32[]{:S(2)}) async-start(), calls=%async_computation.3 | async-start | bytes 16777216 | tf_op jit(solution)/shard_map/psum | solution.py:1165
  632.2 12.8 %copy-start.9 = (bf16[512,2048]{1,0:T(8,128)(2,1)S(1)}, bf16[512,2048]{1,0:T(8,128)(2,1)}, u32[]{:S(2)}) copy-start(bf16[512,2048]{1,0:T(8,128)(2,1)} %get-tuple-element.109) | copy-start | bytes 6291460
  645.0 4.2 copy-start.5
  645.0 4.2 copy-start.12
  645.0 4.2 copy-start.13
  649.1 3.8 copy-start.28
  649.2 3.8 copy-start.29
  664.1 79.2 %copy-start.10 = (bf16[4,64,2048]{2,1,0:T(8,128)(2,1)S(1)}, bf16[4,64,2048]{2,1,0:T(8,128)(2,1)}, u32[]{:S(2)}) copy-start(bf16[4,64,2048]{2,1,0:T(8,128)(2,1)} %get-tuple-element.103) | copy-start | bytes 3145732
  664.1 81.3 %copy-start.15 = (f32[1,2048]{1,0:T(1,128)S(1)}, f32[1,2048]{1,0:T(1,128)}, u32[]{:S(2)}) copy-start(f32[1,2048]{1,0:T(1,128)} %get-tuple-element.133) | copy-start | bytes 24580
  664.1 81.3 %copy-start.16 = (f32[1,2048]{1,0:T(1,128)S(1)}, f32[1,2048]{1,0:T(1,128)}, u32[]{:S(2)}) copy-start(f32[1,2048]{1,0:T(1,128)} %get-tuple-element.134) | copy-start | bytes 24580
  664.1 81.3 %copy-start.25 = (f32[1,128]{1,0:T(1,128)S(1)}, f32[1,128]{1,0:T(1,128)}, u32[]{:S(2)}) copy-start(f32[1,128]{1,0:T(1,128)} %get-tuple-element.136) | copy-start | bytes 1540
  664.1 81.3 %copy-start.27 = (f32[1,128]{1,0:T(1,128)S(1)}, f32[1,128]{1,0:T(1,128)}, u32[]{:S(2)}) copy-start(f32[1,128]{1,0:T(1,128)} %get-tuple-element.137) | copy-start | bytes 1540
  664.1 81.3 %copy-start.24 = (f32[1,128]{1,0:T(1,128)S(1)}, f32[1,128]{1,0:T(1,128)}, u32[]{:S(2)}) copy-start(f32[1,128]{1,0:T(1,128)} %get-tuple-element.138) | copy-start | bytes 1540
  664.1 81.3 %copy-start.26 = (f32[1,128]{1,0:T(1,128)S(1)}, f32[1,128]{1,0:T(1,128)}, u32[]{:S(2)}) copy-start(f32[1,128]{1,0:T(1,128)} %get-tuple-element.139) | copy-start | bytes 1540
  664.1 81.3 %copy-start.14 = (f32[1,2048]{1,0:T(1,128)S(1)}, f32[1,2048]{1,0:T(1,128)}, u32[]{:S(2)}) copy-start(f32[1,2048]{1,0:T(1,128)} %get-tuple-element.135) | copy-start | bytes 24580
  745.4 9.5 %copy-start.4 = (bf16[2048,1536]{1,0:T(8,128)(2,1)S(1)}, bf16[2048,1536]{1,0:T(8,128)(2,1)}, u32[]{:S(2)}) copy-start(bf16[2048,1536]{1,0:T(8,128)(2,1)} %get-tuple-element.131) | copy-start | bytes 18874372
  745.4 16.5 %slice-start = ((s8[6291456]{0:T(1024)(128)(4,1)}), s8[4194304]{0:T(1024)(128)(4,1)S(1)}, s32[]{:S(2)}) async-start(s8[6291456]{0:T(1024)(128)(4,1)} %bitcast.81), calls=%async_computation.5 | async-start | bytes 8388608
  755.0 6.9 slice-start.1
  761.9 6.3 copy-start.8
  822.4 4.1 copy-start.7
Sparse Core Ops, SparseCore 0:
  11.9 48.6 all-gather.9
  62.7 44.5 all-gather.7
  109.4 79.4 all-gather.5
  355.4 272.1 all-reduce.6
  664.2 133.2 all-reduce.4

commit v4 on v3

v4 whole, which is shorter than its diff:
```python
import functools

import jax
import jax.numpy as jnp
from jax import lax
from jax.experimental import pallas as pl
from jax.experimental.pallas import tpu as pltpu
from jax.sharding import PartitionSpec as P

EPS = 1e-06
THETA = 1000000.0
LOG2E = 1.4426950408889634
VMEM_LIMIT = 58 * 1024 * 1024
LOW = jnp.bfloat16
F32 = jnp.float32
MESH = pl.DeviceIdType.MESH


def mm(left, right):
    return jnp.dot(left, right, preferred_element_type=F32)


def mm_t(left, right):
    return lax.dot_general(left, right, (((1,), (1,)), ((), ())), preferred_element_type=F32)


def t_mm(left, right):
    return lax.dot_general(left, right, (((0,), (0,)), ((), ())), preferred_element_type=F32)


def shape_of(rows, columns, kind):
    return jax.ShapeDtypeStruct((rows, columns), kind)


def params(**extra):
    return pltpu.CompilerParams(vmem_limit_bytes=VMEM_LIMIT, **extra)


def takes(microseconds):
    return pl.CostEstimate(
        flops=int(microseconds * 1.15e9), bytes_accessed=int(microseconds * 3.69e6), transcendentals=0
    )


WHOLE = pl.BlockSpec(memory_space=pltpu.VMEM)
SCALARS = pl.BlockSpec(memory_space=pltpu.SMEM)


def full_block(array):
    return pl.BlockSpec(array.shape, lambda i: (0,) * len(array.shape))


def inverse_rms(values):
    return lax.rsqrt(jnp.mean(values * values, axis=-1, keepdims=True) + EPS)


def turn(values, cosine, sine):
    return values * cosine + pltpu.roll(values, values.shape[-1] // 2, 1) * sine


def turn_back(grads, cosine, sine):
    return grads * cosine + pltpu.roll(grads * sine, grads.shape[-1] // 2, 1)


def live_blocks(place_ref, rows):
    start, length = place_ref[0], place_ref[1 + pl.program_id(0)]
    whole = jnp.minimum(start // rows, length // rows)
    end = jnp.minimum(start // rows + 1, (length + rows - 1) // rows)
    end = jnp.where(start < length, end, 0)
    return jnp.minimum(whole, end), end, start, length


def attend_kernel(
    group, head_dim, place_ref, q_ref, kv_ref, gate_ref, att_ref, acted_ref, inv_ref, acc_ref, sum_ref
):
    rows = q_ref.shape[1]
    heads = q_ref.shape[2] // head_dim
    kv_heads = heads // group
    factor = head_dim ** (-0.5) * LOG2E
    acc_ref[...] = jnp.zeros_like(acc_ref)
    sum_ref[...] = jnp.zeros_like(sum_ref)
    whole, end, start, length = live_blocks(place_ref, rows)

    def one_block(j, masked):
        span = pl.ds(pl.multiple_of(j * rows, rows), rows)
        if masked:
            key_pos = j * rows + lax.broadcasted_iota(jnp.int32, (rows, rows), 1)
            query_pos = start + lax.broadcasted_iota(jnp.int32, (rows, rows), 0)
            allowed = (key_pos <= query_pos) & (key_pos < length)
        for h in range(heads):
            c = h // group
            keys = kv_ref[0, span, c * head_dim : (c + 1) * head_dim]
            values = kv_ref[0, span, (kv_heads + c) * head_dim : (kv_heads + c + 1) * head_dim]
            weights = jnp.exp2(mm_t(q_ref[0, :, h * head_dim : (h + 1) * head_dim], keys) * factor)
            if masked:
                weights = jnp.where(allowed, weights, 0.0)
            total = weights[:, :128]
            for piece in range(1, rows // 128):
                total = total + weights[:, piece * 128 : (piece + 1) * 128]
            sum_ref[h] = sum_ref[h] + total
            acc_ref[h] = acc_ref[h] + mm(weights.astype(LOW), values)

    def plain(j, carry):
        one_block(j, False)
        return carry

    def edge(j, carry):
        one_block(j, True)
        return carry

    lax.fori_loop(0, whole, plain, 0)
    lax.fori_loop(whole, end, edge, 0)
    lane = lax.broadcasted_iota(jnp.int32, inv_ref.shape[1:], 1)
    kept = jnp.zeros(inv_ref.shape[1:], F32)
    for h in range(heads):
        total = jnp.sum(sum_ref[h], axis=1, keepdims=True)
        inverse = 1.0 / jnp.where(total > 0.0, total, 1.0)
        attended = acc_ref[h] * inverse
        columns = slice(h * head_dim, (h + 1) * head_dim)
        att_ref[0, :, columns] = attended
        acted_ref[0, :, columns] = (attended * jax.nn.sigmoid(gate_ref[0, :, columns])).astype(LOW)
        kept = jnp.where(lane == h, inverse, kept)
    inv_ref[0] = kept


def by_sequence(array):
    return pl.BlockSpec((1,) + array.shape[1:], lambda b: (b,) + (0,) * (len(array.shape) - 1))


def attend(place, q, kv, gate, group, head_dim):
    batch, rows, width = q.shape
    heads = width // head_dim
    outs = [
        jax.ShapeDtypeStruct((batch, rows, width), F32),
        jax.ShapeDtypeStruct((batch, rows, width), LOW),
        jax.ShapeDtypeStruct((batch, rows, 128), F32),
    ]
    return pl.pallas_call(
        functools.partial(attend_kernel, group, head_dim),
        grid=(batch,),
        in_specs=[SCALARS, by_sequence(q), by_sequence(kv), by_sequence(gate)],
        out_specs=[by_sequence(x) for x in outs],
        out_shape=outs,
        scratch_shapes=[
            pltpu.VMEM((heads, rows, head_dim), F32),
            pltpu.VMEM((heads, rows, 128), F32),
        ],
        compiler_params=params(),
        cost_estimate=takes(18),
        name="attend",
    )(place, q, kv, gate)


def norm_turn_back(grad, raw, head_gain, cosine, sine):
    grad = turn_back(grad, cosine, sine)
    inverse = inverse_rms(raw)
    gain_grad = jnp.sum(grad * raw * inverse, axis=0, keepdims=True)
    grad = grad * head_gain
    mean = jnp.mean(grad * raw, axis=-1, keepdims=True)
    return inverse * (grad - raw * (inverse * inverse * mean)), gain_grad


def attend_back_kernel(
    group, head_dim,
    place_ref, q_ref, kv_ref, r_ref, wo_ref, att_ref, gate_ref, inv_ref, qraw_ref, cos_ref, sin_ref, qgain_ref,
    dq_ref, dkv_ref, dgate_ref, dqgain_ref,
    scaled_ref, corr_ref, acc_ref,
):
    rows = q_ref.shape[1]
    heads = q_ref.shape[2] // head_dim
    kv_heads = heads // group
    scale = head_dim ** (-0.5)
    acted_grad = mm_t(r_ref[0], wo_ref[...])
    lane = lax.broadcasted_iota(jnp.int32, inv_ref.shape[1:], 1)
    kept = jnp.zeros(inv_ref.shape[1:], F32)
    for h in range(heads):
        columns = slice(h * head_dim, (h + 1) * head_dim)
        sigmoid = jax.nn.sigmoid(gate_ref[0, :, columns])
        attended = att_ref[0, :, columns]
        grad = acted_grad[:, columns]
        dgate_ref[0, :, columns] = (grad * attended * sigmoid * (1.0 - sigmoid)).astype(LOW)
        grad = grad * sigmoid
        inverse = inv_ref[0, :, h : h + 1]
        scaled_ref[:, columns] = (grad * inverse).astype(LOW)
        kept = jnp.where(
            lane == h, jnp.sum(grad * attended, axis=1, keepdims=True) * inverse, kept
        )
    corr_ref[...] = kept.T
    acc_ref[...] = jnp.zeros_like(acc_ref)
    whole, end, start, length = live_blocks(place_ref, rows)

    def one_block(j, masked):
        span = pl.ds(pl.multiple_of(j * rows, rows), rows)
        if masked:
            key_pos = j * rows + lax.broadcasted_iota(jnp.int32, (rows, rows), 0)
            query_pos = start + lax.broadcasted_iota(jnp.int32, (rows, rows), 1)
            allowed = (key_pos <= query_pos) & (key_pos < length)
        for c in range(kv_heads):
            key_columns = slice(c * head_dim, (c + 1) * head_dim)
            value_columns = slice((kv_heads + c) * head_dim, (kv_heads + c + 1) * head_dim)
            keys = kv_ref[0, span, key_columns]
            values = kv_ref[0, span, value_columns]
            dk = jnp.zeros((rows, head_dim), F32)
            dv = jnp.zeros((rows, head_dim), F32)
            for h in range(c * group, (c + 1) * group):
                columns = slice(h * head_dim, (h + 1) * head_dim)
                queries = q_ref[0, :, columns]
                scaled = scaled_ref[:, columns]
                weights = jnp.exp2(mm_t(keys, queries) * (scale * LOG2E))
                if masked:
                    weights = jnp.where(allowed, weights, 0.0)
                dv = dv + mm(weights.astype(LOW), scaled)
                score = (weights * (mm_t(values, scaled) - corr_ref[h : h + 1, :])).astype(LOW)
                dk = dk + mm(score, queries)
                acc_ref[h] = acc_ref[h] + t_mm(score, keys)
            dkv_ref[0, span, key_columns] = (dk * scale).astype(LOW)
            dkv_ref[0, span, value_columns] = dv.astype(LOW)

    def plain(j, carry):
        one_block(j, False)
        return carry

    def edge(j, carry):
        one_block(j, True)
        return carry

    def empty(j, carry):
        span = pl.ds(pl.multiple_of(j * rows, rows), rows)
        dkv_ref[0, span, :] = jnp.zeros((rows, dkv_ref.shape[2]), LOW)
        return carry

    lax.fori_loop(0, whole, plain, 0)
    lax.fori_loop(whole, end, edge, 0)
    lax.fori_loop(end, dkv_ref.shape[1] // rows, empty, 0)
    gain_total = jnp.zeros((1, head_dim), F32)
    for h in range(heads):
        columns = slice(h * head_dim, (h + 1) * head_dim)
        grad, gain_grad = norm_turn_back(
            acc_ref[h] * scale, qraw_ref[0, :, columns], qgain_ref[...], cos_ref[...], sin_ref[...]
        )
        dq_ref[0, :, columns] = grad.astype(LOW)
        gain_total = gain_total + gain_grad

    @pl.when(pl.program_id(0) == 0)
    def _():
        dqgain_ref[...] = gain_total

    @pl.when(pl.program_id(0) > 0)
    def _():
        dqgain_ref[...] = dqgain_ref[...] + gain_total


def attend_back(place, q, kv, r, wo, att, gate, inv, qraw, cosine, sine, qgain, group):
    batch, rows, width = q.shape
    head_dim = qgain.shape[1]
    heads = width // head_dim
    outs = [
        jax.ShapeDtypeStruct(q.shape, LOW),
        jax.ShapeDtypeStruct(kv.shape, LOW),
        jax.ShapeDtypeStruct(q.shape, LOW),
    ]
    line = pl.BlockSpec((1, head_dim), lambda b: (0, 0))
    return pl.pallas_call(
        functools.partial(attend_back_kernel, group, head_dim),
        grid=(batch,),
        in_specs=[SCALARS, by_sequence(q), by_sequence(kv), by_sequence(r), full_block(wo)]
        + [by_sequence(x) for x in (att, gate, inv, qraw)]
        + [full_block(x) for x in (cosine, sine, qgain)],
        out_specs=[by_sequence(x) for x in outs] + [line],
        out_shape=outs + [shape_of(1, head_dim, F32)],
        scratch_shapes=[
            pltpu.VMEM((rows, width), LOW),
            pltpu.VMEM((128, rows), F32),
            pltpu.VMEM((heads, rows, head_dim), F32),
        ],
        compiler_params=params(),
        cost_estimate=takes(3),
        name="attend_back",
    )(place, q, kv, r, wo, att, gate, inv, qraw, cosine, sine, qgain)


class Line:
    def __init__(self, pieces, count, part_ref, own_ref, right_ref, left_ref, sems, spread=None):
        self.sums = part_ref is not None
        self.pieces, self.count = pieces, count
        self.place = lax.axis_index("head")
        self.part_ref, self.own_ref = part_ref, own_ref
        self.right_ref, self.left_ref = right_ref, left_ref
        self.sems = sems
        self.spread = spread

    def barrier(self, digits=()):
        sem = pltpu.get_barrier_semaphore()
        place, count = self.place, self.count
        for digit in digits:
            partner = flipped(lax.axis_index("seq"), digit)
            pl.semaphore_signal(sem, inc=1, device_id={"seq": partner}, device_id_type=MESH)

        @pl.when(place > 0)
        def _():
            pl.semaphore_signal(sem, inc=1, device_id={"head": place - 1}, device_id_type=MESH)

        @pl.when(place < count - 1)
        def _():
            pl.semaphore_signal(sem, inc=1, device_id={"head": place + 1}, device_id_type=MESH)

        inside = (place > 0) & (place < count - 1)

        @pl.when(inside)
        def _():
            pl.semaphore_wait(sem, 2 + len(digits))

        @pl.when(jnp.logical_not(inside))
        def _():
            pl.semaphore_wait(sem, 1 + len(digits))

    def barrier_all(self, digits):
        sem = pltpu.get_barrier_semaphore()
        for digit in digits:
            partner = flipped(lax.axis_index("seq"), digit)
            pl.semaphore_signal(sem, inc=1, device_id={"seq": partner}, device_id_type=MESH)
        for distance in range(1, self.count):
            other = lax.rem(self.place + distance, self.count)
            pl.semaphore_signal(sem, inc=1, device_id={"head": other}, device_id_type=MESH)
        pl.semaphore_wait(sem, self.count - 1 + len(digits))

    def copy(self, ref, send, receive, p, t, step):
        return pltpu.make_async_remote_copy(
            src_ref=ref,
            dst_ref=ref,
            send_sem=self.sems[send].at[p, t],
            recv_sem=self.sems[receive].at[p, t],
            device_id={"head": jnp.clip(self.place + step, 0, self.count - 1)},
            device_id_type=MESH,
        )

    def sum_copy(self, p, t, step):
        ref = self.right_ref if step > 0 else self.left_ref
        base = 0 if step > 0 else 2
        return self.copy(ref.at[p, t], base, base + 1, p, t, step)

    def spread_copy(self, p, t, step):
        first = 4 if self.sums else 0
        return self.copy(self.spread(p, t), first if step > 0 else first + 1, first + 2, p, t, step)

    def send_sums(self, p, distance):
        place, count = self.place, self.count
        for step, ref in ((1, self.right_ref), (-1, self.left_ref)):
            t = place + step * distance
            first = place == (0 if step > 0 else count - 1)

            @pl.when((t >= 0) & (t < count))
            def _(t=t, step=step, ref=ref, first=first):
                @pl.when(first)
                def _():
                    ref[p, t] = self.part_ref[t].astype(LOW)

                @pl.when(jnp.logical_not(first))
                def _():
                    self.sum_copy(p, t, step).wait_recv()
                    ref[p, t] = (ref[p, t].astype(F32) + self.part_ref[t].astype(F32)).astype(LOW)

                self.sum_copy(p, t, step).start()

    def keep_own(self, p):
        self.own_ref[p] = self.part_ref[self.place].astype(F32)

    def finish_own(self, p):
        place, count = self.place, self.count
        for step, ref, inner in ((1, self.right_ref, place > 0), (-1, self.left_ref, place < count - 1)):

            @pl.when(inner)
            def _(step=step, ref=ref):
                self.sum_copy(p, place, step).wait_recv()
                self.own_ref[p] = self.own_ref[p] + ref[p, place].astype(F32)

    def hand_out(self, p):
        place, count = self.place, self.count

        @pl.when(place < count - 1)
        def _():
            self.spread_copy(p, place, 1).start()

        @pl.when(place > 0)
        def _():
            self.spread_copy(p, place, -1).start()

    def hand_on(self, p, distance):
        place, count = self.place, self.count
        for step, more in ((1, place < count - 1), (-1, place > 0)):
            t = place - step * distance

            @pl.when((t >= 0) & (t < count))
            def _(t=t, step=step, more=more):
                self.spread_copy(p, t, step).wait_recv()

                @pl.when(more)
                def _():
                    self.spread_copy(p, t, step).start()

    def drain(self):
        place, count = self.place, self.count

        def one(p, carry):
            for t in range(count):
                if self.sums:

                    @pl.when(t > place)
                    def _(t=t):
                        self.sum_copy(p, t, 1).wait_send()

                    @pl.when(t < place)
                    def _(t=t):
                        self.sum_copy(p, t, -1).wait_send()

                if self.spread is not None:

                    @pl.when((t <= place) & (place < count - 1))
                    def _(t=t):
                        self.spread_copy(p, t, 1).wait_send()

                    @pl.when((t >= place) & (place > 0))
                    def _(t=t):
                        self.spread_copy(p, t, -1).wait_send()

            return carry

        lax.fori_loop(0, self.pieces, one, 0)


def line_scratch(pieces, count, rows, model, part_kind, spread):
    slots = (pieces, count)
    scratch = [
        pltpu.VMEM((pieces, rows, model), F32),
        pltpu.VMEM((pieces, count, rows, model), LOW),
        pltpu.VMEM((pieces, count, rows, model), LOW),
    ] + [pltpu.SemaphoreType.DMA(slots)] * (7 if spread else 4)
    if part_kind is not None:
        scratch = [pltpu.VMEM((count, rows, model), part_kind)] + scratch
    return scratch


def both_ways(index, limit, body):
    @pl.when((index >= 0) & (index < limit))
    def _():
        body(index)


def front_kernel(
    pieces, count, head_dim,
    tok_ref, gain_ref, cos_ref, sin_ref, qgain_ref, kgain_ref, wq_ref, wk_ref, wv_ref, wg_ref,
    normed_ref, qraw_ref, q_ref, kraw_ref, kv_ref, gate_ref,
    all_ref, *sems,
):
    rows, model = tok_ref.shape[1], tok_ref.shape[2]
    tall = count * rows
    line = Line(pieces, count, None, None, None, None, sems, spread=lambda p, t: all_ref.at[p, t])
    line.barrier()
    for p in range(pieces):
        all_ref[p, line.place] = tok_ref[p]

    def project(p):
        b, half = p // 2, p % 2

        def keep(ref, value):
            ref[b, :, half] = value.astype(ref.dtype).reshape(count, rows, value.shape[-1])

        x = all_ref[p].reshape(tall, model).astype(F32)
        normed = (x * inverse_rms(x) * gain_ref[...]).astype(LOW)
        keep(normed_ref, normed)
        cosine = cos_ref[:, half].reshape(tall, head_dim)
        sine = sin_ref[:, half].reshape(tall, head_dim)

        def turned(raw, head_gain):
            parts = []
            for h in range(raw.shape[1] // head_dim):
                part = raw[:, h * head_dim : (h + 1) * head_dim]
                parts.append(turn(part * inverse_rms(part) * head_gain, cosine, sine).astype(LOW))
            return parts

        raw = mm(normed, wk_ref[...])
        keep(kraw_ref, raw)
        values = mm(normed, wv_ref[...]).astype(LOW)
        keep(kv_ref, jnp.concatenate(turned(raw, kgain_ref[...]) + [values], axis=1))
        raw = mm(normed, wq_ref[...])
        keep(qraw_ref, raw)
        keep(q_ref, jnp.concatenate(turned(raw, qgain_ref[...]), axis=1))
        keep(gate_ref, mm(normed, wg_ref[...]))

    def turn_once(k, carry):
        both_ways(k, pieces, line.hand_out)
        for distance in range(1, count):
            both_ways(k - 1, pieces, lambda p, d=distance: line.hand_on(p, d))
        both_ways(k - 1, pieces, project)
        return carry

    lax.fori_loop(0, pieces + 1, turn_once, 0)
    line.drain()


def front_step(tok, gain, cosine, sine, qgain, kgain, wq, wk, wv, wg, count):
    pieces, rows, model = tok.shape
    batch = pieces // 2
    head_dim = qgain.shape[1]
    nq, nk = wq.shape[1], wk.shape[1]

    def wide(columns, kind):
        return jax.ShapeDtypeStruct((batch, count, 2, rows, columns), kind)

    slots = (pieces, count)
    return pl.pallas_call(
        functools.partial(front_kernel, pieces, count, head_dim),
        in_specs=[WHOLE] * 10,
        out_specs=[WHOLE] * 6,
        out_shape=[
            wide(model, LOW), wide(nq, F32), wide(nq, LOW), wide(nk, F32), wide(2 * nk, LOW), wide(nq, F32)
        ],
        scratch_shapes=[pltpu.VMEM((pieces, count, rows, model), LOW)]
        + [pltpu.SemaphoreType.DMA(slots)] * 3,
        compiler_params=params(collective_id=2, has_side_effects=True),
        cost_estimate=takes(95),
        name="front",
    )(
        tok, gain, cosine.reshape(count, 2, rows, head_dim), sine.reshape(count, 2, rows, head_dim),
        qgain, kgain, wq, wk, wv, wg,
    )


def middle_kernel(
    pieces, count,
    acted_ref, tok_ref, gain_ref, wo_ref, masked_hbm, wg_hbm, wl_hbm, wd_hbm,
    middle_ref, dgain_ref, normed_hbm, hidden_hbm, dg_hbm, dl_hbm, dn_hbm,
    mid_ref, wg_ref, wl_ref, wd_ref, masked_ref, normed_ref, hidden_ref, dg_ref, dl_ref, dn_ref, acc_ref,
    load_sem, masked_sem, store_sem,
    part_ref, own_ref, right_ref, left_ref, *sems,
):
    rows, model = own_ref.shape[1], own_ref.shape[2]
    tall = count * rows
    hidden = wg_ref.shape[1]
    line = Line(
        pieces, count, part_ref, own_ref, right_ref, left_ref, sems, spread=lambda p, t: mid_ref.at[p, t]
    )
    place = line.place
    loads = [
        pltpu.make_async_copy(source, target, load_sem.at[i])
        for i, (source, target) in enumerate(((wg_hbm, wg_ref), (wl_hbm, wl_ref), (wd_hbm, wd_ref)))
    ]
    line.barrier()
    for load in loads:
        load.start()
    dgain_ref[...] = jnp.zeros_like(dgain_ref)
    tiles = 3
    tile = hidden // tiles

    def masked_copy(p):
        return pltpu.make_async_copy(masked_hbm.at[:, p], masked_ref, masked_sem)

    def stores(p):
        pairs = (
            (normed_ref, normed_hbm), (hidden_ref, hidden_hbm), (dg_ref, dg_hbm), (dl_ref, dl_hbm),
            (dn_ref, dn_hbm),
        )
        return [
            pltpu.make_async_copy(source, target.at[:, p], store_sem.at[i])
            for i, (source, target) in enumerate(pairs)
        ]

    def begin(p):
        acted = acted_ref[p // 2, :, p % 2].reshape(tall, acted_ref.shape[-1])
        part_ref[...] = mm(acted, wo_ref[...]).reshape(count, rows, model)
        line.keep_own(p)

    def own(p):
        line.finish_own(p)
        middle = own_ref[p] + tok_ref[p].astype(F32)
        middle_ref[p] = middle
        mid_ref[p, place] = middle.astype(LOW)
        line.hand_out(p)

    def units_begin(p):
        line.hand_on(p, count - 1)

        @pl.when(p > 0)
        def _():
            for store in stores(p - 1):
                store.wait()

        x = mid_ref[p].reshape(tall, model).astype(F32)
        normed = (x * inverse_rms(x) * gain_ref[...]).astype(LOW)
        normed_ref[...] = normed.reshape(count, rows, model)
        masked_copy(p).wait()

        @pl.when(p == 0)
        def _():
            for load in loads:
                load.wait()

    def units_tile(i):
        span = slice(i * tile, (i + 1) * tile)
        normed = normed_ref[...].reshape(tall, model)
        gate = mm(normed, wg_ref[:, span])
        lift = mm(normed, wl_ref[:, span])
        grad = mm_t(masked_ref[...].reshape(tall, model), wd_ref[span, :])
        sigmoid = jax.nn.sigmoid(gate)
        silu = gate * sigmoid
        lift_grad = (grad * silu).astype(LOW)
        gate_grad = (grad * lift * (sigmoid + silu * (1.0 - sigmoid))).astype(LOW)
        hidden_ref[:, :, span] = (silu * lift).astype(LOW).reshape(count, rows, tile)
        dg_ref[:, :, span] = gate_grad.reshape(count, rows, tile)
        dl_ref[:, :, span] = lift_grad.reshape(count, rows, tile)
        part = mm_t(gate_grad, wg_ref[:, span]) + mm_t(lift_grad, wl_ref[:, span])
        if i == 0:
            acc_ref[...] = part
        else:
            acc_ref[...] = acc_ref[...] + part

    def units_end(p):
        total = acc_ref[...]
        dn_ref[...] = total.astype(LOW).reshape(count, rows, model)
        x = mid_ref[p].reshape(tall, model).astype(F32)
        dgain_ref[...] = dgain_ref[...] + jnp.sum(total * x * inverse_rms(x), axis=0, keepdims=True)
        for store in stores(p):
            store.start()

        @pl.when(p < pieces - 1)
        def _():
            masked_copy(p + 1).start()

    masked_copy(0).start()

    def turn_once(k, carry):
        both_ways(k, pieces, begin)
        for i in range(max(tiles, count - 1)):
            if i < count - 1:
                both_ways(k, pieces, lambda p, i=i: line.send_sums(p, count - 1 - i))
            if i == 0:
                both_ways(k - 1, pieces, own)
                both_ways(k - 2, pieces, units_begin)
            elif i < count - 1:
                both_ways(k - 1, pieces, lambda p, i=i: line.hand_on(p, i))
            if i < tiles:
                both_ways(k - 2, pieces, lambda p, i=i: units_tile(i))
        both_ways(k - 2, pieces, units_end)
        return carry

    lax.fori_loop(0, pieces + 2, turn_once, 0)
    for store in stores(pieces - 1):
        store.wait()
    line.drain()


def middle_step(acted, tok, gain, wo, masked, wg, wl, wd, count):
    pieces, rows, model = tok.shape
    hidden = wg.shape[1]
    any_place = pl.BlockSpec(memory_space=pl.ANY)

    def wide(columns, kind=LOW):
        return jax.ShapeDtypeStruct((count, pieces, rows, columns), kind)

    def room(columns, kind=LOW):
        return pltpu.VMEM((count, rows, columns), kind)

    return pl.pallas_call(
        functools.partial(middle_kernel, pieces, count),
        in_specs=[WHOLE] * 4 + [any_place] * 4,
        out_specs=[WHOLE] * 2 + [any_place] * 5,
        out_shape=[
            jax.ShapeDtypeStruct((pieces, rows, model), F32), shape_of(1, model, F32),
            wide(model), wide(hidden), wide(hidden), wide(hidden), wide(model),
        ],
        scratch_shapes=[
            pltpu.VMEM((pieces, count, rows, model), LOW),
            pltpu.VMEM(wg.shape, LOW), pltpu.VMEM(wl.shape, LOW), pltpu.VMEM(wd.shape, LOW),
            room(model), room(model), room(hidden), room(hidden), room(hidden), room(model),
            pltpu.VMEM((count * rows, model), F32),
            pltpu.SemaphoreType.DMA((3,)), pltpu.SemaphoreType.DMA, pltpu.SemaphoreType.DMA((5,)),
        ]
        + line_scratch(pieces, count, rows, model, F32, True),
        compiler_params=params(collective_id=0, has_side_effects=True),
        cost_estimate=takes(128),
        name="middle",
    )(acted, tok, gain, wo, masked, wg, wl, wd)


def residual_kernel(
    pieces, count, halves,
    dn_ref, middle_ref, masked_ref, gain_ref, residual_ref, r_ref,
    part_ref, own_ref, right_ref, left_ref, *sems,
):
    line = Line(
        pieces, count, part_ref, own_ref, right_ref, left_ref, sems,
        spread=lambda p, t: r_ref.at[p // halves, t, p % halves],
    )
    line.barrier()

    def begin(p):
        part_ref[...] = dn_ref[:, p]
        line.keep_own(p)

    def own(p):
        line.finish_own(p)
        x = middle_ref[p].astype(LOW).astype(F32)
        residual = masked_ref[p] + norm_back(own_ref[p], x, gain_ref[...])
        residual_ref[p] = residual
        r_ref[p // halves, line.place, p % halves] = residual.astype(LOW)
        line.hand_out(p)

    def turn_once(k, carry):
        both_ways(k, pieces, begin)
        for i in range(count - 1):
            both_ways(k, pieces, lambda p, i=i: line.send_sums(p, count - 1 - i))
            if i == 0:
                both_ways(k - 1, pieces, own)
            else:
                both_ways(k - 1, pieces, lambda p, i=i: line.hand_on(p, i))
        both_ways(k - 1, pieces, lambda p: line.hand_on(p, count - 1))
        return carry

    lax.fori_loop(0, pieces + 1, turn_once, 0)
    line.drain()


def residual_step(dn, middle, masked, gain, batch):
    count, pieces, rows, model = dn.shape
    halves = pieces // batch
    return pl.pallas_call(
        functools.partial(residual_kernel, pieces, count, halves),
        in_specs=[WHOLE] * 4,
        out_specs=[WHOLE] * 2,
        out_shape=[
            jax.ShapeDtypeStruct((pieces, rows, model), F32),
            jax.ShapeDtypeStruct((batch, count, halves, rows, model), LOW),
        ],
        scratch_shapes=line_scratch(pieces, count, rows, model, LOW, True),
        compiler_params=params(collective_id=1, has_side_effects=True),
        cost_estimate=takes(10),
        name="residual",
    )(dn, middle, masked, gain)


def flipped(place, mask):
    bit = 1
    while bit <= mask:
        if mask & bit:
            place = place + (1 - 2 * (place // bit % 2)) * bit
        bit *= 2
    return place


def digit_orders(count, batch):
    upper = [1 << i for i in range(1, count.bit_length() - 1)]
    return [(upper if b % 2 == 0 else upper[::-1]) + [1] for b in range(batch)]


def greet(place, digits):
    sem = pltpu.get_barrier_semaphore()
    for digit in digits:
        pl.semaphore_signal(sem, inc=1, device_id={"seq": flipped(place, digit)}, device_id_type=MESH)
    pl.semaphore_wait(sem, len(digits))


def block_gathers(count, batch, out, sources, send_sem, receive_sem):
    place = lax.axis_index("seq")
    orders = digit_orders(count, batch)
    steps = len(orders[0])
    started = []

    def copy(b, mask, step):
        digit = orders[b][step]
        block = out(b).at[flipped(place, mask)]
        return pltpu.make_async_remote_copy(
            src_ref=sources(b) if mask == 0 else block,
            dst_ref=block,
            send_sem=send_sem.at[b, step, mask],
            recv_sem=receive_sem.at[b, mask | digit],
            device_id={"seq": flipped(place, digit)},
            device_id_type=MESH,
        )

    def pass_on(b, mask, first):
        for step in range(first, steps):
            one = copy(b, mask, step)
            one.start()
            started.append(one)

    def arrive(b, mask, level):
        block = out(b).at[flipped(place, mask)]
        pltpu.make_async_remote_copy(
            src_ref=block,
            dst_ref=block,
            send_sem=send_sem.at[b, 0, mask],
            recv_sem=receive_sem.at[b, mask],
            device_id={"seq": flipped(place, orders[b][level])},
            device_id_type=MESH,
        ).wait_recv()
        pass_on(b, mask, level + 1)

    begins = [functools.partial(pass_on, b, 0, 0) for b in range(batch)]
    arrivals = []
    for level in range(steps):
        for turn in range(1 << level):
            for b in range(batch):
                mask = orders[b][level]
                for i in range(level):
                    if turn >> i & 1:
                        mask |= orders[b][i]
                arrivals.append(functools.partial(arrive, b, mask, level))

    def drain():
        for one in started:
            one.wait_send()

    return begins, arrivals, drain


def gather_kernel(count, batch, own_ref, out_ref, local_sem, send_sem, receive_sem):
    place = lax.axis_index("seq")
    greet(place, digit_orders(count, 1)[0])
    local = [
        pltpu.make_async_copy(own_ref.at[b], out_ref.at[b, place], local_sem.at[b]) for b in range(batch)
    ]
    for copy in local:
        copy.start()
    begins, arrivals, drain = block_gathers(
        count, batch, lambda b: out_ref.at[b], lambda b: own_ref.at[b], send_sem, receive_sem
    )
    for event in begins + arrivals:
        event()
    drain()
    for copy in local:
        copy.wait()


def gather_blocks(own):
    batch, rows, columns = own.shape
    count = lax.axis_size("seq")
    steps = count.bit_length() - 1
    any_place = pl.BlockSpec(memory_space=pl.ANY)
    out = pl.pallas_call(
        functools.partial(gather_kernel, count, batch),
        in_specs=[any_place],
        out_specs=any_place,
        out_shape=jax.ShapeDtypeStruct((batch, count, rows, columns), LOW),
        scratch_shapes=[
            pltpu.SemaphoreType.DMA((batch,)),
            pltpu.SemaphoreType.DMA((batch, steps, count)),
            pltpu.SemaphoreType.DMA((batch, count)),
        ],
        compiler_params=params(collective_id=3, has_side_effects=True),
        cost_estimate=takes(41),
        name="gather_blocks",
    )(own)
    return out.reshape(batch, count * rows, columns)


def block_sums(count, batch, parts, finish, slots, send_sem, receive_sem):
    place = lax.axis_index("seq")
    orders = [order[::-1] for order in digit_orders(count, batch)]
    steps = len(orders[0])

    def masks_at(b, step):
        found = [0]
        for digit in orders[b][step + 1 :][::-1]:
            found = [mask | digit for mask in found] + found
        return found

    numbers = {}
    for b in range(batch):
        place_in = 0
        for step in range(steps):
            for mask in masks_at(b, step):
                numbers[b, step, mask] = place_in
                place_in += 1

    def slot(b, step, mask):
        return slots.at[b, numbers[b, step, mask]]

    def transfer(b, step, mask):
        digit = orders[b][step]
        number = numbers[b, step, mask]
        if step == 0:
            source = parts(b).at[flipped(place, mask | digit)]
        else:
            source = slot(b, step - 1, mask | digit)
        return pltpu.make_async_remote_copy(
            src_ref=source,
            dst_ref=slots.at[b, number],
            send_sem=send_sem.at[b, number],
            recv_sem=receive_sem.at[b, number],
            device_id={"seq": flipped(place, digit)},
            device_id_type=MESH,
        )

    started = []

    def begin():
        for turn in range(count // 2):
            for b in range(batch):
                copy = transfer(b, 0, masks_at(b, 0)[turn])
                copy.start()
                started.append(copy)

    def take(b, step, mask):
        transfer(b, step, mask).wait_recv()
        held = parts(b).at[flipped(place, mask)] if step == 0 else slot(b, step - 1, mask)
        total = held[...].astype(F32) + slot(b, step, mask)[...].astype(F32)
        if step == steps - 1:
            finish(b, total)
        else:
            slot(b, step, mask)[...] = total.astype(LOW)
            if mask & orders[b][step + 1]:
                copy = transfer(b, step + 1, mask & ~orders[b][step + 1])
                copy.start()
                started.append(copy)

    events = []
    for step in range(steps):
        for turn in range(len(masks_at(0, step))):
            for b in range(batch):
                events.append(functools.partial(take, b, step, masks_at(b, step)[turn]))

    def drain():
        for copy in started:
            copy.wait_send()

    return begin, events, drain


def interleaved(first, second):
    taken = 0
    for i, call in enumerate(first):
        call()
        due = (i + 1) * len(second) // len(first)
        while taken < due:
            second[taken]()
            taken += 1


def scatter_kernel(
    pieces, count, seq_count, batch, head_dim,
    parts_ref, hidden_hbm, wd_hbm, middle_ref, valid_ref, kraw_ref, cos_ref, sin_ref, kgain_ref,
    dkv_ref, output_ref, dkgain_ref,
    wd_ref, hidden_ref, load_sem, hidden_sem, slots, send_sem, receive_sem,
    part_ref, own_ref, right_ref, left_ref, *sems,
):
    rows, model = own_ref.shape[1], own_ref.shape[2]
    tall = count * rows
    keys = kraw_ref.shape[2]
    line = Line(pieces, count, part_ref, own_ref, right_ref, left_ref, sems)
    load = pltpu.make_async_copy(wd_hbm, wd_ref, load_sem)

    def hidden_copy(p):
        return pltpu.make_async_copy(hidden_hbm.at[:, p], hidden_ref.at[p % 2], hidden_sem.at[p % 2])

    load.start()
    hidden_copy(0).start()
    dkgain_ref[...] = jnp.zeros_like(dkgain_ref)
    line.barrier(digit_orders(seq_count, 1)[0])

    def finish(b, total):
        for h in range(keys // head_dim):
            columns = slice(h * head_dim, (h + 1) * head_dim)
            grad, gain_grad = norm_turn_back(
                total[:, columns], kraw_ref[b, :, columns], kgain_ref[...], cos_ref[...], sin_ref[...]
            )
            dkv_ref[b, :, columns] = grad.astype(LOW)
            dkgain_ref[...] = dkgain_ref[...] + gain_grad
        dkv_ref[b, :, keys:] = total[:, keys:].astype(LOW)

    first, events, drain = block_sums(
        seq_count, batch, lambda b: parts_ref.at[b], finish, slots, send_sem, receive_sem
    )

    def begin(p):
        if p == 0:
            load.wait()
        if p + 1 < pieces:
            hidden_copy(p + 1).start()
        hidden_copy(p).wait()
        hidden = hidden_ref[p % 2].reshape(tall, hidden_ref.shape[-1])
        part_ref[...] = mm(hidden, wd_ref[...]).reshape(count, rows, model)
        line.keep_own(p)

    def own(p):
        line.finish_own(p)
        output_ref[p] = (valid_ref[p] * (middle_ref[p] + own_ref[p])).astype(LOW)

    first()
    interleaved(line_steps(line, begin, own), events)
    drain()
    line.drain()


def line_steps(line, begin, own):
    steps = []
    for k in range(line.pieces + 1):
        for i in range(line.count - 1):
            if i == 0 and k < line.pieces:
                steps.append(functools.partial(begin, k))
            if k < line.pieces:
                steps.append(functools.partial(line.send_sums, k, line.count - 1 - i))
            if i == 0 and k > 0:
                steps.append(functools.partial(own, k - 1))
    return steps


def scatter_blocks(parts, hidden, wd, middle, valid, kraw, cosine, sine, kgain):
    seq_count, batch = lax.axis_size("seq"), parts.shape[0]
    rows, columns = parts.shape[1] // seq_count, parts.shape[2]
    count, pieces, piece_rows, units = hidden.shape
    model, head_dim = wd.shape[1], kgain.shape[1]
    any_place = pl.BlockSpec(memory_space=pl.ANY)
    return pl.pallas_call(
        functools.partial(scatter_kernel, pieces, count, seq_count, batch, head_dim),
        in_specs=[WHOLE, any_place, any_place] + [WHOLE] * 6,
        out_specs=[WHOLE] * 3,
        out_shape=[
            jax.ShapeDtypeStruct((batch, rows, columns), LOW),
            jax.ShapeDtypeStruct((pieces, piece_rows, model), LOW),
            shape_of(1, head_dim, F32),
        ],
        scratch_shapes=[
            pltpu.VMEM(wd.shape, LOW),
            pltpu.VMEM((2, count, piece_rows, units), LOW),
            pltpu.SemaphoreType.DMA,
            pltpu.SemaphoreType.DMA((2,)),
            pltpu.VMEM((batch, seq_count - 1, rows, columns), LOW),
            pltpu.SemaphoreType.DMA((batch, seq_count - 1)),
            pltpu.SemaphoreType.DMA((batch, seq_count - 1)),
        ]
        + line_scratch(pieces, count, piece_rows, model, F32, False),
        compiler_params=params(collective_id=4, has_side_effects=True),
        cost_estimate=takes(10),
        name="scatter_blocks",
    )(
        parts.reshape(batch, seq_count, rows, columns), hidden, wd, middle, valid, kraw, cosine, sine, kgain
    )


def last_kernel(
    pieces, count, seq_count, streams, halves,
    dq_ref, dkv_ref, dgate_ref, wq_ref, wk_ref, wv_ref, wg_ref, tok_ref, residual_ref, gain_ref,
    dmid_ref, dqgain_ref, dkgain_ref, *refs,
):
    grads, refs = refs[:streams], refs[streams:]
    input_ref, total_ref, sums = refs[0], refs[1], refs[2 : 2 + streams]
    (
        slots, scatter_send, scatter_receive, gather_send, gather_receive,
        dgain_ref, turns_ref, round_ref, mixed_ref, round_send, round_receive, mixed_send, mixed_receive,
        part_ref, own_ref, right_ref, left_ref, *sems,
    ) = refs[2 + streams :]
    rows, model = own_ref.shape[1], own_ref.shape[2]
    tall = count * rows
    place_seq = lax.axis_index("seq")
    digits = digit_orders(seq_count, 1)[0]
    line = Line(pieces, count, part_ref, own_ref, right_ref, left_ref, sems)
    line.barrier_all(digits)
    dgain_ref[...] = jnp.zeros_like(dgain_ref)

    begins, arrivals, gather_drain = block_gathers(
        seq_count, streams, lambda b: sums[b], lambda b: sums[b].at[place_seq], gather_send, gather_receive
    )

    def finish(b, total):
        sums[b][place_seq] = total.astype(LOW)
        begins[b]()

    first, events, scatter_drain = block_sums(
        seq_count, streams, lambda b: grads[b], finish, slots, scatter_send, scatter_receive
    )

    def begin(p):
        b, half = p // halves, p % halves
        dq = dq_ref[b, :, half].reshape(tall, dq_ref.shape[-1])
        dkv = dkv_ref[b, :, half].reshape(tall, dkv_ref.shape[-1])
        dgate = dgate_ref[b, :, half].reshape(tall, dgate_ref.shape[-1])
        nk = dkv.shape[1] // 2
        total = mm_t(dq, wq_ref[...]) + mm_t(dgate, wg_ref[...])
        total = total + mm_t(dkv[:, :nk], wk_ref[...]) + mm_t(dkv[:, nk:], wv_ref[...])
        part_ref[...] = total.reshape(count, rows, model)
        line.keep_own(p)

    def own(p):
        line.finish_own(p)
        x = tok_ref[p].astype(F32)
        grad = own_ref[p]
        inverse = inverse_rms(x)
        dgain_ref[...] = dgain_ref[...] + jnp.sum(grad * x * inverse, axis=0, keepdims=True)
        input_ref[p] = residual_ref[p] + norm_back(grad, x, gain_ref[...])

    first()
    interleaved(line_steps(line, begin, own), events + arrivals)

    width = model // count
    lines = width // 128
    turns_ref[0] = jnp.zeros(turns_ref.shape[1:], F32)
    for t in range(count):
        for i in range(lines):
            span = slice(t * width + i * 128, t * width + (i + 1) * 128)
            turns_ref[0, t, i : i + 1, :] = dgain_ref[:, span]
            turns_ref[0, t, lines + i : lines + i + 1, :] = dmid_ref[:, span]
        turns_ref[0, t, 2 * lines : 2 * lines + 1, :] = dqgain_ref[...]
        turns_ref[0, t, 2 * lines + 1 : 2 * lines + 2, :] = dkgain_ref[...]
    copies = []
    for i, digit in enumerate(digits):
        copy = pltpu.make_async_remote_copy(
            src_ref=turns_ref.at[i],
            dst_ref=round_ref.at[i],
            send_sem=round_send.at[i],
            recv_sem=round_receive.at[i],
            device_id={"seq": flipped(place_seq, digit)},
            device_id_type=MESH,
        )
        copy.start()
        copies.append(copy)
        copy.wait_recv()
        turns_ref[i + 1] = turns_ref[i] + round_ref[i]
    done = len(digits)
    for distance in range(1, count):
        other = lax.rem(line.place + distance, count)
        copy = pltpu.make_async_remote_copy(
            src_ref=turns_ref.at[done, other],
            dst_ref=mixed_ref.at[distance - 1],
            send_sem=mixed_send.at[distance - 1],
            recv_sem=mixed_receive.at[distance - 1],
            device_id={"head": other},
            device_id_type=MESH,
        )
        copy.start()
        copies.append(copy)
    total = turns_ref[done, line.place]
    for distance in range(1, count):
        copies[done + distance - 1].wait_recv()
        total = total + mixed_ref[distance - 1]
    total_ref[...] = total
    for copy in copies:
        copy.wait_send()
    scatter_drain()
    gather_drain()
    line.drain()


def last_step(dq, dkv, dgate, wq, wk, wv, wg, tok, residual, gain, dmid, dqgain, dkgain, grads):
    batch, count, halves, rows, nq = dq.shape
    pieces, model = batch * halves, wq.shape[0]
    seq_count, streams = lax.axis_size("seq"), len(grads)
    tall, columns = grads[0].shape
    block = tall // seq_count
    steps = seq_count.bit_length() - 1
    lines = 8 * ((2 * (model // count // 128) + 2 + 7) // 8)
    return pl.pallas_call(
        functools.partial(last_kernel, pieces, count, seq_count, streams, halves),
        in_specs=[WHOLE] * (13 + streams),
        out_specs=[WHOLE] * (2 + streams),
        out_shape=[jax.ShapeDtypeStruct((pieces, rows, model), F32), shape_of(lines, 128, F32)]
        + [jax.ShapeDtypeStruct((seq_count, block, columns), LOW)] * streams,
        scratch_shapes=[
            pltpu.VMEM((streams, seq_count - 1, block, columns), LOW),
            pltpu.SemaphoreType.DMA((streams, seq_count - 1)),
            pltpu.SemaphoreType.DMA((streams, seq_count - 1)),
            pltpu.SemaphoreType.DMA((streams, steps, seq_count)),
            pltpu.SemaphoreType.DMA((streams, seq_count)),
            pltpu.VMEM((1, model), F32),
            pltpu.VMEM((steps + 1, count, lines, 128), F32),
            pltpu.VMEM((steps, count, lines, 128), F32),
            pltpu.VMEM((count - 1, lines, 128), F32),
            pltpu.SemaphoreType.DMA((steps,)),
            pltpu.SemaphoreType.DMA((steps,)),
            pltpu.SemaphoreType.DMA((count - 1,)),
            pltpu.SemaphoreType.DMA((count - 1,)),
        ]
        + line_scratch(pieces, count, rows, model, F32, False),
        compiler_params=params(collective_id=5, has_side_effects=True),
        cost_estimate=takes(5),
        name="last",
    )(
        dq, dkv, dgate, wq, wk, wv, wg, tok, residual, gain, dmid, dqgain, dkgain,
        *[grad.reshape(seq_count, block, columns) for grad in grads],
    )


def widen_kernel(input_ref, dq_ref, dkv_ref, dgate_ref, out_ref, *refs):
    ff_refs, refs = refs[:3], refs[3:]
    input_out, dq_out, dk_out, dv_out, dgate_out, out_out, *ff_outs = refs
    keys = dk_out.shape[1]
    input_out[...] = jnp.stack([input_ref[b] for b in range(input_ref.shape[0])], axis=1)
    dq_out[...] = dq_ref[...].astype(F32)
    dk_out[...] = dkv_ref[:, :keys].astype(F32)
    dv_out[...] = dkv_ref[:, keys:].astype(F32)
    dgate_out[...] = dgate_ref[...].astype(F32)
    out_out[...] = out_ref[...].astype(F32).T
    for ref, out in zip(ff_refs, ff_outs):
        out[...] = ref[...].astype(F32)


def widen(input_grad, dq, dkv, dgate, out, ff, steps=8):
    batch, rows, model = input_grad.shape
    columns, keys = dq.shape[1], dkv.shape[1] // 2

    def tall(array):
        return pl.BlockSpec((array.shape[0] // steps, array.shape[1]), lambda i: (i, 0))

    def wide(array):
        return jax.ShapeDtypeStruct(array.shape, F32)

    outs = [
        jax.ShapeDtypeStruct((rows, batch, model), F32),
        wide(dq), shape_of(model, keys, F32), shape_of(model, keys, F32), wide(dgate), shape_of(columns, model, F32),
    ] + [wide(x) for x in ff]
    specs = [pl.BlockSpec((rows // steps, batch, model), lambda i: (i, 0, 0))]
    specs += [tall(x) for x in outs[1:5]]
    specs += [pl.BlockSpec((columns, model // steps), lambda i: (0, i))]
    specs += [tall(x) for x in ff]
    return pl.pallas_call(
        widen_kernel,
        grid=(steps,),
        in_specs=[pl.BlockSpec((batch, rows // steps, model), lambda i: (0, i, 0))]
        + [tall(x) for x in (dq, dkv, dgate, out, *ff)],
        out_specs=specs,
        out_shape=outs,
        compiler_params=params(),
        cost_estimate=takes(25),
        name="widen",
    )(input_grad, dq, dkv, dgate, out, *ff)


def turn_tables(positions, head_dim):
    half_dim = head_dim // 2
    inverse = THETA ** (-(jnp.arange(half_dim, dtype=F32) * 2.0) / head_dim)
    angles = positions.astype(F32)[:, None] * inverse[None, :]
    cosine, sine = jnp.cos(angles), jnp.sin(angles)
    return jnp.concatenate([cosine, cosine], axis=1), jnp.concatenate([-sine, sine], axis=1)


def norm_back(grad, values, gain):
    inverse = inverse_rms(values)
    grad = grad * gain
    mean = jnp.mean(grad * values, axis=-1, keepdims=True)
    return inverse * (grad - values * (inverse * inverse * mean))


def gather(value, axis):
    return lax.all_gather(value, axis, axis=0, tiled=True)


def on_device(
    tokens, cotangent, lengths,
    query_weight, key_weight, value_weight, gating_weight, output_weight,
    swiglu_gate, swiglu_lift, swiglu_down,
    input_gain, middle_gain, query_gain, key_gain,
):
    block_index = lax.axis_index("seq")
    part_index = lax.axis_index("head")
    parts = lax.axis_size("head")
    local_rows, batch, model = tokens.shape
    head_dim = query_gain.shape[0]
    block_rows = local_rows * parts
    flat_rows = block_rows * batch
    group = query_weight.shape[1] // key_weight.shape[1]
    nq, nk = query_weight.shape[1], key_weight.shape[1]
    halves = 2
    pieces, rows = batch * halves, local_rows // halves

    query_start = block_index * block_rows
    positions = query_start + jnp.arange(block_rows, dtype=jnp.int32)
    cosine, sine = turn_tables(positions, head_dim)
    gain_in, gain_mid = input_gain[None, :], middle_gain[None, :]
    gain_q, gain_k = query_gain[None, :], key_gain[None, :]
    local_pos = query_start + part_index * local_rows + jnp.arange(local_rows, dtype=jnp.int32)
    place = jnp.concatenate([query_start[None], lengths]).astype(jnp.int32)
    valid = (local_pos[None, :] < lengths[:, None]).astype(F32)[..., None]
    tok = jnp.transpose(tokens, (1, 0, 2)).reshape(pieces, rows, model)

    normed, qraw, q, kraw, kv_own, gate = [
        x.reshape(batch, block_rows, x.shape[-1])
        for x in front_step(
            tok, gain_in, cosine, sine, gain_q, gain_k,
            query_weight, key_weight, value_weight, gating_weight, parts,
        )
    ]
    kv_own, masked_own = lax.optimization_barrier(
        (kv_own, valid * jnp.transpose(cotangent, (1, 0, 2)).astype(F32))
    )
    kv = gather_blocks(kv_own)
    masked = gather(masked_own.astype(LOW).reshape(batch * local_rows, model), "head")
    att, acted, inv = attend(place, q, kv, gate, group, head_dim)
    middle, dgain_mid, normed_mid, hidden, dg, dl, dn_mid = middle_step(
        acted.reshape(batch, parts, halves, rows, nq), tok, gain_mid, output_weight,
        masked.reshape(parts, pieces, rows, model), swiglu_gate, swiglu_lift, swiglu_down, parts,
    )

    def flat(array):
        return array.reshape(flat_rows, array.shape[-1])

    normed_mid = flat(normed_mid)
    ff_grads = (
        t_mm(normed_mid, flat(dg)).astype(LOW),
        t_mm(normed_mid, flat(dl)).astype(LOW),
        t_mm(flat(hidden), masked).astype(LOW),
    )
    dn_mid, ff_grads = lax.optimization_barrier((dn_mid, ff_grads))
    ff_grads = lax.psum(ff_grads, "seq")
    residual, r = residual_step(
        dn_mid, middle, masked_own.reshape(pieces, rows, model), gain_mid, batch
    )
    r = r.reshape(batch, block_rows, model)
    dq, dkv_all, dgate, dgain_q = attend_back(
        place, q, kv, r, output_weight, att, gate, inv, qraw, cosine, sine, gain_q, group
    )
    dkv, output, dgain_k = scatter_blocks(
        dkv_all, hidden, swiglu_down, middle, valid.reshape(pieces, rows, 1), kraw, cosine, sine, gain_k
    )
    output = jnp.transpose(output.reshape(batch, local_rows, model), (1, 0, 2))
    grads = [
        t_mm(flat(normed), flat(dq)).astype(LOW),
        t_mm(flat(normed), flat(dkv)).astype(LOW),
        t_mm(flat(normed), flat(dgate)).astype(LOW),
        t_mm(flat(r), flat(acted)).astype(LOW),
    ]

    def pieced(array):
        return array.reshape(batch, parts, halves, rows, array.shape[-1])

    input_grad, gains, *grads = last_step(
        pieced(dq), pieced(dkv), pieced(dgate), query_weight, key_weight, value_weight, gating_weight,
        tok, residual, gain_in, dgain_mid, dgain_q, dgain_k, grads,
    )
    input_grad, dq_weight, dk_weight, dv_weight, dgate_weight, out_weight, *ff_sums = widen(
        input_grad.reshape(batch, local_rows, model), *[x.reshape(model, x.shape[-1]) for x in grads], ff_grads
    )
    share = model // parts
    lines = share // 128
    head_share = head_dim // parts

    def head_gain(line):
        return lax.dynamic_slice(gains[line], (part_index * head_share,), (head_share,))

    return (
        output,
        input_grad,
        dq_weight,
        dk_weight,
        dv_weight,
        dgate_weight,
        out_weight,
        *ff_sums,
        gains[:lines].reshape(share),
        gains[lines : 2 * lines].reshape(share),
        head_gain(2 * lines),
        head_gain(2 * lines + 1),
    )


def solution(mesh):
    return jax.shard_map(
        on_device,
        mesh=mesh,
        in_specs=(
            P(("seq", "head"), None, None),
            P(("seq", "head"), None, None),
            P(),
            P(None, "head"),
            P(None, "head"),
            P(None, "head"),
            P(None, "head"),
            P("head", None),
            P(None, "head"),
            P(None, "head"),
            P("head", None),
            P(),
            P(),
            P(),
            P(),
        ),
        out_specs=(
            P(("seq", "head"), None, None),
            P(("seq", "head"), None, None),
            P(None, "head"),
            P(None, "head"),
            P(None, "head"),
            P(None, "head"),
            P("head", None),
            P(None, "head"),
            P(None, "head"),
            P("head", None),
            P("head"),
            P("head"),
            P("head"),
            P("head"),
        ),
        check_vma=False,
    )
```

time: 844 us -> 780 us (0.924)
  Pallas kernels: 559 us -> 667 us
  waiting for transfers between devices: 91 us -> 29.5 us
  other arithmetic: 54.4 us -> 9.13 us
  blocking collectives: 43.1 us -> 0 us
  local copies, waits for them, and re-layouts: 21.4 us -> 10.1 us
    pallas_call x10 -> x6, Pallas kernels: 281 us -> 386 us  [the longest x1 123 us: last_step(): pl.pallas_call(functools.partial(last_kernel, pieces, count, seq_count, s...]
    all_gather x3 -> x1, waiting for transfers between devices: 91 us -> 29.5 us  [gather(): return lax.all_gather(value, axis, axis=0, tiled=True)]
    psum x1 -> x0, blocking collectives: 43.1 us -> none  [on_device(): gains = lax.psum(gains, ('seq', 'head'))]
    convert_element_type x9 -> x3, other arithmetic: 38.3 us -> 2.59 us  [the longest x2 1.46 us: on_device(): valid = (local_pos[None, :] < lengths[:, None]).astype(F32)[..., None]]
    another operation x5 -> x0, other arithmetic: 10.8 us -> none  [the longest x1 4.14 us: on_device(): jnp.stack(dn_in).reshape(batch, parts, halves, rows, model)]
    slice x4 -> x1, local copies, waits for them, and re-layouts: 10.8 us -> 0.75 us  [head_gain(): gains[line]]
    dot_general x5 -> x7, matrix products: 52.2 us -> 45.8 us  [t_mm(): lax.dot_general(left, right, (((0,), (0,)), ((), ())), preferred_element_...]
  transfers between devices with their start and end apart: 5 -> 2, of which waited for: 3 -> 1; matrix products, arithmetic and copies ran while one was open for 7% -> 3% of each run, Pallas kernels for 51% -> 55%
where the time goes in v4:
time: 780 us; the launch traced here: 777 us
  Pallas kernels  667 us (86%)
  matrix products  45.8 us (6%)
  waiting for transfers between devices  29.5 us (4%)
  between operations  14.7 us (2%)
  local copies, waits for them, and re-layouts  10.1 us (1%)
  other arithmetic  9.13 us (1%)
    pallas_call x1, Pallas kernels, middle_step(): pl.pallas_call(functools.partial(middle_kernel, pieces, count), in_specs=...  129 us
    pallas_call x1, Pallas kernels, last_step(): pl.pallas_call(functools.partial(last_kernel, pieces, count, seq_count, s...  123 us
    pallas_call x1, Pallas kernels, residual_step(): pl.pallas_call(functools.partial(residual_kernel, pieces, count, halves),...  117 us
    pallas_call x1, Pallas kernels, scatter_blocks(): pl.pallas_call(functools.partial(scatter_kernel, pieces, count, seq_count...  111 us
    pallas_call x1, Pallas kernels, front_step(): pl.pallas_call(functools.partial(front_kernel, pieces, count, head_dim),...  84.3 us
    dot_general x7, matrix products, t_mm(): lax.dot_general(left, right, (((0,), (0,)), ((), ())), preferred_element_...  45.8 us
    pallas_call x1, Pallas kernels, gather_blocks(): pl.pallas_call(functools.partial(gather_kernel, count, batch), in_specs=[...  41.5 us
    all_gather x1, waiting for transfers between devices, gather(): return lax.all_gather(value, axis, axis=0, tiled=True)  29.5 us
  transfers between devices with their start and end apart: 2, of which 1 were waited for; matrix products, arithmetic and copies ran while one was open for 3% of the time, Pallas kernels for 55%

profile of v4, /device:TPU:0, one launch (start us, length us, event | category | flops | bytes accessed | tf_op | source)
XLA Modules:
  0.0 776.6 jit_solution(9880302970861638802)
XLA Ops:
  7.2 0.0 all-gather.2.cloned.1.call-start
  7.2 0.0 copy-start.2
  7.3 2.5 copy.36
  9.8 0.7 compare_convert_fusion.1
  10.6 1.0 fusion.1
  11.6 1.7 bitcast_multiply_fusion
  13.3 0.0 copy-start
  13.3 1.3 pad_maximum_fusion
  14.5 84.3 %front.1 = (bf16[2,4,2,64,2048]{4,3,2,1,0:T(8,128)(2,1)}, f32[2,4,2,64,512]{4,3,2,1,0:T(8,128)}, bf16[2,4,2,64,512]{4,3,2,1,0:T(8,128)(2,1)}, f32[2,4,2,64,256]{...) custom-call(bf16[4,64,2048]{2,1,0:T(8,128)(2,1)} %bitcast.87, ...), custom_call_target="tpu_custom_call" | custom-call | flops 109250002944 | bytes 350550016 | tf_op jit(solution)/shard_map/front/pallas_call | solution.py:511
  98.8 0.0 copy-done.2
  98.8 0.0 copy-start.4
  98.8 0.0 copy-done
  98.8 1.1 convert_element_type.60
  100.0 0.0 all-gather.2.cloned.1.call-update
  100.0 0.0 all-reduce.3.cloned.1.call-start
  100.0 0.0 copy-done.4
  100.1 0.6 pad_add_fusion.place_ref
  100.6 41.5 %gather_blocks.1 = bf16[2,8,512,512]{3,2,1,0:T(8,128)(2,1)} custom-call(bf16[2,512,512]{2,1,0:T(8,128)(2,1)} %bitcast.125), custom_call_target="tpu_custom_call" | custom-call | flops 47149998080 | bytes 151290000 | tf_op jit(solution)/shard_map/gather_blocks/pallas_call | solution.py:839
  142.2 8.3 %attend.1 = (f32[2,512,512]{2,1,0:T(8,128)}, bf16[2,512,512]{2,1,0:T(8,128)(2,1)}, f32[2,512,128]{2,1,0:T(8,128)}) custom-call(s32[3]{0:T(128)} %pad_add_fusion.place_ref, bf16[2,512,512]{2,1,0:T(8,128)(2,1)} %bitcast.84, bf16[2,4096,512]{2,1,0:T(8,128)(2,1)} %bitcast.75, f32[2,512,512]{2,1,0:T(8,128)} %bitcast.82), custom_call_target="tpu_custom_call" | custom-call | flops 20700000256 | bytes 66420000 | tf_op jit(solution)/shard_map/attend/pallas_call | solution.py:138
  150.4 29.5 %all-gather.2.cloned.1.call-done = bf16[1024,2048]{1,0:T(8,128)(2,1)} async-done(((bf16[256,2048]{1,0:T(8,128)(2,1)}), bf16[1024,2048]{1,0:T(8,128)(2,1)}) %all-gather.2.cloned.1.call-update) | async-done | bytes 4194320 | tf_op jit(solution)/shard_map/all_gather | solution.py:1243
  179.9 129.0 %middle.1 = (f32[4,64,2048]{2,1,0:T(8,128)}, f32[1,2048]{1,0:T(1,128)}, bf16[4,4,64,2048]{3,2,1,0:T(8,128)(2,1)}, bf16[4,4,64,1536]{3,2,1,0:T(8,128)(2,1)}, bf16...) custom-call(bf16[2,4,2,64,512]{4,3,2,1,0:T(8,128)(2,1)} %bitcast.121, ...), custom_call_target="tpu_custom_call" | custom-call | flops 147200000000 | bytes 472320000 | tf_op jit(solution)/shard_map/middle/pallas_call | solution.py:663
  309.0 11.9 %bitcast_convert_fusion.1 = bf16[2048,1536]{1,0:T(8,128)(2,1)} fusion(bf16[4,4,64,2048]{3,2,1,0:T(8,128)(2,1)} %get-tuple-element.67, bf16[4,4,64,1536]{3,2,1,0:T(8,128)(2,1)} %get-tuple-element.68), kind=kOutput, calls=%fused_computation.1 | convolution fusion | flops 6445596672 | bytes 13631488 | tf_op jit(solution)/shard_map/dot_general | solution.py:28
  320.9 8.8 %bitcast_convert_fusion = bf16[2048,1536]{1,0:T(8,128)(2,1)} fusion(bf16[4,4,64,2048]{3,2,1,0:T(8,128)(2,1)S(1)} %copy-done.12, bf16[4,4,64,1536]{3,2,1,0:T(8,128)(2,1)S(1)} %copy-done.13), kind=kOutput, calls=%fused_computation | convolution fusion | flops 6445596672 | bytes 13631488 | tf_op jit(solution)/shard_map/dot_general | solution.py:28
  329.7 8.8 %convolution_convert_fusion = bf16[1536,2048]{1,0:T(8,128)(2,1)} fusion(bf16[1024,1536]{1,0:T(8,128)(2,1)S(1)} %bitcast.110, bf16[1024,2048]{1,0:T(8,128)(2,1)S(1)} %copy-done.6), kind=kOutput, calls=%fused_computation.2 | convolution fusion | flops 6445596672 | bytes 13631488 | tf_op jit(solution)/shard_map/dot_general | solution.py:28
  338.5 0.0 all-reduce.3.cloned.1.call-update
  338.5 0.6 copy-done.5
  339.2 0.1 lt.45
  339.2 0.1 lt.46
  339.3 0.1 copy.38
  339.5 1.0 fusion
  340.5 1.0 pad_maximum_fusion.2
  341.5 0.7 compare_convert_fusion.valid_ref
  342.2 117.3 %residual.1 = (f32[4,64,2048]{2,1,0:T(8,128)}, bf16[2,4,2,64,2048]{4,3,2,1,0:T(8,128)(2,1)}) custom-call(bf16[4,4,64,2048]{3,2,1,0:T(8,128)(2,1)} %get-tuple-element.71.dn_ref, f32[4,64,2048]{2,1,0:T(8,128)} %get-tuple-element.72.middle_ref, f32[4,64,2048]{2,1,0:T(8,128)} %bitcast.77, f32[1,2048]{1,0:T(1,128)} %bitcast.102), custom_call_target="tpu_custom_call" | custom-call | flops 11500000256 | bytes 36900000 | tf_op jit(solution)/shard_map/residual/pallas_call | solution.py:726
  459.5 24.6 %attend_back.1 = (bf16[2,512,512]{2,1,0:T(8,128)(2,1)}, bf16[2,4096,512]{2,1,0:T(8,128)(2,1)}, bf16[2,512,512]{2,1,0:T(8,128)(2,1)}, f32[1,128]{1,0:T(1,128)}) custom-call(s32[3]{0:T(128)} %pad_add_fusion.place_ref, bf16[2,512,512]{2,1,0:T(8,128)(2,1)} %bitcast.85, bf16[2,4096,512]{2,1,0:T(8,128)(2,1)} %bitcast.76, bf16[2,512,2048]{2,1,0:T(8,128)(2,1)} %bitcast.79, ...), custom_call_target="tpu_custom_call" | custom-call | flops 3449999872 | bytes 11070000 | tf_op jit(solution)/shard_map/attend_back/pallas_call | solution.py:263
  484.1 0.0 copy-start.9
  484.1 110.5 %scatter_blocks.1 = (bf16[2,512,512]{2,1,0:T(8,128)(2,1)}, bf16[4,64,2048]{2,1,0:T(8,128)(2,1)}, f32[1,128]{1,0:T(1,128)}) custom-call(bf16[2,8,512,512]{3,2,1,0:T(8,128)(2,1)} %bitcast.95, bf16[4,4,64,1536]{3,2,1,0:T(8,128)(2,1)} %get-tuple-element.70.hidden_hbm, bf16[1536,2048]{1,0:T(8,128)(2,1)} %wd_hbm.3, f32[4,64,2048]{2,1,0:T(8,128)} %get-tuple-element.72.middle_ref, ...), custom_call_target="tpu_custom_call" | custom-call | flops 11500000256 | bytes 36900000 | tf_op jit(solution)/shard_map/scatter_blocks/pallas_call | solution.py:1013
  594.7 3.3 copy.45
  598.0 5.1 convolution_convert_fusion.3
  603.0 0.0 copy-done.8
  603.1 3.7 convolution_convert_fusion.2
  606.8 3.7 convolution_convert_fusion.4
  610.5 3.8 convolution_convert_fusion.1
  614.3 122.8 %last.1 = (f32[4,64,2048]{2,1,0:T(8,128)}, f32[16,128]{1,0:T(8,128)}, bf16[8,256,512]{2,1,0:T(8,128)(2,1)}, bf16[8,256,512]{2,1,0:T(8,128)(2,1)}, bf16[8,256,512...) custom-call(bf16[2,4,2,64,512]{4,3,2,1,0:T(8,128)(2,1)} %bitcast.97, bf16[2,4,2,64,512]{4,3,2,1,0:T(8,128)(2,1)} %bitcast.124, ...), custom_call_target="tpu_custom_call" | custom-call | flops 5750000128 | bytes 18450000 | tf_op jit(solution)/shard_map/last/pallas_call | solution.py:1151
  737.1 0.8 fusion.2
  737.8 0.6 dynamic-slice_bitcast_fusion
  738.4 0.6 dynamic-slice_bitcast_fusion.1
  739.0 1.3 slice_bitcast_fusion
  740.3 29.0 %widen.1 = (f32[128,2,2048]{2,1,0:T(2,128)}, f32[2048,512]{1,0:T(8,128)}, f32[2048,256]{1,0:T(8,128)}, f32[2048,256]{1,0:T(8,128)}, f32[2048,512]{1,0:T(8,128)},...) custom-call(f32[2,128,2048]{2,1,0:T(8,128)} %bitcast.111, ...), custom_call_target="tpu_custom_call" | custom-call | flops 28750000128 | bytes 92250000 | tf_op jit(solution)/shard_map/widen/pallas_call | solution.py:1214
  (26 shorter events, 0.1 us)
Async XLA Ops:
  7.2 172.7 %all-gather.2.cloned.1.call-start = ((), (), s32[]{:S(2)}) async-start(), calls=%async_computation | async-start | bytes 5242880 | tf_op jit(solution)/shard_map/all_gather | solution.py:1243
  7.2 91.6 %copy-start.2 = (f32[64]{0:T(128)}, f32[64]{0:T(128)S(1)}, u32[]{:S(2)}) copy-start(f32[64]{0:T(128)S(1)} %multiply_power_fusion) | copy-start | bytes 772
  13.3 85.6 %copy-start = (f32[2,128,2048]{2,1,0:T(8,128)}, f32[2,128,2048]{2,1,0:T(8,128)S(1)}, u32[]{:S(2)}) copy-start(f32[2,128,2048]{2,1,0:T(8,128)S(1)} %bitcast_multiply_fusion) | copy-start | bytes 6291460
  98.8 1.2 copy-start.4
  100.0 640.4 %all-reduce.3.cloned.1.call-start = ((), (), s32[]{:S(2)}) async-start(), calls=%async_computation.1 | async-start | bytes 37748736 | tf_op jit(solution)/shard_map/psum | solution.py:1302
  308.9 11.9 %copy-start.12 = (bf16[4,4,64,2048]{3,2,1,0:T(8,128)(2,1)S(1)}, bf16[4,4,64,2048]{3,2,1,0:T(8,128)(2,1)}, u32[]{:S(2)}) copy-start(bf16[4,4,64,2048]{3,2,1,0:T(8,128)(2,1)} %get-tuple-element.67) | copy-start | bytes 12582916
  308.9 11.9 %copy-start.13 = (bf16[4,4,64,1536]{3,2,1,0:T(8,128)(2,1)S(1)}, bf16[4,4,64,1536]{3,2,1,0:T(8,128)(2,1)}, u32[]{:S(2)}) copy-start(bf16[4,4,64,1536]{3,2,1,0:T(8,128)(2,1)} %get-tuple-element.69) | copy-start | bytes 9437188
  320.9 8.8 %copy-start.6 = (bf16[1024,2048]{1,0:T(8,128)(2,1)S(1)}, bf16[1024,2048]{1,0:T(8,128)(2,1)}, u32[]{:S(2)}) copy-start(bf16[1024,2048]{1,0:T(8,128)(2,1)} %all-gather.2.cloned.1.call-done) | copy-start | bytes 12582916
  320.9 8.8 %copy-start.10 = (bf16[4,4,64,1536]{3,2,1,0:T(8,128)(2,1)S(1)}, bf16[4,4,64,1536]{3,2,1,0:T(8,128)(2,1)}, u32[]{:S(2)}) copy-start(bf16[4,4,64,1536]{3,2,1,0:T(8,128)(2,1)} %get-tuple-element.70.hidden_hbm) | copy-start | bytes 9437188
  338.5 0.7 copy-start.5
  338.5 1.0 copy-start.3
  484.1 113.8 %copy-start.9 = (bf16[2,4,2,64,2048]{4,3,2,1,0:T(8,128)(2,1)S(1)}, bf16[2,4,2,64,2048]{4,3,2,1,0:T(8,128)(2,1)}, u32[]{:S(2)}) copy-start(bf16[2,4,2,64,2048]{4,3,2,1,0:T(8,128)(2,1)} %get-tuple-element.87) | copy-start | bytes 12582916
  598.0 5.1 copy-start.8
  603.1 3.7 copy-start.7
  606.8 3.7 copy-start.1
  606.8 3.7 copy-start.11
Sparse Core Ops, SparseCore 0:
  100.1 79.7 all-gather.1
  338.7 272.1 all-reduce.2

commit v5 on v4

--- a/solution.py
+++ b/solution.py
@@ -10,7 +10,7 @@
 EPS = 1e-06
 THETA = 1000000.0
 LOG2E = 1.4426950408889634
-VMEM_LIMIT = 58 * 1024 * 1024
+MIB = 1024 * 1024
 LOW = jnp.bfloat16
 F32 = jnp.float32
 MESH = pl.DeviceIdType.MESH
@@ -32,8 +32,8 @@
     return jax.ShapeDtypeStruct((rows, columns), kind)
 
 
-def params(**extra):
-    return pltpu.CompilerParams(vmem_limit_bytes=VMEM_LIMIT, **extra)
+def params(mib, **extra):
+    return pltpu.CompilerParams(vmem_limit_bytes=mib * MIB, **extra)
 
 
 def takes(microseconds):
@@ -81,8 +81,9 @@
     sum_ref[...] = jnp.zeros_like(sum_ref)
     whole, end, start, length = live_blocks(place_ref, rows)
 
-    def one_block(j, masked):
-        span = pl.ds(pl.multiple_of(j * rows, rows), rows)
+    def one_block(j, masked, width=1):
+        tall = width * rows
+        span = pl.ds(pl.multiple_of(j * rows, rows), tall)
         if masked:
             key_pos = j * rows + lax.broadcasted_iota(jnp.int32, (rows, rows), 1)
             query_pos = start + lax.broadcasted_iota(jnp.int32, (rows, rows), 0)
@@ -95,7 +96,7 @@
             if masked:
                 weights = jnp.where(allowed, weights, 0.0)
             total = weights[:, :128]
-            for piece in range(1, rows // 128):
+            for piece in range(1, tall // 128):
                 total = total + weights[:, piece * 128 : (piece + 1) * 128]
             sum_ref[h] = sum_ref[h] + total
             acc_ref[h] = acc_ref[h] + mm(weights.astype(LOW), values)
@@ -104,11 +105,16 @@
         one_block(j, False)
         return carry
 
+    def pair(j, carry):
+        one_block(2 * j, False, 2)
+        return carry
+
     def edge(j, carry):
         one_block(j, True)
         return carry
 
-    lax.fori_loop(0, whole, plain, 0)
+    lax.fori_loop(0, whole // 2, pair, 0)
+    lax.fori_loop(whole // 2 * 2, whole, plain, 0)
     lax.fori_loop(whole, end, edge, 0)
     lane = lax.broadcasted_iota(jnp.int32, inv_ref.shape[1:], 1)
     kept = jnp.zeros(inv_ref.shape[1:], F32)
@@ -145,7 +151,7 @@
             pltpu.VMEM((heads, rows, head_dim), F32),
             pltpu.VMEM((heads, rows, 128), F32),
         ],
-        compiler_params=params(),
+        compiler_params=params(58),
         cost_estimate=takes(18),
         name="attend",
     )(place, q, kv, gate)
@@ -189,8 +195,9 @@
     acc_ref[...] = jnp.zeros_like(acc_ref)
     whole, end, start, length = live_blocks(place_ref, rows)
 
-    def one_block(j, masked):
-        span = pl.ds(pl.multiple_of(j * rows, rows), rows)
+    def one_block(j, masked, width=1):
+        tall = width * rows
+        span = pl.ds(pl.multiple_of(j * rows, rows), tall)
         if masked:
             key_pos = j * rows + lax.broadcasted_iota(jnp.int32, (rows, rows), 0)
             query_pos = start + lax.broadcasted_iota(jnp.int32, (rows, rows), 1)
@@ -200,8 +207,8 @@
             value_columns = slice((kv_heads + c) * head_dim, (kv_heads + c + 1) * head_dim)
             keys = kv_ref[0, span, key_columns]
             values = kv_ref[0, span, value_columns]
-            dk = jnp.zeros((rows, head_dim), F32)
-            dv = jnp.zeros((rows, head_dim), F32)
+            dk = jnp.zeros((tall, head_dim), F32)
+            dv = jnp.zeros((tall, head_dim), F32)
             for h in range(c * group, (c + 1) * group):
                 columns = slice(h * head_dim, (h + 1) * head_dim)
                 queries = q_ref[0, :, columns]
@@ -212,12 +219,16 @@
                 dv = dv + mm(weights.astype(LOW), scaled)
                 score = (weights * (mm_t(values, scaled) - corr_ref[h : h + 1, :])).astype(LOW)
                 dk = dk + mm(score, queries)
-                acc_ref[h] = acc_ref[h] + t_mm(score, keys)
+                acc_ref[h] = acc_ref[h] + t_mm(keys, score)
             dkv_ref[0, span, key_columns] = (dk * scale).astype(LOW)
             dkv_ref[0, span, value_columns] = dv.astype(LOW)
 
     def plain(j, carry):
         one_block(j, False)
+        return carry
+
+    def pair(j, carry):
+        one_block(2 * j, False, 2)
         return carry
 
     def edge(j, carry):
@@ -229,14 +240,15 @@
         dkv_ref[0, span, :] = jnp.zeros((rows, dkv_ref.shape[2]), LOW)
         return carry
 
-    lax.fori_loop(0, whole, plain, 0)
+    lax.fori_loop(0, whole // 2, pair, 0)
+    lax.fori_loop(whole // 2 * 2, whole, plain, 0)
     lax.fori_loop(whole, end, edge, 0)
     lax.fori_loop(end, dkv_ref.shape[1] // rows, empty, 0)
     gain_total = jnp.zeros((1, head_dim), F32)
     for h in range(heads):
         columns = slice(h * head_dim, (h + 1) * head_dim)
         grad, gain_grad = norm_turn_back(
-            acc_ref[h] * scale, qraw_ref[0, :, columns], qgain_ref[...], cos_ref[...], sin_ref[...]
+            acc_ref[h].T * scale, qraw_ref[0, :, columns], qgain_ref[...], cos_ref[...], sin_ref[...]
         )
         dq_ref[0, :, columns] = grad.astype(LOW)
         gain_total = gain_total + gain_grad
@@ -271,9 +283,9 @@
         scratch_shapes=[
             pltpu.VMEM((rows, width), LOW),
             pltpu.VMEM((128, rows), F32),
-            pltpu.VMEM((heads, rows, head_dim), F32),
+            pltpu.VMEM((heads, head_dim, rows), F32),
         ],
-        compiler_params=params(),
+        compiler_params=params(58),
         cost_estimate=takes(3),
         name="attend_back",
     )(place, q, kv, r, wo, att, gate, inv, qraw, cosine, sine, qgain)
@@ -517,7 +529,7 @@
         ],
         scratch_shapes=[pltpu.VMEM((pieces, count, rows, model), LOW)]
         + [pltpu.SemaphoreType.DMA(slots)] * 3,
-        compiler_params=params(collective_id=2, has_side_effects=True),
+        compiler_params=params(34, collective_id=2, has_side_effects=True),
         cost_estimate=takes(95),
         name="front",
     )(
@@ -676,7 +688,7 @@
             pltpu.SemaphoreType.DMA((3,)), pltpu.SemaphoreType.DMA, pltpu.SemaphoreType.DMA((5,)),
         ]
         + line_scratch(pieces, count, rows, model, F32, True),
-        compiler_params=params(collective_id=0, has_side_effects=True),
+        compiler_params=params(58, collective_id=0, has_side_effects=True),
         cost_estimate=takes(128),
         name="middle",
     )(acted, tok, gain, wo, masked, wg, wl, wd)
@@ -732,7 +744,7 @@
             jax.ShapeDtypeStruct((batch, count, halves, rows, model), LOW),
         ],
         scratch_shapes=line_scratch(pieces, count, rows, model, LOW, True),
-        compiler_params=params(collective_id=1, has_side_effects=True),
+        compiler_params=params(36, collective_id=1, has_side_effects=True),
         cost_estimate=takes(10),
         name="residual",
     )(dn, middle, masked, gain)
@@ -804,7 +816,7 @@
                 for i in range(level):
                     if turn >> i & 1:
                         mask |= orders[b][i]
-                arrivals.append(functools.partial(arrive, b, mask, level))
+                arrivals.append((1.0 if level == steps - 1 else 4.0, functools.partial(arrive, b, mask, level)))
 
     def drain():
         for one in started:
@@ -824,7 +836,9 @@
     begins, arrivals, drain = block_gathers(
         count, batch, lambda b: out_ref.at[b], lambda b: own_ref.at[b], send_sem, receive_sem
     )
-    for event in begins + arrivals:
+    for begin in begins:
+        begin()
+    for _, event in arrivals:
         event()
     drain()
     for copy in local:
@@ -846,14 +860,14 @@
             pltpu.SemaphoreType.DMA((batch, steps, count)),
             pltpu.SemaphoreType.DMA((batch, count)),
         ],
-        compiler_params=params(collective_id=3, has_side_effects=True),
+        compiler_params=params(4, collective_id=3, has_side_effects=True),
         cost_estimate=takes(41),
         name="gather_blocks",
     )(own)
     return out.reshape(batch, count * rows, columns)
 
 
-def block_sums(count, batch, parts, finish, slots, send_sem, receive_sem):
+def block_sums(count, batch, parts, finish, slots, send_sem, receive_sem, near):
     place = lax.axis_index("seq")
     orders = [order[::-1] for order in digit_orders(count, batch)]
     steps = len(orders[0])
@@ -917,7 +931,7 @@
     for step in range(steps):
         for turn in range(len(masks_at(0, step))):
             for b in range(batch):
-                events.append(functools.partial(take, b, step, masks_at(b, step)[turn]))
+                events.append((near if step == 0 else 4.0, functools.partial(take, b, step, masks_at(b, step)[turn])))
 
     def drain():
         for copy in started:
@@ -926,15 +940,16 @@
     return begin, events, drain
 
 
-def interleaved(first, second):
-    taken = 0
-    for i, call in enumerate(first):
+def interleaved(*lists):
+    spent = [0.0] * len(lists)
+    whole = [sum(time for time, _ in calls) for calls in lists]
+    taken = [0] * len(lists)
+    while any(taken[i] < len(calls) for i, calls in enumerate(lists)):
+        i = min((i for i, calls in enumerate(lists) if taken[i] < len(calls)), key=lambda i: spent[i])
+        time, call = lists[i][taken[i]]
         call()
-        due = (i + 1) * len(second) // len(first)
-        while taken < due:
-            second[taken]()
-            taken += 1
-
+        spent[i] += time / whole[i]
+        taken[i] += 1
 
 def scatter_kernel(
     pieces, count, seq_count, batch, head_dim,
@@ -968,7 +983,7 @@
         dkv_ref[b, :, keys:] = total[:, keys:].astype(LOW)
 
     first, events, drain = block_sums(
-        seq_count, batch, lambda b: parts_ref.at[b], finish, slots, send_sem, receive_sem
+        seq_count, batch, lambda b: parts_ref.at[b], finish, slots, send_sem, receive_sem, 4.0
     )
 
     def begin(p):
@@ -996,11 +1011,11 @@
     for k in range(line.pieces + 1):
         for i in range(line.count - 1):
             if i == 0 and k < line.pieces:
-                steps.append(functools.partial(begin, k))
+                steps.append((1.0, functools.partial(begin, k)))
             if k < line.pieces:
-                steps.append(functools.partial(line.send_sums, k, line.count - 1 - i))
+                steps.append((8.0, functools.partial(line.send_sums, k, line.count - 1 - i)))
             if i == 0 and k > 0:
-                steps.append(functools.partial(own, k - 1))
+                steps.append((1.0, functools.partial(own, k - 1)))
     return steps
 
 
@@ -1029,7 +1044,7 @@
             pltpu.SemaphoreType.DMA((batch, seq_count - 1)),
         ]
         + line_scratch(pieces, count, piece_rows, model, F32, False),
-        compiler_params=params(collective_id=4, has_side_effects=True),
+        compiler_params=params(46, collective_id=4, has_side_effects=True),
         cost_estimate=takes(10),
         name="scatter_blocks",
     )(
@@ -1045,7 +1060,7 @@
     grads, refs = refs[:streams], refs[streams:]
     input_ref, total_ref, sums = refs[0], refs[1], refs[2 : 2 + streams]
     (
-        slots, scatter_send, scatter_receive, gather_send, gather_receive,
+        slots, scatter_send, scatter_receive, gather_send, gather_receive, mine_ref, mine_sem,
         dgain_ref, turns_ref, round_ref, mixed_ref, round_send, round_receive, mixed_send, mixed_receive,
         part_ref, own_ref, right_ref, left_ref, *sems,
     ) = refs[2 + streams :]
@@ -1058,15 +1073,19 @@
     dgain_ref[...] = jnp.zeros_like(dgain_ref)
 
     begins, arrivals, gather_drain = block_gathers(
-        seq_count, streams, lambda b: sums[b], lambda b: sums[b].at[place_seq], gather_send, gather_receive
-    )
+        seq_count, streams, lambda b: sums[b], lambda b: mine_ref.at[b], gather_send, gather_receive
+    )
+
+    def keep(b):
+        return pltpu.make_async_copy(mine_ref.at[b], sums[b].at[place_seq], mine_sem.at[b])
 
     def finish(b, total):
-        sums[b][place_seq] = total.astype(LOW)
+        mine_ref[b] = total.astype(LOW)
         begins[b]()
+        keep(b).start()
 
     first, events, scatter_drain = block_sums(
-        seq_count, streams, lambda b: grads[b], finish, slots, scatter_send, scatter_receive
+        seq_count, streams, lambda b: grads[b], finish, slots, scatter_send, scatter_receive, 1.0
     )
 
     def begin(p):
@@ -1088,22 +1107,10 @@
         dgain_ref[...] = dgain_ref[...] + jnp.sum(grad * x * inverse, axis=0, keepdims=True)
         input_ref[p] = residual_ref[p] + norm_back(grad, x, gain_ref[...])
 
-    first()
-    interleaved(line_steps(line, begin, own), events + arrivals)
-
     width = model // count
     lines = width // 128
-    turns_ref[0] = jnp.zeros(turns_ref.shape[1:], F32)
-    for t in range(count):
-        for i in range(lines):
-            span = slice(t * width + i * 128, t * width + (i + 1) * 128)
-            turns_ref[0, t, i : i + 1, :] = dgain_ref[:, span]
-            turns_ref[0, t, lines + i : lines + i + 1, :] = dmid_ref[:, span]
-        turns_ref[0, t, 2 * lines : 2 * lines + 1, :] = dqgain_ref[...]
-        turns_ref[0, t, 2 * lines + 1 : 2 * lines + 2, :] = dkgain_ref[...]
-    copies = []
-    for i, digit in enumerate(digits):
-        copy = pltpu.make_async_remote_copy(
+    rounds = [
+        pltpu.make_async_remote_copy(
             src_ref=turns_ref.at[i],
             dst_ref=round_ref.at[i],
             send_sem=round_send.at[i],
@@ -1111,30 +1118,55 @@
             device_id={"seq": flipped(place_seq, digit)},
             device_id_type=MESH,
         )
-        copy.start()
-        copies.append(copy)
-        copy.wait_recv()
-        turns_ref[i + 1] = turns_ref[i] + round_ref[i]
+        for i, digit in enumerate(digits)
+    ]
     done = len(digits)
+    shares = []
     for distance in range(1, count):
         other = lax.rem(line.place + distance, count)
-        copy = pltpu.make_async_remote_copy(
-            src_ref=turns_ref.at[done, other],
-            dst_ref=mixed_ref.at[distance - 1],
-            send_sem=mixed_send.at[distance - 1],
-            recv_sem=mixed_receive.at[distance - 1],
-            device_id={"head": other},
-            device_id_type=MESH,
+        shares.append(
+            pltpu.make_async_remote_copy(
+                src_ref=turns_ref.at[done, other],
+                dst_ref=mixed_ref.at[distance - 1],
+                send_sem=mixed_send.at[distance - 1],
+                recv_sem=mixed_receive.at[distance - 1],
+                device_id={"head": other},
+                device_id_type=MESH,
+            )
         )
-        copy.start()
-        copies.append(copy)
-    total = turns_ref[done, line.place]
-    for distance in range(1, count):
-        copies[done + distance - 1].wait_recv()
-        total = total + mixed_ref[distance - 1]
-    total_ref[...] = total
-    for copy in copies:
+
+    def pack():
+        turns_ref[0] = jnp.zeros(turns_ref.shape[1:], F32)
+        for t in range(count):
+            for i in range(lines):
+                span = slice(t * width + i * 128, t * width + (i + 1) * 128)
+                turns_ref[0, t, i : i + 1, :] = dgain_ref[:, span]
+                turns_ref[0, t, lines + i : lines + i + 1, :] = dmid_ref[:, span]
+            turns_ref[0, t, 2 * lines : 2 * lines + 1, :] = dqgain_ref[...]
+            turns_ref[0, t, 2 * lines + 1 : 2 * lines + 2, :] = dkgain_ref[...]
+        rounds[0].start()
+
+    def one_round(i):
+        rounds[i].wait_recv()
+        turns_ref[i + 1] = turns_ref[i] + round_ref[i]
+        for copy in rounds[i + 1 : i + 2] if i + 1 < done else shares:
+            copy.start()
+
+    def total():
+        found = turns_ref[done, line.place]
+        for i, copy in enumerate(shares):
+            copy.wait_recv()
+            found = found + mixed_ref[i]
+        total_ref[...] = found
+
+    steps = line_steps(line, begin, own) + [(1.0, pack)]
+    steps += [(4.0, functools.partial(one_round, i)) for i in range(done)] + [(4.0, total)]
+    first()
+    interleaved(steps, events + arrivals)
+    for copy in rounds + shares:
         copy.wait_send()
+    for b in range(streams):
+        keep(b).wait()
     scatter_drain()
     gather_drain()
     line.drain()
@@ -1151,7 +1183,7 @@
     return pl.pallas_call(
         functools.partial(last_kernel, pieces, count, seq_count, streams, halves),
         in_specs=[WHOLE] * (13 + streams),
-        out_specs=[WHOLE] * (2 + streams),
+        out_specs=[WHOLE] * 2 + [pl.BlockSpec(memory_space=pl.ANY)] * streams,
         out_shape=[jax.ShapeDtypeStruct((pieces, rows, model), F32), shape_of(lines, 128, F32)]
         + [jax.ShapeDtypeStruct((seq_count, block, columns), LOW)] * streams,
         scratch_shapes=[
@@ -1160,6 +1192,8 @@
             pltpu.SemaphoreType.DMA((streams, seq_count - 1)),
             pltpu.SemaphoreType.DMA((streams, steps, seq_count)),
             pltpu.SemaphoreType.DMA((streams, seq_count)),
+            pltpu.VMEM((streams, block, columns), LOW),
+            pltpu.SemaphoreType.DMA((streams,)),
             pltpu.VMEM((1, model), F32),
             pltpu.VMEM((steps + 1, count, lines, 128), F32),
             pltpu.VMEM((steps, count, lines, 128), F32),
@@ -1170,7 +1204,7 @@
             pltpu.SemaphoreType.DMA((count - 1,)),
         ]
         + line_scratch(pieces, count, rows, model, F32, False),
-        compiler_params=params(collective_id=5, has_side_effects=True),
+        compiler_params=params(60, collective_id=5, has_side_effects=True),
         cost_estimate=takes(5),
         name="last",
     )(
@@ -1179,11 +1213,12 @@
     )
 
 
-def widen_kernel(input_ref, dq_ref, dkv_ref, dgate_ref, out_ref, *refs):
+def widen_kernel(input_ref, output_ref, dq_ref, dkv_ref, dgate_ref, out_ref, *refs):
     ff_refs, refs = refs[:3], refs[3:]
-    input_out, dq_out, dk_out, dv_out, dgate_out, out_out, *ff_outs = refs
+    input_out, output_out, dq_out, dk_out, dv_out, dgate_out, out_out, *ff_outs = refs
     keys = dk_out.shape[1]
     input_out[...] = jnp.stack([input_ref[b] for b in range(input_ref.shape[0])], axis=1)
+    output_out[...] = jnp.stack([output_ref[b].astype(F32) for b in range(input_ref.shape[0])], axis=1).astype(LOW)
     dq_out[...] = dq_ref[...].astype(F32)
     dk_out[...] = dkv_ref[:, :keys].astype(F32)
     dv_out[...] = dkv_ref[:, keys:].astype(F32)
@@ -1193,7 +1228,7 @@
         out[...] = ref[...].astype(F32)
 
 
-def widen(input_grad, dq, dkv, dgate, out, ff, steps=8):
+def widen(input_grad, output, dq, dkv, dgate, out, ff, steps=8):
     batch, rows, model = input_grad.shape
     columns, keys = dq.shape[1], dkv.shape[1] // 2
 
@@ -1204,24 +1239,24 @@
         return jax.ShapeDtypeStruct(array.shape, F32)
 
     outs = [
-        jax.ShapeDtypeStruct((rows, batch, model), F32),
+        jax.ShapeDtypeStruct((rows, batch, model), F32), jax.ShapeDtypeStruct((rows, batch, model), LOW),
         wide(dq), shape_of(model, keys, F32), shape_of(model, keys, F32), wide(dgate), shape_of(columns, model, F32),
     ] + [wide(x) for x in ff]
-    specs = [pl.BlockSpec((rows // steps, batch, model), lambda i: (i, 0, 0))]
-    specs += [tall(x) for x in outs[1:5]]
+    specs = [pl.BlockSpec((rows // steps, batch, model), lambda i: (i, 0, 0))] * 2
+    specs += [tall(x) for x in outs[2:6]]
     specs += [pl.BlockSpec((columns, model // steps), lambda i: (0, i))]
     specs += [tall(x) for x in ff]
     return pl.pallas_call(
         widen_kernel,
         grid=(steps,),
-        in_specs=[pl.BlockSpec((batch, rows // steps, model), lambda i: (0, i, 0))]
+        in_specs=[pl.BlockSpec((batch, rows // steps, model), lambda i: (0, i, 0))] * 2
         + [tall(x) for x in (dq, dkv, dgate, out, *ff)],
         out_specs=specs,
         out_shape=outs,
-        compiler_params=params(),
+        compiler_params=params(58),
         cost_estimate=takes(25),
         name="widen",
-    )(input_grad, dq, dkv, dgate, out, *ff)
+    )(input_grad, output, dq, dkv, dgate, out, *ff)
 
 
 def turn_tables(positions, head_dim):
@@ -1310,7 +1345,6 @@
     dkv, output, dgain_k = scatter_blocks(
         dkv_all, hidden, swiglu_down, middle, valid.reshape(pieces, rows, 1), kraw, cosine, sine, gain_k
     )
-    output = jnp.transpose(output.reshape(batch, local_rows, model), (1, 0, 2))
     grads = [
         t_mm(flat(normed), flat(dq)).astype(LOW),
         t_mm(flat(normed), flat(dkv)).astype(LOW),
@@ -1325,8 +1359,11 @@
         pieced(dq), pieced(dkv), pieced(dgate), query_weight, key_weight, value_weight, gating_weight,
         tok, residual, gain_in, dgain_mid, dgain_q, dgain_k, grads,
     )
-    input_grad, dq_weight, dk_weight, dv_weight, dgate_weight, out_weight, *ff_sums = widen(
-        input_grad.reshape(batch, local_rows, model), *[x.reshape(model, x.shape[-1]) for x in grads], ff_grads
+    input_grad, output, dq_weight, dk_weight, dv_weight, dgate_weight, out_weight, *ff_sums = widen(
+        input_grad.reshape(batch, local_rows, model),
+        output.reshape(batch, local_rows, model),
+        *[x.reshape(model, x.shape[-1]) for x in grads],
+        ff_grads,
     )
     share = model // parts
     lines = share // 128

time: 780 us -> 759 us (0.973)
  Pallas kernels: 667 us -> 637 us
  local copies, waits for them, and re-layouts: 10.1 us -> 23.3 us
    unnamed x28 -> x88, local copies, waits for them, and re-layouts: 0.68 us -> 18 us
    pallas_call x1, Pallas kernels: 123 us -> 113 us  [last_step(): pl.pallas_call(functools.partial(last_kernel, pieces, count, seq_count, s...]
    pallas_call x1, Pallas kernels: 111 us -> 103 us  [scatter_blocks(): pl.pallas_call(functools.partial(scatter_kernel, pieces, count, seq_count...]
  transfers between devices with their start and end apart: 2 -> 2, of which waited for: 1 -> 1; matrix products, arithmetic and copies ran while one was open for 3% -> 3% of each run, Pallas kernels for 55% -> 53%
where the time goes in v5:
time: 759 us; the launch traced here: 755 us
  Pallas kernels  637 us (84%)
  matrix products  44.5 us (6%)
  waiting for transfers between devices  27 us (4%)
  local copies, waits for them, and re-layouts  23.3 us (3%)
  between operations  14.8 us (2%)
  other arithmetic  8.11 us (1%)
    pallas_call x1, Pallas kernels, middle_step(): pl.pallas_call(functools.partial(middle_kernel, pieces, count), in_specs=...  129 us
    pallas_call x1, Pallas kernels, last_step(): pl.pallas_call(functools.partial(last_kernel, pieces, count, seq_count, s...  113 us
    pallas_call x1, Pallas kernels, residual_step(): pl.pallas_call(functools.partial(residual_kernel, pieces, count, halves),...  112 us
    pallas_call x1, Pallas kernels, scatter_blocks(): pl.pallas_call(functools.partial(scatter_kernel, pieces, count, seq_count...  103 us
    pallas_call x1, Pallas kernels, front_step(): pl.pallas_call(functools.partial(front_kernel, pieces, count, head_dim),...  76.5 us
    dot_general x7, matrix products, t_mm(): lax.dot_general(left, right, (((0,), (0,)), ((), ())), preferred_element_...  44.5 us
    pallas_call x1, Pallas kernels, gather_blocks(): pl.pallas_call(functools.partial(gather_kernel, count, batch), in_specs=[...  40.7 us
    pallas_call x1, Pallas kernels, widen(): pl.pallas_call(widen_kernel, grid=(steps,), in_specs=[pl.BlockSpec((batch...  29.9 us
  transfers between devices with their start and end apart: 2, of which 1 were waited for; matrix products, arithmetic and copies ran while one was open for 3% of the time, Pallas kernels for 53%

profile of v5, /device:TPU:0, one launch (start us, length us, event | category | flops | bytes accessed | tf_op | source)
XLA Modules:
  0.0 755.1 jit_solution(13708163593037472894)
XLA Ops:
  7.2 0.0 all-gather.2.cloned.1.call-start
  7.4 1.7 copy.34
  9.1 1.4 compare_convert_fusion.1
  10.5 1.0 fusion.1
  11.5 1.7 bitcast_multiply_fusion
  13.2 0.2 pad_maximum_fusion
  13.5 76.5 %front.1 = (bf16[2,4,2,64,2048]{4,3,2,1,0:T(8,128)(2,1)S(1)}, f32[2,4,2,64,512]{4,3,2,1,0:T(8,128)S(1)}, bf16[2,4,2,64,512]{4,3,2,1,0:T(8,128)(2,1)S(1)}, f32[2,...) custom-call(bf16[4,64,2048]{2,1,0:T(8,128)(2,1)S(1)} %bitcast.82, ...), custom_call_target="tpu_custom_call" | custom-call | flops 109250002944 | bytes 350550016 | tf_op jit(solution)/shard_map/front/pallas_call | solution.py:523
  90.0 1.3 copy-done.6
  91.3 2.0 copy-done.20
  93.3 1.0 copy-done.22
  94.3 1.0 copy-done.26
  95.3 1.1 convert_element_type.60
  96.5 0.5 copy-done.5
  97.0 0.3 copy-done.9
  97.3 0.0 all-reduce.3.cloned.1.call-start
  97.4 0.6 pad_add_fusion.place_ref
  98.0 40.7 %gather_blocks.1 = bf16[2,8,512,512]{3,2,1,0:T(8,128)(2,1)S(1)} custom-call(bf16[2,512,512]{2,1,0:T(8,128)(2,1)S(1)} %bitcast.100), custom_call_target="tpu_custom_call" | custom-call | flops 47149998080 | bytes 151290000 | tf_op jit(solution)/shard_map/gather_blocks/pallas_call | solution.py:853
  138.7 3.4 copy-done
  142.1 8.2 %attend.1 = (f32[2,512,512]{2,1,0:T(8,128)}, bf16[2,512,512]{2,1,0:T(8,128)(2,1)}, f32[2,512,128]{2,1,0:T(8,128)}) custom-call(s32[3]{0:T(128)} %pad_add_fusion.place_ref, bf16[2,512,512]{2,1,0:T(8,128)(2,1)} %bitcast.80, bf16[2,4096,512]{2,1,0:T(8,128)(2,1)} %bitcast.72, f32[2,512,512]{2,1,0:T(8,128)} %bitcast.78), custom_call_target="tpu_custom_call" | custom-call | flops 20700000256 | bytes 66420000 | tf_op jit(solution)/shard_map/attend/pallas_call | solution.py:144
  150.3 26.9 %all-gather.2.cloned.1.call-done = bf16[1024,2048]{1,0:T(8,128)(2,1)} async-done(((bf16[256,2048]{1,0:T(8,128)(2,1)}), bf16[1024,2048]{1,0:T(8,128)(2,1)}) %all-gather.2.cloned.1.call-update) | async-done | bytes 4194320 | tf_op jit(solution)/shard_map/all_gather | solution.py:1278
  177.2 129.1 %middle.1 = (f32[4,64,2048]{2,1,0:T(8,128)}, f32[1,2048]{1,0:T(1,128)}, bf16[4,4,64,2048]{3,2,1,0:T(8,128)(2,1)}, bf16[4,4,64,1536]{3,2,1,0:T(8,128)(2,1)}, bf16...) custom-call(bf16[2,4,2,64,512]{4,3,2,1,0:T(8,128)(2,1)} %bitcast.120, ...), custom_call_target="tpu_custom_call" | custom-call | flops 147200000000 | bytes 472320000 | tf_op jit(solution)/shard_map/middle/pallas_call | solution.py:675
  306.3 12.1 %bitcast_convert_fusion.1 = bf16[2048,1536]{1,0:T(8,128)(2,1)} fusion(bf16[4,4,64,2048]{3,2,1,0:T(8,128)(2,1)} %get-tuple-element.68, bf16[4,4,64,1536]{3,2,1,0:T(8,128)(2,1)} %get-tuple-element.69), kind=kOutput, calls=%fused_computation.1 | convolution fusion | flops 6445596672 | bytes 13631488 | tf_op jit(solution)/shard_map/dot_general | solution.py:28
  318.4 8.8 %bitcast_convert_fusion = bf16[2048,1536]{1,0:T(8,128)(2,1)} fusion(bf16[4,4,64,2048]{3,2,1,0:T(8,128)(2,1)S(1)} %copy-done.42, bf16[4,4,64,1536]{3,2,1,0:T(8,128)(2,1)S(1)} %copy-done.43), kind=kOutput, calls=%fused_computation | convolution fusion | flops 6445596672 | bytes 13631488 | tf_op jit(solution)/shard_map/dot_general | solution.py:28
  327.3 8.8 %convolution_convert_fusion = bf16[1536,2048]{1,0:T(8,128)(2,1)} fusion(bf16[1024,1536]{1,0:T(8,128)(2,1)S(1)} %bitcast.110, bf16[1024,2048]{1,0:T(8,128)(2,1)S(1)} %copy-done.37), kind=kOutput, calls=%fused_computation.2 | convolution fusion | flops 6445596672 | bytes 13631488 | tf_op jit(solution)/shard_map/dot_general | solution.py:28
  336.1 0.6 copy-done.36
  336.7 0.1 lt.45
  336.8 0.1 lt.46
  336.9 0.1 copy.36
  337.0 1.0 fusion
  338.0 1.0 pad_maximum_fusion.2
  339.0 0.1 compare_convert_fusion.valid_ref
  339.1 2.2 copy-done.30
  341.3 2.2 copy-done.32
  343.5 112.2 %residual.1 = (f32[4,64,2048]{2,1,0:T(8,128)S(1)}, bf16[2,4,2,64,2048]{4,3,2,1,0:T(8,128)(2,1)S(1)}) custom-call(bf16[4,4,64,2048]{3,2,1,0:T(8,128)(2,1)S(1)} %copy-done.32, f32[4,64,2048]{2,1,0:T(8,128)S(1)} %copy-done.30, f32[4,64,2048]{2,1,0:T(8,128)S(1)} %bitcast.74, f32[1,2048]{1,0:T(1,128)S(1)} %bitcast.88), custom_call_target="tpu_custom_call" | custom-call | flops 11500000256 | bytes 36900000 | tf_op jit(solution)/shard_map/residual/pallas_call | solution.py:738
  455.7 2.0 copy-done.3
  457.7 1.3 copy-done.28
  459.1 25.1 %attend_back.1 = (bf16[2,512,512]{2,1,0:T(8,128)(2,1)}, bf16[2,4096,512]{2,1,0:T(8,128)(2,1)}, bf16[2,512,512]{2,1,0:T(8,128)(2,1)}, f32[1,128]{1,0:T(1,128)}) custom-call(s32[3]{0:T(128)} %pad_add_fusion.place_ref, bf16[2,512,512]{2,1,0:T(8,128)(2,1)} %bitcast.81, bf16[2,4096,512]{2,1,0:T(8,128)(2,1)} %bitcast.73, bf16[2,512,2048]{2,1,0:T(8,128)(2,1)} %bitcast.75, ...), custom_call_target="tpu_custom_call" | custom-call | flops 3449999872 | bytes 11070000 | tf_op jit(solution)/shard_map/attend_back/pallas_call | solution.py:275
  484.2 102.6 %scatter_blocks.1 = (bf16[2,512,512]{2,1,0:T(8,128)(2,1)S(1)}, bf16[4,64,2048]{2,1,0:T(8,128)(2,1)S(1)}, f32[1,128]{1,0:T(1,128)S(1)}) custom-call(bf16[2,8,512,512]{3,2,1,0:T(8,128)(2,1)} %bitcast.104, bf16[4,4,64,1536]{3,2,1,0:T(8,128)(2,1)} %get-tuple-element.71.hidden_hbm, bf16[1536,2048]{1,0:T(8,128)(2,1)} %wd_hbm.3, f32[4,64,2048]{2,1,0:T(8,128)S(1)} %copy-done.31, ...), custom_call_target="tpu_custom_call" | custom-call | flops 11500000256 | bytes 36900000 | tf_op jit(solution)/shard_map/scatter_blocks/pallas_call | solution.py:1028
  586.9 3.7 convolution_convert_fusion.3
  590.6 3.7 convolution_convert_fusion.2
  594.3 3.7 convolution_convert_fusion.4
  598.0 3.8 convolution_convert_fusion.1
  601.8 113.1 %last.1 = (f32[4,64,2048]{2,1,0:T(8,128)}, f32[16,128]{1,0:T(8,128)}, bf16[8,256,512]{2,1,0:T(8,128)(2,1)}, bf16[8,256,512]{2,1,0:T(8,128)(2,1)}, bf16[8,256,512...) custom-call(bf16[2,4,2,64,512]{4,3,2,1,0:T(8,128)(2,1)} %bitcast.106, bf16[2,4,2,64,512]{4,3,2,1,0:T(8,128)(2,1)} %bitcast.99, ...), custom_call_target="tpu_custom_call" | custom-call | flops 5750000128 | bytes 18450000 | tf_op jit(solution)/shard_map/last/pallas_call | solution.py:1183
  714.9 0.8 fusion.2
  715.6 0.6 dynamic-slice_bitcast_fusion
  716.2 0.6 dynamic-slice_bitcast_fusion.1
  716.8 1.3 slice_bitcast_fusion
  718.2 29.9 %widen.1 = (f32[128,2,2048]{2,1,0:T(2,128)}, bf16[128,2,2048]{2,1,0:T(2,128)(2,1)}, f32[2048,512]{1,0:T(8,128)}, f32[2048,256]{1,0:T(8,128)}, f32[2048,256]{1,0:...) custom-call(f32[2,128,2048]{2,1,0:T(8,128)} %bitcast.111, ...), custom_call_target="tpu_custom_call" | custom-call | flops 28750000128 | bytes 92250000 | tf_op jit(solution)/shard_map/widen/pallas_call | solution.py:1249
  (85 shorter events, 0.3 us)
Async XLA Ops:
  7.2 6.2 copy-start.14
  7.2 6.2 copy-start.18
  7.2 6.2 copy-start.11
  7.2 6.2 copy-start.17
  7.2 170.0 %all-gather.2.cloned.1.call-start = ((), (), s32[]{:S(2)}) async-start(), calls=%async_computation | async-start | bytes 5242880 | tf_op jit(solution)/shard_map/all_gather | solution.py:1278
  7.3 82.7 %copy-start.33 = (f32[64]{0:T(128)}, f32[64]{0:T(128)S(1)}, u32[]{:S(2)}) copy-start(f32[64]{0:T(128)S(1)} %multiply_power_fusion) | copy-start | bytes 772
  7.3 6.1 copy-start.12
  7.3 6.1 copy-start.13
  7.4 6.1 copy-start.15
  9.1 80.9 %copy-start.10 = (bf16[2,128,2048]{2,1,0:T(8,128)(2,1)}, bf16[2,128,2048]{2,1,0:T(8,128)(2,1)S(1)}, u32[]{:S(2)}) copy-start(bf16[2,128,2048]{2,1,0:T(8,128)(2,1)S(1)} %copy.34) | copy-start | bytes 3145732
  13.2 82.1 %copy-start.1 = (f32[2,128,2048]{2,1,0:T(8,128)}, f32[2,128,2048]{2,1,0:T(8,128)S(1)}, u32[]{:S(2)}) copy-start(f32[2,128,2048]{2,1,0:T(8,128)S(1)} %bitcast_multiply_fusion) | copy-start | bytes 6291460
  90.0 1.3 copy-start.6
  91.3 2.0 copy-start.20
  93.3 1.0 copy-start.22
  94.3 1.0 copy-start.26
  95.3 1.7 copy-start.5
  95.3 2.0 copy-start.9
  95.3 2.1 copy-start.35
  95.3 2.7 copy-start.27
  97.3 620.8 %all-reduce.3.cloned.1.call-start = ((), (), s32[]{:S(2)}) async-start(), calls=%async_computation.1 | async-start | bytes 37748736 | tf_op jit(solution)/shard_map/psum | solution.py:1337
  138.7 3.4 copy-start
  306.3 12.1 %copy-start.42 = (bf16[4,4,64,2048]{3,2,1,0:T(8,128)(2,1)S(1)}, bf16[4,4,64,2048]{3,2,1,0:T(8,128)(2,1)}, u32[]{:S(2)}) copy-start(bf16[4,4,64,2048]{3,2,1,0:T(8,128)(2,1)} %get-tuple-element.68) | copy-start | bytes 12582916
  306.3 12.1 %copy-start.43 = (bf16[4,4,64,1536]{3,2,1,0:T(8,128)(2,1)S(1)}, bf16[4,4,64,1536]{3,2,1,0:T(8,128)(2,1)}, u32[]{:S(2)}) copy-start(bf16[4,4,64,1536]{3,2,1,0:T(8,128)(2,1)} %get-tuple-element.70) | copy-start | bytes 9437188
  318.4 8.8 %copy-start.37 = (bf16[1024,2048]{1,0:T(8,128)(2,1)S(1)}, bf16[1024,2048]{1,0:T(8,128)(2,1)}, u32[]{:S(2)}) copy-start(bf16[1024,2048]{1,0:T(8,128)(2,1)} %all-gather.2.cloned.1.call-done) | copy-start | bytes 12582916
  318.4 8.8 %copy-start.40 = (bf16[4,4,64,1536]{3,2,1,0:T(8,128)(2,1)S(1)}, bf16[4,4,64,1536]{3,2,1,0:T(8,128)(2,1)}, u32[]{:S(2)}) copy-start(bf16[4,4,64,1536]{3,2,1,0:T(8,128)(2,1)} %get-tuple-element.71.hidden_hbm) | copy-start | bytes 9437188
  336.0 0.7 copy-start.36
  336.0 1.0 copy-start.34
  336.0 3.1 copy-start.2
  336.0 3.1 copy-start.16
  339.1 2.2 copy-start.30
  341.3 2.2 copy-start.32
  455.7 2.0 copy-start.3
  457.7 1.3 copy-start.28
  459.0 25.1 %copy-start.7 = (f32[512,128]{1,0:T(8,128)S(1)}, f32[512,128]{1,0:T(8,128)}, u32[]{:S(2)}) copy-start(f32[512,128]{1,0:T(8,128)} %get-tuple-element.123.cos_ref) | copy-start | bytes 786436
  459.0 25.1 %copy-start.8 = (f32[512,128]{1,0:T(8,128)S(1)}, f32[512,128]{1,0:T(8,128)}, u32[]{:S(2)}) copy-start(f32[512,128]{1,0:T(8,128)} %get-tuple-element.124.sin_ref) | copy-start | bytes 786436
  459.0 25.2 %copy-start.19 = (f32[128]{0:T(128)S(1)}, f32[128]{0:T(128)}, u32[]{:S(2)}) copy-start(f32[128]{0:T(128)} %param.29) | copy-start | bytes 1540
  459.0 25.2 %copy-start.23 = (f32[2,4,2,64,256]{4,3,2,1,0:T(8,128)S(1)}, f32[2,4,2,64,256]{4,3,2,1,0:T(8,128)}, u32[]{:S(2)}) copy-start(f32[2,4,2,64,256]{4,3,2,1,0:T(8,128)} %copy-done.22) | copy-start | bytes 3145732
  459.0 25.2 %copy-start.31 = (f32[4,64,2048]{2,1,0:T(8,128)S(1)}, f32[4,64,2048]{2,1,0:T(8,128)}, u32[]{:S(2)}) copy-start(f32[4,64,2048]{2,1,0:T(8,128)} %get-tuple-element.73.middle_ref) | copy-start | bytes 6291460
  484.2 102.7 %copy-start.21 = (bf16[2,4,2,64,2048]{4,3,2,1,0:T(8,128)(2,1)S(1)}, bf16[2,4,2,64,2048]{4,3,2,1,0:T(8,128)(2,1)}, u32[]{:S(2)}) copy-start(bf16[2,4,2,64,2048]{4,3,2,1,0:T(8,128)(2,1)} %copy-done.20) | copy-start | bytes 12582916
  586.9 3.8 copy-start.24
  586.9 3.7 copy-start.25
  586.9 3.7 copy-start.29
  586.9 3.7 copy-start.39
  590.6 3.7 copy-start.38
  594.3 3.7 copy-start.4
  594.3 3.7 copy-start.41
Sparse Core Ops, SparseCore 0:
  97.5 79.7 all-gather.1
  336.2 272.1 all-reduce.2

commit v6 on v5

--- a/solution.py
+++ b/solution.py
@@ -62,8 +62,8 @@
     return grads * cosine + pltpu.roll(grads * sine, grads.shape[-1] // 2, 1)
 
 
-def live_blocks(place_ref, rows):
-    start, length = place_ref[0], place_ref[1 + pl.program_id(0)]
+def live_blocks(place_ref, rows, first=0):
+    start, length = place_ref[0], place_ref[1 + first + pl.program_id(0)]
     whole = jnp.minimum(start // rows, length // rows)
     end = jnp.minimum(start // rows + 1, (length + rows - 1) // rows)
     end = jnp.where(start < length, end, 0)
@@ -166,129 +166,164 @@
     return inverse * (grad - raw * (inverse * inverse * mean)), gain_grad
 
 
+class HeadsBack:
+    def __init__(
+        self, group, start, length, q, kv, wo, att, gate, inv, qraw, cos, sin, qgain,
+        dq, dkv, dgate, scaled, corr, acc,
+    ):
+        self.group, self.start, self.length = group, start, length
+        self.q, self.kv, self.wo, self.att, self.gate, self.inv, self.qraw = q, kv, wo, att, gate, inv, qraw
+        self.cos, self.sin, self.qgain = cos, sin, qgain
+        self.dq, self.dkv, self.dgate, self.scaled, self.corr, self.acc = dq, dkv, dgate, scaled, corr, acc
+        self.rows, self.head_dim = q.shape[0], cos.shape[1]
+        self.heads = q.shape[1] // self.head_dim
+        self.kv_heads = self.heads // group
+        self.scale = self.head_dim ** (-0.5)
+
+    def columns(self, h):
+        return slice(h * self.head_dim, (h + 1) * self.head_dim)
+
+    def begin(self, r):
+        acted_grad = mm_t(r, self.wo[...])
+        lane = lax.broadcasted_iota(jnp.int32, self.inv.shape, 1)
+        kept = jnp.zeros(self.inv.shape, F32)
+        for h in range(self.heads):
+            columns = self.columns(h)
+            sigmoid = jax.nn.sigmoid(self.gate[:, columns])
+            attended = self.att[:, columns]
+            grad = acted_grad[:, columns]
+            self.dgate[:, columns] = (grad * attended * sigmoid * (1.0 - sigmoid)).astype(LOW)
+            grad = grad * sigmoid
+            inverse = self.inv[:, h : h + 1]
+            self.scaled[:, columns] = (grad * inverse).astype(LOW)
+            total = jnp.sum(grad * attended, axis=1, keepdims=True) * inverse
+            kept = jnp.where(lane == h, total, kept)
+        self.corr[...] = kept.T
+        self.acc[...] = jnp.zeros_like(self.acc)
+
+    def block(self, j, masked, width=1):
+        rows, group = self.rows, self.group
+        tall = width * rows
+        span = pl.ds(pl.multiple_of(j * rows, rows), tall)
+        if masked:
+            key_pos = j * rows + lax.broadcasted_iota(jnp.int32, (tall, rows), 0)
+            query_pos = self.start + lax.broadcasted_iota(jnp.int32, (tall, rows), 1)
+            allowed = (key_pos <= query_pos) & (key_pos < self.length)
+        for c in range(self.kv_heads):
+            key_columns, value_columns = self.columns(c), self.columns(self.kv_heads + c)
+            keys = self.kv[span, key_columns]
+            values = self.kv[span, value_columns]
+            dk = jnp.zeros((tall, self.head_dim), F32)
+            dv = jnp.zeros((tall, self.head_dim), F32)
+            for h in range(c * group, (c + 1) * group):
+                queries = self.q[:, self.columns(h)]
+                scaled = self.scaled[:, self.columns(h)]
+                weights = jnp.exp2(mm_t(keys, queries) * (self.scale * LOG2E))
+                if masked:
+                    weights = jnp.where(allowed, weights, 0.0)
+                dv = dv + mm(weights.astype(LOW), scaled)
+                score = (weights * (mm_t(values, scaled) - self.corr[h : h + 1, :])).astype(LOW)
+                dk = dk + mm(score, queries)
+                self.acc[h] = self.acc[h] + t_mm(keys, score)
+            self.dkv[span, key_columns] = (dk * self.scale).astype(LOW)
+            self.dkv[span, value_columns] = dv.astype(LOW)
+
+    def clear(self, j):
+        span = pl.ds(pl.multiple_of(j * self.rows, self.rows), self.rows)
+        self.dkv[span, :] = jnp.zeros((self.rows, self.dkv.shape[1]), LOW)
+
+    def end(self):
+        gain_total = jnp.zeros((1, self.head_dim), F32)
+        for h in range(self.heads):
+            columns = self.columns(h)
+            grad, gain_grad = norm_turn_back(
+                self.acc[h].T * self.scale, self.qraw[:, columns], self.qgain[...], self.cos[...], self.sin[...]
+            )
+            self.dq[:, columns] = grad.astype(LOW)
+            gain_total = gain_total + gain_grad
+        return gain_total
+
+
+def heads_back_scratch(heads, rows, head_dim):
+    return [
+        pltpu.VMEM((rows, heads * head_dim), LOW),
+        pltpu.VMEM((128, rows), F32),
+        pltpu.VMEM((heads, head_dim, rows), F32),
+    ]
+
+
 def attend_back_kernel(
-    group, head_dim,
+    group,
     place_ref, q_ref, kv_ref, r_ref, wo_ref, att_ref, gate_ref, inv_ref, qraw_ref, cos_ref, sin_ref, qgain_ref,
+    first_gain_ref, first_dq, first_dkv, first_dgate,
     dq_ref, dkv_ref, dgate_ref, dqgain_ref,
     scaled_ref, corr_ref, acc_ref,
 ):
+    del first_dq, first_dkv, first_dgate
     rows = q_ref.shape[1]
-    heads = q_ref.shape[2] // head_dim
-    kv_heads = heads // group
-    scale = head_dim ** (-0.5)
-    acted_grad = mm_t(r_ref[0], wo_ref[...])
-    lane = lax.broadcasted_iota(jnp.int32, inv_ref.shape[1:], 1)
-    kept = jnp.zeros(inv_ref.shape[1:], F32)
-    for h in range(heads):
-        columns = slice(h * head_dim, (h + 1) * head_dim)
-        sigmoid = jax.nn.sigmoid(gate_ref[0, :, columns])
-        attended = att_ref[0, :, columns]
-        grad = acted_grad[:, columns]
-        dgate_ref[0, :, columns] = (grad * attended * sigmoid * (1.0 - sigmoid)).astype(LOW)
-        grad = grad * sigmoid
-        inverse = inv_ref[0, :, h : h + 1]
-        scaled_ref[:, columns] = (grad * inverse).astype(LOW)
-        kept = jnp.where(
-            lane == h, jnp.sum(grad * attended, axis=1, keepdims=True) * inverse, kept
-        )
-    corr_ref[...] = kept.T
-    acc_ref[...] = jnp.zeros_like(acc_ref)
-    whole, end, start, length = live_blocks(place_ref, rows)
-
-    def one_block(j, masked, width=1):
-        tall = width * rows
-        span = pl.ds(pl.multiple_of(j * rows, rows), tall)
-        if masked:
-            key_pos = j * rows + lax.broadcasted_iota(jnp.int32, (rows, rows), 0)
-            query_pos = start + lax.broadcasted_iota(jnp.int32, (rows, rows), 1)
-            allowed = (key_pos <= query_pos) & (key_pos < length)
-        for c in range(kv_heads):
-            key_columns = slice(c * head_dim, (c + 1) * head_dim)
-            value_columns = slice((kv_heads + c) * head_dim, (kv_heads + c + 1) * head_dim)
-            keys = kv_ref[0, span, key_columns]
-            values = kv_ref[0, span, value_columns]
-            dk = jnp.zeros((tall, head_dim), F32)
-            dv = jnp.zeros((tall, head_dim), F32)
-            for h in range(c * group, (c + 1) * group):
-                columns = slice(h * head_dim, (h + 1) * head_dim)
-                queries = q_ref[0, :, columns]
-                scaled = scaled_ref[:, columns]
-                weights = jnp.exp2(mm_t(keys, queries) * (scale * LOG2E))
-                if masked:
-                    weights = jnp.where(allowed, weights, 0.0)
-                dv = dv + mm(weights.astype(LOW), scaled)
-                score = (weights * (mm_t(values, scaled) - corr_ref[h : h + 1, :])).astype(LOW)
-                dk = dk + mm(score, queries)
-                acc_ref[h] = acc_ref[h] + t_mm(keys, score)
-            dkv_ref[0, span, key_columns] = (dk * scale).astype(LOW)
-            dkv_ref[0, span, value_columns] = dv.astype(LOW)
+    whole, end, start, length = live_blocks(place_ref, rows, 1)
+    back = HeadsBack(
+        group, start, length, q_ref.at[0], kv_ref.at[0], wo_ref, att_ref.at[0], gate_ref.at[0], inv_ref.at[0],
+        qraw_ref.at[0], cos_ref, sin_ref, qgain_ref, dq_ref.at[0], dkv_ref.at[0], dgate_ref.at[0],
+        scaled_ref, corr_ref, acc_ref,
+    )
+    back.begin(r_ref[0])
 
     def plain(j, carry):
-        one_block(j, False)
+        back.block(j, False)
         return carry
 
     def pair(j, carry):
-        one_block(2 * j, False, 2)
+        back.block(2 * j, False, 2)
         return carry
 
     def edge(j, carry):
-        one_block(j, True)
+        back.block(j, True)
         return carry
 
     def empty(j, carry):
-        span = pl.ds(pl.multiple_of(j * rows, rows), rows)
-        dkv_ref[0, span, :] = jnp.zeros((rows, dkv_ref.shape[2]), LOW)
+        back.clear(j)
         return carry
 
     lax.fori_loop(0, whole // 2, pair, 0)
     lax.fori_loop(whole // 2 * 2, whole, plain, 0)
     lax.fori_loop(whole, end, edge, 0)
     lax.fori_loop(end, dkv_ref.shape[1] // rows, empty, 0)
-    gain_total = jnp.zeros((1, head_dim), F32)
-    for h in range(heads):
-        columns = slice(h * head_dim, (h + 1) * head_dim)
-        grad, gain_grad = norm_turn_back(
-            acc_ref[h].T * scale, qraw_ref[0, :, columns], qgain_ref[...], cos_ref[...], sin_ref[...]
-        )
-        dq_ref[0, :, columns] = grad.astype(LOW)
-        gain_total = gain_total + gain_grad
+    gain_total = back.end()
 
     @pl.when(pl.program_id(0) == 0)
     def _():
-        dqgain_ref[...] = gain_total
+        dqgain_ref[...] = first_gain_ref[...] + gain_total
 
     @pl.when(pl.program_id(0) > 0)
     def _():
         dqgain_ref[...] = dqgain_ref[...] + gain_total
 
 
-def attend_back(place, q, kv, r, wo, att, gate, inv, qraw, cosine, sine, qgain, group):
+def attend_back(place, q, kv, r, wo, att, gate, inv, qraw, cosine, sine, qgain, group, first_gain, firsts):
     batch, rows, width = q.shape
     head_dim = qgain.shape[1]
-    heads = width // head_dim
-    outs = [
-        jax.ShapeDtypeStruct(q.shape, LOW),
-        jax.ShapeDtypeStruct(kv.shape, LOW),
-        jax.ShapeDtypeStruct(q.shape, LOW),
-    ]
+    any_place = pl.BlockSpec(memory_space=pl.ANY)
+
+    def later(array):
+        return pl.BlockSpec((1,) + array.shape[1:], lambda b: (b + 1,) + (0,) * (len(array.shape) - 1))
+
     line = pl.BlockSpec((1, head_dim), lambda b: (0, 0))
     return pl.pallas_call(
-        functools.partial(attend_back_kernel, group, head_dim),
-        grid=(batch,),
-        in_specs=[SCALARS, by_sequence(q), by_sequence(kv), by_sequence(r), full_block(wo)]
-        + [by_sequence(x) for x in (att, gate, inv, qraw)]
-        + [full_block(x) for x in (cosine, sine, qgain)],
-        out_specs=[by_sequence(x) for x in outs] + [line],
-        out_shape=outs + [shape_of(1, head_dim, F32)],
-        scratch_shapes=[
-            pltpu.VMEM((rows, width), LOW),
-            pltpu.VMEM((128, rows), F32),
-            pltpu.VMEM((heads, head_dim, rows), F32),
-        ],
+        functools.partial(attend_back_kernel, group),
+        grid=(batch - 1,),
+        in_specs=[SCALARS, later(q), later(kv), later(r), full_block(wo)]
+        + [later(x) for x in (att, gate, inv, qraw)]
+        + [full_block(x) for x in (cosine, sine, qgain, first_gain)]
+        + [any_place] * 3,
+        out_specs=[later(x) for x in firsts] + [line],
+        out_shape=[jax.ShapeDtypeStruct(x.shape, x.dtype) for x in firsts] + [shape_of(1, head_dim, F32)],
+        scratch_shapes=heads_back_scratch(width // head_dim, rows, head_dim),
+        input_output_aliases={13: 0, 14: 1, 15: 2},
         compiler_params=params(58),
         cost_estimate=takes(3),
         name="attend_back",
-    )(place, q, kv, r, wo, att, gate, inv, qraw, cosine, sine, qgain)
+    )(place, q, kv, r, wo, att, gate, inv, qraw, cosine, sine, qgain, first_gain, *firsts)
 
 
 class Line:
@@ -694,62 +729,6 @@
     )(acted, tok, gain, wo, masked, wg, wl, wd)
 
 
-def residual_kernel(
-    pieces, count, halves,
-    dn_ref, middle_ref, masked_ref, gain_ref, residual_ref, r_ref,
-    part_ref, own_ref, right_ref, left_ref, *sems,
-):
-    line = Line(
-        pieces, count, part_ref, own_ref, right_ref, left_ref, sems,
-        spread=lambda p, t: r_ref.at[p // halves, t, p % halves],
-    )
-    line.barrier()
-
-    def begin(p):
-        part_ref[...] = dn_ref[:, p]
-        line.keep_own(p)
-
-    def own(p):
-        line.finish_own(p)
-        x = middle_ref[p].astype(LOW).astype(F32)
-        residual = masked_ref[p] + norm_back(own_ref[p], x, gain_ref[...])
-        residual_ref[p] = residual
-        r_ref[p // halves, line.place, p % halves] = residual.astype(LOW)
-        line.hand_out(p)
-
-    def turn_once(k, carry):
-        both_ways(k, pieces, begin)
-        for i in range(count - 1):
-            both_ways(k, pieces, lambda p, i=i: line.send_sums(p, count - 1 - i))
-            if i == 0:
-                both_ways(k - 1, pieces, own)
-            else:
-                both_ways(k - 1, pieces, lambda p, i=i: line.hand_on(p, i))
-        both_ways(k - 1, pieces, lambda p: line.hand_on(p, count - 1))
-        return carry
-
-    lax.fori_loop(0, pieces + 1, turn_once, 0)
-    line.drain()
-
-
-def residual_step(dn, middle, masked, gain, batch):
-    count, pieces, rows, model = dn.shape
-    halves = pieces // batch
-    return pl.pallas_call(
-        functools.partial(residual_kernel, pieces, count, halves),
-        in_specs=[WHOLE] * 4,
-        out_specs=[WHOLE] * 2,
-        out_shape=[
-            jax.ShapeDtypeStruct((pieces, rows, model), F32),
-            jax.ShapeDtypeStruct((batch, count, halves, rows, model), LOW),
-        ],
-        scratch_shapes=line_scratch(pieces, count, rows, model, LOW, True),
-        compiler_params=params(36, collective_id=1, has_side_effects=True),
-        cost_estimate=takes(10),
-        name="residual",
-    )(dn, middle, masked, gain)
-
-
 def flipped(place, mask):
     bit = 1
     while bit <= mask:
@@ -950,6 +929,141 @@
         call()
         spent[i] += time / whole[i]
         taken[i] += 1
+
+def residual_kernel(
+    pieces, count, halves, group, seq_count,
+    place_ref, dn_ref, middle_ref, masked_ref, gain_ref, wo_ref, cos_ref, sin_ref, qgain_ref,
+    q_hbm, kv_hbm, att_hbm, gate_hbm, inv_hbm, qraw_hbm,
+    residual_ref, r_ref, dqgain_ref, dq_hbm, dkv_hbm, dgate_hbm,
+    q_ref, kv_ref, att_ref, gate_ref, inv_ref, qraw_ref, dq_ref, dkv_ref, dgate_ref,
+    scaled_ref, corr_ref, acc_ref, load_sem, store_sem, block_sem,
+    part_ref, own_ref, right_ref, left_ref, *sems,
+):
+    rows, model = own_ref.shape[1], own_ref.shape[2]
+    query_rows = q_ref.shape[0]
+    line = Line(
+        pieces, count, part_ref, own_ref, right_ref, left_ref, sems,
+        spread=lambda p, t: r_ref.at[p // halves, t, p % halves],
+    )
+    pairs = (
+        (q_hbm, q_ref), (kv_hbm, kv_ref), (att_hbm, att_ref), (gate_hbm, gate_ref), (inv_hbm, inv_ref),
+        (qraw_hbm, qraw_ref),
+    )
+    loads = [
+        pltpu.make_async_copy(source.at[0], target, load_sem.at[i]) for i, (source, target) in enumerate(pairs)
+    ]
+    stores = [
+        pltpu.make_async_copy(dq_ref, dq_hbm.at[0], store_sem.at[0]),
+        pltpu.make_async_copy(dgate_ref, dgate_hbm.at[0], store_sem.at[1]),
+    ]
+    line.barrier()
+    for load in loads:
+        load.start()
+    block_index = lax.axis_index("seq")
+    back = HeadsBack(
+        group, block_index * query_rows, place_ref[1], q_ref, kv_ref, wo_ref, att_ref, gate_ref, inv_ref, qraw_ref,
+        cos_ref, sin_ref, qgain_ref, dq_ref, dkv_ref, dgate_ref, scaled_ref, corr_ref, acc_ref,
+    )
+
+    def begin(p):
+        part_ref[...] = dn_ref[:, p]
+        line.keep_own(p)
+
+    def own(p):
+        line.finish_own(p)
+        x = middle_ref[p].astype(LOW).astype(F32)
+        residual = masked_ref[p] + norm_back(own_ref[p], x, gain_ref[...])
+        residual_ref[p] = residual
+        r_ref[p // halves, line.place, p % halves] = residual.astype(LOW)
+        line.hand_out(p)
+
+    def block_store(j):
+        span = pl.ds(j * query_rows, query_rows)
+        return pltpu.make_async_copy(dkv_ref.at[span, :], dkv_hbm.at[0, span, :], block_sem.at[j])
+
+    def heads_begin():
+        for load in loads:
+            load.wait()
+        back.begin(r_ref[0].reshape(query_rows, model))
+
+    def heads_block(j):
+        @pl.when(j <= block_index)
+        def _():
+            back.block(j, True)
+
+        @pl.when(j > block_index)
+        def _():
+            back.clear(j)
+
+        block_store(j).start()
+
+    def heads_end():
+        dqgain_ref[...] = back.end()
+        for store in stores:
+            store.start()
+
+    steps = []
+    for k in range(pieces + 1):
+        for i in range(count - 1):
+            if i == 0 and k < pieces:
+                steps.append((1.0, functools.partial(begin, k)))
+            if k < pieces:
+                steps.append((8.0, functools.partial(line.send_sums, k, count - 1 - i)))
+            if i == 0 and k > 0:
+                steps.append((1.0, functools.partial(own, k - 1)))
+            elif k > 0:
+                steps.append((1.0 if k < pieces else 6.0, functools.partial(line.hand_on, k - 1, i)))
+        if k > 0:
+            steps.append((1.0 if k < pieces else 6.0, functools.partial(line.hand_on, k - 1, count - 1)))
+        if k == halves:
+            ready = len(steps)
+    heads = [(3.0, heads_begin)]
+    heads += [(3.0, functools.partial(heads_block, j)) for j in range(seq_count)]
+    heads += [(2.0, heads_end)]
+    for _, call in steps[:ready]:
+        call()
+    interleaved(steps[ready:], heads)
+    for j in range(seq_count):
+        block_store(j).wait()
+    for store in stores:
+        store.wait()
+    line.drain()
+
+
+def residual_step(dn, middle, masked, gain, place, wo, cosine, sine, qgain, q, kv, att, gate, inv, qraw, group):
+    count, pieces, rows, model = dn.shape
+    batch, query_rows, width = q.shape
+    halves = pieces // batch
+    head_dim = qgain.shape[1]
+    seq_count = lax.axis_size("seq")
+    any_place = pl.BlockSpec(memory_space=pl.ANY)
+    held = (q, kv, att, gate, inv, qraw)
+    return pl.pallas_call(
+        functools.partial(residual_kernel, pieces, count, halves, group, seq_count),
+        in_specs=[SCALARS] + [WHOLE] * 8 + [any_place] * 6,
+        out_specs=[WHOLE] * 3 + [any_place] * 3,
+        out_shape=[
+            jax.ShapeDtypeStruct((pieces, rows, model), F32),
+            jax.ShapeDtypeStruct((batch, count, halves, rows, model), LOW),
+            shape_of(1, head_dim, F32),
+            jax.ShapeDtypeStruct(q.shape, LOW),
+            jax.ShapeDtypeStruct(kv.shape, LOW),
+            jax.ShapeDtypeStruct(q.shape, LOW),
+        ],
+        scratch_shapes=[pltpu.VMEM(x.shape[1:], x.dtype) for x in held]
+        + [pltpu.VMEM(q.shape[1:], LOW), pltpu.VMEM(kv.shape[1:], LOW), pltpu.VMEM(q.shape[1:], LOW)]
+        + heads_back_scratch(width // head_dim, query_rows, head_dim)
+        + [
+            pltpu.SemaphoreType.DMA((6,)),
+            pltpu.SemaphoreType.DMA((2,)),
+            pltpu.SemaphoreType.DMA((seq_count,)),
+        ]
+        + line_scratch(pieces, count, rows, model, LOW, True),
+        compiler_params=params(60, collective_id=1, has_side_effects=True),
+        cost_estimate=takes(10),
+        name="residual",
+    )(place, dn, middle, masked, gain, wo, cosine, sine, qgain, *held)
+
 
 def scatter_kernel(
     pieces, count, seq_count, batch, head_dim,
@@ -1335,12 +1449,13 @@
     )
     dn_mid, ff_grads = lax.optimization_barrier((dn_mid, ff_grads))
     ff_grads = lax.psum(ff_grads, "seq")
-    residual, r = residual_step(
-        dn_mid, middle, masked_own.reshape(pieces, rows, model), gain_mid, batch
+    residual, r, dgain_q, *firsts = residual_step(
+        dn_mid, middle, masked_own.reshape(pieces, rows, model), gain_mid,
+        place, output_weight, cosine, sine, gain_q, q, kv, att, gate, inv, qraw, group,
     )
     r = r.reshape(batch, block_rows, model)
     dq, dkv_all, dgate, dgain_q = attend_back(
-        place, q, kv, r, output_weight, att, gate, inv, qraw, cosine, sine, gain_q, group
+        place, q, kv, r, output_weight, att, gate, inv, qraw, cosine, sine, gain_q, group, dgain_q, firsts
     )
     dkv, output, dgain_k = scatter_blocks(
         dkv_all, hidden, swiglu_down, middle, valid.reshape(pieces, rows, 1), kraw, cosine, sine, gain_k

time: 759 us -> 750 us (0.988)
  Pallas kernels: 637 us -> 628 us
    pallas_call x1, Pallas kernels: 103 us -> 91.8 us  [scatter_blocks(): pl.pallas_call(functools.partial(scatter_kernel, pieces, count, seq_count...]
    unnamed x88 -> x74, local copies, waits for them, and re-layouts: 18 us -> 11.7 us
where the time goes in v6:
time: 750 us; the launch traced here: 739 us
  Pallas kernels  628 us (84%)
  matrix products  44.3 us (6%)
  waiting for transfers between devices  26.9 us (4%)
  local copies, waits for them, and re-layouts  17 us (2%)
  between operations  14.8 us (2%)
  other arithmetic  8.09 us (1%)
    pallas_call x1, Pallas kernels, middle_step(): pl.pallas_call(functools.partial(middle_kernel, pieces, count), in_specs=...  129 us
    pallas_call x1, Pallas kernels, residual_step(): pl.pallas_call(functools.partial(residual_kernel, pieces, count, halves,...  122 us
    pallas_call x1, Pallas kernels, last_step(): pl.pallas_call(functools.partial(last_kernel, pieces, count, seq_count, s...  115 us
    pallas_call x1, Pallas kernels, scatter_blocks(): pl.pallas_call(functools.partial(scatter_kernel, pieces, count, seq_count...  91.8 us
    pallas_call x1, Pallas kernels, front_step(): pl.pallas_call(functools.partial(front_kernel, pieces, count, head_dim),...  76.6 us
    dot_general x7, matrix products, t_mm(): lax.dot_general(left, right, (((0,), (0,)), ((), ())), preferred_element_...  44.3 us
    pallas_call x1, Pallas kernels, gather_blocks(): pl.pallas_call(functools.partial(gather_kernel, count, batch), in_specs=[...  40.7 us
    pallas_call x1, Pallas kernels, widen(): pl.pallas_call(widen_kernel, grid=(steps,), in_specs=[pl.BlockSpec((batch...  29.9 us
  transfers between devices with their start and end apart: 2, of which 1 were waited for; matrix products, arithmetic and copies ran while one was open for 3% of the time, Pallas kernels for 53%

profile of v6, /device:TPU:0, one launch (start us, length us, event | category | flops | bytes accessed | tf_op | source)
XLA Modules:
  0.0 738.8 jit_solution(1920304843511066374)
XLA Ops:
  7.2 0.0 copy-start.12
  7.2 0.0 all-gather.2.cloned.1.call-start
  7.3 0.0 copy-start.10
  7.4 1.7 copy.37
  9.1 1.4 compare_convert_fusion.1
  10.5 1.0 fusion.1
  11.5 1.7 bitcast_multiply_fusion
  13.2 0.2 pad_maximum_fusion
  13.5 76.6 %front.1 = (bf16[2,4,2,64,2048]{4,3,2,1,0:T(8,128)(2,1)S(1)}, f32[2,4,2,64,512]{4,3,2,1,0:T(8,128)S(1)}, bf16[2,4,2,64,512]{4,3,2,1,0:T(8,128)(2,1)S(1)}, f32[2,...) custom-call(bf16[4,64,2048]{2,1,0:T(8,128)(2,1)S(1)} %bitcast.83, ...), custom_call_target="tpu_custom_call" | custom-call | flops 109250002944 | bytes 350550016 | tf_op jit(solution)/shard_map/front/pallas_call | solution.py:558
  90.1 1.3 copy-done.1
  91.4 1.3 copy-done.2
  92.7 1.0 copy-done.5
  93.7 2.0 copy-done.14
  95.7 1.0 copy-done.16
  96.7 1.0 copy-done.20
  97.7 1.1 convert_element_type.60
  98.8 0.0 all-gather.2.cloned.1.call-update
  98.8 0.0 all-reduce.3.cloned.1.call-start
  98.9 0.6 pad_add_fusion.place_ref
  99.5 40.7 %gather_blocks.1 = bf16[2,8,512,512]{3,2,1,0:T(8,128)(2,1)S(1)} custom-call(bf16[2,512,512]{2,1,0:T(8,128)(2,1)S(1)} %bitcast.100), custom_call_target="tpu_custom_call" | custom-call | flops 47149998080 | bytes 151290000 | tf_op jit(solution)/shard_map/gather_blocks/pallas_call | solution.py:832
  140.2 3.4 copy-done
  143.6 8.3 %attend.1 = (f32[2,512,512]{2,1,0:T(8,128)}, bf16[2,512,512]{2,1,0:T(8,128)(2,1)}, f32[2,512,128]{2,1,0:T(8,128)}) custom-call(s32[3]{0:T(128)} %pad_add_fusion.place_ref, bf16[2,512,512]{2,1,0:T(8,128)(2,1)} %bitcast.80, bf16[2,4096,512]{2,1,0:T(8,128)(2,1)} %bitcast.72, f32[2,512,512]{2,1,0:T(8,128)} %bitcast.77), custom_call_target="tpu_custom_call" | custom-call | flops 20700000256 | bytes 66420000 | tf_op jit(solution)/shard_map/attend/pallas_call | solution.py:144
  151.9 26.9 %all-gather.2.cloned.1.call-done = bf16[1024,2048]{1,0:T(8,128)(2,1)} async-done(((bf16[256,2048]{1,0:T(8,128)(2,1)}), bf16[1024,2048]{1,0:T(8,128)(2,1)}) %all-gather.2.cloned.1.call-update) | async-done | bytes 4194320 | tf_op jit(solution)/shard_map/all_gather | solution.py:1392
  178.7 129.4 %middle.1 = (f32[4,64,2048]{2,1,0:T(8,128)}, f32[1,2048]{1,0:T(1,128)}, bf16[4,4,64,2048]{3,2,1,0:T(8,128)(2,1)}, bf16[4,4,64,1536]{3,2,1,0:T(8,128)(2,1)}, bf16...) custom-call(bf16[2,4,2,64,512]{4,3,2,1,0:T(8,128)(2,1)} %bitcast.125, ...), custom_call_target="tpu_custom_call" | custom-call | flops 147200000000 | bytes 472320000 | tf_op jit(solution)/shard_map/middle/pallas_call | solution.py:710
  308.1 11.9 %bitcast_convert_fusion.1 = bf16[2048,1536]{1,0:T(8,128)(2,1)} fusion(bf16[4,4,64,2048]{3,2,1,0:T(8,128)(2,1)} %get-tuple-element.72, bf16[4,4,64,1536]{3,2,1,0:T(8,128)(2,1)} %get-tuple-element.73), kind=kOutput, calls=%fused_computation.1 | convolution fusion | flops 6445596672 | bytes 13631488 | tf_op jit(solution)/shard_map/dot_general | solution.py:28
  320.1 8.6 %bitcast_convert_fusion = bf16[2048,1536]{1,0:T(8,128)(2,1)} fusion(bf16[4,4,64,2048]{3,2,1,0:T(8,128)(2,1)S(1)} %copy-done.35, bf16[4,4,64,1536]{3,2,1,0:T(8,128)(2,1)S(1)} %copy-done.36), kind=kOutput, calls=%fused_computation | convolution fusion | flops 6445596672 | bytes 13631488 | tf_op jit(solution)/shard_map/dot_general | solution.py:28
  328.8 8.6 %convolution_convert_fusion = bf16[1536,2048]{1,0:T(8,128)(2,1)} fusion(bf16[1024,1536]{1,0:T(8,128)(2,1)S(1)} %bitcast.115, bf16[1024,2048]{1,0:T(8,128)(2,1)S(1)} %copy-done.32), kind=kOutput, calls=%fused_computation.2 | convolution fusion | flops 6445596672 | bytes 13631488 | tf_op jit(solution)/shard_map/dot_general | solution.py:28
  337.4 0.0 all-reduce.3.cloned.1.call-update
  337.4 0.6 copy-done.31
  338.0 0.1 lt.45
  338.1 0.1 lt.46
  338.2 0.1 copy.39
  338.4 1.0 fusion
  339.4 1.0 pad_maximum_fusion.2
  340.3 0.1 compare_convert_fusion.valid_ref
  340.4 122.5 %residual.1 = (f32[4,64,2048]{2,1,0:T(8,128)}, bf16[2,4,2,64,2048]{4,3,2,1,0:T(8,128)(2,1)}, f32[1,128]{1,0:T(1,128)}, bf16[2,512,512]{2,1,0:T(8,128)(2,1)}, bf1...) custom-call(s32[3]{0:T(128)} %pad_add_fusion.place_ref, bf16[4,4,64,2048]{3,2,1,0:T(8,128)(2,1)} %get-tuple-element.76.dn_ref, ...), custom_call_target="tpu_custom_call" | custom-call | flops 11500000256 | bytes 36900000 | tf_op jit(solution)/shard_map/residual/pallas_call | solution.py:1041
  463.0 13.8 %attend_back.1 = (bf16[2,512,512]{2,1,0:T(8,128)(2,1)}, bf16[2,4096,512]{2,1,0:T(8,128)(2,1)}, bf16[2,512,512]{2,1,0:T(8,128)(2,1)}, f32[1,128]{1,0:T(1,128)}) custom-call(s32[3]{0:T(128)} %pad_add_fusion.place_ref, bf16[2,512,512]{2,1,0:T(8,128)(2,1)} %bitcast.82, ...), custom_call_target="tpu_custom_call", output_to_operand_aliasing={{0}: (13, {}), {1}: (14, {}), {2}: (15, {})} | custom-call | flops 3449999872 | bytes 11070000 | tf_op jit(solution)/shard_map/attend_back/pallas_call | solution.py:312
  476.8 91.8 %scatter_blocks.1 = (bf16[2,512,512]{2,1,0:T(8,128)(2,1)S(1)}, bf16[4,64,2048]{2,1,0:T(8,128)(2,1)S(1)}, f32[1,128]{1,0:T(1,128)S(1)}) custom-call(bf16[2,8,512,512]{3,2,1,0:T(8,128)(2,1)} %bitcast.102, bf16[4,4,64,1536]{3,2,1,0:T(8,128)(2,1)} %get-tuple-element.75.hidden_hbm, bf16[1536,2048]{1,0:T(8,128)(2,1)} %wd_hbm.3, f32[4,64,2048]{2,1,0:T(8,128)S(1)} %copy-done.22, ...), custom_call_target="tpu_custom_call" | custom-call | flops 11500000256 | bytes 36900000 | tf_op jit(solution)/shard_map/scatter_blocks/pallas_call | solution.py:1142
  568.7 3.8 convolution_convert_fusion.3
  572.5 3.8 convolution_convert_fusion.2
  576.2 3.8 convolution_convert_fusion.4
  580.0 3.8 convolution_convert_fusion.1
  583.8 114.7 %last.1 = (f32[4,64,2048]{2,1,0:T(8,128)}, f32[16,128]{1,0:T(8,128)}, bf16[8,256,512]{2,1,0:T(8,128)(2,1)}, bf16[8,256,512]{2,1,0:T(8,128)(2,1)}, bf16[8,256,512...) custom-call(bf16[2,4,2,64,512]{4,3,2,1,0:T(8,128)(2,1)} %bitcast.106, bf16[2,4,2,64,512]{4,3,2,1,0:T(8,128)(2,1)} %bitcast.99, ...), custom_call_target="tpu_custom_call" | custom-call | flops 5750000128 | bytes 18450000 | tf_op jit(solution)/shard_map/last/pallas_call | solution.py:1297
  698.5 0.8 fusion.2
  699.3 0.6 dynamic-slice_bitcast_fusion
  699.9 0.6 dynamic-slice_bitcast_fusion.1
  700.5 1.3 slice_bitcast_fusion
  701.8 29.9 %widen.1 = (f32[128,2,2048]{2,1,0:T(2,128)}, bf16[128,2,2048]{2,1,0:T(2,128)(2,1)}, f32[2048,512]{1,0:T(8,128)}, f32[2048,256]{1,0:T(8,128)}, f32[2048,256]{1,0:...) custom-call(f32[2,128,2048]{2,1,0:T(8,128)} %bitcast.116, ...), custom_call_target="tpu_custom_call" | custom-call | flops 28750000128 | bytes 92250000 | tf_op jit(solution)/shard_map/widen/pallas_call | solution.py:1363
  (71 shorter events, 0.2 us)
Async XLA Ops:
  7.2 6.3 copy-start.8
  7.2 6.2 copy-start.13
  7.2 6.2 copy-start.7
  7.2 6.2 copy-start.12
  7.2 171.5 %all-gather.2.cloned.1.call-start = ((), (), s32[]{:S(2)}) async-start(), calls=%async_computation | async-start | bytes 5242880 | tf_op jit(solution)/shard_map/all_gather | solution.py:1392
  7.3 82.8 %copy-start.28 = (f32[64]{0:T(128)}, f32[64]{0:T(128)S(1)}, u32[]{:S(2)}) copy-start(f32[64]{0:T(128)S(1)} %multiply_power_fusion) | copy-start | bytes 772
  7.3 6.1 copy-start.9
  7.3 6.1 copy-start.10
  7.4 6.1 copy-start.11
  9.1 81.0 %copy-start.6 = (bf16[2,128,2048]{2,1,0:T(8,128)(2,1)}, bf16[2,128,2048]{2,1,0:T(8,128)(2,1)S(1)}, u32[]{:S(2)}) copy-start(bf16[2,128,2048]{2,1,0:T(8,128)(2,1)S(1)} %copy.37) | copy-start | bytes 3145732
  13.2 84.5 %copy-start.24 = (f32[2,128,2048]{2,1,0:T(8,128)}, f32[2,128,2048]{2,1,0:T(8,128)S(1)}, u32[]{:S(2)}) copy-start(f32[2,128,2048]{2,1,0:T(8,128)S(1)} %bitcast_multiply_fusion) | copy-start | bytes 6291460
  90.1 1.3 copy-start.1
  91.4 1.3 copy-start.2
  92.7 1.0 copy-start.5
  93.7 2.0 copy-start.14
  95.7 1.0 copy-start.16
  96.7 1.0 copy-start.20
  97.7 1.2 copy-start.30
  97.7 1.8 copy-start.21
  98.8 603.0 %all-reduce.3.cloned.1.call-start = ((), (), s32[]{:S(2)}) async-start(), calls=%async_computation.1 | async-start | bytes 37748736 | tf_op jit(solution)/shard_map/psum | solution.py:1451
  140.2 3.4 copy-start
  308.1 12.0 %copy-start.35 = (bf16[4,4,64,2048]{3,2,1,0:T(8,128)(2,1)S(1)}, bf16[4,4,64,2048]{3,2,1,0:T(8,128)(2,1)}, u32[]{:S(2)}) copy-start(bf16[4,4,64,2048]{3,2,1,0:T(8,128)(2,1)} %get-tuple-element.72) | copy-start | bytes 12582916
  308.1 12.0 %copy-start.36 = (bf16[4,4,64,1536]{3,2,1,0:T(8,128)(2,1)S(1)}, bf16[4,4,64,1536]{3,2,1,0:T(8,128)(2,1)}, u32[]{:S(2)}) copy-start(bf16[4,4,64,1536]{3,2,1,0:T(8,128)(2,1)} %get-tuple-element.74) | copy-start | bytes 9437188
  320.1 8.7 %copy-start.32 = (bf16[1024,2048]{1,0:T(8,128)(2,1)S(1)}, bf16[1024,2048]{1,0:T(8,128)(2,1)}, u32[]{:S(2)}) copy-start(bf16[1024,2048]{1,0:T(8,128)(2,1)} %all-gather.2.cloned.1.call-done) | copy-start | bytes 12582916
  320.1 8.7 %copy-start.33 = (bf16[4,4,64,1536]{3,2,1,0:T(8,128)(2,1)S(1)}, bf16[4,4,64,1536]{3,2,1,0:T(8,128)(2,1)}, u32[]{:S(2)}) copy-start(bf16[4,4,64,1536]{3,2,1,0:T(8,128)(2,1)} %get-tuple-element.75.hidden_hbm) | copy-start | bytes 9437188
  337.4 0.7 copy-start.31
  337.4 1.0 copy-start.29
  462.9 13.8 %copy-start.3 = (f32[512,128]{1,0:T(8,128)S(1)}, f32[512,128]{1,0:T(8,128)}, u32[]{:S(2)}) copy-start(f32[512,128]{1,0:T(8,128)} %get-tuple-element.131.cos_ref) | copy-start | bytes 786436
  462.9 13.8 %copy-start.4 = (f32[512,128]{1,0:T(8,128)S(1)}, f32[512,128]{1,0:T(8,128)}, u32[]{:S(2)}) copy-start(f32[512,128]{1,0:T(8,128)} %get-tuple-element.132.sin_ref) | copy-start | bytes 786436
  462.9 13.8 %copy-start.17 = (f32[2,4,2,64,256]{4,3,2,1,0:T(8,128)S(1)}, f32[2,4,2,64,256]{4,3,2,1,0:T(8,128)}, u32[]{:S(2)}) copy-start(f32[2,4,2,64,256]{4,3,2,1,0:T(8,128)} %copy-done.16) | copy-start | bytes 3145732
  462.9 13.8 %copy-start.22 = (f32[4,64,2048]{2,1,0:T(8,128)S(1)}, f32[4,64,2048]{2,1,0:T(8,128)}, u32[]{:S(2)}) copy-start(f32[4,64,2048]{2,1,0:T(8,128)} %get-tuple-element.77.middle_ref) | copy-start | bytes 6291460
  476.8 91.9 %copy-start.15 = (bf16[2,4,2,64,2048]{4,3,2,1,0:T(8,128)(2,1)S(1)}, bf16[2,4,2,64,2048]{4,3,2,1,0:T(8,128)(2,1)}, u32[]{:S(2)}) copy-start(bf16[2,4,2,64,2048]{4,3,2,1,0:T(8,128)(2,1)} %copy-done.14) | copy-start | bytes 12582916
  568.6 3.8 copy-start.18
  568.6 3.8 copy-start.19
  568.6 3.8 copy-start.23
  568.7 3.8 copy-start.27
  572.5 3.8 copy-start.26
  576.2 3.8 copy-start.25
  576.2 3.8 copy-start.34
Sparse Core Ops, SparseCore 0:
  98.9 79.7 all-gather.1
  337.5 276.7 all-reduce.2

commit v7 on v6

--- a/solution.py
+++ b/solution.py
@@ -495,22 +495,47 @@
 
 def front_kernel(
     pieces, count, head_dim,
-    tok_ref, gain_ref, cos_ref, sin_ref, qgain_ref, kgain_ref, wq_ref, wk_ref, wv_ref, wg_ref,
-    normed_ref, qraw_ref, q_ref, kraw_ref, kv_ref, gate_ref,
-    all_ref, *sems,
+    tok_ref, gain_ref, cos_ref, sin_ref, qgain_ref, kgain_ref, wq_hbm, wk_hbm, wv_hbm, wg_hbm,
+    normed_hbm, qraw_hbm, q_hbm, kraw_hbm, kv_hbm, gate_hbm,
+    all_ref, normed_ref, qraw_ref, q_ref, kraw_ref, kv_ref, gate_ref, store_sem,
+    wq_ref, wk_ref, wv_ref, wg_ref, load_sem, *sems,
 ):
     rows, model = tok_ref.shape[1], tok_ref.shape[2]
     tall = count * rows
     line = Line(pieces, count, None, None, None, None, sems, spread=lambda p, t: all_ref.at[p, t])
+    weights = ((wq_hbm, wq_ref), (wk_hbm, wk_ref), (wv_hbm, wv_ref), (wg_hbm, wg_ref))
+    loads = [pltpu.make_async_copy(*pair, load_sem.at[i]) for i, pair in enumerate(weights)]
+    for load in loads:
+        load.start()
     line.barrier()
     for p in range(pieces):
         all_ref[p, line.place] = tok_ref[p]
 
+    def stores(p):
+        pairs = (
+            (normed_ref, normed_hbm), (qraw_ref, qraw_hbm), (q_ref, q_hbm), (kraw_ref, kraw_hbm), (kv_ref, kv_hbm),
+            (gate_ref, gate_hbm),
+        )
+        return [
+            pltpu.make_async_copy(source, target.at[p // 2, :, p % 2], store_sem.at[i])
+            for i, (source, target) in enumerate(pairs)
+        ]
+
     def project(p):
-        b, half = p // 2, p % 2
+        half = p % 2
+
+        @pl.when(p == 0)
+        def _():
+            for load in loads:
+                load.wait()
+
+        @pl.when(p > 0)
+        def _():
+            for store in stores(p - 1):
+                store.wait()
 
         def keep(ref, value):
-            ref[b, :, half] = value.astype(ref.dtype).reshape(count, rows, value.shape[-1])
+            ref[...] = value.astype(ref.dtype).reshape(count, rows, value.shape[-1])
 
         x = all_ref[p].reshape(tall, model).astype(F32)
         normed = (x * inverse_rms(x) * gain_ref[...]).astype(LOW)
@@ -533,6 +558,8 @@
         keep(qraw_ref, raw)
         keep(q_ref, jnp.concatenate(turned(raw, qgain_ref[...]), axis=1))
         keep(gate_ref, mm(normed, wg_ref[...]))
+        for store in stores(p):
+            store.start()
 
     def turn_once(k, carry):
         both_ways(k, pieces, line.hand_out)
@@ -542,6 +569,8 @@
         return carry
 
     lax.fori_loop(0, pieces + 1, turn_once, 0)
+    for store in stores(pieces - 1):
+        store.wait()
     line.drain()
 
 
@@ -555,16 +584,19 @@
         return jax.ShapeDtypeStruct((batch, count, 2, rows, columns), kind)
 
     slots = (pieces, count)
+    kinds = [(model, LOW), (nq, F32), (nq, LOW), (nk, F32), (2 * nk, LOW), (nq, F32)]
     return pl.pallas_call(
         functools.partial(front_kernel, pieces, count, head_dim),
-        in_specs=[WHOLE] * 10,
-        out_specs=[WHOLE] * 6,
-        out_shape=[
-            wide(model, LOW), wide(nq, F32), wide(nq, LOW), wide(nk, F32), wide(2 * nk, LOW), wide(nq, F32)
-        ],
+        in_specs=[WHOLE] * 6 + [pl.BlockSpec(memory_space=pl.ANY)] * 4,
+        out_specs=[pl.BlockSpec(memory_space=pl.ANY)] * 6,
+        out_shape=[wide(*kind) for kind in kinds],
         scratch_shapes=[pltpu.VMEM((pieces, count, rows, model), LOW)]
+        + [pltpu.VMEM((count, rows, columns), kind) for columns, kind in kinds]
+        + [pltpu.SemaphoreType.DMA((6,))]
+        + [pltpu.VMEM(x.shape, LOW) for x in (wq, wk, wv, wg)]
+        + [pltpu.SemaphoreType.DMA((4,))]
         + [pltpu.SemaphoreType.DMA(slots)] * 3,
-        compiler_params=params(34, collective_id=2, has_side_effects=True),
+        compiler_params=params(58, collective_id=2, has_side_effects=True),
         cost_estimate=takes(95),
         name="front",
     )(
@@ -839,14 +871,14 @@
             pltpu.SemaphoreType.DMA((batch, steps, count)),
             pltpu.SemaphoreType.DMA((batch, count)),
         ],
-        compiler_params=params(4, collective_id=3, has_side_effects=True),
+        compiler_params=params(58, collective_id=3, has_side_effects=True),
         cost_estimate=takes(41),
         name="gather_blocks",
     )(own)
     return out.reshape(batch, count * rows, columns)
 
 
-def block_sums(count, batch, parts, finish, slots, send_sem, receive_sem, near):
+def block_sums(count, batch, parts, finish, slots, send_sem, receive_sem, kept_ref, kept_sem, near):
     place = lax.axis_index("seq")
     orders = [order[::-1] for order in digit_orders(count, batch)]
     steps = len(orders[0])
@@ -886,16 +918,30 @@
 
     started = []
 
+    def kept(b, turn):
+        mask = masks_at(b, 0)[turn]
+        return pltpu.make_async_copy(
+            parts(b).at[flipped(place, mask)], kept_ref.at[b, turn], kept_sem.at[b, turn]
+        )
+
     def begin():
         for turn in range(count // 2):
             for b in range(batch):
                 copy = transfer(b, 0, masks_at(b, 0)[turn])
                 copy.start()
                 started.append(copy)
+        for turn in range(count // 2):
+            for b in range(batch):
+                kept(b, turn).start()
 
     def take(b, step, mask):
         transfer(b, step, mask).wait_recv()
-        held = parts(b).at[flipped(place, mask)] if step == 0 else slot(b, step - 1, mask)
+        if step == 0:
+            turn = masks_at(b, 0).index(mask)
+            kept(b, turn).wait()
+            held = kept_ref.at[b, turn]
+        else:
+            held = slot(b, step - 1, mask)
         total = held[...].astype(F32) + slot(b, step, mask)[...].astype(F32)
         if step == steps - 1:
             finish(b, total)
@@ -972,7 +1018,7 @@
     def own(p):
         line.finish_own(p)
         x = middle_ref[p].astype(LOW).astype(F32)
-        residual = masked_ref[p] + norm_back(own_ref[p], x, gain_ref[...])
+        residual = masked_ref[p].astype(F32) + norm_back(own_ref[p], x, gain_ref[...])
         residual_ref[p] = residual
         r_ref[p // halves, line.place, p % halves] = residual.astype(LOW)
         line.hand_out(p)
@@ -1069,7 +1115,7 @@
     pieces, count, seq_count, batch, head_dim,
     parts_ref, hidden_hbm, wd_hbm, middle_ref, valid_ref, kraw_ref, cos_ref, sin_ref, kgain_ref,
     dkv_ref, output_ref, dkgain_ref,
-    wd_ref, hidden_ref, load_sem, hidden_sem, slots, send_sem, receive_sem,
+    wd_ref, hidden_ref, load_sem, hidden_sem, kept_ref, kept_sem, slots, send_sem, receive_sem,
     part_ref, own_ref, right_ref, left_ref, *sems,
 ):
     rows, model = own_ref.shape[1], own_ref.shape[2]
@@ -1097,7 +1143,7 @@
         dkv_ref[b, :, keys:] = total[:, keys:].astype(LOW)
 
     first, events, drain = block_sums(
-        seq_count, batch, lambda b: parts_ref.at[b], finish, slots, send_sem, receive_sem, 4.0
+        seq_count, batch, lambda b: parts_ref.at[b], finish, slots, send_sem, receive_sem, kept_ref, kept_sem, 4.0
     )
 
     def begin(p):
@@ -1141,7 +1187,7 @@
     any_place = pl.BlockSpec(memory_space=pl.ANY)
     return pl.pallas_call(
         functools.partial(scatter_kernel, pieces, count, seq_count, batch, head_dim),
-        in_specs=[WHOLE, any_place, any_place] + [WHOLE] * 6,
+        in_specs=[any_place] * 3 + [WHOLE] * 6,
         out_specs=[WHOLE] * 3,
         out_shape=[
             jax.ShapeDtypeStruct((batch, rows, columns), LOW),
@@ -1153,12 +1199,14 @@
             pltpu.VMEM((2, count, piece_rows, units), LOW),
             pltpu.SemaphoreType.DMA,
             pltpu.SemaphoreType.DMA((2,)),
+            pltpu.VMEM((batch, seq_count // 2, rows, columns), LOW),
+            pltpu.SemaphoreType.DMA((batch, seq_count // 2)),
             pltpu.VMEM((batch, seq_count - 1, rows, columns), LOW),
             pltpu.SemaphoreType.DMA((batch, seq_count - 1)),
             pltpu.SemaphoreType.DMA((batch, seq_count - 1)),
         ]
         + line_scratch(pieces, count, piece_rows, model, F32, False),
-        compiler_params=params(46, collective_id=4, has_side_effects=True),
+        compiler_params=params(58, collective_id=4, has_side_effects=True),
         cost_estimate=takes(10),
         name="scatter_blocks",
     )(
@@ -1168,12 +1216,13 @@
 
 def last_kernel(
     pieces, count, seq_count, streams, halves,
-    dq_ref, dkv_ref, dgate_ref, wq_ref, wk_ref, wv_ref, wg_ref, tok_ref, residual_ref, gain_ref,
-    dmid_ref, dqgain_ref, dkgain_ref, *refs,
+    dq_ref, dkv_ref, dgate_ref, gain_ref, dmid_ref, dqgain_ref, dkgain_ref,
+    wq_hbm, wk_hbm, wv_hbm, wg_hbm, tok_hbm, residual_hbm, *refs,
 ):
     grads, refs = refs[:streams], refs[streams:]
     input_ref, total_ref, sums = refs[0], refs[1], refs[2 : 2 + streams]
     (
+        wq_ref, wk_ref, wv_ref, wg_ref, tok_ref, residual_ref, load_sem, kept_ref, kept_sem,
         slots, scatter_send, scatter_receive, gather_send, gather_receive, mine_ref, mine_sem,
         dgain_ref, turns_ref, round_ref, mixed_ref, round_send, round_receive, mixed_send, mixed_receive,
         part_ref, own_ref, right_ref, left_ref, *sems,
@@ -1183,6 +1232,13 @@
     place_seq = lax.axis_index("seq")
     digits = digit_orders(seq_count, 1)[0]
     line = Line(pieces, count, part_ref, own_ref, right_ref, left_ref, sems)
+    pairs = (
+        (wq_hbm, wq_ref), (wg_hbm, wg_ref), (wk_hbm, wk_ref), (wv_hbm, wv_ref), (tok_hbm, tok_ref),
+        (residual_hbm, residual_ref),
+    )
+    loads = [pltpu.make_async_copy(*pair, load_sem.at[i]) for i, pair in enumerate(pairs)]
+    for load in loads:
+        load.start()
     line.barrier_all(digits)
     dgain_ref[...] = jnp.zeros_like(dgain_ref)
 
@@ -1199,10 +1255,13 @@
         keep(b).start()
 
     first, events, scatter_drain = block_sums(
-        seq_count, streams, lambda b: grads[b], finish, slots, scatter_send, scatter_receive, 1.0
+        seq_count, streams, lambda b: grads[b], finish, slots, scatter_send, scatter_receive, kept_ref, kept_sem, 1.0
     )
 
     def begin(p):
+        if p == 0:
+            for load in loads[:4]:
+                load.wait()
         b, half = p // halves, p % halves
         dq = dq_ref[b, :, half].reshape(tall, dq_ref.shape[-1])
         dkv = dkv_ref[b, :, half].reshape(tall, dkv_ref.shape[-1])
@@ -1214,6 +1273,9 @@
         line.keep_own(p)
 
     def own(p):
+        if p == 0:
+            for load in loads[4:]:
+                load.wait()
         line.finish_own(p)
         x = tok_ref[p].astype(F32)
         grad = own_ref[p]
@@ -1296,11 +1358,15 @@
     lines = 8 * ((2 * (model // count // 128) + 2 + 7) // 8)
     return pl.pallas_call(
         functools.partial(last_kernel, pieces, count, seq_count, streams, halves),
-        in_specs=[WHOLE] * (13 + streams),
+        in_specs=[WHOLE] * 7 + [pl.BlockSpec(memory_space=pl.ANY)] * (6 + streams),
         out_specs=[WHOLE] * 2 + [pl.BlockSpec(memory_space=pl.ANY)] * streams,
         out_shape=[jax.ShapeDtypeStruct((pieces, rows, model), F32), shape_of(lines, 128, F32)]
         + [jax.ShapeDtypeStruct((seq_count, block, columns), LOW)] * streams,
-        scratch_shapes=[
+        scratch_shapes=[pltpu.VMEM(x.shape, x.dtype) for x in (wq, wk, wv, wg, tok, residual)]
+        + [
+            pltpu.SemaphoreType.DMA((6,)),
+            pltpu.VMEM((streams, seq_count // 2, block, columns), LOW),
+            pltpu.SemaphoreType.DMA((streams, seq_count // 2)),
             pltpu.VMEM((streams, seq_count - 1, block, columns), LOW),
             pltpu.SemaphoreType.DMA((streams, seq_count - 1)),
             pltpu.SemaphoreType.DMA((streams, seq_count - 1)),
@@ -1322,7 +1388,7 @@
         cost_estimate=takes(5),
         name="last",
     )(
-        dq, dkv, dgate, wq, wk, wv, wg, tok, residual, gain, dmid, dqgain, dkgain,
+        dq, dkv, dgate, gain, dmid, dqgain, dkgain, wq, wk, wv, wg, tok, residual,
         *[grad.reshape(seq_count, block, columns) for grad in grads],
     )
 
@@ -1375,10 +1441,10 @@
 
 def turn_tables(positions, head_dim):
     half_dim = head_dim // 2
-    inverse = THETA ** (-(jnp.arange(half_dim, dtype=F32) * 2.0) / head_dim)
+    lane = jnp.arange(head_dim, dtype=jnp.int32)
+    inverse = THETA ** (-((lane % half_dim).astype(F32) * 2.0) / head_dim)
     angles = positions.astype(F32)[:, None] * inverse[None, :]
-    cosine, sine = jnp.cos(angles), jnp.sin(angles)
-    return jnp.concatenate([cosine, cosine], axis=1), jnp.concatenate([-sine, sine], axis=1)
+    return jnp.cos(angles), jnp.where(lane < half_dim, -1.0, 1.0)[None, :] * jnp.sin(angles)
 
 
 def norm_back(grad, values, gain):
@@ -1412,7 +1478,7 @@
 
     query_start = block_index * block_rows
     positions = query_start + jnp.arange(block_rows, dtype=jnp.int32)
-    cosine, sine = turn_tables(positions, head_dim)
+    cosine, sine = lax.optimization_barrier(turn_tables(positions, head_dim))
     gain_in, gain_mid = input_gain[None, :], middle_gain[None, :]
     gain_q, gain_k = query_gain[None, :], key_gain[None, :]
     local_pos = query_start + part_index * local_rows + jnp.arange(local_rows, dtype=jnp.int32)
@@ -1427,11 +1493,10 @@
             query_weight, key_weight, value_weight, gating_weight, parts,
         )
     ]
-    kv_own, masked_own = lax.optimization_barrier(
-        (kv_own, valid * jnp.transpose(cotangent, (1, 0, 2)).astype(F32))
-    )
+    masked_own = (valid * jnp.transpose(cotangent, (1, 0, 2)).astype(F32)).astype(LOW)
+    kv_own, masked_own = lax.optimization_barrier((kv_own, masked_own))
     kv = gather_blocks(kv_own)
-    masked = gather(masked_own.astype(LOW).reshape(batch * local_rows, model), "head")
+    masked = gather(masked_own.reshape(batch * local_rows, model), "head")
     att, acted, inv = attend(place, q, kv, gate, group, head_dim)
     middle, dgain_mid, normed_mid, hidden, dg, dl, dn_mid = middle_step(
         acted.reshape(batch, parts, halves, rows, nq), tok, gain_mid, output_weight,

time: 750 us -> 738 us (0.984)
  local copies, waits for them, and re-layouts: 17 us -> 6.73 us
    unnamed x74 -> x22, local copies, waits for them, and re-layouts: 11.7 us -> 0.66 us
where the time goes in v7:
time: 738 us; the launch traced here: 730 us
  Pallas kernels  627 us (85%)
  matrix products  45.6 us (6%)
  waiting for transfers between devices  29.5 us (4%)
  between operations  14.5 us (2%)
    pallas_call x1, Pallas kernels, middle_step(): pl.pallas_call(functools.partial(middle_kernel, pieces, count), in_specs=...  129 us
    pallas_call x1, Pallas kernels, residual_step(): pl.pallas_call(functools.partial(residual_kernel, pieces, count, halves,...  123 us
    pallas_call x1, Pallas kernels, last_step(): pl.pallas_call(functools.partial(last_kernel, pieces, count, seq_count, s...  115 us
    pallas_call x1, Pallas kernels, scatter_blocks(): pl.pallas_call(functools.partial(scatter_kernel, pieces, count, seq_count...  87.3 us
    pallas_call x1, Pallas kernels, front_step(): pl.pallas_call(functools.partial(front_kernel, pieces, count, head_dim),...  78.8 us
    dot_general x7, matrix products, t_mm(): lax.dot_general(left, right, (((0,), (0,)), ((), ())), preferred_element_...  45.6 us
    pallas_call x1, Pallas kernels, gather_blocks(): pl.pallas_call(functools.partial(gather_kernel, count, batch), in_specs=[...  41.5 us
    pallas_call x1, Pallas kernels, widen(): pl.pallas_call(widen_kernel, grid=(steps,), in_specs=[pl.BlockSpec((batch...  29.9 us
  transfers between devices with their start and end apart: 2, of which 1 were waited for; matrix products, arithmetic and copies ran while one was open for 3% of the time, Pallas kernels for 53%

profile of v7, /device:TPU:0, one launch (start us, length us, event | category | flops | bytes accessed | tf_op | source)
XLA Modules:
  0.0 729.8 jit_solution(3867541039913872945)
XLA Ops:
  7.2 0.0 all-gather.2.cloned.1.call-start
  7.3 1.8 fusion.1
  9.1 2.5 copy.37
  11.7 0.7 compare_convert_fusion.1
  12.4 2.7 fusion
  15.1 78.8 %front.1 = (bf16[2,4,2,64,2048]{4,3,2,1,0:T(8,128)(2,1)}, f32[2,4,2,64,512]{4,3,2,1,0:T(8,128)}, bf16[2,4,2,64,512]{4,3,2,1,0:T(8,128)(2,1)}, f32[2,4,2,64,256]{...) custom-call(bf16[4,64,2048]{2,1,0:T(8,128)(2,1)} %bitcast.99, ...), custom_call_target="tpu_custom_call" | custom-call | flops 109250002944 | bytes 350550016 | tf_op jit(solution)/shard_map/front/pallas_call | solution.py:588
  93.9 0.0 all-gather.2.cloned.1.call-update
  93.9 0.0 all-reduce.3.cloned.1.call-start
  94.0 0.0 copy-done.3
  94.0 0.6 pad_add_fusion.place_ref
  94.6 41.5 %gather_blocks.1 = bf16[2,8,512,512]{3,2,1,0:T(8,128)(2,1)} custom-call(bf16[2,512,512]{2,1,0:T(8,128)(2,1)} %bitcast.132), custom_call_target="tpu_custom_call" | custom-call | flops 47149998080 | bytes 151290000 | tf_op jit(solution)/shard_map/gather_blocks/pallas_call | solution.py:864
  136.1 8.3 %attend.1 = (f32[2,512,512]{2,1,0:T(8,128)}, bf16[2,512,512]{2,1,0:T(8,128)(2,1)}, f32[2,512,128]{2,1,0:T(8,128)}) custom-call(s32[3]{0:T(128)} %pad_add_fusion.place_ref, bf16[2,512,512]{2,1,0:T(8,128)(2,1)} %bitcast.91, bf16[2,4096,512]{2,1,0:T(8,128)(2,1)} %bitcast.76, f32[2,512,512]{2,1,0:T(8,128)} %bitcast.86), custom_call_target="tpu_custom_call" | custom-call | flops 20700000256 | bytes 66420000 | tf_op jit(solution)/shard_map/attend/pallas_call | solution.py:144
  144.4 29.5 %all-gather.2.cloned.1.call-done = bf16[1024,2048]{1,0:T(8,128)(2,1)} async-done(((bf16[256,2048]{1,0:T(8,128)(2,1)}), bf16[1024,2048]{1,0:T(8,128)(2,1)}) %all-gather.2.cloned.1.call-update) | async-done | bytes 4194320 | tf_op jit(solution)/shard_map/all_gather | solution.py:1458
  173.8 129.3 %middle.1 = (f32[4,64,2048]{2,1,0:T(8,128)}, f32[1,2048]{1,0:T(1,128)}, bf16[4,4,64,2048]{3,2,1,0:T(8,128)(2,1)}, bf16[4,4,64,1536]{3,2,1,0:T(8,128)(2,1)}, bf16...) custom-call(bf16[2,4,2,64,512]{4,3,2,1,0:T(8,128)(2,1)} %bitcast.127, ...), custom_call_target="tpu_custom_call" | custom-call | flops 147200000000 | bytes 472320000 | tf_op jit(solution)/shard_map/middle/pallas_call | solution.py:742
  303.2 0.0 copy-start.9
  303.2 0.0 copy-start.10
  303.2 11.8 %bitcast_convert_fusion.1 = bf16[2048,1536]{1,0:T(8,128)(2,1)} fusion(bf16[4,4,64,2048]{3,2,1,0:T(8,128)(2,1)} %get-tuple-element.76, bf16[4,4,64,1536]{3,2,1,0:T(8,128)(2,1)} %get-tuple-element.77), kind=kOutput, calls=%fused_computation.1 | convolution fusion | flops 6445596672 | bytes 13631488 | tf_op jit(solution)/shard_map/dot_general | solution.py:28
  315.0 0.0 copy-done.9
  315.0 0.0 copy-done.10
  315.0 0.0 copy-start.7
  315.0 8.8 %bitcast_convert_fusion = bf16[2048,1536]{1,0:T(8,128)(2,1)} fusion(bf16[4,4,64,2048]{3,2,1,0:T(8,128)(2,1)S(1)} %copy-done.9, bf16[4,4,64,1536]{3,2,1,0:T(8,128)(2,1)S(1)} %copy-done.10), kind=kOutput, calls=%fused_computation | convolution fusion | flops 6445596672 | bytes 13631488 | tf_op jit(solution)/shard_map/dot_general | solution.py:28
  323.8 0.0 copy-done.5
  323.8 0.0 copy-done.7
  323.8 8.8 %convolution_convert_fusion = bf16[1536,2048]{1,0:T(8,128)(2,1)} fusion(bf16[1024,1536]{1,0:T(8,128)(2,1)S(1)} %bitcast.116, bf16[1024,2048]{1,0:T(8,128)(2,1)S(1)} %copy-done.5), kind=kOutput, calls=%fused_computation.2 | convolution fusion | flops 6445596672 | bytes 13631488 | tf_op jit(solution)/shard_map/dot_general | solution.py:28
  332.6 0.0 all-reduce.3.cloned.1.call-update
  332.6 0.6 copy-done.4
  333.2 0.1 lt.61
  333.3 0.1 lt.62
  333.4 0.1 copy.39
  333.5 0.7 compare_convert_fusion.valid_ref
  334.2 122.7 %residual.1 = (f32[4,64,2048]{2,1,0:T(8,128)}, bf16[2,4,2,64,2048]{4,3,2,1,0:T(8,128)(2,1)}, f32[1,128]{1,0:T(1,128)}, bf16[2,512,512]{2,1,0:T(8,128)(2,1)}, bf1...) custom-call(s32[3]{0:T(128)} %pad_add_fusion.place_ref, bf16[4,4,64,2048]{3,2,1,0:T(8,128)(2,1)} %get-tuple-element.80.dn_ref, ...), custom_call_target="tpu_custom_call" | custom-call | flops 11500000256 | bytes 36900000 | tf_op jit(solution)/shard_map/residual/pallas_call | solution.py:1087
  457.0 14.0 %attend_back.1 = (bf16[2,512,512]{2,1,0:T(8,128)(2,1)}, bf16[2,4096,512]{2,1,0:T(8,128)(2,1)}, bf16[2,512,512]{2,1,0:T(8,128)(2,1)}, f32[1,128]{1,0:T(1,128)}) custom-call(s32[3]{0:T(128)} %pad_add_fusion.place_ref, bf16[2,512,512]{2,1,0:T(8,128)(2,1)} %bitcast.93, ...), custom_call_target="tpu_custom_call", output_to_operand_aliasing={{0}: (13, {}), {1}: (14, {}), {2}: (15, {})} | custom-call | flops 3449999872 | bytes 11070000 | tf_op jit(solution)/shard_map/attend_back/pallas_call | solution.py:312
  471.0 87.3 %scatter_blocks.1 = (bf16[2,512,512]{2,1,0:T(8,128)(2,1)}, bf16[4,64,2048]{2,1,0:T(8,128)(2,1)}, f32[1,128]{1,0:T(1,128)}) custom-call(bf16[2,8,512,512]{3,2,1,0:T(8,128)(2,1)} %bitcast.79, bf16[4,4,64,1536]{3,2,1,0:T(8,128)(2,1)} %get-tuple-element.79.hidden_hbm, bf16[1536,2048]{1,0:T(8,128)(2,1)} %wd_hbm.3, f32[4,64,2048]{2,1,0:T(8,128)} %get-tuple-element.81.middle_ref, ...), custom_call_target="tpu_custom_call" | custom-call | flops 11500000256 | bytes 36900000 | tf_op jit(solution)/shard_map/scatter_blocks/pallas_call | solution.py:1188
  558.3 0.0 copy-done.6
  558.3 0.0 copy-start.2
  558.3 5.0 convolution_convert_fusion.3
  563.3 0.0 copy-done.2
  563.3 3.7 convolution_convert_fusion.2
  567.0 0.0 copy-done.1
  567.0 3.7 convolution_convert_fusion.4
  570.8 0.0 copy-done
  570.8 3.8 convolution_convert_fusion.1
  574.5 115.0 %last.1 = (f32[4,64,2048]{2,1,0:T(8,128)}, f32[16,128]{1,0:T(8,128)}, bf16[8,256,512]{2,1,0:T(8,128)(2,1)}, bf16[8,256,512]{2,1,0:T(8,128)(2,1)}, bf16[8,256,512...) custom-call(bf16[2,4,2,64,512]{4,3,2,1,0:T(8,128)(2,1)} %bitcast.94, bf16[2,4,2,64,512]{4,3,2,1,0:T(8,128)(2,1)} %bitcast.131, ...), custom_call_target="tpu_custom_call" | custom-call | flops 5750000128 | bytes 18450000 | tf_op jit(solution)/shard_map/last/pallas_call | solution.py:1359
  689.6 0.8 fusion.7
  690.3 0.6 dynamic-slice_bitcast_fusion
  690.9 0.6 dynamic-slice_bitcast_fusion.1
  691.5 1.3 slice_bitcast_fusion
  692.8 29.9 %widen.1 = (f32[128,2,2048]{2,1,0:T(2,128)}, bf16[128,2,2048]{2,1,0:T(2,128)(2,1)}, f32[2048,512]{1,0:T(8,128)}, f32[2048,256]{1,0:T(8,128)}, f32[2048,256]{1,0:...) custom-call(f32[2,128,2048]{2,1,0:T(8,128)} %bitcast.117, ...), custom_call_target="tpu_custom_call" | custom-call | flops 28750000128 | bytes 92250000 | tf_op jit(solution)/shard_map/widen/pallas_call | solution.py:1429
  (14 shorter events, 0.0 us)
Async XLA Ops:
  7.2 166.7 %all-gather.2.cloned.1.call-start = ((), (), s32[]{:S(2)}) async-start(), calls=%async_computation | async-start | bytes 5242880 | tf_op jit(solution)/shard_map/all_gather | solution.py:1458
  15.1 78.9 %copy-start.3 = (s32[2]{0:T(128)S(1)}, s32[2]{0:T(128)}, u32[]{:S(2)}) copy-start(s32[2]{0:T(128)} %param.17) | copy-start | bytes 28
  93.9 598.9 %all-reduce.3.cloned.1.call-start = ((), (), s32[]{:S(2)}) async-start(), calls=%async_computation.1 | async-start | bytes 37748736 | tf_op jit(solution)/shard_map/psum | solution.py:1516
  303.2 11.8 %copy-start.9 = (bf16[4,4,64,2048]{3,2,1,0:T(8,128)(2,1)S(1)}, bf16[4,4,64,2048]{3,2,1,0:T(8,128)(2,1)}, u32[]{:S(2)}) copy-start(bf16[4,4,64,2048]{3,2,1,0:T(8,128)(2,1)} %get-tuple-element.76) | copy-start | bytes 12582916
  303.2 11.8 %copy-start.10 = (bf16[4,4,64,1536]{3,2,1,0:T(8,128)(2,1)S(1)}, bf16[4,4,64,1536]{3,2,1,0:T(8,128)(2,1)}, u32[]{:S(2)}) copy-start(bf16[4,4,64,1536]{3,2,1,0:T(8,128)(2,1)} %get-tuple-element.78) | copy-start | bytes 9437188
  315.0 8.8 %copy-start.5 = (bf16[1024,2048]{1,0:T(8,128)(2,1)S(1)}, bf16[1024,2048]{1,0:T(8,128)(2,1)}, u32[]{:S(2)}) copy-start(bf16[1024,2048]{1,0:T(8,128)(2,1)} %all-gather.2.cloned.1.call-done) | copy-start | bytes 12582916
  315.0 8.8 %copy-start.7 = (bf16[4,4,64,1536]{3,2,1,0:T(8,128)(2,1)S(1)}, bf16[4,4,64,1536]{3,2,1,0:T(8,128)(2,1)}, u32[]{:S(2)}) copy-start(bf16[4,4,64,1536]{3,2,1,0:T(8,128)(2,1)} %get-tuple-element.79.hidden_hbm) | copy-start | bytes 9437188
  332.6 0.7 copy-start.4
  471.0 87.3 %copy-start.6 = (bf16[2,4,2,64,2048]{4,3,2,1,0:T(8,128)(2,1)S(1)}, bf16[2,4,2,64,2048]{4,3,2,1,0:T(8,128)(2,1)}, u32[]{:S(2)}) copy-start(bf16[2,4,2,64,2048]{4,3,2,1,0:T(8,128)(2,1)} %get-tuple-element.99) | copy-start | bytes 12582916
  558.3 5.0 copy-start.2
  563.3 3.7 copy-start.1
  567.0 3.7 copy-start
  567.0 3.7 copy-start.8
Sparse Core Ops, SparseCore 0:
  94.1 79.7 all-gather.1
  332.7 275.9 all-reduce.2

commit v8 on v7

--- a/solution.py
+++ b/solution.py
@@ -978,11 +978,12 @@
 
 def residual_kernel(
     pieces, count, halves, group, seq_count,
-    place_ref, dn_ref, middle_ref, masked_ref, gain_ref, wo_ref, cos_ref, sin_ref, qgain_ref,
-    q_hbm, kv_hbm, att_hbm, gate_hbm, inv_hbm, qraw_hbm,
+    place_ref, masked_ref, gain_ref, cos_ref, sin_ref, qgain_ref,
+    dn_hbm, middle_hbm, wo_hbm, q_hbm, kv_hbm, att_hbm, gate_hbm, inv_hbm, qraw_hbm,
     residual_ref, r_ref, dqgain_ref, dq_hbm, dkv_hbm, dgate_hbm,
     q_ref, kv_ref, att_ref, gate_ref, inv_ref, qraw_ref, dq_ref, dkv_ref, dgate_ref,
     scaled_ref, corr_ref, acc_ref, load_sem, store_sem, block_sem,
+    dn_ref, middle_ref, wo_ref, dn_sem, middle_sem, wo_sem,
     part_ref, own_ref, right_ref, left_ref, *sems,
 ):
     rows, model = own_ref.shape[1], own_ref.shape[2]
@@ -1002,6 +1003,11 @@
         pltpu.make_async_copy(dq_ref, dq_hbm.at[0], store_sem.at[0]),
         pltpu.make_async_copy(dgate_ref, dgate_hbm.at[0], store_sem.at[1]),
     ]
+    dn_loads = [pltpu.make_async_copy(dn_hbm.at[:, p], dn_ref.at[:, p], dn_sem.at[p]) for p in range(pieces)]
+    middle_load = pltpu.make_async_copy(middle_hbm, middle_ref, middle_sem)
+    loads.append(pltpu.make_async_copy(wo_hbm, wo_ref, wo_sem))
+    for load in dn_loads + [middle_load]:
+        load.start()
     line.barrier()
     for load in loads:
         load.start()
@@ -1012,10 +1018,13 @@
     )
 
     def begin(p):
+        dn_loads[p].wait()
         part_ref[...] = dn_ref[:, p]
         line.keep_own(p)
 
     def own(p):
+        if p == 0:
+            middle_load.wait()
         line.finish_own(p)
         x = middle_ref[p].astype(LOW).astype(F32)
         residual = masked_ref[p].astype(F32) + norm_back(own_ref[p], x, gain_ref[...])
@@ -1086,7 +1095,7 @@
     held = (q, kv, att, gate, inv, qraw)
     return pl.pallas_call(
         functools.partial(residual_kernel, pieces, count, halves, group, seq_count),
-        in_specs=[SCALARS] + [WHOLE] * 8 + [any_place] * 6,
+        in_specs=[SCALARS] + [WHOLE] * 5 + [any_place] * 9,
         out_specs=[WHOLE] * 3 + [any_place] * 3,
         out_shape=[
             jax.ShapeDtypeStruct((pieces, rows, model), F32),
@@ -1104,18 +1113,20 @@
             pltpu.SemaphoreType.DMA((2,)),
             pltpu.SemaphoreType.DMA((seq_count,)),
         ]
+        + [pltpu.VMEM(x.shape, x.dtype) for x in (dn, middle, wo)]
+        + [pltpu.SemaphoreType.DMA((pieces,)), pltpu.SemaphoreType.DMA, pltpu.SemaphoreType.DMA]
         + line_scratch(pieces, count, rows, model, LOW, True),
         compiler_params=params(60, collective_id=1, has_side_effects=True),
         cost_estimate=takes(10),
         name="residual",
-    )(place, dn, middle, masked, gain, wo, cosine, sine, qgain, *held)
+    )(place, masked, gain, cosine, sine, qgain, dn, middle, wo, *held)
 
 
 def scatter_kernel(
     pieces, count, seq_count, batch, head_dim,
-    parts_ref, hidden_hbm, wd_hbm, middle_ref, valid_ref, kraw_ref, cos_ref, sin_ref, kgain_ref,
+    parts_ref, hidden_hbm, wd_hbm, middle_hbm, valid_ref, kraw_ref, cos_ref, sin_ref, kgain_ref,
     dkv_ref, output_ref, dkgain_ref,
-    wd_ref, hidden_ref, load_sem, hidden_sem, kept_ref, kept_sem, slots, send_sem, receive_sem,
+    wd_ref, middle_ref, hidden_ref, load_sem, middle_sem, hidden_sem, kept_ref, kept_sem, slots, send_sem, receive_sem,
     part_ref, own_ref, right_ref, left_ref, *sems,
 ):
     rows, model = own_ref.shape[1], own_ref.shape[2]
@@ -1127,8 +1138,10 @@
     def hidden_copy(p):
         return pltpu.make_async_copy(hidden_hbm.at[:, p], hidden_ref.at[p % 2], hidden_sem.at[p % 2])
 
+    middle_load = pltpu.make_async_copy(middle_hbm, middle_ref, middle_sem)
     load.start()
     hidden_copy(0).start()
+    middle_load.start()
     dkgain_ref[...] = jnp.zeros_like(dkgain_ref)
     line.barrier(digit_orders(seq_count, 1)[0])
 
@@ -1157,6 +1170,8 @@
         line.keep_own(p)
 
     def own(p):
+        if p == 0:
+            middle_load.wait()
         line.finish_own(p)
         output_ref[p] = (valid_ref[p] * (middle_ref[p] + own_ref[p])).astype(LOW)
 
@@ -1187,7 +1202,7 @@
     any_place = pl.BlockSpec(memory_space=pl.ANY)
     return pl.pallas_call(
         functools.partial(scatter_kernel, pieces, count, seq_count, batch, head_dim),
-        in_specs=[any_place] * 3 + [WHOLE] * 6,
+        in_specs=[any_place] * 4 + [WHOLE] * 5,
         out_specs=[WHOLE] * 3,
         out_shape=[
             jax.ShapeDtypeStruct((batch, rows, columns), LOW),
@@ -1196,7 +1211,9 @@
         ],
         scratch_shapes=[
             pltpu.VMEM(wd.shape, LOW),
+            pltpu.VMEM(middle.shape, F32),
             pltpu.VMEM((2, count, piece_rows, units), LOW),
+            pltpu.SemaphoreType.DMA,
             pltpu.SemaphoreType.DMA,
             pltpu.SemaphoreType.DMA((2,)),
             pltpu.VMEM((batch, seq_count // 2, rows, columns), LOW),
@@ -1408,7 +1425,7 @@
         out[...] = ref[...].astype(F32)
 
 
-def widen(input_grad, output, dq, dkv, dgate, out, ff, steps=8):
+def widen(input_grad, output, dq, dkv, dgate, out, ff, steps=4):
     batch, rows, model = input_grad.shape
     columns, keys = dq.shape[1], dkv.shape[1] // 2
 

time: 738 us -> 739 us (level)
  no operation moved by 1% of the time
where the time goes in v8:
time: 739 us; the launch traced here: 728 us
  Pallas kernels  624 us (84%)
  matrix products  46 us (6%)
  waiting for transfers between devices  29.5 us (4%)
  between operations  14.5 us (2%)
    pallas_call x1, Pallas kernels, middle_step(): pl.pallas_call(functools.partial(middle_kernel, pieces, count), in_specs=...  129 us
    pallas_call x1, Pallas kernels, residual_step(): pl.pallas_call(functools.partial(residual_kernel, pieces, count, halves,...  120 us
    pallas_call x1, Pallas kernels, last_step(): pl.pallas_call(functools.partial(last_kernel, pieces, count, seq_count, s...  116 us
    pallas_call x1, Pallas kernels, scatter_blocks(): pl.pallas_call(functools.partial(scatter_kernel, pieces, count, seq_count...  88.5 us
    pallas_call x1, Pallas kernels, front_step(): pl.pallas_call(functools.partial(front_kernel, pieces, count, head_dim),...  78.8 us
    dot_general x7, matrix products, t_mm(): lax.dot_general(left, right, (((0,), (0,)), ((), ())), preferred_element_...  46 us
    pallas_call x1, Pallas kernels, gather_blocks(): pl.pallas_call(functools.partial(gather_kernel, count, batch), in_specs=[...  41.5 us
    all_gather x1, waiting for transfers between devices, gather(): return lax.all_gather(value, axis, axis=0, tiled=True)  29.5 us
  transfers between devices with their start and end apart: 2, of which 1 were waited for; matrix products, arithmetic and copies ran while one was open for 3% of the time, Pallas kernels for 53%

profile of v8, /device:TPU:0, one launch (start us, length us, event | category | flops | bytes accessed | tf_op | source)
XLA Modules:
  0.0 727.9 jit_solution(5634065613482225870)
XLA Ops:
  7.2 0.0 all-gather.2.cloned.1.call-start
  7.3 1.8 fusion.1
  9.1 2.5 copy.37
  11.7 0.7 compare_convert_fusion.1
  12.4 2.7 fusion
  15.1 78.8 %front.1 = (bf16[2,4,2,64,2048]{4,3,2,1,0:T(8,128)(2,1)}, f32[2,4,2,64,512]{4,3,2,1,0:T(8,128)}, bf16[2,4,2,64,512]{4,3,2,1,0:T(8,128)(2,1)}, f32[2,4,2,64,256]{...) custom-call(bf16[4,64,2048]{2,1,0:T(8,128)(2,1)} %bitcast.99, ...), custom_call_target="tpu_custom_call" | custom-call | flops 109250002944 | bytes 350550016 | tf_op jit(solution)/shard_map/front/pallas_call | solution.py:588
  93.9 0.0 all-gather.2.cloned.1.call-update
  93.9 0.0 all-reduce.3.cloned.1.call-start
  94.0 0.0 copy-done.3
  94.0 0.6 pad_add_fusion.place_ref
  94.6 41.5 %gather_blocks.1 = bf16[2,8,512,512]{3,2,1,0:T(8,128)(2,1)} custom-call(bf16[2,512,512]{2,1,0:T(8,128)(2,1)} %bitcast.132), custom_call_target="tpu_custom_call" | custom-call | flops 47149998080 | bytes 151290000 | tf_op jit(solution)/shard_map/gather_blocks/pallas_call | solution.py:864
  136.1 8.3 %attend.1 = (f32[2,512,512]{2,1,0:T(8,128)}, bf16[2,512,512]{2,1,0:T(8,128)(2,1)}, f32[2,512,128]{2,1,0:T(8,128)}) custom-call(s32[3]{0:T(128)} %pad_add_fusion.place_ref, bf16[2,512,512]{2,1,0:T(8,128)(2,1)} %bitcast.91, bf16[2,4096,512]{2,1,0:T(8,128)(2,1)} %bitcast.76, f32[2,512,512]{2,1,0:T(8,128)} %bitcast.86), custom_call_target="tpu_custom_call" | custom-call | flops 20700000256 | bytes 66420000 | tf_op jit(solution)/shard_map/attend/pallas_call | solution.py:144
  144.4 29.5 %all-gather.2.cloned.1.call-done = bf16[1024,2048]{1,0:T(8,128)(2,1)} async-done(((bf16[256,2048]{1,0:T(8,128)(2,1)}), bf16[1024,2048]{1,0:T(8,128)(2,1)}) %all-gather.2.cloned.1.call-update) | async-done | bytes 4194320 | tf_op jit(solution)/shard_map/all_gather | solution.py:1475
  173.8 129.1 %middle.1 = (f32[4,64,2048]{2,1,0:T(8,128)}, f32[1,2048]{1,0:T(1,128)}, bf16[4,4,64,2048]{3,2,1,0:T(8,128)(2,1)}, bf16[4,4,64,1536]{3,2,1,0:T(8,128)(2,1)}, bf16...) custom-call(bf16[2,4,2,64,512]{4,3,2,1,0:T(8,128)(2,1)} %bitcast.127, ...), custom_call_target="tpu_custom_call" | custom-call | flops 147200000000 | bytes 472320000 | tf_op jit(solution)/shard_map/middle/pallas_call | solution.py:742
  303.0 0.0 copy-start.9
  303.0 0.0 copy-start.10
  303.0 12.2 %bitcast_convert_fusion.1 = bf16[2048,1536]{1,0:T(8,128)(2,1)} fusion(bf16[4,4,64,2048]{3,2,1,0:T(8,128)(2,1)} %get-tuple-element.76, bf16[4,4,64,1536]{3,2,1,0:T(8,128)(2,1)} %get-tuple-element.77), kind=kOutput, calls=%fused_computation.1 | convolution fusion | flops 6445596672 | bytes 13631488 | tf_op jit(solution)/shard_map/dot_general | solution.py:28
  315.2 0.0 copy-done.9
  315.2 0.0 copy-done.10
  315.2 0.0 copy-start.7
  315.2 8.8 %bitcast_convert_fusion = bf16[2048,1536]{1,0:T(8,128)(2,1)} fusion(bf16[4,4,64,2048]{3,2,1,0:T(8,128)(2,1)S(1)} %copy-done.9, bf16[4,4,64,1536]{3,2,1,0:T(8,128)(2,1)S(1)} %copy-done.10), kind=kOutput, calls=%fused_computation | convolution fusion | flops 6445596672 | bytes 13631488 | tf_op jit(solution)/shard_map/dot_general | solution.py:28
  324.1 0.0 copy-done.5
  324.1 0.0 copy-done.7
  324.1 8.8 %convolution_convert_fusion = bf16[1536,2048]{1,0:T(8,128)(2,1)} fusion(bf16[1024,1536]{1,0:T(8,128)(2,1)S(1)} %bitcast.116, bf16[1024,2048]{1,0:T(8,128)(2,1)S(1)} %copy-done.5), kind=kOutput, calls=%fused_computation.2 | convolution fusion | flops 6445596672 | bytes 13631488 | tf_op jit(solution)/shard_map/dot_general | solution.py:28
  332.8 0.0 all-reduce.3.cloned.1.call-update
  332.9 0.6 copy-done.4
  333.5 0.1 lt.61
  333.6 0.1 lt.62
  333.6 0.1 copy.39
  333.8 0.7 compare_convert_fusion.valid_ref
  334.5 120.0 %residual.1 = (f32[4,64,2048]{2,1,0:T(8,128)}, bf16[2,4,2,64,2048]{4,3,2,1,0:T(8,128)(2,1)}, f32[1,128]{1,0:T(1,128)}, bf16[2,512,512]{2,1,0:T(8,128)(2,1)}, bf1...) custom-call(s32[3]{0:T(128)} %pad_add_fusion.place_ref, bf16[4,64,2048]{2,1,0:T(8,128)(2,1)} %bitcast.81, ...), custom_call_target="tpu_custom_call" | custom-call | flops 11500000256 | bytes 36900000 | tf_op jit(solution)/shard_map/residual/pallas_call | solution.py:1096
  454.5 14.4 %attend_back.1 = (bf16[2,512,512]{2,1,0:T(8,128)(2,1)}, bf16[2,4096,512]{2,1,0:T(8,128)(2,1)}, bf16[2,512,512]{2,1,0:T(8,128)(2,1)}, f32[1,128]{1,0:T(1,128)}) custom-call(s32[3]{0:T(128)} %pad_add_fusion.place_ref, bf16[2,512,512]{2,1,0:T(8,128)(2,1)} %bitcast.93, ...), custom_call_target="tpu_custom_call", output_to_operand_aliasing={{0}: (13, {}), {1}: (14, {}), {2}: (15, {})} | custom-call | flops 3449999872 | bytes 11070000 | tf_op jit(solution)/shard_map/attend_back/pallas_call | solution.py:312
  468.9 88.5 %scatter_blocks.1 = (bf16[2,512,512]{2,1,0:T(8,128)(2,1)}, bf16[4,64,2048]{2,1,0:T(8,128)(2,1)}, f32[1,128]{1,0:T(1,128)}) custom-call(bf16[2,8,512,512]{3,2,1,0:T(8,128)(2,1)} %bitcast.79, bf16[4,4,64,1536]{3,2,1,0:T(8,128)(2,1)} %get-tuple-element.79.hidden_hbm, bf16[1536,2048]{1,0:T(8,128)(2,1)} %wd_hbm.3, f32[4,64,2048]{2,1,0:T(8,128)} %get-tuple-element.81.middle_hbm, ...), custom_call_target="tpu_custom_call" | custom-call | flops 11500000256 | bytes 36900000 | tf_op jit(solution)/shard_map/scatter_blocks/pallas_call | solution.py:1203
  557.4 0.0 copy-done.6
  557.4 0.0 copy-start.2
  557.4 5.0 convolution_convert_fusion.3
  562.5 0.0 copy-done.2
  562.5 3.7 convolution_convert_fusion.2
  566.2 0.0 copy-done.1
  566.2 3.7 convolution_convert_fusion.4
  569.9 0.0 copy-done
  569.9 3.8 convolution_convert_fusion.1
  573.7 116.4 %last.1 = (f32[4,64,2048]{2,1,0:T(8,128)}, f32[16,128]{1,0:T(8,128)}, bf16[8,256,512]{2,1,0:T(8,128)(2,1)}, bf16[8,256,512]{2,1,0:T(8,128)(2,1)}, bf16[8,256,512...) custom-call(bf16[2,4,2,64,512]{4,3,2,1,0:T(8,128)(2,1)} %bitcast.94, bf16[2,4,2,64,512]{4,3,2,1,0:T(8,128)(2,1)} %bitcast.131, ...), custom_call_target="tpu_custom_call" | custom-call | flops 5750000128 | bytes 18450000 | tf_op jit(solution)/shard_map/last/pallas_call | solution.py:1376
  690.1 0.8 fusion.7
  690.9 0.6 dynamic-slice_bitcast_fusion
  691.5 0.6 dynamic-slice_bitcast_fusion.1
  692.1 1.3 slice_bitcast_fusion
  693.4 27.4 %widen.1 = (f32[128,2,2048]{2,1,0:T(2,128)}, bf16[128,2,2048]{2,1,0:T(2,128)(2,1)}, f32[2048,512]{1,0:T(8,128)}, f32[2048,256]{1,0:T(8,128)}, f32[2048,256]{1,0:...) custom-call(f32[2,128,2048]{2,1,0:T(8,128)} %bitcast.117, ...), custom_call_target="tpu_custom_call" | custom-call | flops 28750000128 | bytes 92250000 | tf_op jit(solution)/shard_map/widen/pallas_call | solution.py:1446
  (14 shorter events, 0.0 us)
Async XLA Ops:
  7.2 166.7 %all-gather.2.cloned.1.call-start = ((), (), s32[]{:S(2)}) async-start(), calls=%async_computation | async-start | bytes 5242880 | tf_op jit(solution)/shard_map/all_gather | solution.py:1475
  15.1 78.9 %copy-start.3 = (s32[2]{0:T(128)S(1)}, s32[2]{0:T(128)}, u32[]{:S(2)}) copy-start(s32[2]{0:T(128)} %param.17) | copy-start | bytes 28
  93.9 599.5 %all-reduce.3.cloned.1.call-start = ((), (), s32[]{:S(2)}) async-start(), calls=%async_computation.1 | async-start | bytes 37748736 | tf_op jit(solution)/shard_map/psum | solution.py:1533
  303.0 12.2 %copy-start.9 = (bf16[4,4,64,2048]{3,2,1,0:T(8,128)(2,1)S(1)}, bf16[4,4,64,2048]{3,2,1,0:T(8,128)(2,1)}, u32[]{:S(2)}) copy-start(bf16[4,4,64,2048]{3,2,1,0:T(8,128)(2,1)} %get-tuple-element.76) | copy-start | bytes 12582916
  303.0 12.2 %copy-start.10 = (bf16[4,4,64,1536]{3,2,1,0:T(8,128)(2,1)S(1)}, bf16[4,4,64,1536]{3,2,1,0:T(8,128)(2,1)}, u32[]{:S(2)}) copy-start(bf16[4,4,64,1536]{3,2,1,0:T(8,128)(2,1)} %get-tuple-element.78) | copy-start | bytes 9437188
  315.2 8.8 %copy-start.5 = (bf16[1024,2048]{1,0:T(8,128)(2,1)S(1)}, bf16[1024,2048]{1,0:T(8,128)(2,1)}, u32[]{:S(2)}) copy-start(bf16[1024,2048]{1,0:T(8,128)(2,1)} %all-gather.2.cloned.1.call-done) | copy-start | bytes 12582916
  315.2 8.8 %copy-start.7 = (bf16[4,4,64,1536]{3,2,1,0:T(8,128)(2,1)S(1)}, bf16[4,4,64,1536]{3,2,1,0:T(8,128)(2,1)}, u32[]{:S(2)}) copy-start(bf16[4,4,64,1536]{3,2,1,0:T(8,128)(2,1)} %get-tuple-element.79.hidden_hbm) | copy-start | bytes 9437188
  332.8 0.7 copy-start.4
  468.9 88.5 %copy-start.6 = (bf16[2,4,2,64,2048]{4,3,2,1,0:T(8,128)(2,1)S(1)}, bf16[2,4,2,64,2048]{4,3,2,1,0:T(8,128)(2,1)}, u32[]{:S(2)}) copy-start(bf16[2,4,2,64,2048]{4,3,2,1,0:T(8,128)(2,1)} %get-tuple-element.99) | copy-start | bytes 12582916
  557.4 5.0 copy-start.2
  562.5 3.7 copy-start.1
  566.2 3.7 copy-start
  566.2 3.7 copy-start.8
Sparse Core Ops, SparseCore 0:
  94.1 79.7 all-gather.1
  333.0 276.9 all-reduce.2

commit v9 on v8

--- a/solution.py
+++ b/solution.py
@@ -1075,6 +1075,7 @@
     heads = [(3.0, heads_begin)]
     heads += [(3.0, functools.partial(heads_block, j)) for j in range(seq_count)]
     heads += [(2.0, heads_end)]
+    heads += [(5.0, lambda: None)]
     for _, call in steps[:ready]:
         call()
     interleaved(steps[ready:], heads)

time: 739 us -> 738 us (level); the launches traced: 728 us -> 734 us
    pallas_call x1, Pallas kernels: 88.5 us -> 101 us  [scatter_blocks(): pl.pallas_call(functools.partial(scatter_kernel, pieces, count, seq_count...]
    pallas_call x1, Pallas kernels: 116 us -> 105 us  [last_step(): pl.pallas_call(functools.partial(last_kernel, pieces, count, seq_count, s...]
  transfers between devices with their start and end apart: 2 -> 2, of which waited for: 1 -> 1; matrix products, arithmetic and copies ran while one was open for 3% -> 3% of each run, Pallas kernels for 53% -> 54%
where the time goes in v9:
time: 738 us; the launch traced here: 734 us
  Pallas kernels  631 us (86%)
  matrix products  45.8 us (6%)
  waiting for transfers between devices  29.5 us (4%)
  between operations  14.4 us (2%)
    pallas_call x1, Pallas kernels, middle_step(): pl.pallas_call(functools.partial(middle_kernel, pieces, count), in_specs=...  129 us
    pallas_call x1, Pallas kernels, residual_step(): pl.pallas_call(functools.partial(residual_kernel, pieces, count, halves,...  121 us
    pallas_call x1, Pallas kernels, last_step(): pl.pallas_call(functools.partial(last_kernel, pieces, count, seq_count, s...  105 us
    pallas_call x1, Pallas kernels, scatter_blocks(): pl.pallas_call(functools.partial(scatter_kernel, pieces, count, seq_count...  101 us
    pallas_call x1, Pallas kernels, front_step(): pl.pallas_call(functools.partial(front_kernel, pieces, count, head_dim),...  78.8 us
    dot_general x7, matrix products, t_mm(): lax.dot_general(left, right, (((0,), (0,)), ((), ())), preferred_element_...  45.8 us
    pallas_call x1, Pallas kernels, gather_blocks(): pl.pallas_call(functools.partial(gather_kernel, count, batch), in_specs=[...  41.5 us
    all_gather x1, waiting for transfers between devices, gather(): return lax.all_gather(value, axis, axis=0, tiled=True)  29.5 us
  transfers between devices with their start and end apart: 2, of which 1 were waited for; matrix products, arithmetic and copies ran while one was open for 3% of the time, Pallas kernels for 54%

profile of v9, /device:TPU:0, one launch (start us, length us, event | category | flops | bytes accessed | tf_op | source)
XLA Modules:
  0.0 734.4 jit_solution(12957978385562775168)
XLA Ops:
  7.2 0.0 all-gather.2.cloned.1.call-start
  7.3 1.8 fusion.1
  9.1 2.5 copy.37
  11.7 0.7 compare_convert_fusion.1
  12.4 2.7 fusion
  15.1 78.8 %front.1 = (bf16[2,4,2,64,2048]{4,3,2,1,0:T(8,128)(2,1)}, f32[2,4,2,64,512]{4,3,2,1,0:T(8,128)}, bf16[2,4,2,64,512]{4,3,2,1,0:T(8,128)(2,1)}, f32[2,4,2,64,256]{...) custom-call(bf16[4,64,2048]{2,1,0:T(8,128)(2,1)} %bitcast.99, ...), custom_call_target="tpu_custom_call" | custom-call | flops 109250002944 | bytes 350550016 | tf_op jit(solution)/shard_map/front/pallas_call | solution.py:588
  93.9 0.0 all-gather.2.cloned.1.call-update
  93.9 0.0 all-reduce.3.cloned.1.call-start
  94.0 0.0 copy-done.3
  94.0 0.6 pad_add_fusion.place_ref
  94.6 41.5 %gather_blocks.1 = bf16[2,8,512,512]{3,2,1,0:T(8,128)(2,1)} custom-call(bf16[2,512,512]{2,1,0:T(8,128)(2,1)} %bitcast.132), custom_call_target="tpu_custom_call" | custom-call | flops 47149998080 | bytes 151290000 | tf_op jit(solution)/shard_map/gather_blocks/pallas_call | solution.py:864
  136.1 8.3 %attend.1 = (f32[2,512,512]{2,1,0:T(8,128)}, bf16[2,512,512]{2,1,0:T(8,128)(2,1)}, f32[2,512,128]{2,1,0:T(8,128)}) custom-call(s32[3]{0:T(128)} %pad_add_fusion.place_ref, bf16[2,512,512]{2,1,0:T(8,128)(2,1)} %bitcast.91, bf16[2,4096,512]{2,1,0:T(8,128)(2,1)} %bitcast.76, f32[2,512,512]{2,1,0:T(8,128)} %bitcast.86), custom_call_target="tpu_custom_call" | custom-call | flops 20700000256 | bytes 66420000 | tf_op jit(solution)/shard_map/attend/pallas_call | solution.py:144
  144.4 29.5 %all-gather.2.cloned.1.call-done = bf16[1024,2048]{1,0:T(8,128)(2,1)} async-done(((bf16[256,2048]{1,0:T(8,128)(2,1)}), bf16[1024,2048]{1,0:T(8,128)(2,1)}) %all-gather.2.cloned.1.call-update) | async-done | bytes 4194320 | tf_op jit(solution)/shard_map/all_gather | solution.py:1476
  173.9 129.0 %middle.1 = (f32[4,64,2048]{2,1,0:T(8,128)}, f32[1,2048]{1,0:T(1,128)}, bf16[4,4,64,2048]{3,2,1,0:T(8,128)(2,1)}, bf16[4,4,64,1536]{3,2,1,0:T(8,128)(2,1)}, bf16...) custom-call(bf16[2,4,2,64,512]{4,3,2,1,0:T(8,128)(2,1)} %bitcast.127, ...), custom_call_target="tpu_custom_call" | custom-call | flops 147200000000 | bytes 472320000 | tf_op jit(solution)/shard_map/middle/pallas_call | solution.py:742
  302.9 0.0 copy-start.9
  302.9 0.0 copy-start.10
  302.9 11.8 %bitcast_convert_fusion.1 = bf16[2048,1536]{1,0:T(8,128)(2,1)} fusion(bf16[4,4,64,2048]{3,2,1,0:T(8,128)(2,1)} %get-tuple-element.76, bf16[4,4,64,1536]{3,2,1,0:T(8,128)(2,1)} %get-tuple-element.77), kind=kOutput, calls=%fused_computation.1 | convolution fusion | flops 6445596672 | bytes 13631488 | tf_op jit(solution)/shard_map/dot_general | solution.py:28
  314.7 0.0 copy-done.9
  314.7 0.0 copy-done.10
  314.7 0.0 copy-start.7
  314.7 8.8 %bitcast_convert_fusion = bf16[2048,1536]{1,0:T(8,128)(2,1)} fusion(bf16[4,4,64,2048]{3,2,1,0:T(8,128)(2,1)S(1)} %copy-done.9, bf16[4,4,64,1536]{3,2,1,0:T(8,128)(2,1)S(1)} %copy-done.10), kind=kOutput, calls=%fused_computation | convolution fusion | flops 6445596672 | bytes 13631488 | tf_op jit(solution)/shard_map/dot_general | solution.py:28
  323.5 0.0 copy-done.5
  323.5 0.0 copy-done.7
  323.5 8.8 %convolution_convert_fusion = bf16[1536,2048]{1,0:T(8,128)(2,1)} fusion(bf16[1024,1536]{1,0:T(8,128)(2,1)S(1)} %bitcast.116, bf16[1024,2048]{1,0:T(8,128)(2,1)S(1)} %copy-done.5), kind=kOutput, calls=%fused_computation.2 | convolution fusion | flops 6445596672 | bytes 13631488 | tf_op jit(solution)/shard_map/dot_general | solution.py:28
  332.3 0.0 all-reduce.3.cloned.1.call-update
  332.3 0.6 copy-done.4
  333.0 0.1 lt.61
  333.0 0.1 lt.62
  333.1 0.1 copy.39
  333.3 0.7 compare_convert_fusion.valid_ref
  334.0 120.9 %residual.1 = (f32[4,64,2048]{2,1,0:T(8,128)}, bf16[2,4,2,64,2048]{4,3,2,1,0:T(8,128)(2,1)}, f32[1,128]{1,0:T(1,128)}, bf16[2,512,512]{2,1,0:T(8,128)(2,1)}, bf1...) custom-call(s32[3]{0:T(128)} %pad_add_fusion.place_ref, bf16[4,64,2048]{2,1,0:T(8,128)(2,1)} %bitcast.81, ...), custom_call_target="tpu_custom_call" | custom-call | flops 11500000256 | bytes 36900000 | tf_op jit(solution)/shard_map/residual/pallas_call | solution.py:1097
  454.9 19.1 %attend_back.1 = (bf16[2,512,512]{2,1,0:T(8,128)(2,1)}, bf16[2,4096,512]{2,1,0:T(8,128)(2,1)}, bf16[2,512,512]{2,1,0:T(8,128)(2,1)}, f32[1,128]{1,0:T(1,128)}) custom-call(s32[3]{0:T(128)} %pad_add_fusion.place_ref, bf16[2,512,512]{2,1,0:T(8,128)(2,1)} %bitcast.93, ...), custom_call_target="tpu_custom_call", output_to_operand_aliasing={{0}: (13, {}), {1}: (14, {}), {2}: (15, {})} | custom-call | flops 3449999872 | bytes 11070000 | tf_op jit(solution)/shard_map/attend_back/pallas_call | solution.py:312
  474.1 101.0 %scatter_blocks.1 = (bf16[2,512,512]{2,1,0:T(8,128)(2,1)}, bf16[4,64,2048]{2,1,0:T(8,128)(2,1)}, f32[1,128]{1,0:T(1,128)}) custom-call(bf16[2,8,512,512]{3,2,1,0:T(8,128)(2,1)} %bitcast.79, bf16[4,4,64,1536]{3,2,1,0:T(8,128)(2,1)} %get-tuple-element.79.hidden_hbm, bf16[1536,2048]{1,0:T(8,128)(2,1)} %wd_hbm.3, f32[4,64,2048]{2,1,0:T(8,128)} %get-tuple-element.81.middle_hbm, ...), custom_call_target="tpu_custom_call" | custom-call | flops 11500000256 | bytes 36900000 | tf_op jit(solution)/shard_map/scatter_blocks/pallas_call | solution.py:1204
  575.0 0.0 copy-done.6
  575.1 0.0 copy-start.2
  575.1 5.2 convolution_convert_fusion.3
  580.3 0.0 copy-done.2
  580.3 3.7 convolution_convert_fusion.2
  584.0 0.0 copy-done.1
  584.0 3.7 convolution_convert_fusion.4
  587.7 0.0 copy-done.8
  587.7 3.8 convolution_convert_fusion.1
  591.5 105.2 %last.1 = (f32[4,64,2048]{2,1,0:T(8,128)}, f32[16,128]{1,0:T(8,128)}, bf16[8,256,512]{2,1,0:T(8,128)(2,1)}, bf16[8,256,512]{2,1,0:T(8,128)(2,1)}, bf16[8,256,512...) custom-call(bf16[2,4,2,64,512]{4,3,2,1,0:T(8,128)(2,1)} %bitcast.94, bf16[2,4,2,64,512]{4,3,2,1,0:T(8,128)(2,1)} %bitcast.131, ...), custom_call_target="tpu_custom_call" | custom-call | flops 5750000128 | bytes 18450000 | tf_op jit(solution)/shard_map/last/pallas_call | solution.py:1377
  696.7 0.8 fusion.7
  697.4 0.6 dynamic-slice_bitcast_fusion
  698.0 0.6 dynamic-slice_bitcast_fusion.1
  698.6 1.3 slice_bitcast_fusion
  699.9 27.4 %widen.1 = (f32[128,2,2048]{2,1,0:T(2,128)}, bf16[128,2,2048]{2,1,0:T(2,128)(2,1)}, f32[2048,512]{1,0:T(8,128)}, f32[2048,256]{1,0:T(8,128)}, f32[2048,256]{1,0:...) custom-call(f32[2,128,2048]{2,1,0:T(8,128)} %bitcast.117, ...), custom_call_target="tpu_custom_call" | custom-call | flops 28750000128 | bytes 92250000 | tf_op jit(solution)/shard_map/widen/pallas_call | solution.py:1447
  (14 shorter events, 0.0 us)
Async XLA Ops:
  7.2 166.7 %all-gather.2.cloned.1.call-start = ((), (), s32[]{:S(2)}) async-start(), calls=%async_computation | async-start | bytes 5242880 | tf_op jit(solution)/shard_map/all_gather | solution.py:1476
  15.1 78.9 %copy-start.3 = (s32[2]{0:T(128)S(1)}, s32[2]{0:T(128)}, u32[]{:S(2)}) copy-start(s32[2]{0:T(128)} %param.17) | copy-start | bytes 28
  93.9 606.0 %all-reduce.3.cloned.1.call-start = ((), (), s32[]{:S(2)}) async-start(), calls=%async_computation.1 | async-start | bytes 37748736 | tf_op jit(solution)/shard_map/psum | solution.py:1534
  302.9 11.8 %copy-start.9 = (bf16[4,4,64,2048]{3,2,1,0:T(8,128)(2,1)S(1)}, bf16[4,4,64,2048]{3,2,1,0:T(8,128)(2,1)}, u32[]{:S(2)}) copy-start(bf16[4,4,64,2048]{3,2,1,0:T(8,128)(2,1)} %get-tuple-element.76) | copy-start | bytes 12582916
  302.9 11.8 %copy-start.10 = (bf16[4,4,64,1536]{3,2,1,0:T(8,128)(2,1)S(1)}, bf16[4,4,64,1536]{3,2,1,0:T(8,128)(2,1)}, u32[]{:S(2)}) copy-start(bf16[4,4,64,1536]{3,2,1,0:T(8,128)(2,1)} %get-tuple-element.78) | copy-start | bytes 9437188
  314.7 8.8 %copy-start.5 = (bf16[1024,2048]{1,0:T(8,128)(2,1)S(1)}, bf16[1024,2048]{1,0:T(8,128)(2,1)}, u32[]{:S(2)}) copy-start(bf16[1024,2048]{1,0:T(8,128)(2,1)} %all-gather.2.cloned.1.call-done) | copy-start | bytes 12582916
  314.7 8.8 %copy-start.7 = (bf16[4,4,64,1536]{3,2,1,0:T(8,128)(2,1)S(1)}, bf16[4,4,64,1536]{3,2,1,0:T(8,128)(2,1)}, u32[]{:S(2)}) copy-start(bf16[4,4,64,1536]{3,2,1,0:T(8,128)(2,1)} %get-tuple-element.79.hidden_hbm) | copy-start | bytes 9437188
  332.3 0.7 copy-start.4
  474.1 101.0 %copy-start.6 = (bf16[2,4,2,64,2048]{4,3,2,1,0:T(8,128)(2,1)S(1)}, bf16[2,4,2,64,2048]{4,3,2,1,0:T(8,128)(2,1)}, u32[]{:S(2)}) copy-start(bf16[2,4,2,64,2048]{4,3,2,1,0:T(8,128)(2,1)} %get-tuple-element.99) | copy-start | bytes 12582916
  575.1 5.2 copy-start.2
  580.3 3.7 copy-start.1
  584.0 3.7 copy-start
  584.0 3.7 copy-start.8
Sparse Core Ops, SparseCore 0:
  94.1 79.7 all-gather.1
  332.5 277.4 all-reduce.2
